TPU v7x, 32 devices: a whole 2x2x4 slice. The times are simulated.
32 devices in a mesh: layer: 4 (over z), ex: 8 (over y, x, core).
Axes of the slice: x: 2, y: 2, z: 4, core: 2. Of those that a mesh axis runs over, the one named last changes fastest.
Arguments:
- train_grads: bfloat16 [4096, 4, 4096], P('ex', 'layer'), may hold values from -0.3984375 to 0.3984375
- query_grads: bfloat16 [512, 4, 4096], P('ex', 'layer'), may hold values from -0.3984375 to 0.3984375
- in_precond: float32 [4, 64, 64], P('layer'), as said below
- out_precond: float32 [4, 64, 64], P('layer'), as said below
- pair_blocks: int32 [48], replicated, may hold values from -1 to 31, as said below
Outputs:
- tile_out: float32 [16, 48, 512], P('layer', 'ex')
Inputs may be any that keep to these rules, and one draw needn't show every extreme that they name: `pair_blocks`: slots p of training block p // 6 name query blocks (query block q holds judged examples q * 16 to q * 16 + 15 and lies on ex index q // 4), or -1 for an empty slot; the blocks named by one training block lie on distinct ex indices; empty slots come after filled ones; every training block fills at least 1 slots and some training block fills all 6. `in_precond`: each layer's factor is symmetric positive definite. `out_precond`: each layer's factor is symmetric positive definite.
All inputs are finite; a program needn't handle non-finite values.
Results may differ from a plain program's by a relative error of at most 0.0029.
Values may be sent and summed in bfloat16 or wider, within the bound.
No kernel may reach another device: no remote copies, remote signals or barrier semaphores. Data moves between devices by JAX's collectives and lax.ppermute only.
A program may use at most 64 MiB of HBM per device.

v0:
```python
import jax
import jax.numpy as jnp
from jax import lax
from jax.sharding import PartitionSpec as P

QBLK = 16


def precondition(blocks, in_precond, out_precond):
    leading = blocks.shape[:-2]
    layers = blocks.shape[-2]
    out_width = out_precond.shape[-1]
    in_width = in_precond.shape[-1]
    matrices = blocks.astype(jnp.float32).reshape((-1, layers, out_width, in_width))
    left_side = jnp.einsum("loj,rlji->rloi", out_precond, matrices, precision=lax.Precision.HIGHEST)
    precond = jnp.einsum("rloi,lik->rlok", left_side, in_precond, precision=lax.Precision.HIGHEST)
    return precond.reshape(leading + (layers, out_width * in_width)).astype(jnp.bfloat16)


def shards(train_grads, query_grads, in_precond, out_precond, pair_blocks):
    ex_count = lax.axis_size("ex")
    my_index = lax.axis_index("ex")
    layers = train_grads.shape[1]
    features = train_grads.shape[2]
    held_blocks = query_grads.shape[0] // QBLK
    slot_count = pair_blocks.shape[0] // ex_count
    wanted = pair_blocks.reshape(ex_count, slot_count)
    holder = jnp.where(wanted >= 0, wanted // held_blocks, -1)
    local_block = wanted - my_index * held_blocks
    matches = (holder == my_index)[:, :, None] & (
        local_block[:, :, None] == jnp.arange(held_blocks)[None, None, :]
    )
    picker = jnp.any(matches, axis=1).astype(jnp.bfloat16)
    blocks = query_grads.reshape(held_blocks, QBLK, layers, features)
    blocks = precondition(blocks, in_precond, out_precond)
    outgoing = jnp.einsum(
        "dk,kalf->dalf", picker, blocks, preferred_element_type=jnp.float32
    ).astype(jnp.bfloat16)
    received = lax.all_to_all(outgoing, "ex", split_axis=0, concat_axis=0, tiled=True)
    own_slots = lax.dynamic_slice_in_dim(pair_blocks, my_index * slot_count, slot_count, 0)
    source = jnp.where(own_slots >= 0, own_slots // held_blocks, -1)
    chooser = (source[:, None] == jnp.arange(ex_count)[None, :]).astype(jnp.bfloat16)
    chosen = jnp.einsum(
        "sn,nalf->salf", chooser, received, preferred_element_type=jnp.float32
    ).astype(jnp.bfloat16)
    return lax.psum_scatter(
        jnp.einsum("salf,rlf->asr", chosen, train_grads, preferred_element_type=jnp.float32),
        "layer",
        scatter_dimension=0,
        tiled=True,
    )


def solution(mesh):
    in_specs = (
        P("ex", "layer", None),
        P("ex", "layer", None),
        P("layer", None, None),
        P("layer", None, None),
        P(),
    )
    out_specs = P("layer", "ex", None)
    return jax.shard_map(shards, mesh=mesh, in_specs=in_specs, out_specs=out_specs, check_vma=False)
```

profile of v0, /device:TPU:0, one launch (start us, length us, event | category | flops | bytes accessed | tf_op | source)
XLA Modules:
  0.0 85.7 jit_solution(12948704476495567730)
XLA Ops:
  6.5 0.0 copy-start
  6.5 0.0 copy-start.1
  6.5 2.1 %reshape.82 = bf16[64,64,64]{2,1,0:T(8,128)(2,1)S(1)} reshape(bf16[64,1,4096]{2,0,1:T(8,128)(2,1)} %param.6) | data formatting | bytes 1048576 | tf_op jit(solution)/shard_map/reshape.1
  8.6 0.0 copy-done
  8.6 1.2 %fusion.19 = f32[64,64,64]{2,1,0:T(8,128)S(1)} fusion(bf16[64,64,64]{2,1,0:T(8,128)(2,1)S(1)} %reshape.82, f32[1,64,64]{2,1,0:T(8,128)S(1)} %copy-done), kind=kOutput, calls=%fused_computation.15 | convolution fusion | flops 201326592 | bytes 1589248 | tf_op jit(solution)/shard_map/loj,rlji->rloi/dot_general | solution.py:15
  9.9 0.0 copy-done.1
  9.9 0.0 copy-start.2
  9.9 3.5 %fusion.8 = bf16[64,1,64,64]{3,2,0,1:T(8,128)(2,1)S(1)} fusion(f32[64,64,64]{2,1,0:T(8,128)S(1)} %fusion.19, f32[1,64,64]{2,1,0:T(8,128)S(1)} %copy-done.1), kind=kOutput, calls=%fused_computation.8 | convolution fusion | flops 201588736 | bytes 1589248 | tf_op jit(solution)/shard_map/rloi,lik->rlok/dot_general | solution.py:16
  13.4 0.8 convert_element_type.35
  14.2 0.0 copy-done.2
  14.2 0.1 reshape.81
  14.4 0.1 copy.14
  14.4 0.1 copy.13
  14.6 0.6 fusion
  15.2 1.5 %copy.18 = bf16[8,16,1,4096]{3,1,2,0:T(8,128)(2,1)} copy(bf16[8,16,1,4096]{3,0,1,2:T(8,128)(2,1)S(1)} %fusion) | data formatting | bytes 2097152 | tf_op jit(solution)/shard_map/convert_element_type | solution.py:38
  16.7 5.2 %all-to-all-start = ((bf16[8,16,1,4096]{3,1,2,0:T(8,128)(2,1)}), bf16[8,16,1,4096]{3,1,2,0:T(8,128)(2,1)S(1)}, u32[]{:S(2)}, u32[]{:S(2)}) async-start(bf16[8,16,1,4096]{3,1,2,0:T(8,128)(2,1)} %copy.18), calls=%async_computation | async-start | bytes 2097152 | tf_op jit(solution)/shard_map/all_to_all | solution.py:39
  21.9 0.0 all-reduce.3.cloned.1.call-start
  21.9 0.1 compare_select_fusion
  22.0 15.3 %all-to-all-done = bf16[8,16,1,4096]{3,1,2,0:T(8,128)(2,1)S(1)} async-done(((bf16[8,16,1,4096]{3,1,2,0:T(8,128)(2,1)}), bf16[8,16,1,4096]{3,1,2,0:T(8,128)(2,1)S(1)}, u32[]{:S(2)}, u32[]{:S(2)}) %all-to-all-start) | async-done | bytes 1048608 | tf_op jit(solution)/shard_map/all_to_all | solution.py:39
  37.3 1.2 %convolution_convert_fusion = bf16[6,16,4096]{2,0,1:T(8,128)(2,1)S(1)} fusion(bf16[8,16,1,4096]{3,1,2,0:T(8,128)(2,1)S(1)} %all-to-all-done, s32[6]{0:T(128)S(1)} %compare_select_fusion), kind=kOutput, calls=%fused_computation | convolution fusion | flops 6684720 | bytes 1835032 | tf_op jit(solution)/shard_map/sn,nalf->salf/dot_general | solution.py:43
  38.5 0.0 copy-start.3
  38.6 4.4 %fusion.11 = f32[16,6,512]{2,0,1:T(8,128)} fusion(bf16[512,1,4096]{2,0,1:T(8,128)(2,1)} %param.5, bf16[6,16,4096]{2,0,1:T(8,128)(2,1)S(1)} %convolution_convert_fusion), kind=kOutput, calls=%fused_computation.9 | convolution fusion | flops 402653184 | bytes 5177344 | tf_op jit(solution)/shard_map/salf,rlf->asr/dot_general | solution.py:47
  42.9 0.0 all-reduce.3.cloned.1.call-update
  42.9 0.0 copy-done.3
  43.0 0.6 dynamic-slice
  44.2 33.1 %all-reduce.3.cloned.1.call-done = f32[16,6,512]{2,0,1:T(8,128)} async-done(((f32[16,6,512]{2,0,1:T(8,128)}), f32[16,6,512]{2,0,1:T(8,128)}) %all-reduce.3.cloned.1.call-update) | async-done | bytes 196624
  77.3 1.5 %constant_dynamic-slice_fusion = f32[4,6,512]{2,0,1:T(4,128)} fusion(f32[16,6,512]{2,0,1:T(8,128)} %all-reduce.3.cloned.1.call-done, u32[]{:T(128)S(6)} %multiply.1), kind=kLoop, calls=%fused_computation.39 | loop fusion | bytes 98308
  (3 shorter events, 0.0 us)
Async XLA Ops:
  6.5 2.1 %copy-start = (f32[1,64,64]{2,1,0:T(8,128)S(1)}, f32[1,64,64]{2,1,0:T(8,128)}, u32[]{:S(2)}) copy-start(f32[1,64,64]{2,1,0:T(8,128)} %param.8) | copy-start | bytes 49156
  6.5 3.3 %copy-start.1 = (f32[1,64,64]{2,1,0:T(8,128)S(1)}, f32[1,64,64]{2,1,0:T(8,128)}, u32[]{:S(2)}) copy-start(f32[1,64,64]{2,1,0:T(8,128)} %param.7) | copy-start | bytes 49156
  9.9 4.4 %copy-start.2 = (s32[48]{0:T(128)S(1)}, s32[48]{0:T(128)}, u32[]{:S(2)}) copy-start(s32[48]{0:T(128)} %param.9) | copy-start | bytes 580
  16.7 20.6 %all-to-all-start = ((bf16[8,16,1,4096]{3,1,2,0:T(8,128)(2,1)}), bf16[8,16,1,4096]{3,1,2,0:T(8,128)(2,1)S(1)}, u32[]{:S(2)}, u32[]{:S(2)}) async-start(bf16[8,16,1,4096]{3,1,2,0:T(8,128)(2,1)} %copy.18), calls=%async_computation | async-start | bytes 2097152 | tf_op jit(solution)/shard_map/all_to_all | solution.py:39
  21.9 55.4 %all-reduce.3.cloned.1.call-start = ((), (), s32[]{:S(2)}) async-start(), calls=%async_computation.1 | async-start | bytes 393216
  38.5 4.4 %copy-start.3 = (u32[32]{0:T(128)S(1)}, u32[32]{0:T(128)}, u32[]{:S(2)}) copy-start(u32[32]{0:T(128)} %constant.46) | copy-start | bytes 388
Sparse Core Ops, SparseCore 0:
  43.1 34.2 all-reduce.2
where the time goes:
time: 85.9 us; the launch traced here: 85.7 us
  waiting for transfers between devices  48.4 us (56%)
  between operations  14.2 us (17%)
  matrix products  11 us (13%)
  local copies, waits for them, and re-layouts  6.8 us (8%)
  starting transfers between devices  5.21 us (6%)
    unnamed x2, waiting for transfers between devices  33.1 us
    all_to_all x1, waiting for transfers between devices, shards(): lax.all_to_all(outgoing, 'ex', split_axis=0, concat_axis=0, tiled=True)  15.3 us
    all_to_all x1, starting transfers between devices, shards(): lax.all_to_all(outgoing, 'ex', split_axis=0, concat_axis=0, tiled=True)  5.17 us
    dot_general x1, matrix products, shards(): jnp.einsum('salf,rlf->asr', chosen, train_grads, preferred_element_type=j...  4.37 us
    dot_general x1, matrix products, precondition(): jnp.einsum('rloi,lik->rlok', left_side, in_precond, precision=lax.Precisi...  3.53 us
    unnamed x10, local copies, waits for them, and re-layouts  2.13 us
    another operation x1, local copies, waits for them, and re-layouts  2.06 us
  transfers between devices with their start and end apart: 2, of which 2 were waited for; matrix products, arithmetic and copies ran while one was open for 1% of the time, Pallas kernels for 0%

commit v1 on v0

v1 whole, which is shorter than its diff:
```python
import functools

import jax
import jax.numpy as jnp
from jax import lax
from jax.experimental import pallas as pl
from jax.experimental.pallas import tpu as pltpu
from jax.sharding import PartitionSpec as P

QBLK = 16
LANES = 128
F32 = jnp.float32
BF16 = jnp.bfloat16

ANY = pl.BlockSpec(memory_space=pl.ANY)
VMEM = pl.BlockSpec(memory_space=pltpu.VMEM)
SMEM = pl.BlockSpec(memory_space=pltpu.SMEM)


def split_bf16(x):
    high = x.astype(BF16)
    return high, (x - high.astype(F32)).astype(BF16)


def over_slots(slots, body, init):
    if slots > 8:
        return lax.fori_loop(0, slots, body, init)
    for slot in range(slots):
        init = body(slot, init)
    return init


def pick_kernel(ex, held, slots, pairs_ref, query_ref, *rest):
    outs, sems = rest[:ex], rest[ex]
    me = lax.axis_index("ex")
    copies = []
    for k in reversed(range(ex)):
        first = (me ^ k) * slots

        def body(slot, block):
            local = pairs_ref[first + slot] - me * held
            return jnp.where((local >= 0) & (local < held), local, block)

        block = over_slots(slots, body, jnp.int32(0))
        start = pl.multiple_of(block * QBLK, QBLK)
        copy = pltpu.make_async_copy(query_ref.at[pl.ds(start, QBLK)], outs[k], sems.at[k])
        copy.start()
        copies.append(copy)
    for copy in copies:
        copy.wait()


def factor_kernel(out_ref, in_ref, left_ref, right_ref):
    width = out_ref.shape[0]
    in_width = in_ref.shape[0]
    half = left_ref.shape[2]
    span = right_ref.shape[1]
    outs = split_bf16(out_ref[...])
    ins = split_bf16(in_ref[...])
    row = lax.broadcasted_iota(jnp.int32, (half, width), 0) // QBLK
    row_o = lax.broadcasted_iota(jnp.int32, (half, width), 1)
    col = lax.broadcasted_iota(jnp.int32, (width, half), 1) // QBLK
    col_o = lax.broadcasted_iota(jnp.int32, (width, half), 0)
    same = (lax.broadcasted_iota(jnp.int32, (half, half), 0) % QBLK) == (
        lax.broadcasted_iota(jnp.int32, (half, half), 1) % QBLK
    )
    for h in range(2):
        for s in range(2):
            pick_rows = (row * 2 + s == row_o).astype(BF16)
            rows = jnp.dot(pick_rows, outs[h], preferred_element_type=F32).astype(BF16)
            for t in range(2):
                pick_cols = (col * 2 + (s ^ t) == col_o).astype(BF16)
                spread = jnp.dot(rows, pick_cols, preferred_element_type=F32)
                left_ref[h, s, :, t * half : (t + 1) * half] = jnp.where(same, spread, 0.0).astype(BF16)
        up = (
            lax.broadcasted_iota(jnp.int32, (span, in_width), 0) % in_width
            == lax.broadcasted_iota(jnp.int32, (span, in_width), 1)
        ).astype(BF16)
        down = (
            lax.broadcasted_iota(jnp.int32, (in_width, span), 1) % in_width
            == lax.broadcasted_iota(jnp.int32, (in_width, span), 0)
        ).astype(BF16)
        wide = jnp.dot(
            jnp.dot(up, ins[h], preferred_element_type=F32).astype(BF16), down, preferred_element_type=F32
        )
        block = (lax.broadcasted_iota(jnp.int32, (span, span), 0) // in_width) == (
            lax.broadcasted_iota(jnp.int32, (span, span), 1) // in_width
        )
        right_ref[h] = jnp.where(block, wide, 0.0).astype(BF16)


def prepare(blocks, left_ref, right_ref, prep_ref):
    chunks = blocks[0].shape[1] // LANES
    half = LANES // 2
    stacked = []
    for block in blocks:
        tall = jnp.concatenate([block[:, c * LANES : (c + 1) * LANES] for c in range(chunks)], axis=0)
        turned = jnp.concatenate([tall[:, half:], tall[:, :half]], axis=1)
        stacked.append(jnp.concatenate([tall, turned], axis=0))
    stacked = jnp.concatenate(stacked, axis=1)
    parts = [
        jnp.dot(left_ref[0, s], stacked, preferred_element_type=F32)
        + jnp.dot(left_ref[1, s], stacked, preferred_element_type=F32)
        for s in range(2)
    ]
    lane = lax.broadcasted_iota(jnp.int32, parts[0].shape, 1) % LANES
    high, low = split_bf16(jnp.where(lane < half, parts[0], parts[1]))
    done = (
        jnp.dot(high, right_ref[0], preferred_element_type=F32)
        + jnp.dot(low, right_ref[0], preferred_element_type=F32)
        + jnp.dot(high, right_ref[1], preferred_element_type=F32)
    ).astype(BF16)
    for b in range(len(blocks)):
        for c in range(chunks):
            prep_ref[b * QBLK : (b + 1) * QBLK, c * LANES : (c + 1) * LANES] = done[
                c * QBLK : (c + 1) * QBLK, b * LANES : (b + 1) * LANES
            ]


def tile_kernel(ex, layer, *refs):
    blocks = refs[:ex]
    train_ref, left_ref, right_ref = refs[ex : ex + 3]
    outs = refs[ex + 3 : ex + 3 + layer]
    prep_ref, tile_ref = refs[ex + 3 + layer :]
    rows = QBLK // layer
    for pair in range(ex // 2):
        prepare(
            [blocks[2 * pair][...], blocks[2 * pair + 1][...]],
            left_ref,
            right_ref,
            prep_ref.at[pl.ds(pair * 2 * QBLK, 2 * QBLK)],
        )
    tile = lax.dot_general(
        prep_ref[...], train_ref[...], (((1,), (1,)), ((), ())), preferred_element_type=F32
    )
    me = lax.axis_index("layer")
    for c in range(tile_ref.shape[0]):
        lanes = slice(c * LANES, (c + 1) * LANES)
        tile_ref[c] = tile[:, lanes]
        for m in range(layer):
            first = (me ^ m) * rows
            part = jnp.concatenate(
                [tile_ref[c, pl.ds(first + j, ex, stride=QBLK), :] for j in range(rows)], axis=0
            )
            outs[m][:, lanes] = part.astype(outs[m].dtype)


def finish_kernel(ex, layer, held, slots, pairs_ref, *refs):
    parts, out_ref, sum_ref = refs[:layer], refs[layer], refs[layer + 1]
    total = parts[0][...]
    for part in parts[1:]:
        total = total + part[...].astype(F32)
    chunks = sum_ref.shape[0]
    for c in range(chunks):
        sum_ref[c] = total[:, c * LANES : (c + 1) * LANES]
    rows = QBLK // layer
    me = lax.axis_index("ex")

    def body(slot, carry):
        q = pairs_ref[me * slots + slot]
        k = jnp.where(q >= 0, (q // held) ^ me, 0)
        for c in range(chunks):
            value = sum_ref[c, pl.ds(k, rows, stride=ex), :]
            out_ref[slot, :, c * LANES : (c + 1) * LANES] = jnp.where(q >= 0, value, jnp.zeros_like(value))
        return carry

    over_slots(slots, body, 0)


def shards(train_grads, query_grads, in_precond, out_precond, pair_blocks):
    ex = lax.axis_size("ex")
    layer = lax.axis_size("layer")
    train_rows, layers, features = train_grads.shape
    assert layers == 1
    held = query_grads.shape[0] // QBLK
    slots = pair_blocks.shape[0] // ex
    rows = QBLK // layer
    train = train_grads.reshape(train_rows, features)
    query = query_grads.reshape(query_grads.shape[0], features)
    in_factor = in_precond.reshape(in_precond.shape[1:])
    out_factor = out_precond.reshape(out_precond.shape[1:])
    limit = pltpu.CompilerParams(vmem_limit_bytes=48 * 2**20)

    picked = pl.pallas_call(
        functools.partial(pick_kernel, ex, held, slots),
        out_shape=[jax.ShapeDtypeStruct((QBLK, features), BF16)] * ex,
        in_specs=[SMEM, ANY],
        out_specs=[ANY] * ex,
        scratch_shapes=[pltpu.SemaphoreType.DMA((ex,))],
        name="pick",
    )(pair_blocks, query)

    blocks = [None] * ex
    blocks[0] = picked[0]
    for k in reversed(range(1, ex)):
        blocks[k] = lax.ppermute(picked[k], "ex", [(i, i ^ k) for i in range(ex)])

    stack = features // LANES * QBLK
    span = 2 * LANES
    left, right = pl.pallas_call(
        factor_kernel,
        out_shape=[
            jax.ShapeDtypeStruct((2, 2, stack, 2 * stack), BF16),
            jax.ShapeDtypeStruct((2, span, span), BF16),
        ],
        in_specs=[VMEM, VMEM],
        out_specs=[VMEM, VMEM],
        compiler_params=limit,
        name="factors",
    )(out_factor, in_factor)

    parts = pl.pallas_call(
        functools.partial(tile_kernel, ex, layer),
        out_shape=[jax.ShapeDtypeStruct((rows * ex, train_rows), F32)]
        + [jax.ShapeDtypeStruct((rows * ex, train_rows), BF16)] * (layer - 1),
        in_specs=[VMEM] * (ex + 3),
        out_specs=[VMEM] * layer,
        scratch_shapes=[
            pltpu.VMEM((ex * QBLK, features), BF16),
            pltpu.VMEM((train_rows // LANES, ex * QBLK, LANES), F32),
        ],
        compiler_params=limit,
        name="tiles",
    )(*blocks, train, left, right)

    terms = [parts[0]] + [
        lax.ppermute(parts[m], "layer", [(i, i ^ m) for i in range(layer)]) for m in range(1, layer)
    ]
    out = pl.pallas_call(
        functools.partial(finish_kernel, ex, layer, held, slots),
        out_shape=jax.ShapeDtypeStruct((slots, rows, train_rows), F32),
        in_specs=[SMEM] + [VMEM] * layer,
        out_specs=VMEM,
        scratch_shapes=[pltpu.VMEM((train_rows // LANES, rows * ex, LANES), F32)],
        name="finish",
    )(pair_blocks, *terms)
    return jnp.transpose(out, (1, 0, 2))


def solution(mesh):
    in_specs = (
        P("ex", "layer", None),
        P("ex", "layer", None),
        P("layer", None, None),
        P("layer", None, None),
        P(),
    )
    out_specs = P("layer", "ex", None)
    return jax.shard_map(shards, mesh=mesh, in_specs=in_specs, out_specs=out_specs, check_vma=False)
```

time: 85.9 us -> 76.6 us (0.89)
  Pallas kernels: 0 us -> 46.8 us
  waiting for transfers between devices: 48.4 us -> 7.84 us
  between operations: 14.2 us -> 0.06 us
  matrix products: 11 us -> 0 us
  starting transfers between devices: 5.21 us -> 13.7 us
  local copies, waits for them, and re-layouts: 6.8 us -> 7.76 us
    pallas_call x0 -> x4, Pallas kernels: none -> 46.8 us  [the longest x1 33.6 us: shards(): pl.pallas_call(functools.partial(pick_kernel, ex, held, slots), out_shape...]
    unnamed x2 -> x0, waiting for transfers between devices: 33.1 us -> none
    all_to_all x1 -> x0, waiting for transfers between devices: 15.3 us -> none  [shards(): lax.all_to_all(outgoing, 'ex', split_axis=0, concat_axis=0, tiled=True)]
    ppermute x0 -> x10, starting transfers between devices: none -> 13.7 us  [the longest x7 9.25 us: shards(): blocks[k] = lax.ppermute(picked[k], 'ex', [(i, i ^ k) for i in range(ex)])]
    dot_general x5 -> x0, matrix products: 11 us -> none  [the longest x1 4.37 us: shards(): jnp.einsum('salf,rlf->asr', chosen, train_grads, preferred_element_type=j...]
    ppermute x0 -> x10, waiting for transfers between devices: none -> 7.84 us  [the longest x3 5.7 us: shards(): lax.ppermute(parts[m], 'layer', [(i, i ^ m) for i in range(layer)])]
    unnamed x10 -> x18, local copies, waits for them, and re-layouts: 2.13 us -> 7.76 us
    all_to_all x1 -> x0, starting transfers between devices: 5.17 us -> none  [shards(): lax.all_to_all(outgoing, 'ex', split_axis=0, concat_axis=0, tiled=True)]
  transfers between devices with their start and end apart: 2 -> 10, of which waited for: 2 -> 4; matrix products, arithmetic and copies ran while one was open for 1% -> 0% of each run, Pallas kernels for 0% -> 3%
where the time goes in v1:
time: 76.6 us; the launch traced here: 76.2 us
  Pallas kernels  46.8 us (61%)
  starting transfers between devices  13.7 us (18%)
  waiting for transfers between devices  7.84 us (10%)
  local copies, waits for them, and re-layouts  7.76 us (10%)
    pallas_call x1, Pallas kernels, shards(): pl.pallas_call(functools.partial(pick_kernel, ex, held, slots), out_shape...  33.6 us
    pallas_call x1, Pallas kernels, shards(): pl.pallas_call(functools.partial(tile_kernel, ex, layer), out_shape=[jax....  9.6 us
    ppermute x7, starting transfers between devices, shards(): blocks[k] = lax.ppermute(picked[k], 'ex', [(i, i ^ k) for i in range(ex)])  9.25 us
    unnamed x18, local copies, waits for them, and re-layouts  7.76 us
    ppermute x3, waiting for transfers between devices, shards(): lax.ppermute(parts[m], 'layer', [(i, i ^ m) for i in range(layer)])  5.7 us
    ppermute x3, starting transfers between devices, shards(): lax.ppermute(parts[m], 'layer', [(i, i ^ m) for i in range(layer)])  4.48 us
    ppermute x7, waiting for transfers between devices, shards(): blocks[k] = lax.ppermute(picked[k], 'ex', [(i, i ^ k) for i in range(ex)])  2.14 us
    pallas_call x1, Pallas kernels, shards(): pl.pallas_call(factor_kernel, out_shape=[jax.ShapeDtypeStruct((2, 2, stac...  2.06 us
  transfers between devices with their start and end apart: 10, of which 4 were waited for; matrix products, arithmetic and copies ran while one was open for 0% of the time, Pallas kernels for 3%

profile of v1, /device:TPU:0, one launch (start us, length us, event | category | flops | bytes accessed | tf_op | source)
XLA Modules:
  0.0 76.2 jit_solution(5552851444789137757)
XLA Ops:
  0.0 33.6 %pick.1 = (bf16[16,4096]{1,0:T(8,128)(2,1)}, bf16[16,4096]{1,0:T(8,128)(2,1)}, bf16[16,4096]{1,0:T(8,128)(2,1)}, bf16[16,4096]{1,0:T(8,128)(2,1)}, bf16[16,4096]...) custom-call(s32[48]{0:T(128)} %pairs_ref.3, bf16[64,4096]{1,0:T(8,128)(2,1)} %bitcast.8), custom_call_target="tpu_custom_call" | custom-call | tf_op jit(solution)/shard_map/pick/pallas_call | solution.py:184
  33.6 0.5 collective-permute-start
  34.1 2.6 %collective-permute-start.1 = (bf16[16,4096]{1,0:T(8,128)(2,1)}, bf16[16,4096]{1,0:T(8,128)(2,1)S(1)}, u32[]{:S(2)}, u32[]{:S(2)}) collective-permute-start(bf16[16,4096]{1,0:T(8,128)(2,1)} %get-tuple-element.21), channel_id=1, source_target_pairs={{0,2},{1,3},{2,0},{3,1},{4,6},{5,7},{6,4},{7,5},{8,10},{9,11},{10,... | collective-permute-start | bytes 393224 | tf_op jit(solution)/shard_map/ppermute | solution.py:196
  36.7 0.1 collective-permute-start.2
  36.8 1.8 %collective-permute-start.3 = (bf16[16,4096]{1,0:T(8,128)(2,1)}, bf16[16,4096]{1,0:T(8,128)(2,1)S(1)}, u32[]{:S(2)}, u32[]{:S(2)}) collective-permute-start(bf16[16,4096]{1,0:T(8,128)(2,1)} %get-tuple-element.23), channel_id=1, source_target_pairs={{0,4},{1,5},{2,6},{3,7},{4,0},{5,1},{6,2},{7,3},{8,12},{9,13},{10,... | collective-permute-start | bytes 393224 | tf_op jit(solution)/shard_map/ppermute | solution.py:196
  38.6 0.0 collective-permute-start.4
  38.6 0.0 collective-permute-done.refs_1_
  38.6 2.6 %collective-permute-start.5 = (bf16[16,4096]{1,0:T(8,128)(2,1)}, bf16[16,4096]{1,0:T(8,128)(2,1)S(1)}, u32[]{:S(2)}, u32[]{:S(2)}) collective-permute-start(bf16[16,4096]{1,0:T(8,128)(2,1)} %get-tuple-element.25), channel_id=1, source_target_pairs={{0,6},{1,7},{2,4},{3,5},{4,2},{5,3},{6,0},{7,1},{8,14},{9,15},{10,... | collective-permute-start | bytes 393224 | tf_op jit(solution)/shard_map/ppermute | solution.py:196
  41.2 0.1 collective-permute-done.1.refs_2_
  41.3 1.7 %collective-permute-start.6 = (bf16[16,4096]{1,0:T(8,128)(2,1)}, bf16[16,4096]{1,0:T(8,128)(2,1)S(1)}, u32[]{:S(2)}, u32[]{:S(2)}) collective-permute-start(bf16[16,4096]{1,0:T(8,128)(2,1)} %get-tuple-element.26), channel_id=1, source_target_pairs={{0,7},{1,6},{2,5},{3,4},{4,3},{5,2},{6,1},{7,0},{8,15},{9,14},{10,... | collective-permute-start | bytes 393224 | tf_op jit(solution)/shard_map/ppermute | solution.py:196
  43.0 0.0 copy-start.4
  43.0 0.8 copy-done.4
  43.7 0.0 copy-start.5
  43.8 0.8 copy-done.5
  44.5 2.1 %factors.1 = (bf16[2,2,512,1024]{3,2,1,0:T(8,128)(2,1)S(1)}, bf16[2,256,256]{2,1,0:T(8,128)(2,1)S(1)}) custom-call(f32[64,64]{1,0:T(8,128)S(1)} %bitcast.6, f32[64,64]{1,0:T(8,128)S(1)} %bitcast.7), custom_call_target="tpu_custom_call" | custom-call | tf_op jit(solution)/shard_map/factors/pallas_call | solution.py:200
  46.6 0.0 copy-start.1
  46.6 1.9 %copy-done.1 = bf16[2,2,512,1024]{3,2,1,0:T(8,128)(2,1)} copy-done((bf16[2,2,512,1024]{3,2,1,0:T(8,128)(2,1)}, bf16[2,2,512,1024]{3,2,1,0:T(8,128)(2,1)S(1)}, u32[]{:S(2)}) %copy-start.1) | copy-done | bytes 4194328
  48.5 0.0 collective-permute-done.2.refs_3_
  48.5 0.0 collective-permute-done.3.refs_4_
  48.5 2.0 %collective-permute-done.4.refs_5_ = bf16[16,4096]{1,0:T(8,128)(2,1)S(1)} collective-permute-done((bf16[16,4096]{1,0:T(8,128)(2,1)}, bf16[16,4096]{1,0:T(8,128)(2,1)S(1)}, u32[]{:S(2)}, u32[]{:S(2)}) %collective-permute-start.4) | collective-permute-done | bytes 131104 | tf_op jit(solution)/shard_map/ppermute | solution.py:196
  50.5 0.0 collective-permute-done.5.refs_6_
  50.5 0.0 collective-permute-done.6.refs_7_
  50.6 0.0 copy-start
  50.6 2.2 %copy-done = bf16[512,1,4096]{2,0,1:T(8,128)(2,1)S(1)} copy-done((bf16[512,1,4096]{2,0,1:T(8,128)(2,1)S(1)}, bf16[512,1,4096]{2,0,1:T(8,128)(2,1)}, u32[]{:S(2)}) %copy-start) | copy-done | bytes 4194328
  52.7 0.0 copy-start.2
  52.7 0.9 %copy-done.2 = bf16[16,4096]{1,0:T(8,128)(2,1)S(1)} copy-done((bf16[16,4096]{1,0:T(8,128)(2,1)S(1)}, bf16[16,4096]{1,0:T(8,128)(2,1)}, u32[]{:S(2)}) %copy-start.2) | copy-done | bytes 131096
  53.6 9.6 %tiles.1 = (f32[32,512]{1,0:T(8,128)S(1)}, bf16[32,512]{1,0:T(8,128)(2,1)S(1)}, bf16[32,512]{1,0:T(8,128)(2,1)S(1)}, bf16[32,512]{1,0:T(8,128)(2,1)S(1)}) custom-call(bf16[16,4096]{1,0:T(8,128)(2,1)S(1)} %copy-done.2, bf16[16,4096]{1,0:T(8,128)(2,1)S(1)} %collective-permute-done.refs_1_, bf16[16,4096]{1,0:T(8,128)(2,1)S(1)} %collective-permute-done.1.refs_2_, ...), custom_call_target="tpu_custom_call" | custom-call | tf_op jit(solution)/shard_map/tiles/pallas_call | solution.py:212
  63.3 0.0 copy-start.3
  63.3 0.6 copy-done.3
  63.9 1.9 %collective-permute-start.7 = (bf16[32,512]{1,0:T(8,128)(2,1)S(1)}, bf16[32,512]{1,0:T(8,128)(2,1)S(1)}, u32[]{:S(2)}, u32[]{:S(2)}) collective-permute-start(bf16[32,512]{1,0:T(8,128)(2,1)S(1)} %get-tuple-element.30), channel_id=1, source_target_pairs={{0,8},{8,0},{16,24},{24,16},{1,9},{9,1},{17,25},{25,17},{2,10},{10... | collective-permute-start | bytes 98312 | tf_op jit(solution)/shard_map/ppermute | solution.py:227
  65.7 2.6 %collective-permute-start.8 = (bf16[32,512]{1,0:T(8,128)(2,1)S(1)}, bf16[32,512]{1,0:T(8,128)(2,1)S(1)}, u32[]{:S(2)}, u32[]{:S(2)}) collective-permute-start(bf16[32,512]{1,0:T(8,128)(2,1)S(1)} %get-tuple-element.31), channel_id=1, source_target_pairs={{0,16},{8,24},{16,0},{24,8},{1,17},{9,25},{17,1},{25,9},{2,18},{10... | collective-permute-start | bytes 98312 | tf_op jit(solution)/shard_map/ppermute | solution.py:227
  68.4 0.0 collective-permute-start.9
  68.4 0.0 collective-permute-done.7.refs_1_
  68.4 0.0 copy-start.6
  68.4 2.7 %collective-permute-done.8.refs_2_ = bf16[32,512]{1,0:T(8,128)(2,1)S(1)} collective-permute-done((bf16[32,512]{1,0:T(8,128)(2,1)S(1)}, bf16[32,512]{1,0:T(8,128)(2,1)S(1)}, u32[]{:S(2)}, u32[]{:S(2)}) %collective-permute-start.8) | collective-permute-done | bytes 32800 | tf_op jit(solution)/shard_map/ppermute | solution.py:227
  71.1 0.0 copy-start.7
  71.1 2.9 %collective-permute-done.9.refs_3_ = bf16[32,512]{1,0:T(8,128)(2,1)S(1)} collective-permute-done((bf16[32,512]{1,0:T(8,128)(2,1)S(1)}, bf16[32,512]{1,0:T(8,128)(2,1)S(1)}, u32[]{:S(2)}, u32[]{:S(2)}) %collective-permute-start.9) | collective-permute-done | bytes 32800 | tf_op jit(solution)/shard_map/ppermute | solution.py:227
  74.1 0.0 copy-start.8
  74.1 0.0 copy-done.6
  74.1 0.0 copy-done.7
  74.1 0.6 copy-done.8
  74.7 1.5 %finish.1 = f32[6,4,512]{2,1,0:T(4,128)} custom-call(s32[48]{0:T(128)} %pairs_ref.3, f32[32,512]{1,0:T(8,128)} %copy-done.3, bf16[32,512]{1,0:T(8,128)(2,1)} %copy-done.6, bf16[32,512]{1,0:T(8,128)(2,1)} %copy-done.7, bf16[32,512]{1,0:T(8,128)(2,1)} %copy-done.8), custom_call_target="tpu_custom_call" | custom-call | tf_op jit(solution)/shard_map/finish/pallas_call | solution.py:229
Async XLA Ops:
  33.6 4.9 %collective-permute-start = (bf16[16,4096]{1,0:T(8,128)(2,1)}, bf16[16,4096]{1,0:T(8,128)(2,1)S(1)}, u32[]{:S(2)}, u32[]{:S(2)}) collective-permute-start(bf16[16,4096]{1,0:T(8,128)(2,1)} %get-tuple-element.20), channel_id=1, source_target_pairs={{0,1},{1,0},{2,3},{3,2},{4,5},{5,4},{6,7},{7,6},{8,9},{9,8},{10,11... | collective-permute-start | bytes 393224 | tf_op jit(solution)/shard_map/ppermute | solution.py:196
  34.1 7.1 %collective-permute-start.1 = (bf16[16,4096]{1,0:T(8,128)(2,1)}, bf16[16,4096]{1,0:T(8,128)(2,1)S(1)}, u32[]{:S(2)}, u32[]{:S(2)}) collective-permute-start(bf16[16,4096]{1,0:T(8,128)(2,1)} %get-tuple-element.21), channel_id=1, source_target_pairs={{0,2},{1,3},{2,0},{3,1},{4,6},{5,7},{6,4},{7,5},{8,10},{9,11},{10,... | collective-permute-start | bytes 393224 | tf_op jit(solution)/shard_map/ppermute | solution.py:196
  36.7 11.8 %collective-permute-start.2 = (bf16[16,4096]{1,0:T(8,128)(2,1)}, bf16[16,4096]{1,0:T(8,128)(2,1)S(1)}, u32[]{:S(2)}, u32[]{:S(2)}) collective-permute-start(bf16[16,4096]{1,0:T(8,128)(2,1)} %get-tuple-element.22), channel_id=1, source_target_pairs={{0,3},{1,2},{2,1},{3,0},{4,7},{5,6},{6,5},{7,4},{8,11},{9,10},{10,... | collective-permute-start | bytes 393224 | tf_op jit(solution)/shard_map/ppermute | solution.py:196
  36.8 11.7 %collective-permute-start.3 = (bf16[16,4096]{1,0:T(8,128)(2,1)}, bf16[16,4096]{1,0:T(8,128)(2,1)S(1)}, u32[]{:S(2)}, u32[]{:S(2)}) collective-permute-start(bf16[16,4096]{1,0:T(8,128)(2,1)} %get-tuple-element.23), channel_id=1, source_target_pairs={{0,4},{1,5},{2,6},{3,7},{4,0},{5,1},{6,2},{7,3},{8,12},{9,13},{10,... | collective-permute-start | bytes 393224 | tf_op jit(solution)/shard_map/ppermute | solution.py:196
  38.6 12.0 %collective-permute-start.4 = (bf16[16,4096]{1,0:T(8,128)(2,1)}, bf16[16,4096]{1,0:T(8,128)(2,1)S(1)}, u32[]{:S(2)}, u32[]{:S(2)}) collective-permute-start(bf16[16,4096]{1,0:T(8,128)(2,1)} %get-tuple-element.24), channel_id=1, source_target_pairs={{0,5},{1,4},{2,7},{3,6},{4,1},{5,0},{6,3},{7,2},{8,13},{9,12},{10,... | collective-permute-start | bytes 393224 | tf_op jit(solution)/shard_map/ppermute | solution.py:196
  38.6 12.0 %collective-permute-start.5 = (bf16[16,4096]{1,0:T(8,128)(2,1)}, bf16[16,4096]{1,0:T(8,128)(2,1)S(1)}, u32[]{:S(2)}, u32[]{:S(2)}) collective-permute-start(bf16[16,4096]{1,0:T(8,128)(2,1)} %get-tuple-element.25), channel_id=1, source_target_pairs={{0,6},{1,7},{2,4},{3,5},{4,2},{5,3},{6,0},{7,1},{8,14},{9,15},{10,... | collective-permute-start | bytes 393224 | tf_op jit(solution)/shard_map/ppermute | solution.py:196
  41.3 9.3 %collective-permute-start.6 = (bf16[16,4096]{1,0:T(8,128)(2,1)}, bf16[16,4096]{1,0:T(8,128)(2,1)S(1)}, u32[]{:S(2)}, u32[]{:S(2)}) collective-permute-start(bf16[16,4096]{1,0:T(8,128)(2,1)} %get-tuple-element.26), channel_id=1, source_target_pairs={{0,7},{1,6},{2,5},{3,4},{4,3},{5,2},{6,1},{7,0},{8,15},{9,14},{10,... | collective-permute-start | bytes 393224 | tf_op jit(solution)/shard_map/ppermute | solution.py:196
  43.0 0.8 copy-start.4
  43.7 0.8 copy-start.5
  46.6 1.9 %copy-start.1 = (bf16[2,2,512,1024]{3,2,1,0:T(8,128)(2,1)}, bf16[2,2,512,1024]{3,2,1,0:T(8,128)(2,1)S(1)}, u32[]{:S(2)}) copy-start(bf16[2,2,512,1024]{3,2,1,0:T(8,128)(2,1)S(1)} %get-tuple-element.27.refs_9_) | copy-start | bytes 12582916
  50.6 2.2 %copy-start = (bf16[512,1,4096]{2,0,1:T(8,128)(2,1)S(1)}, bf16[512,1,4096]{2,0,1:T(8,128)(2,1)}, u32[]{:S(2)}) copy-start(bf16[512,1,4096]{2,0,1:T(8,128)(2,1)} %param.5) | copy-start | bytes 12582916
  52.7 0.9 %copy-start.2 = (bf16[16,4096]{1,0:T(8,128)(2,1)S(1)}, bf16[16,4096]{1,0:T(8,128)(2,1)}, u32[]{:S(2)}) copy-start(bf16[16,4096]{1,0:T(8,128)(2,1)} %get-tuple-element.19.refs_0_) | copy-start | bytes 393220
  63.3 0.6 copy-start.3
  63.9 4.5 %collective-permute-start.7 = (bf16[32,512]{1,0:T(8,128)(2,1)S(1)}, bf16[32,512]{1,0:T(8,128)(2,1)S(1)}, u32[]{:S(2)}, u32[]{:S(2)}) collective-permute-start(bf16[32,512]{1,0:T(8,128)(2,1)S(1)} %get-tuple-element.30), channel_id=1, source_target_pairs={{0,8},{8,0},{16,24},{24,16},{1,9},{9,1},{17,25},{25,17},{2,10},{10... | collective-permute-start | bytes 98312 | tf_op jit(solution)/shard_map/ppermute | solution.py:227
  65.7 5.4 %collective-permute-start.8 = (bf16[32,512]{1,0:T(8,128)(2,1)S(1)}, bf16[32,512]{1,0:T(8,128)(2,1)S(1)}, u32[]{:S(2)}, u32[]{:S(2)}) collective-permute-start(bf16[32,512]{1,0:T(8,128)(2,1)S(1)} %get-tuple-element.31), channel_id=1, source_target_pairs={{0,16},{8,24},{16,0},{24,8},{1,17},{9,25},{17,1},{25,9},{2,18},{10... | collective-permute-start | bytes 98312 | tf_op jit(solution)/shard_map/ppermute | solution.py:227
  68.4 5.7 %collective-permute-start.9 = (bf16[32,512]{1,0:T(8,128)(2,1)S(1)}, bf16[32,512]{1,0:T(8,128)(2,1)S(1)}, u32[]{:S(2)}, u32[]{:S(2)}) collective-permute-start(bf16[32,512]{1,0:T(8,128)(2,1)S(1)} %get-tuple-element.32), channel_id=1, source_target_pairs={{0,24},{8,16},{16,8},{24,0},{1,25},{9,17},{17,9},{25,1},{2,26},{10... | collective-permute-start | bytes 98312 | tf_op jit(solution)/shard_map/ppermute | solution.py:227
  68.4 5.7 %copy-start.6 = (bf16[32,512]{1,0:T(8,128)(2,1)}, bf16[32,512]{1,0:T(8,128)(2,1)S(1)}, u32[]{:S(2)}) copy-start(bf16[32,512]{1,0:T(8,128)(2,1)S(1)} %collective-permute-done.7.refs_1_) | copy-start | bytes 98308
  71.1 3.0 %copy-start.7 = (bf16[32,512]{1,0:T(8,128)(2,1)}, bf16[32,512]{1,0:T(8,128)(2,1)S(1)}, u32[]{:S(2)}) copy-start(bf16[32,512]{1,0:T(8,128)(2,1)S(1)} %collective-permute-done.8.refs_2_) | copy-start | bytes 98308
  74.1 0.6 copy-start.8

commit v2 on v1

--- a/solution.py
+++ b/solution.py
@@ -12,7 +12,6 @@
 F32 = jnp.float32
 BF16 = jnp.bfloat16
 
-ANY = pl.BlockSpec(memory_space=pl.ANY)
 VMEM = pl.BlockSpec(memory_space=pltpu.VMEM)
 SMEM = pl.BlockSpec(memory_space=pltpu.SMEM)
 
@@ -30,11 +29,9 @@
     return init
 
 
-def pick_kernel(ex, held, slots, pairs_ref, query_ref, *rest):
-    outs, sems = rest[:ex], rest[ex]
+def pick_kernel(ex, held, slots, pairs_ref, query_ref, *outs):
     me = lax.axis_index("ex")
-    copies = []
-    for k in reversed(range(ex)):
+    for k in range(ex):
         first = (me ^ k) * slots
 
         def body(slot, block):
@@ -42,15 +39,10 @@
             return jnp.where((local >= 0) & (local < held), local, block)
 
         block = over_slots(slots, body, jnp.int32(0))
-        start = pl.multiple_of(block * QBLK, QBLK)
-        copy = pltpu.make_async_copy(query_ref.at[pl.ds(start, QBLK)], outs[k], sems.at[k])
-        copy.start()
-        copies.append(copy)
-    for copy in copies:
-        copy.wait()
-
-
-def factor_kernel(out_ref, in_ref, left_ref, right_ref):
+        outs[k][...] = query_ref[pl.ds(pl.multiple_of(block * QBLK, QBLK), QBLK), :]
+
+
+def factor_kernel(rows, out_ref, in_ref, left_ref, right_ref):
     width = out_ref.shape[0]
     in_width = in_ref.shape[0]
     half = left_ref.shape[2]
@@ -61,9 +53,9 @@
     row_o = lax.broadcasted_iota(jnp.int32, (half, width), 1)
     col = lax.broadcasted_iota(jnp.int32, (width, half), 1) // QBLK
     col_o = lax.broadcasted_iota(jnp.int32, (width, half), 0)
-    same = (lax.broadcasted_iota(jnp.int32, (half, half), 0) % QBLK) == (
-        lax.broadcasted_iota(jnp.int32, (half, half), 1) % QBLK
-    )
+    a = lax.broadcasted_iota(jnp.int32, (half, half), 0) % QBLK
+    a = ((a // rows) ^ lax.axis_index("layer")) * rows + a % rows
+    same = a == (lax.broadcasted_iota(jnp.int32, (half, half), 1) % QBLK)
     for h in range(2):
         for s in range(2):
             pick_rows = (row * 2 + s == row_o).astype(BF16)
@@ -117,54 +109,62 @@
             ]
 
 
-def tile_kernel(ex, layer, *refs):
-    blocks = refs[:ex]
-    train_ref, left_ref, right_ref = refs[ex : ex + 3]
-    outs = refs[ex + 3 : ex + 3 + layer]
-    prep_ref, tile_ref = refs[ex + 3 + layer :]
-    rows = QBLK // layer
-    for pair in range(ex // 2):
+def group_tile(blocks, train_ref, left_ref, right_ref, prep_ref):
+    for pair in range(len(blocks) // 2):
         prepare(
             [blocks[2 * pair][...], blocks[2 * pair + 1][...]],
             left_ref,
             right_ref,
             prep_ref.at[pl.ds(pair * 2 * QBLK, 2 * QBLK)],
         )
-    tile = lax.dot_general(
+    return lax.dot_general(
         prep_ref[...], train_ref[...], (((1,), (1,)), ((), ())), preferred_element_type=F32
     )
-    me = lax.axis_index("layer")
-    for c in range(tile_ref.shape[0]):
-        lanes = slice(c * LANES, (c + 1) * LANES)
-        tile_ref[c] = tile[:, lanes]
-        for m in range(layer):
-            first = (me ^ m) * rows
-            part = jnp.concatenate(
-                [tile_ref[c, pl.ds(first + j, ex, stride=QBLK), :] for j in range(rows)], axis=0
-            )
-            outs[m][:, lanes] = part.astype(outs[m].dtype)
-
-
-def finish_kernel(ex, layer, held, slots, pairs_ref, *refs):
-    parts, out_ref, sum_ref = refs[:layer], refs[layer], refs[layer + 1]
+
+
+def tile_kernel(count, *refs):
+    blocks, consts = refs[:count], refs[count : count + 3]
+    early, (out_ref, prep_ref) = refs[count + 3 : -2], refs[-2:]
+    start = 0
+    for ref in early:
+        start = ref.shape[0]
+        out_ref[:start] = ref[...]
+    out_ref[start:] = group_tile(blocks, *consts, prep_ref)
+
+
+def last_kernel(count, order, layer, held, slots, pairs_ref, *refs):
+    blocks, consts, early_ref = refs[:count], refs[count : count + 3], refs[count + 3]
+    refs = refs[count + 4 :]
+    outs, prep_ref, tile_ref = refs[:layer], refs[layer], refs[layer + 1]
+    place = 0
+    for tile in (early_ref[...], group_tile(blocks, *consts, prep_ref)):
+        for i in range(tile.shape[0] // QBLK):
+            tile_ref[place] = tile[i * QBLK : (i + 1) * QBLK]
+            place += 1
+    rows = QBLK // layer
+    me = lax.axis_index("ex")
+    chosen = []
+    for slot in range(slots):
+        q = pairs_ref[me * slots + slot]
+        k = (jnp.maximum(q, 0) // held) ^ me
+        place = jnp.int32(0)
+        for index, offset in enumerate(order):
+            place = jnp.where(k == offset, index, place)
+        value = tile_ref[place]
+        chosen.append(jnp.where(q >= 0, value, jnp.zeros_like(value)))
+    for m in range(layer):
+        part = jnp.concatenate([value[m * rows : (m + 1) * rows] for value in chosen], axis=0)
+        outs[m][...] = part.astype(outs[m].dtype)
+
+
+def finish_kernel(layer, *refs):
+    parts, out_ref = refs[:layer], refs[layer]
     total = parts[0][...]
     for part in parts[1:]:
         total = total + part[...].astype(F32)
-    chunks = sum_ref.shape[0]
-    for c in range(chunks):
-        sum_ref[c] = total[:, c * LANES : (c + 1) * LANES]
-    rows = QBLK // layer
-    me = lax.axis_index("ex")
-
-    def body(slot, carry):
-        q = pairs_ref[me * slots + slot]
-        k = jnp.where(q >= 0, (q // held) ^ me, 0)
-        for c in range(chunks):
-            value = sum_ref[c, pl.ds(k, rows, stride=ex), :]
-            out_ref[slot, :, c * LANES : (c + 1) * LANES] = jnp.where(q >= 0, value, jnp.zeros_like(value))
-        return carry
-
-    over_slots(slots, body, 0)
+    rows = out_ref.shape[1]
+    for slot in range(out_ref.shape[0]):
+        out_ref[slot] = total[slot * rows : (slot + 1) * rows]
 
 
 def shards(train_grads, query_grads, in_precond, out_precond, pair_blocks):
@@ -179,26 +179,27 @@
     query = query_grads.reshape(query_grads.shape[0], features)
     in_factor = in_precond.reshape(in_precond.shape[1:])
     out_factor = out_precond.reshape(out_precond.shape[1:])
-    limit = pltpu.CompilerParams(vmem_limit_bytes=48 * 2**20)
+    limit = pltpu.CompilerParams(vmem_limit_bytes=24 * 2**20)
 
     picked = pl.pallas_call(
         functools.partial(pick_kernel, ex, held, slots),
         out_shape=[jax.ShapeDtypeStruct((QBLK, features), BF16)] * ex,
-        in_specs=[SMEM, ANY],
-        out_specs=[ANY] * ex,
-        scratch_shapes=[pltpu.SemaphoreType.DMA((ex,))],
+        in_specs=[SMEM, VMEM],
+        out_specs=[VMEM] * ex,
+        compiler_params=limit,
         name="pick",
     )(pair_blocks, query)
 
-    blocks = [None] * ex
-    blocks[0] = picked[0]
-    for k in reversed(range(1, ex)):
-        blocks[k] = lax.ppermute(picked[k], "ex", [(i, i ^ k) for i in range(ex)])
+    far = lambda k: (-bin(k >> 1).count("1"), -(k & 1), -k)
+    order = [0, 1] + sorted(range(2, ex), key=far)
+    blocks = [picked[0]] + [
+        lax.ppermute(picked[k], "ex", [(i, i ^ k) for i in range(ex)]) for k in order[1:]
+    ]
 
     stack = features // LANES * QBLK
     span = 2 * LANES
     left, right = pl.pallas_call(
-        factor_kernel,
+        functools.partial(factor_kernel, rows),
         out_shape=[
             jax.ShapeDtypeStruct((2, 2, stack, 2 * stack), BF16),
             jax.ShapeDtypeStruct((2, span, span), BF16),
@@ -209,31 +210,44 @@
         name="factors",
     )(out_factor, in_factor)
 
+    early = []
+    for group in (blocks[:-4], blocks[-4:-2]):
+        done = sum(tile.shape[0] for tile in early)
+        early = [
+            pl.pallas_call(
+                functools.partial(tile_kernel, len(group)),
+                out_shape=jax.ShapeDtypeStruct((done + len(group) * QBLK, train_rows), F32),
+                in_specs=[VMEM] * (len(group) + 3 + len(early)),
+                out_specs=VMEM,
+                scratch_shapes=[pltpu.VMEM((len(group) * QBLK, features), BF16)],
+                compiler_params=limit,
+                name=f"tiles_{len(early)}",
+            )(*group, train, left, right, *early)
+        ]
     parts = pl.pallas_call(
-        functools.partial(tile_kernel, ex, layer),
-        out_shape=[jax.ShapeDtypeStruct((rows * ex, train_rows), F32)]
-        + [jax.ShapeDtypeStruct((rows * ex, train_rows), BF16)] * (layer - 1),
-        in_specs=[VMEM] * (ex + 3),
+        functools.partial(last_kernel, 2, order, layer, held, slots),
+        out_shape=[jax.ShapeDtypeStruct((slots * rows, train_rows), F32)]
+        + [jax.ShapeDtypeStruct((slots * rows, train_rows), BF16)] * (layer - 1),
+        in_specs=[SMEM] + [VMEM] * (2 + 3 + len(early)),
         out_specs=[VMEM] * layer,
         scratch_shapes=[
-            pltpu.VMEM((ex * QBLK, features), BF16),
-            pltpu.VMEM((train_rows // LANES, ex * QBLK, LANES), F32),
+            pltpu.VMEM((2 * QBLK, features), BF16),
+            pltpu.VMEM((ex, QBLK, train_rows), F32),
         ],
         compiler_params=limit,
-        name="tiles",
-    )(*blocks, train, left, right)
+        name="last",
+    )(pair_blocks, *blocks[-2:], train, left, right, *early)
 
     terms = [parts[0]] + [
         lax.ppermute(parts[m], "layer", [(i, i ^ m) for i in range(layer)]) for m in range(1, layer)
     ]
     out = pl.pallas_call(
-        functools.partial(finish_kernel, ex, layer, held, slots),
+        functools.partial(finish_kernel, layer),
         out_shape=jax.ShapeDtypeStruct((slots, rows, train_rows), F32),
-        in_specs=[SMEM] + [VMEM] * layer,
+        in_specs=[VMEM] * layer,
         out_specs=VMEM,
-        scratch_shapes=[pltpu.VMEM((train_rows // LANES, rows * ex, LANES), F32)],
         name="finish",
-    )(pair_blocks, *terms)
+    )(*terms)
     return jnp.transpose(out, (1, 0, 2))
 
 

time: 76.6 us -> 41.1 us (0.54)
  Pallas kernels: 46.8 us -> 14.9 us
  waiting for transfers between devices: 7.84 us -> 5.57 us
  local copies, waits for them, and re-layouts: 7.76 us -> 6.62 us
    pallas_call x1, Pallas kernels: 33.6 us -> 0.66 us  [shards(): pl.pallas_call(functools.partial(pick_kernel, ex, held, slots), out_shape...]
    ppermute x7, waiting for transfers between devices: 2.14 us -> 0.17 us  [shards(): lax.ppermute(picked[k], 'ex', [(i, i ^ k) for i in range(ex)])]
    unnamed x18 -> x22, local copies, waits for them, and re-layouts: 7.76 us -> 6.62 us
    pallas_call x3 -> x5, Pallas kernels: 13.2 us -> 14.2 us  [the longest x2 7.2 us: shards(): pl.pallas_call(functools.partial(tile_kernel, len(group)), out_shape=jax....]
  transfers between devices with their start and end apart: 10 -> 10, of which waited for: 4 -> 3; matrix products, arithmetic and copies ran while one was open for 0% -> 0% of each run, Pallas kernels for 3% -> 23%
where the time goes in v2:
time: 41.1 us; the launch traced here: 40.7 us
  Pallas kernels  14.9 us (36%)
  starting transfers between devices  13.5 us (33%)
  local copies, waits for them, and re-layouts  6.62 us (16%)
  waiting for transfers between devices  5.57 us (14%)
    ppermute x7, starting transfers between devices, shards(): lax.ppermute(picked[k], 'ex', [(i, i ^ k) for i in range(ex)])  9.13 us
    pallas_call x2, Pallas kernels, shards(): pl.pallas_call(functools.partial(tile_kernel, len(group)), out_shape=jax....  7.2 us
    unnamed x22, local copies, waits for them, and re-layouts  6.62 us
    ppermute x3, waiting for transfers between devices, shards(): lax.ppermute(parts[m], 'layer', [(i, i ^ m) for i in range(layer)])  5.4 us
    ppermute x3, starting transfers between devices, shards(): lax.ppermute(parts[m], 'layer', [(i, i ^ m) for i in range(layer)])  4.39 us
    pallas_call x1, Pallas kernels, shards(): pl.pallas_call(functools.partial(last_kernel, 2, order, layer, held, slot...  3.43 us
    pallas_call x1, Pallas kernels, shards(): pl.pallas_call(functools.partial(factor_kernel, rows), out_shape=[jax.Sha...  2.11 us
    pallas_call x1, Pallas kernels, shards(): pl.pallas_call(functools.partial(finish_kernel, layer), out_shape=jax.Sha...  1.45 us
  transfers between devices with their start and end apart: 10, of which 3 were waited for; matrix products, arithmetic and copies ran while one was open for 0% of the time, Pallas kernels for 23%

profile of v2, /device:TPU:0, one launch (start us, length us, event | category | flops | bytes accessed | tf_op | source)
XLA Modules:
  0.0 40.7 jit_solution(14091126735976428189)
XLA Ops:
  0.0 0.0 copy-start.2
  0.0 1.0 %copy-done.2 = bf16[64,1,4096]{2,0,1:T(8,128)(2,1)S(1)} copy-done((bf16[64,1,4096]{2,0,1:T(8,128)(2,1)S(1)}, bf16[64,1,4096]{2,0,1:T(8,128)(2,1)}, u32[]{:S(2)}) %copy-start.2) | copy-done | bytes 524312
  1.0 0.0 copy-start.6
  1.0 0.7 %copy-done.6 = s32[48]{0:T(128)S(1)} copy-done((s32[48]{0:T(128)S(1)}, s32[48]{0:T(128)}, u32[]{:S(2)}) %copy-start.6) | copy-done | bytes 216
  1.7 0.7 %pick.1 = (bf16[16,4096]{1,0:T(8,128)(2,1)S(1)}, bf16[16,4096]{1,0:T(8,128)(2,1)S(1)}, bf16[16,4096]{1,0:T(8,128)(2,1)S(1)}, bf16[16,4096]{1,0:T(8,128)(2,1)S(1)...) custom-call(s32[48]{0:T(128)S(1)} %copy-done.6, ...), custom_call_target="tpu_custom_call" | custom-call | tf_op jit(solution)/shard_map/pick/pallas_call | solution.py:184
  2.4 0.5 %collective-permute-start.4 = (bf16[16,4096]{1,0:T(8,128)(2,1)S(1)}, bf16[16,4096]{1,0:T(8,128)(2,1)S(1)}, u32[]{:S(2)}, u32[]{:S(2)}) collective-permute-start(bf16[16,4096]{1,0:T(8,128)(2,1)S(1)} %get-tuple-element.26), channel_id=1, source_target_pairs={{0,1},{1,0},{2,3},{3,2},{4,5},{5,4},{6,7},{7,6},{8,9},{9,8},{10,11... | collective-permute-start | bytes 393224 | tf_op jit(solution)/shard_map/ppermute | solution.py:196
  2.9 3.6 %collective-permute-start.5 = (bf16[16,4096]{1,0:T(8,128)(2,1)S(1)}, bf16[16,4096]{1,0:T(8,128)(2,1)S(1)}, u32[]{:S(2)}, u32[]{:S(2)}) collective-permute-start(bf16[16,4096]{1,0:T(8,128)(2,1)S(1)} %get-tuple-element.27), channel_id=1, source_target_pairs={{0,7},{1,6},{2,5},{3,4},{4,3},{5,2},{6,1},{7,0},{8,15},{9,14},{10,... | collective-permute-start | bytes 393224 | tf_op jit(solution)/shard_map/ppermute | solution.py:196
  6.5 0.0 collective-permute-start.6
  6.5 2.0 %collective-permute-start = (bf16[16,4096]{1,0:T(8,128)(2,1)S(1)}, bf16[16,4096]{1,0:T(8,128)(2,1)S(1)}, u32[]{:S(2)}, u32[]{:S(2)}) collective-permute-start(bf16[16,4096]{1,0:T(8,128)(2,1)S(1)} %get-tuple-element.19), channel_id=1, source_target_pairs={{0,4},{1,5},{2,6},{3,7},{4,0},{5,1},{6,2},{7,3},{8,12},{9,13},{10,... | collective-permute-start | bytes 393224 | tf_op jit(solution)/shard_map/ppermute | solution.py:196
  8.5 0.0 collective-permute-start.2
  8.5 0.0 collective-permute-done.4.refs_1_
  8.5 1.7 %collective-permute-start.3 = (bf16[16,4096]{1,0:T(8,128)(2,1)S(1)}, bf16[16,4096]{1,0:T(8,128)(2,1)S(1)}, u32[]{:S(2)}, u32[]{:S(2)}) collective-permute-start(bf16[16,4096]{1,0:T(8,128)(2,1)S(1)} %get-tuple-element.24), channel_id=1, source_target_pairs={{0,3},{1,2},{2,1},{3,0},{4,7},{5,6},{6,5},{7,4},{8,11},{9,10},{10,... | collective-permute-start | bytes 393224 | tf_op jit(solution)/shard_map/ppermute | solution.py:196
  10.2 0.2 collective-permute-done.5.refs_2_
  10.3 1.3 %collective-permute-start.1 = (bf16[16,4096]{1,0:T(8,128)(2,1)S(1)}, bf16[16,4096]{1,0:T(8,128)(2,1)S(1)}, u32[]{:S(2)}, u32[]{:S(2)}) collective-permute-start(bf16[16,4096]{1,0:T(8,128)(2,1)S(1)} %get-tuple-element.20), channel_id=1, source_target_pairs={{0,2},{1,3},{2,0},{3,1},{4,6},{5,7},{6,4},{7,5},{8,10},{9,11},{10,... | collective-permute-start | bytes 393224 | tf_op jit(solution)/shard_map/ppermute | solution.py:196
  11.7 0.0 copy-start.4
  11.7 0.8 %copy-done.4 = f32[1,64,64]{2,1,0:T(8,128)S(1)} copy-done((f32[1,64,64]{2,1,0:T(8,128)S(1)}, f32[1,64,64]{2,1,0:T(8,128)}, u32[]{:S(2)}) %copy-start.4) | copy-done | bytes 16408
  12.4 0.0 copy-start.5
  12.4 0.8 %copy-done.5 = f32[1,64,64]{2,1,0:T(8,128)S(1)} copy-done((f32[1,64,64]{2,1,0:T(8,128)S(1)}, f32[1,64,64]{2,1,0:T(8,128)}, u32[]{:S(2)}) %copy-start.5) | copy-done | bytes 16408
  13.2 2.1 %factors.1 = (bf16[2,2,512,1024]{3,2,1,0:T(8,128)(2,1)S(1)}, bf16[2,256,256]{2,1,0:T(8,128)(2,1)S(1)}) custom-call(f32[64,64]{1,0:T(8,128)S(1)} %bitcast.9, f32[64,64]{1,0:T(8,128)S(1)} %bitcast.10), custom_call_target="tpu_custom_call" | custom-call | tf_op jit(solution)/shard_map/factors/pallas_call | solution.py:201
  15.3 0.0 collective-permute-done.6.refs_3_
  15.3 0.0 copy-start
  15.3 2.2 %copy-done = bf16[512,1,4096]{2,0,1:T(8,128)(2,1)S(1)} copy-done((bf16[512,1,4096]{2,0,1:T(8,128)(2,1)S(1)}, bf16[512,1,4096]{2,0,1:T(8,128)(2,1)}, u32[]{:S(2)}) %copy-start) | copy-done | bytes 4194328
  17.5 0.0 copy-start.1
  17.5 4.3 %tiles_0.1.refs_5_ = f32[64,512]{1,0:T(8,128)S(1)} custom-call(bf16[16,4096]{1,0:T(8,128)(2,1)S(1)} %get-tuple-element.25.refs_0_, bf16[16,4096]{1,0:T(8,128)(2,1)S(1)} %collective-permute-done.4.refs_1_, bf16[16,4096]{1,0:T(8,128)(2,1)S(1)} %collective-permute-done.5.refs_2_, bf16[16,4096]{1,0:T(8,128)(2,1)S(1)} %collective-permute-done.6.refs_3_, ...), custom_call_target="tpu_custom_call" | custom-call | tf_op jit(solution)/shard_map/tiles_0/pallas_call | solution.py:217
  21.8 0.0 copy-start.7
  21.9 0.0 collective-permute-done.2.refs_0_
  21.9 0.0 collective-permute-done.3.refs_1_
  21.9 0.0 copy-done.1
  21.9 2.9 %tiles_1.1.refs_5_ = f32[96,512]{1,0:T(8,128)S(1)} custom-call(bf16[16,4096]{1,0:T(8,128)(2,1)S(1)} %collective-permute-done.2.refs_0_, bf16[16,4096]{1,0:T(8,128)(2,1)S(1)} %collective-permute-done.3.refs_1_, bf16[512,4096]{1,0:T(8,128)(2,1)S(1)} %bitcast.6, bf16[2,2,512,1024]{3,2,1,0:T(8,128)(2,1)S(1)} %get-tuple-element.21.refs_5_.refs_3_, ...), custom_call_target="tpu_custom_call" | custom-call | tf_op jit(solution)/shard_map/tiles_1/pallas_call | solution.py:217
  24.8 0.0 collective-permute-done.refs_0_
  24.8 0.0 collective-permute-done.1.refs_1_
  24.8 0.0 copy-done.7
  24.8 3.4 %last.1 = (f32[24,512]{1,0:T(8,128)S(1)}, bf16[24,512]{1,0:T(8,128)(2,1)S(1)}, bf16[24,512]{1,0:T(8,128)(2,1)S(1)}, bf16[24,512]{1,0:T(8,128)(2,1)S(1)}) custom-call(s32[48]{0:T(128)S(1)} %copy-done.7, bf16[16,4096]{1,0:T(8,128)(2,1)S(1)} %collective-permute-done.refs_0_, bf16[16,4096]{1,0:T(8,128)(2,1)S(1)} %collective-permute-done.1.refs_1_, ...), custom_call_target="tpu_custom_call" | custom-call | tf_op jit(solution)/shard_map/last/pallas_call | solution.py:227
  28.2 0.0 copy-start.3
  28.2 0.6 %copy-done.3 = f32[24,512]{1,0:T(8,128)} copy-done((f32[24,512]{1,0:T(8,128)}, f32[24,512]{1,0:T(8,128)S(1)}, u32[]{:S(2)}) %copy-start.3) | copy-done | bytes 49176
  28.8 1.6 %collective-permute-start.7 = (bf16[24,512]{1,0:T(8,128)(2,1)S(1)}, bf16[24,512]{1,0:T(8,128)(2,1)S(1)}, u32[]{:S(2)}, u32[]{:S(2)}) collective-permute-start(bf16[24,512]{1,0:T(8,128)(2,1)S(1)} %get-tuple-element.30), channel_id=1, source_target_pairs={{0,8},{8,0},{16,24},{24,16},{1,9},{9,1},{17,25},{25,17},{2,10},{10... | collective-permute-start | bytes 73736 | tf_op jit(solution)/shard_map/ppermute | solution.py:242
  30.4 2.6 %collective-permute-start.8 = (bf16[24,512]{1,0:T(8,128)(2,1)S(1)}, bf16[24,512]{1,0:T(8,128)(2,1)S(1)}, u32[]{:S(2)}, u32[]{:S(2)}) collective-permute-start(bf16[24,512]{1,0:T(8,128)(2,1)S(1)} %get-tuple-element.31), channel_id=1, source_target_pairs={{0,16},{8,24},{16,0},{24,8},{1,17},{9,25},{17,1},{25,9},{2,18},{10... | collective-permute-start | bytes 73736 | tf_op jit(solution)/shard_map/ppermute | solution.py:242
  33.0 0.2 collective-permute-start.9
  33.2 0.0 collective-permute-done.7.refs_1_
  33.2 0.0 copy-start.8
  33.2 2.2 %collective-permute-done.8.refs_2_ = bf16[24,512]{1,0:T(8,128)(2,1)S(1)} collective-permute-done((bf16[24,512]{1,0:T(8,128)(2,1)S(1)}, bf16[24,512]{1,0:T(8,128)(2,1)S(1)}, u32[]{:S(2)}, u32[]{:S(2)}) %collective-permute-start.8) | collective-permute-done | bytes 24608 | tf_op jit(solution)/shard_map/ppermute | solution.py:242
  35.4 0.0 copy-start.9
  35.4 3.2 %collective-permute-done.9.refs_3_ = bf16[24,512]{1,0:T(8,128)(2,1)S(1)} collective-permute-done((bf16[24,512]{1,0:T(8,128)(2,1)S(1)}, bf16[24,512]{1,0:T(8,128)(2,1)S(1)}, u32[]{:S(2)}, u32[]{:S(2)}) %collective-permute-start.9) | collective-permute-done | bytes 24608 | tf_op jit(solution)/shard_map/ppermute | solution.py:242
  38.6 0.0 copy-start.10
  38.6 0.0 copy-done.8
  38.6 0.0 copy-done.9
  38.6 0.6 %copy-done.10 = bf16[24,512]{1,0:T(8,128)(2,1)} copy-done((bf16[24,512]{1,0:T(8,128)(2,1)}, bf16[24,512]{1,0:T(8,128)(2,1)S(1)}, u32[]{:S(2)}) %copy-start.10) | copy-done | bytes 24600
  39.2 1.5 %finish.1 = f32[6,4,512]{2,1,0:T(4,128)} custom-call(f32[24,512]{1,0:T(8,128)} %copy-done.3, bf16[24,512]{1,0:T(8,128)(2,1)} %copy-done.8, bf16[24,512]{1,0:T(8,128)(2,1)} %copy-done.9, bf16[24,512]{1,0:T(8,128)(2,1)} %copy-done.10), custom_call_target="tpu_custom_call" | custom-call | tf_op jit(solution)/shard_map/finish/pallas_call | solution.py:244
Async XLA Ops:
  0.0 1.0 %copy-start.2 = (bf16[64,1,4096]{2,0,1:T(8,128)(2,1)S(1)}, bf16[64,1,4096]{2,0,1:T(8,128)(2,1)}, u32[]{:S(2)}) copy-start(bf16[64,1,4096]{2,0,1:T(8,128)(2,1)} %param.6) | copy-start | bytes 1572868
  1.0 0.7 %copy-start.6 = (s32[48]{0:T(128)S(1)}, s32[48]{0:T(128)}, u32[]{:S(2)}) copy-start(s32[48]{0:T(128)} %pairs_ref.3) | copy-start | bytes 580
  2.4 6.1 %collective-permute-start.4 = (bf16[16,4096]{1,0:T(8,128)(2,1)S(1)}, bf16[16,4096]{1,0:T(8,128)(2,1)S(1)}, u32[]{:S(2)}, u32[]{:S(2)}) collective-permute-start(bf16[16,4096]{1,0:T(8,128)(2,1)S(1)} %get-tuple-element.26), channel_id=1, source_target_pairs={{0,1},{1,0},{2,3},{3,2},{4,5},{5,4},{6,7},{7,6},{8,9},{9,8},{10,11... | collective-permute-start | bytes 393224 | tf_op jit(solution)/shard_map/ppermute | solution.py:196
  2.9 7.4 %collective-permute-start.5 = (bf16[16,4096]{1,0:T(8,128)(2,1)S(1)}, bf16[16,4096]{1,0:T(8,128)(2,1)S(1)}, u32[]{:S(2)}, u32[]{:S(2)}) collective-permute-start(bf16[16,4096]{1,0:T(8,128)(2,1)S(1)} %get-tuple-element.27), channel_id=1, source_target_pairs={{0,7},{1,6},{2,5},{3,4},{4,3},{5,2},{6,1},{7,0},{8,15},{9,14},{10,... | collective-permute-start | bytes 393224 | tf_op jit(solution)/shard_map/ppermute | solution.py:196
  6.5 8.8 %collective-permute-start.6 = (bf16[16,4096]{1,0:T(8,128)(2,1)S(1)}, bf16[16,4096]{1,0:T(8,128)(2,1)S(1)}, u32[]{:S(2)}, u32[]{:S(2)}) collective-permute-start(bf16[16,4096]{1,0:T(8,128)(2,1)S(1)} %get-tuple-element.28), channel_id=1, source_target_pairs={{0,6},{1,7},{2,4},{3,5},{4,2},{5,3},{6,0},{7,1},{8,14},{9,15},{10,... | collective-permute-start | bytes 393224 | tf_op jit(solution)/shard_map/ppermute | solution.py:196
  6.5 18.3 %collective-permute-start = (bf16[16,4096]{1,0:T(8,128)(2,1)S(1)}, bf16[16,4096]{1,0:T(8,128)(2,1)S(1)}, u32[]{:S(2)}, u32[]{:S(2)}) collective-permute-start(bf16[16,4096]{1,0:T(8,128)(2,1)S(1)} %get-tuple-element.19), channel_id=1, source_target_pairs={{0,4},{1,5},{2,6},{3,7},{4,0},{5,1},{6,2},{7,3},{8,12},{9,13},{10,... | collective-permute-start | bytes 393224 | tf_op jit(solution)/shard_map/ppermute | solution.py:196
  8.5 13.4 %collective-permute-start.2 = (bf16[16,4096]{1,0:T(8,128)(2,1)S(1)}, bf16[16,4096]{1,0:T(8,128)(2,1)S(1)}, u32[]{:S(2)}, u32[]{:S(2)}) collective-permute-start(bf16[16,4096]{1,0:T(8,128)(2,1)S(1)} %get-tuple-element.23), channel_id=1, source_target_pairs={{0,5},{1,4},{2,7},{3,6},{4,1},{5,0},{6,3},{7,2},{8,13},{9,12},{10,... | collective-permute-start | bytes 393224 | tf_op jit(solution)/shard_map/ppermute | solution.py:196
  8.5 13.4 %collective-permute-start.3 = (bf16[16,4096]{1,0:T(8,128)(2,1)S(1)}, bf16[16,4096]{1,0:T(8,128)(2,1)S(1)}, u32[]{:S(2)}, u32[]{:S(2)}) collective-permute-start(bf16[16,4096]{1,0:T(8,128)(2,1)S(1)} %get-tuple-element.24), channel_id=1, source_target_pairs={{0,3},{1,2},{2,1},{3,0},{4,7},{5,6},{6,5},{7,4},{8,11},{9,10},{10,... | collective-permute-start | bytes 393224 | tf_op jit(solution)/shard_map/ppermute | solution.py:196
  10.3 14.4 %collective-permute-start.1 = (bf16[16,4096]{1,0:T(8,128)(2,1)S(1)}, bf16[16,4096]{1,0:T(8,128)(2,1)S(1)}, u32[]{:S(2)}, u32[]{:S(2)}) collective-permute-start(bf16[16,4096]{1,0:T(8,128)(2,1)S(1)} %get-tuple-element.20), channel_id=1, source_target_pairs={{0,2},{1,3},{2,0},{3,1},{4,6},{5,7},{6,4},{7,5},{8,10},{9,11},{10,... | collective-permute-start | bytes 393224 | tf_op jit(solution)/shard_map/ppermute | solution.py:196
  11.7 0.8 %copy-start.4 = (f32[1,64,64]{2,1,0:T(8,128)S(1)}, f32[1,64,64]{2,1,0:T(8,128)}, u32[]{:S(2)}) copy-start(f32[1,64,64]{2,1,0:T(8,128)} %param.8) | copy-start | bytes 49156
  12.4 0.8 %copy-start.5 = (f32[1,64,64]{2,1,0:T(8,128)S(1)}, f32[1,64,64]{2,1,0:T(8,128)}, u32[]{:S(2)}) copy-start(f32[1,64,64]{2,1,0:T(8,128)} %param.7) | copy-start | bytes 49156
  15.3 2.2 %copy-start = (bf16[512,1,4096]{2,0,1:T(8,128)(2,1)S(1)}, bf16[512,1,4096]{2,0,1:T(8,128)(2,1)}, u32[]{:S(2)}) copy-start(bf16[512,1,4096]{2,0,1:T(8,128)(2,1)} %param.5) | copy-start | bytes 12582916
  17.5 4.4 %copy-start.1 = (bf16[512,1,4096]{2,0,1:T(8,128)(2,1)S(1)}, bf16[512,1,4096]{2,0,1:T(8,128)(2,1)}, u32[]{:S(2)}) copy-start(bf16[512,1,4096]{2,0,1:T(8,128)(2,1)} %param.5) | copy-start | bytes 12582916
  21.8 2.9 %copy-start.7 = (s32[48]{0:T(128)S(1)}, s32[48]{0:T(128)}, u32[]{:S(2)}) copy-start(s32[48]{0:T(128)} %pairs_ref.3) | copy-start | bytes 580
  28.2 0.6 %copy-start.3 = (f32[24,512]{1,0:T(8,128)}, f32[24,512]{1,0:T(8,128)S(1)}, u32[]{:S(2)}) copy-start(f32[24,512]{1,0:T(8,128)S(1)} %get-tuple-element.29.refs_0_) | copy-start | bytes 147460
  28.8 4.4 %collective-permute-start.7 = (bf16[24,512]{1,0:T(8,128)(2,1)S(1)}, bf16[24,512]{1,0:T(8,128)(2,1)S(1)}, u32[]{:S(2)}, u32[]{:S(2)}) collective-permute-start(bf16[24,512]{1,0:T(8,128)(2,1)S(1)} %get-tuple-element.30), channel_id=1, source_target_pairs={{0,8},{8,0},{16,24},{24,16},{1,9},{9,1},{17,25},{25,17},{2,10},{10... | collective-permute-start | bytes 73736 | tf_op jit(solution)/shard_map/ppermute | solution.py:242
  30.4 5.0 %collective-permute-start.8 = (bf16[24,512]{1,0:T(8,128)(2,1)S(1)}, bf16[24,512]{1,0:T(8,128)(2,1)S(1)}, u32[]{:S(2)}, u32[]{:S(2)}) collective-permute-start(bf16[24,512]{1,0:T(8,128)(2,1)S(1)} %get-tuple-element.31), channel_id=1, source_target_pairs={{0,16},{8,24},{16,0},{24,8},{1,17},{9,25},{17,1},{25,9},{2,18},{10... | collective-permute-start | bytes 73736 | tf_op jit(solution)/shard_map/ppermute | solution.py:242
  33.0 5.6 %collective-permute-start.9 = (bf16[24,512]{1,0:T(8,128)(2,1)S(1)}, bf16[24,512]{1,0:T(8,128)(2,1)S(1)}, u32[]{:S(2)}, u32[]{:S(2)}) collective-permute-start(bf16[24,512]{1,0:T(8,128)(2,1)S(1)} %get-tuple-element.32), channel_id=1, source_target_pairs={{0,24},{8,16},{16,8},{24,0},{1,25},{9,17},{17,9},{25,1},{2,26},{10... | collective-permute-start | bytes 73736 | tf_op jit(solution)/shard_map/ppermute | solution.py:242
  33.2 5.4 %copy-start.8 = (bf16[24,512]{1,0:T(8,128)(2,1)}, bf16[24,512]{1,0:T(8,128)(2,1)S(1)}, u32[]{:S(2)}) copy-start(bf16[24,512]{1,0:T(8,128)(2,1)S(1)} %collective-permute-done.7.refs_1_) | copy-start | bytes 73732
  35.4 3.2 %copy-start.9 = (bf16[24,512]{1,0:T(8,128)(2,1)}, bf16[24,512]{1,0:T(8,128)(2,1)S(1)}, u32[]{:S(2)}) copy-start(bf16[24,512]{1,0:T(8,128)(2,1)S(1)} %collective-permute-done.8.refs_2_) | copy-start | bytes 73732
  38.6 0.6 %copy-start.10 = (bf16[24,512]{1,0:T(8,128)(2,1)}, bf16[24,512]{1,0:T(8,128)(2,1)S(1)}, u32[]{:S(2)}) copy-start(bf16[24,512]{1,0:T(8,128)(2,1)S(1)} %collective-permute-done.9.refs_3_) | copy-start | bytes 73732

commit v3 on v2

v3 whole, which is shorter than its diff:
```python
import functools

import jax
import jax.numpy as jnp
from jax import lax
from jax.experimental import pallas as pl
from jax.experimental.pallas import tpu as pltpu
from jax.sharding import PartitionSpec as P

QBLK = 16
LANES = 128
F32 = jnp.float32
BF16 = jnp.bfloat16

VMEM = pl.BlockSpec(memory_space=pltpu.VMEM)
SMEM = pl.BlockSpec(memory_space=pltpu.SMEM)


def split_bf16(x):
    high = x.astype(BF16)
    return high, (x - high.astype(F32)).astype(BF16)


def over_slots(slots, body, init):
    if slots > 8:
        return lax.fori_loop(0, slots, body, init)
    for slot in range(slots):
        init = body(slot, init)
    return init


def pick_kernel(ex, held, slots, pairs_ref, own_ref, other_ref, *outs):
    me = lax.axis_index("ex")
    for group in range(ex // 2):
        first = (me ^ (2 * group)) * slots
        for side, source in enumerate((own_ref, other_ref)):
            base = (me ^ side) * held

            def body(slot, block):
                local = pairs_ref[first + slot] - base
                return jnp.where((local >= 0) & (local < held), local, block)

            block = over_slots(slots, body, jnp.int32(0))
            start = pl.multiple_of(block * QBLK, QBLK)
            outs[group][side * QBLK : (side + 1) * QBLK, :] = source[pl.ds(start, QBLK), :]


def make_factors(rows, out_ref, in_ref, left_ref, right_ref):
    width = out_ref.shape[0]
    in_width = in_ref.shape[0]
    half = left_ref.shape[2]
    span = right_ref.shape[1]
    outs = split_bf16(out_ref[...])
    ins = split_bf16(in_ref[...])
    row = lax.broadcasted_iota(jnp.int32, (half, width), 0) // QBLK
    row_o = lax.broadcasted_iota(jnp.int32, (half, width), 1)
    col = lax.broadcasted_iota(jnp.int32, (width, half), 1) // QBLK
    col_o = lax.broadcasted_iota(jnp.int32, (width, half), 0)
    a = lax.broadcasted_iota(jnp.int32, (half, half), 0) % QBLK
    a = ((a // rows) ^ lax.axis_index("layer")) * rows + a % rows
    same = a == (lax.broadcasted_iota(jnp.int32, (half, half), 1) % QBLK)
    for h in range(2):
        for s in range(2):
            pick_rows = (row * 2 + s == row_o).astype(BF16)
            rows = jnp.dot(pick_rows, outs[h], preferred_element_type=F32).astype(BF16)
            for t in range(2):
                pick_cols = (col * 2 + (s ^ t) == col_o).astype(BF16)
                spread = jnp.dot(rows, pick_cols, preferred_element_type=F32)
                left_ref[h, s, :, t * half : (t + 1) * half] = jnp.where(same, spread, 0.0).astype(BF16)
        up = (
            lax.broadcasted_iota(jnp.int32, (span, in_width), 0) % in_width
            == lax.broadcasted_iota(jnp.int32, (span, in_width), 1)
        ).astype(BF16)
        down = (
            lax.broadcasted_iota(jnp.int32, (in_width, span), 1) % in_width
            == lax.broadcasted_iota(jnp.int32, (in_width, span), 0)
        ).astype(BF16)
        wide = jnp.dot(
            jnp.dot(up, ins[h], preferred_element_type=F32).astype(BF16), down, preferred_element_type=F32
        )
        block = (lax.broadcasted_iota(jnp.int32, (span, span), 0) // in_width) == (
            lax.broadcasted_iota(jnp.int32, (span, span), 1) // in_width
        )
        right_ref[h] = jnp.where(block, wide, 0.0).astype(BF16)


def prepare(pair_ref, left_ref, right_ref, prep_ref):
    chunks = pair_ref.shape[1] // LANES
    half = LANES // 2
    stacked = []
    for side in range(2):
        block = pair_ref[side * QBLK : (side + 1) * QBLK, :]
        tall = jnp.concatenate([block[:, c * LANES : (c + 1) * LANES] for c in range(chunks)], axis=0)
        turned = jnp.concatenate([tall[:, half:], tall[:, :half]], axis=1)
        stacked.append(jnp.concatenate([tall, turned], axis=0))
    stacked = jnp.concatenate(stacked, axis=1)
    parts = [
        jnp.dot(left_ref[0, s], stacked, preferred_element_type=F32)
        + jnp.dot(left_ref[1, s], stacked, preferred_element_type=F32)
        for s in range(2)
    ]
    lane = lax.broadcasted_iota(jnp.int32, parts[0].shape, 1) % LANES
    high, low = split_bf16(jnp.where(lane < half, parts[0], parts[1]))
    done = (
        jnp.dot(high, right_ref[0], preferred_element_type=F32)
        + jnp.dot(low, right_ref[0], preferred_element_type=F32)
        + jnp.dot(high, right_ref[1], preferred_element_type=F32)
    ).astype(BF16)
    for side in range(2):
        for c in range(chunks):
            prep_ref[side, :, c * LANES : (c + 1) * LANES] = done[
                c * QBLK : (c + 1) * QBLK, side * LANES : (side + 1) * LANES
            ]


def first_kernel(rows, out_ref, in_ref, pair_ref, left_ref, right_ref, prep_ref):
    make_factors(rows, out_ref, in_ref, left_ref, right_ref)
    prepare(pair_ref, left_ref, right_ref, prep_ref)


def middle_kernel(*refs):
    early_ref, left_ref, right_ref = refs[:3]
    pairs, prep_ref = refs[3:-1], refs[-1]
    prep_ref[:2] = early_ref[...]
    for index, pair_ref in enumerate(pairs):
        prepare(pair_ref, left_ref, right_ref, prep_ref.at[pl.ds(2 + 2 * index, 2)])


def last_kernel(order, layer, held, slots, pairs_ref, pair_ref, early_ref, train_ref, left_ref, right_ref, *refs):
    outs, late_ref, rows_ref = refs[:layer], refs[layer], refs[layer + 1]
    ready = early_ref.shape[0]
    prepare(pair_ref, left_ref, right_ref, late_ref)
    me = lax.axis_index("ex")
    wanted = [pairs_ref[me * slots + slot] for slot in range(slots)]
    for slot, q in enumerate(wanted):
        k = (jnp.maximum(q, 0) // held) ^ me
        place = jnp.int32(0)
        for index, group in enumerate(order):
            place = jnp.where(k // 2 == group, 2 * index + k % 2, place)

        @pl.when(place < ready)
        def _():
            rows_ref[slot * QBLK : (slot + 1) * QBLK, :] = early_ref[jnp.minimum(place, ready - 1)]

        @pl.when(place >= ready)
        def _():
            rows_ref[slot * QBLK : (slot + 1) * QBLK, :] = late_ref[jnp.maximum(place - ready, 0)]

    tile = lax.dot_general(
        rows_ref[...], train_ref[...], (((1,), (1,)), ((), ())), preferred_element_type=F32
    )
    rows = QBLK // layer
    chosen = []
    for slot, q in enumerate(wanted):
        value = tile[slot * QBLK : (slot + 1) * QBLK]
        chosen.append(jnp.where(q >= 0, value, jnp.zeros_like(value)))
    for m in range(layer):
        part = jnp.concatenate([value[m * rows : (m + 1) * rows] for value in chosen], axis=0)
        outs[m][...] = part.astype(outs[m].dtype)


def finish_kernel(layer, *refs):
    parts, out_ref = refs[:layer], refs[layer]
    total = parts[0][...]
    for part in parts[1:]:
        total = total + part[...].astype(F32)
    rows = out_ref.shape[1]
    for slot in range(out_ref.shape[0]):
        out_ref[slot] = total[slot * rows : (slot + 1) * rows]


def shards(train_grads, query_grads, in_precond, out_precond, pair_blocks):
    ex = lax.axis_size("ex")
    layer = lax.axis_size("layer")
    train_rows, layers, features = train_grads.shape
    assert layers == 1
    held = query_grads.shape[0] // QBLK
    slots = pair_blocks.shape[0] // ex
    rows = QBLK // layer
    train = train_grads.reshape(train_rows, features)
    query = query_grads.reshape(query_grads.shape[0], features)
    in_factor = in_precond.reshape(in_precond.shape[1:])
    out_factor = out_precond.reshape(out_precond.shape[1:])
    limit = pltpu.CompilerParams(vmem_limit_bytes=24 * 2**20)

    def from_index(array, k):
        return lax.ppermute(array, "ex", [(i, i ^ k) for i in range(ex)])

    picked = pl.pallas_call(
        functools.partial(pick_kernel, ex, held, slots),
        out_shape=[jax.ShapeDtypeStruct((2 * QBLK, features), BF16)] * (ex // 2),
        in_specs=[SMEM, VMEM, VMEM],
        out_specs=[VMEM] * (ex // 2),
        compiler_params=limit,
        name="pick",
    )(pair_blocks, query, from_index(query, 1))

    order = sorted(range(ex // 2), key=lambda group: (bin(group).count("1"), group))
    blocks = [picked[0]] + [from_index(picked[group], 2 * group) for group in order[1:]]

    stack = features // LANES * QBLK
    span = 2 * LANES
    left, right, early = pl.pallas_call(
        functools.partial(first_kernel, rows),
        out_shape=[
            jax.ShapeDtypeStruct((2, 2, stack, 2 * stack), BF16),
            jax.ShapeDtypeStruct((2, span, span), BF16),
            jax.ShapeDtypeStruct((2, QBLK, features), BF16),
        ],
        in_specs=[VMEM] * 3,
        out_specs=[VMEM] * 3,
        compiler_params=limit,
        name="first",
    )(out_factor, in_factor, blocks[0])
    early = pl.pallas_call(
        middle_kernel,
        out_shape=jax.ShapeDtypeStruct((ex - 2, QBLK, features), BF16),
        in_specs=[VMEM] * (3 + len(order) - 2),
        out_specs=VMEM,
        compiler_params=limit,
        name="middle",
    )(early, left, right, *blocks[1:-1])
    parts = pl.pallas_call(
        functools.partial(last_kernel, order, layer, held, slots),
        out_shape=[jax.ShapeDtypeStruct((slots * rows, train_rows), F32)]
        + [jax.ShapeDtypeStruct((slots * rows, train_rows), BF16)] * (layer - 1),
        in_specs=[SMEM] + [VMEM] * 5,
        out_specs=[VMEM] * layer,
        scratch_shapes=[
            pltpu.VMEM((2, QBLK, features), BF16),
            pltpu.VMEM((slots * QBLK, features), BF16),
        ],
        compiler_params=limit,
        name="last",
    )(pair_blocks, blocks[-1], early, train, left, right)

    terms = [parts[0]] + [
        lax.ppermute(parts[m], "layer", [(i, i ^ m) for i in range(layer)]) for m in range(1, layer)
    ]
    out = pl.pallas_call(
        functools.partial(finish_kernel, layer),
        out_shape=jax.ShapeDtypeStruct((slots, rows, train_rows), F32),
        in_specs=[VMEM] * layer,
        out_specs=VMEM,
        compiler_params=limit,
        name="finish",
    )(*terms)
    return jnp.transpose(out, (1, 0, 2))


def solution(mesh):
    in_specs = (
        P("ex", "layer", None),
        P("ex", "layer", None),
        P("layer", None, None),
        P("layer", None, None),
        P(),
    )
    out_specs = P("layer", "ex", None)
    return jax.shard_map(shards, mesh=mesh, in_specs=in_specs, out_specs=out_specs, check_vma=False)
```

time: 41.1 us -> 39.1 us (0.951)
  waiting for transfers between devices: 5.57 us -> 14.1 us
  starting transfers between devices: 13.5 us -> 9.37 us
  local copies, waits for them, and re-layouts: 6.62 us -> 3.21 us
  Pallas kernels: 14.9 us -> 12.1 us
    ppermute x7 -> x4, waiting for transfers between devices: 0.17 us -> 8.75 us  [from_index(): return lax.ppermute(array, 'ex', [(i, i ^ k) for i in range(ex)])]
    ppermute x7 -> x4, starting transfers between devices: 9.13 us -> 4.92 us  [from_index(): return lax.ppermute(array, 'ex', [(i, i ^ k) for i in range(ex)])]
    unnamed x22 -> x10, local copies, waits for them, and re-layouts: 6.62 us -> 3.21 us
    pallas_call x4 -> x3, Pallas kernels: 12.7 us -> 10.8 us  [the longest x1 3.99 us: shards(): pl.pallas_call(functools.partial(last_kernel, order, layer, held, slots),...]
    pallas_call x1, Pallas kernels: 1.45 us -> 0.64 us  [shards(): pl.pallas_call(functools.partial(finish_kernel, layer), out_shape=jax.Sha...]
  transfers between devices with their start and end apart: 10 -> 7, of which waited for: 3 -> 5; matrix products, arithmetic and copies ran while one was open for 0% -> 0% of each run, Pallas kernels for 23% -> 17%
where the time goes in v3:
time: 39.1 us; the launch traced here: 38.8 us
  waiting for transfers between devices  14.1 us (36%)
  Pallas kernels  12.1 us (31%)
  starting transfers between devices  9.37 us (24%)
  local copies, waits for them, and re-layouts  3.21 us (8%)
    ppermute x4, waiting for transfers between devices, from_index(): return lax.ppermute(array, 'ex', [(i, i ^ k) for i in range(ex)])  8.75 us
    ppermute x3, waiting for transfers between devices, shards(): lax.ppermute(parts[m], 'layer', [(i, i ^ m) for i in range(layer)])  5.4 us
    ppermute x4, starting transfers between devices, from_index(): return lax.ppermute(array, 'ex', [(i, i ^ k) for i in range(ex)])  4.92 us
    ppermute x3, starting transfers between devices, shards(): lax.ppermute(parts[m], 'layer', [(i, i ^ m) for i in range(layer)])  4.45 us
    pallas_call x1, Pallas kernels, shards(): pl.pallas_call(functools.partial(last_kernel, order, layer, held, slots),...  3.99 us
    pallas_call x1, Pallas kernels, shards(): pl.pallas_call(functools.partial(first_kernel, rows), out_shape=[jax.Shap...  3.62 us
    unnamed x10, local copies, waits for them, and re-layouts  3.21 us
    pallas_call x1, Pallas kernels, shards(): pl.pallas_call(middle_kernel, out_shape=jax.ShapeDtypeStruct((ex - 2, QBL...  3.15 us
  transfers between devices with their start and end apart: 7, of which 5 were waited for; matrix products, arithmetic and copies ran while one was open for 0% of the time, Pallas kernels for 17%

profile of v3, /device:TPU:0, one launch (start us, length us, event | category | flops | bytes accessed | tf_op | source)
XLA Modules:
  0.0 38.8 jit_solution(12898209068215970630)
XLA Ops:
  0.0 0.0 copy-start
  0.0 0.5 %collective-permute-start = (bf16[64,4096]{1,0:T(8,128)(2,1)}, bf16[64,4096]{1,0:T(8,128)(2,1)S(1)}, u32[]{:S(2)}, u32[]{:S(2)}) collective-permute-start(bf16[64,4096]{1,0:T(8,128)(2,1)} %bitcast.6), channel_id=1, source_target_pairs={{0,1},{1,0},{2,3},{3,2},{4,5},{5,4},{6,7},{7,6},{8,9},{9,8},{10,11... | collective-permute-start | bytes 1572872 | tf_op jit(solution)/shard_map/ppermute | solution.py:187
  0.5 1.7 %collective-permute-done.other_ref = bf16[64,4096]{1,0:T(8,128)(2,1)S(1)} collective-permute-done((bf16[64,4096]{1,0:T(8,128)(2,1)}, bf16[64,4096]{1,0:T(8,128)(2,1)S(1)}, u32[]{:S(2)}, u32[]{:S(2)}) %collective-permute-start) | collective-permute-done | bytes 524320 | tf_op jit(solution)/shard_map/ppermute | solution.py:187
  2.2 0.0 copy-start.1
  2.2 1.0 %copy-done.1 = bf16[64,1,4096]{2,0,1:T(8,128)(2,1)S(1)} copy-done((bf16[64,1,4096]{2,0,1:T(8,128)(2,1)S(1)}, bf16[64,1,4096]{2,0,1:T(8,128)(2,1)}, u32[]{:S(2)}) %copy-start.1) | copy-done | bytes 524312
  3.2 0.0 copy-start.4
  3.2 0.7 %copy-done.4 = s32[48]{0:T(128)S(1)} copy-done((s32[48]{0:T(128)S(1)}, s32[48]{0:T(128)}, u32[]{:S(2)}) %copy-start.4) | copy-done | bytes 216
  3.9 0.7 %pick.1 = (bf16[32,4096]{1,0:T(8,128)(2,1)S(1)}, bf16[32,4096]{1,0:T(8,128)(2,1)S(1)}, bf16[32,4096]{1,0:T(8,128)(2,1)S(1)}, bf16[32,4096]{1,0:T(8,128)(2,1)S(1)}) custom-call(s32[48]{0:T(128)S(1)} %copy-done.4, bf16[64,4096]{1,0:T(8,128)(2,1)S(1)} %bitcast.7, bf16[64,4096]{1,0:T(8,128)(2,1)S(1)} %collective-permute-done.other_ref), custom_call_target="tpu_custom_call" | custom-call | tf_op jit(solution)/shard_map/pick/pallas_call | solution.py:189
  4.6 2.9 %collective-permute-start.2 = (bf16[32,4096]{1,0:T(8,128)(2,1)S(1)}, bf16[32,4096]{1,0:T(8,128)(2,1)S(1)}, u32[]{:S(2)}, u32[]{:S(2)}) collective-permute-start(bf16[32,4096]{1,0:T(8,128)(2,1)S(1)} %get-tuple-element.21), channel_id=1, source_target_pairs={{0,2},{1,3},{2,0},{3,1},{4,6},{5,7},{6,4},{7,5},{8,10},{9,11},{10,... | collective-permute-start | bytes 786440 | tf_op jit(solution)/shard_map/ppermute | solution.py:187
  7.5 1.5 %collective-permute-start.3 = (bf16[32,4096]{1,0:T(8,128)(2,1)S(1)}, bf16[32,4096]{1,0:T(8,128)(2,1)S(1)}, u32[]{:S(2)}, u32[]{:S(2)}) collective-permute-start(bf16[32,4096]{1,0:T(8,128)(2,1)S(1)} %get-tuple-element.22), channel_id=1, source_target_pairs={{0,4},{1,5},{2,6},{3,7},{4,0},{5,1},{6,2},{7,3},{8,12},{9,13},{10,... | collective-permute-start | bytes 786440 | tf_op jit(solution)/shard_map/ppermute | solution.py:187
  9.0 0.0 collective-permute-start.1
  9.0 0.0 copy-start.2
  9.0 0.8 %copy-done.2 = f32[1,64,64]{2,1,0:T(8,128)S(1)} copy-done((f32[1,64,64]{2,1,0:T(8,128)S(1)}, f32[1,64,64]{2,1,0:T(8,128)}, u32[]{:S(2)}) %copy-start.2) | copy-done | bytes 16408
  9.8 0.0 copy-start.3
  9.8 0.8 %copy-done.3 = f32[1,64,64]{2,1,0:T(8,128)S(1)} copy-done((f32[1,64,64]{2,1,0:T(8,128)S(1)}, f32[1,64,64]{2,1,0:T(8,128)}, u32[]{:S(2)}) %copy-start.3) | copy-done | bytes 16408
  10.5 3.6 %first.1 = (bf16[2,2,512,1024]{3,2,1,0:T(8,128)(2,1)S(1)}, bf16[2,256,256]{2,1,0:T(8,128)(2,1)S(1)}, bf16[2,16,4096]{2,1,0:T(8,128)(2,1)S(1)}) custom-call(f32[64,64]{1,0:T(8,128)S(1)} %bitcast.8, f32[64,64]{1,0:T(8,128)S(1)} %bitcast.9, bf16[32,4096]{1,0:T(8,128)(2,1)S(1)} %get-tuple-element.17.pair_ref), custom_call_target="tpu_custom_call" | custom-call | tf_op jit(solution)/shard_map/first/pallas_call | solution.py:203
  14.2 0.4 %collective-permute-done.2.refs_3_ = bf16[32,4096]{1,0:T(8,128)(2,1)S(1)} collective-permute-done((bf16[32,4096]{1,0:T(8,128)(2,1)S(1)}, bf16[32,4096]{1,0:T(8,128)(2,1)S(1)}, u32[]{:S(2)}, u32[]{:S(2)}) %collective-permute-start.2) | collective-permute-done | bytes 262176 | tf_op jit(solution)/shard_map/ppermute | solution.py:187
  14.6 6.6 %collective-permute-done.3.refs_4_ = bf16[32,4096]{1,0:T(8,128)(2,1)S(1)} collective-permute-done((bf16[32,4096]{1,0:T(8,128)(2,1)S(1)}, bf16[32,4096]{1,0:T(8,128)(2,1)S(1)}, u32[]{:S(2)}, u32[]{:S(2)}) %collective-permute-start.3) | collective-permute-done | bytes 262176 | tf_op jit(solution)/shard_map/ppermute | solution.py:187
  21.2 3.2 %middle.1.early_ref = bf16[6,16,4096]{2,1,0:T(8,128)(2,1)S(1)} custom-call(bf16[2,16,4096]{2,1,0:T(8,128)(2,1)S(1)} %get-tuple-element.18.refs_0_, bf16[2,2,512,1024]{3,2,1,0:T(8,128)(2,1)S(1)} %get-tuple-element.19.refs_1_.left_ref, bf16[2,256,256]{2,1,0:T(8,128)(2,1)S(1)} %get-tuple-element.20.refs_2_.right_ref, ...), custom_call_target="tpu_custom_call" | custom-call | tf_op jit(solution)/shard_map/middle/pallas_call | solution.py:215
  24.3 0.0 collective-permute-done.1.pair_ref
  24.3 0.0 copy-done
  24.4 4.0 %last.1 = (f32[24,512]{1,0:T(8,128)S(1)}, bf16[24,512]{1,0:T(8,128)(2,1)S(1)}, bf16[24,512]{1,0:T(8,128)(2,1)S(1)}, bf16[24,512]{1,0:T(8,128)(2,1)S(1)}) custom-call(s32[48]{0:T(128)S(1)} %copy-done.4, bf16[32,4096]{1,0:T(8,128)(2,1)S(1)} %collective-permute-done.1.pair_ref, bf16[6,16,4096]{2,1,0:T(8,128)(2,1)S(1)} %middle.1.early_ref, ...), custom_call_target="tpu_custom_call" | custom-call | tf_op jit(solution)/shard_map/last/pallas_call | solution.py:223
  28.4 1.6 %collective-permute-start.4 = (bf16[24,512]{1,0:T(8,128)(2,1)S(1)}, bf16[24,512]{1,0:T(8,128)(2,1)S(1)}, u32[]{:S(2)}, u32[]{:S(2)}) collective-permute-start(bf16[24,512]{1,0:T(8,128)(2,1)S(1)} %get-tuple-element.24), channel_id=1, source_target_pairs={{0,8},{8,0},{16,24},{24,16},{1,9},{9,1},{17,25},{25,17},{2,10},{10... | collective-permute-start | bytes 73736 | tf_op jit(solution)/shard_map/ppermute | solution.py:238
  30.0 2.6 %collective-permute-start.5 = (bf16[24,512]{1,0:T(8,128)(2,1)S(1)}, bf16[24,512]{1,0:T(8,128)(2,1)S(1)}, u32[]{:S(2)}, u32[]{:S(2)}) collective-permute-start(bf16[24,512]{1,0:T(8,128)(2,1)S(1)} %get-tuple-element.25), channel_id=1, source_target_pairs={{0,16},{8,24},{16,0},{24,8},{1,17},{9,25},{17,1},{25,9},{2,18},{10... | collective-permute-start | bytes 73736 | tf_op jit(solution)/shard_map/ppermute | solution.py:238
  32.6 0.2 collective-permute-start.6
  32.8 0.0 collective-permute-done.4.refs_1_
  32.8 2.1 %collective-permute-done.5.refs_2_ = bf16[24,512]{1,0:T(8,128)(2,1)S(1)} collective-permute-done((bf16[24,512]{1,0:T(8,128)(2,1)S(1)}, bf16[24,512]{1,0:T(8,128)(2,1)S(1)}, u32[]{:S(2)}, u32[]{:S(2)}) %collective-permute-start.5) | collective-permute-done | bytes 24608 | tf_op jit(solution)/shard_map/ppermute | solution.py:238
  34.9 3.3 %collective-permute-done.6.refs_3_ = bf16[24,512]{1,0:T(8,128)(2,1)S(1)} collective-permute-done((bf16[24,512]{1,0:T(8,128)(2,1)S(1)}, bf16[24,512]{1,0:T(8,128)(2,1)S(1)}, u32[]{:S(2)}, u32[]{:S(2)}) %collective-permute-start.6) | collective-permute-done | bytes 24608 | tf_op jit(solution)/shard_map/ppermute | solution.py:238
  38.2 0.6 %finish.1 = f32[6,4,512]{2,1,0:T(4,128)} custom-call(f32[24,512]{1,0:T(8,128)S(1)} %get-tuple-element.23.refs_0_, bf16[24,512]{1,0:T(8,128)(2,1)S(1)} %collective-permute-done.4.refs_1_, bf16[24,512]{1,0:T(8,128)(2,1)S(1)} %collective-permute-done.5.refs_2_, bf16[24,512]{1,0:T(8,128)(2,1)S(1)} %collective-permute-done.6.refs_3_), custom_call_target="tpu_custom_call" | custom-call | tf_op jit(solution)/shard_map/finish/pallas_call | solution.py:240
Async XLA Ops:
  0.0 24.3 %copy-start = (bf16[512,1,4096]{2,0,1:T(8,128)(2,1)S(1)}, bf16[512,1,4096]{2,0,1:T(8,128)(2,1)}, u32[]{:S(2)}) copy-start(bf16[512,1,4096]{2,0,1:T(8,128)(2,1)} %param.5) | copy-start | bytes 12582916
  0.0 2.2 %collective-permute-start = (bf16[64,4096]{1,0:T(8,128)(2,1)}, bf16[64,4096]{1,0:T(8,128)(2,1)S(1)}, u32[]{:S(2)}, u32[]{:S(2)}) collective-permute-start(bf16[64,4096]{1,0:T(8,128)(2,1)} %bitcast.6), channel_id=1, source_target_pairs={{0,1},{1,0},{2,3},{3,2},{4,5},{5,4},{6,7},{7,6},{8,9},{9,8},{10,11... | collective-permute-start | bytes 1572872 | tf_op jit(solution)/shard_map/ppermute | solution.py:187
  2.2 1.0 %copy-start.1 = (bf16[64,1,4096]{2,0,1:T(8,128)(2,1)S(1)}, bf16[64,1,4096]{2,0,1:T(8,128)(2,1)}, u32[]{:S(2)}) copy-start(bf16[64,1,4096]{2,0,1:T(8,128)(2,1)} %param.6) | copy-start | bytes 1572868
  3.2 0.7 %copy-start.4 = (s32[48]{0:T(128)S(1)}, s32[48]{0:T(128)}, u32[]{:S(2)}) copy-start(s32[48]{0:T(128)} %pairs_ref.3) | copy-start | bytes 580
  4.6 10.0 %collective-permute-start.2 = (bf16[32,4096]{1,0:T(8,128)(2,1)S(1)}, bf16[32,4096]{1,0:T(8,128)(2,1)S(1)}, u32[]{:S(2)}, u32[]{:S(2)}) collective-permute-start(bf16[32,4096]{1,0:T(8,128)(2,1)S(1)} %get-tuple-element.21), channel_id=1, source_target_pairs={{0,2},{1,3},{2,0},{3,1},{4,6},{5,7},{6,4},{7,5},{8,10},{9,11},{10,... | collective-permute-start | bytes 786440 | tf_op jit(solution)/shard_map/ppermute | solution.py:187
  7.5 13.7 %collective-permute-start.3 = (bf16[32,4096]{1,0:T(8,128)(2,1)S(1)}, bf16[32,4096]{1,0:T(8,128)(2,1)S(1)}, u32[]{:S(2)}, u32[]{:S(2)}) collective-permute-start(bf16[32,4096]{1,0:T(8,128)(2,1)S(1)} %get-tuple-element.22), channel_id=1, source_target_pairs={{0,4},{1,5},{2,6},{3,7},{4,0},{5,1},{6,2},{7,3},{8,12},{9,13},{10,... | collective-permute-start | bytes 786440 | tf_op jit(solution)/shard_map/ppermute | solution.py:187
  9.0 15.3 %collective-permute-start.1 = (bf16[32,4096]{1,0:T(8,128)(2,1)S(1)}, bf16[32,4096]{1,0:T(8,128)(2,1)S(1)}, u32[]{:S(2)}, u32[]{:S(2)}) collective-permute-start(bf16[32,4096]{1,0:T(8,128)(2,1)S(1)} %get-tuple-element.16), channel_id=1, source_target_pairs={{0,6},{1,7},{2,4},{3,5},{4,2},{5,3},{6,0},{7,1},{8,14},{9,15},{10,... | collective-permute-start | bytes 786440 | tf_op jit(solution)/shard_map/ppermute | solution.py:187
  9.0 0.8 %copy-start.2 = (f32[1,64,64]{2,1,0:T(8,128)S(1)}, f32[1,64,64]{2,1,0:T(8,128)}, u32[]{:S(2)}) copy-start(f32[1,64,64]{2,1,0:T(8,128)} %param.8) | copy-start | bytes 49156
  9.8 0.8 %copy-start.3 = (f32[1,64,64]{2,1,0:T(8,128)S(1)}, f32[1,64,64]{2,1,0:T(8,128)}, u32[]{:S(2)}) copy-start(f32[1,64,64]{2,1,0:T(8,128)} %param.7) | copy-start | bytes 49156
  28.4 4.5 %collective-permute-start.4 = (bf16[24,512]{1,0:T(8,128)(2,1)S(1)}, bf16[24,512]{1,0:T(8,128)(2,1)S(1)}, u32[]{:S(2)}, u32[]{:S(2)}) collective-permute-start(bf16[24,512]{1,0:T(8,128)(2,1)S(1)} %get-tuple-element.24), channel_id=1, source_target_pairs={{0,8},{8,0},{16,24},{24,16},{1,9},{9,1},{17,25},{25,17},{2,10},{10... | collective-permute-start | bytes 73736 | tf_op jit(solution)/shard_map/ppermute | solution.py:238
  30.0 4.9 %collective-permute-start.5 = (bf16[24,512]{1,0:T(8,128)(2,1)S(1)}, bf16[24,512]{1,0:T(8,128)(2,1)S(1)}, u32[]{:S(2)}, u32[]{:S(2)}) collective-permute-start(bf16[24,512]{1,0:T(8,128)(2,1)S(1)} %get-tuple-element.25), channel_id=1, source_target_pairs={{0,16},{8,24},{16,0},{24,8},{1,17},{9,25},{17,1},{25,9},{2,18},{10... | collective-permute-start | bytes 73736 | tf_op jit(solution)/shard_map/ppermute | solution.py:238
  32.6 5.6 %collective-permute-start.6 = (bf16[24,512]{1,0:T(8,128)(2,1)S(1)}, bf16[24,512]{1,0:T(8,128)(2,1)S(1)}, u32[]{:S(2)}, u32[]{:S(2)}) collective-permute-start(bf16[24,512]{1,0:T(8,128)(2,1)S(1)} %get-tuple-element.26), channel_id=1, source_target_pairs={{0,24},{8,16},{16,8},{24,0},{1,25},{9,17},{17,9},{25,1},{2,26},{10... | collective-permute-start | bytes 73736 | tf_op jit(solution)/shard_map/ppermute | solution.py:238

commit v4 on v3

--- a/solution.py
+++ b/solution.py
@@ -29,20 +29,28 @@
     return init
 
 
-def pick_kernel(ex, held, slots, pairs_ref, own_ref, other_ref, *outs):
+def wanted_block(ex, held, slots, pairs_ref, group, side):
     me = lax.axis_index("ex")
-    for group in range(ex // 2):
-        first = (me ^ (2 * group)) * slots
-        for side, source in enumerate((own_ref, other_ref)):
-            base = (me ^ side) * held
-
-            def body(slot, block):
-                local = pairs_ref[first + slot] - base
-                return jnp.where((local >= 0) & (local < held), local, block)
-
-            block = over_slots(slots, body, jnp.int32(0))
-            start = pl.multiple_of(block * QBLK, QBLK)
-            outs[group][side * QBLK : (side + 1) * QBLK, :] = source[pl.ds(start, QBLK), :]
+    first = (me ^ (2 * group)) * slots
+    base = (me ^ side) * held
+
+    def body(slot, block):
+        local = pairs_ref[first + slot] - base
+        return jnp.where((local >= 0) & (local < held), local, block)
+
+    return pl.multiple_of(over_slots(slots, body, jnp.int32(0)) * QBLK, QBLK)
+
+
+def own_kernel(find, pairs_ref, query_ref, *outs):
+    for group, out_ref in enumerate(outs):
+        out_ref[...] = query_ref[pl.ds(find(pairs_ref, group, 0), QBLK), :]
+
+
+def pick_kernel(find, groups, pairs_ref, other_ref, *refs):
+    for group in range(groups):
+        out_ref = refs[groups + group]
+        out_ref[:QBLK] = refs[group][...]
+        out_ref[QBLK:] = other_ref[pl.ds(find(pairs_ref, group, 1), QBLK), :]
 
 
 def make_factors(rows, out_ref, in_ref, left_ref, right_ref):
@@ -56,9 +64,8 @@
     row_o = lax.broadcasted_iota(jnp.int32, (half, width), 1)
     col = lax.broadcasted_iota(jnp.int32, (width, half), 1) // QBLK
     col_o = lax.broadcasted_iota(jnp.int32, (width, half), 0)
-    a = lax.broadcasted_iota(jnp.int32, (half, half), 0) % QBLK
-    a = ((a // rows) ^ lax.axis_index("layer")) * rows + a % rows
-    same = a == (lax.broadcasted_iota(jnp.int32, (half, half), 1) % QBLK)
+    a = lax.broadcasted_iota(jnp.int32, (half, half), 0) ^ lax.broadcasted_iota(jnp.int32, (half, half), 1)
+    same = (a & (QBLK - 1)) == lax.axis_index("layer") * rows
     for h in range(2):
         for s in range(2):
             pick_rows = (row * 2 + s == row_o).astype(BF16)
@@ -118,18 +125,17 @@
     prepare(pair_ref, left_ref, right_ref, prep_ref)
 
 
-def middle_kernel(*refs):
-    early_ref, left_ref, right_ref = refs[:3]
-    pairs, prep_ref = refs[3:-1], refs[-1]
-    prep_ref[:2] = early_ref[...]
-    for index, pair_ref in enumerate(pairs):
-        prepare(pair_ref, left_ref, right_ref, prep_ref.at[pl.ds(2 + 2 * index, 2)])
-
-
-def last_kernel(order, layer, held, slots, pairs_ref, pair_ref, early_ref, train_ref, left_ref, right_ref, *refs):
-    outs, late_ref, rows_ref = refs[:layer], refs[layer], refs[layer + 1]
+def near_kernel(done, left_ref, right_ref, *refs):
+    prep_ref = refs[-1]
+    if done:
+        prep_ref[:done] = refs[0][...]
+    for index, pair_ref in enumerate(refs[min(done, 1) : -1]):
+        prepare(pair_ref, left_ref, right_ref, prep_ref.at[pl.ds(done + 2 * index, 2)])
+
+
+def last_kernel(order, layer, held, slots, pairs_ref, late_ref, early_ref, train_ref, *refs):
+    outs, rows_ref = refs[:layer], refs[layer]
     ready = early_ref.shape[0]
-    prepare(pair_ref, left_ref, right_ref, late_ref)
     me = lax.axis_index("ex")
     wanted = [pairs_ref[me * slots + slot] for slot in range(slots)]
     for slot, q in enumerate(wanted):
@@ -186,21 +192,32 @@
     def from_index(array, k):
         return lax.ppermute(array, "ex", [(i, i ^ k) for i in range(ex)])
 
+    groups = ex // 2
+    find = functools.partial(wanted_block, ex, held, slots)
+    other = from_index(query, 1)
+    own = pl.pallas_call(
+        functools.partial(own_kernel, find),
+        out_shape=[jax.ShapeDtypeStruct((QBLK, features), BF16)] * groups,
+        in_specs=[SMEM, VMEM],
+        out_specs=[VMEM] * groups,
+        compiler_params=limit,
+        name="own",
+    )(pair_blocks, query)
     picked = pl.pallas_call(
-        functools.partial(pick_kernel, ex, held, slots),
-        out_shape=[jax.ShapeDtypeStruct((2 * QBLK, features), BF16)] * (ex // 2),
-        in_specs=[SMEM, VMEM, VMEM],
-        out_specs=[VMEM] * (ex // 2),
+        functools.partial(pick_kernel, find, groups),
+        out_shape=[jax.ShapeDtypeStruct((2 * QBLK, features), BF16)] * groups,
+        in_specs=[SMEM] + [VMEM] * (1 + groups),
+        out_specs=[VMEM] * groups,
         compiler_params=limit,
         name="pick",
-    )(pair_blocks, query, from_index(query, 1))
-
-    order = sorted(range(ex // 2), key=lambda group: (bin(group).count("1"), group))
-    blocks = [picked[0]] + [from_index(picked[group], 2 * group) for group in order[1:]]
+    )(pair_blocks, other, *own)
+
+    order = sorted(range(groups), key=lambda group: (bin(group).count("1"), group))
+    raw = [from_index(picked[group], 2 * group) for group in order[1:-1]]
 
     stack = features // LANES * QBLK
     span = 2 * LANES
-    left, right, early = pl.pallas_call(
+    left, right, far = pl.pallas_call(
         functools.partial(first_kernel, rows),
         out_shape=[
             jax.ShapeDtypeStruct((2, 2, stack, 2 * stack), BF16),
@@ -211,28 +228,33 @@
         out_specs=[VMEM] * 3,
         compiler_params=limit,
         name="first",
-    )(out_factor, in_factor, blocks[0])
-    early = pl.pallas_call(
-        middle_kernel,
-        out_shape=jax.ShapeDtypeStruct((ex - 2, QBLK, features), BF16),
-        in_specs=[VMEM] * (3 + len(order) - 2),
-        out_specs=VMEM,
-        compiler_params=limit,
-        name="middle",
-    )(early, left, right, *blocks[1:-1])
+    )(out_factor, in_factor, picked[order[-1]])
+    far = from_index(far, 2 * order[-1])
+
+    early, done = [], 0
+    half = len(raw) // 2
+    for index, pairs in enumerate(([picked[0]], raw[:half], raw[half:])):
+        early = [
+            pl.pallas_call(
+                functools.partial(near_kernel, done),
+                out_shape=jax.ShapeDtypeStruct((done + 2 * len(pairs), QBLK, features), BF16),
+                in_specs=[VMEM] * (2 + len(early) + len(pairs)),
+                out_specs=VMEM,
+                compiler_params=limit,
+                name=f"near{index}",
+            )(left, right, *early, *pairs)
+        ]
+        done += 2 * len(pairs)
     parts = pl.pallas_call(
         functools.partial(last_kernel, order, layer, held, slots),
         out_shape=[jax.ShapeDtypeStruct((slots * rows, train_rows), F32)]
         + [jax.ShapeDtypeStruct((slots * rows, train_rows), BF16)] * (layer - 1),
-        in_specs=[SMEM] + [VMEM] * 5,
+        in_specs=[SMEM] + [VMEM] * 3,
         out_specs=[VMEM] * layer,
-        scratch_shapes=[
-            pltpu.VMEM((2, QBLK, features), BF16),
-            pltpu.VMEM((slots * QBLK, features), BF16),
-        ],
+        scratch_shapes=[pltpu.VMEM((slots * QBLK, features), BF16)],
         compiler_params=limit,
         name="last",
-    )(pair_blocks, blocks[-1], early, train, left, right)
+    )(pair_blocks, far, *early, train)
 
     terms = [parts[0]] + [
         lax.ppermute(parts[m], "layer", [(i, i ^ m) for i in range(layer)]) for m in range(1, layer)

time: 39.1 us -> 34.7 us (0.89)
  waiting for transfers between devices: 14.1 us -> 8.8 us
  Pallas kernels: 12.1 us -> 13.2 us
    ppermute x4, waiting for transfers between devices: 8.75 us -> 3.4 us  [from_index(): return lax.ppermute(array, 'ex', [(i, i ^ k) for i in range(ex)])]
    pallas_call x2 -> x5, Pallas kernels: 3.81 us -> 6.82 us  [the longest x3 5.58 us: shards(): pl.pallas_call(functools.partial(near_kernel, done), out_shape=jax.ShapeD...]
    pallas_call x1, Pallas kernels: 3.99 us -> 2.15 us  [shards(): pl.pallas_call(functools.partial(last_kernel, order, layer, held, slots),...]
    unnamed x10 -> x12, local copies, waits for them, and re-layouts: 3.21 us -> 3.22 us
  transfers between devices with their start and end apart: 7 -> 7, of which waited for: 5 -> 3; matrix products, arithmetic and copies ran while one was open for 0% -> 0% of each run, Pallas kernels for 17% -> 28%
where the time goes in v4:
time: 34.7 us; the launch traced here: 34.4 us
  Pallas kernels  13.2 us (38%)
  starting transfers between devices  9.06 us (26%)
  waiting for transfers between devices  8.8 us (25%)
  local copies, waits for them, and re-layouts  3.22 us (9%)
    pallas_call x3, Pallas kernels, shards(): pl.pallas_call(functools.partial(near_kernel, done), out_shape=jax.ShapeD...  5.58 us
    ppermute x3, waiting for transfers between devices, shards(): lax.ppermute(parts[m], 'layer', [(i, i ^ m) for i in range(layer)])  5.4 us
    ppermute x4, starting transfers between devices, from_index(): return lax.ppermute(array, 'ex', [(i, i ^ k) for i in range(ex)])  4.61 us
    ppermute x3, starting transfers between devices, shards(): lax.ppermute(parts[m], 'layer', [(i, i ^ m) for i in range(layer)])  4.45 us
    pallas_call x1, Pallas kernels, shards(): pl.pallas_call(functools.partial(first_kernel, rows), out_shape=[jax.Shap...  3.6 us
    ppermute x4, waiting for transfers between devices, from_index(): return lax.ppermute(array, 'ex', [(i, i ^ k) for i in range(ex)])  3.4 us
    unnamed x12, local copies, waits for them, and re-layouts  3.22 us
    pallas_call x1, Pallas kernels, shards(): pl.pallas_call(functools.partial(last_kernel, order, layer, held, slots),...  2.15 us
  transfers between devices with their start and end apart: 7, of which 3 were waited for; matrix products, arithmetic and copies ran while one was open for 0% of the time, Pallas kernels for 28%

profile of v4, /device:TPU:0, one launch (start us, length us, event | category | flops | bytes accessed | tf_op | source)
XLA Modules:
  0.0 34.4 jit_solution(2656133264577368834)
XLA Ops:
  0.0 0.5 %collective-permute-start = (bf16[64,4096]{1,0:T(8,128)(2,1)}, bf16[64,4096]{1,0:T(8,128)(2,1)S(1)}, u32[]{:S(2)}, u32[]{:S(2)}) collective-permute-start(bf16[64,4096]{1,0:T(8,128)(2,1)} %bitcast.6), channel_id=1, source_target_pairs={{0,1},{1,0},{2,3},{3,2},{4,5},{5,4},{6,7},{7,6},{8,9},{9,8},{10,11... | collective-permute-start | bytes 1572872 | tf_op jit(solution)/shard_map/ppermute | solution.py:193
  0.5 0.0 copy-start.1
  0.5 1.0 %copy-done.1 = bf16[64,1,4096]{2,0,1:T(8,128)(2,1)S(1)} copy-done((bf16[64,1,4096]{2,0,1:T(8,128)(2,1)S(1)}, bf16[64,1,4096]{2,0,1:T(8,128)(2,1)}, u32[]{:S(2)}) %copy-start.1) | copy-done | bytes 524312
  1.5 0.0 copy-start.4
  1.5 0.7 %copy-done.4 = s32[48]{0:T(128)S(1)} copy-done((s32[48]{0:T(128)S(1)}, s32[48]{0:T(128)}, u32[]{:S(2)}) %copy-start.4) | copy-done | bytes 216
  2.2 0.6 %own.1 = (bf16[16,4096]{1,0:T(8,128)(2,1)S(1)}, bf16[16,4096]{1,0:T(8,128)(2,1)S(1)}, bf16[16,4096]{1,0:T(8,128)(2,1)S(1)}, bf16[16,4096]{1,0:T(8,128)(2,1)S(1)}) custom-call(s32[48]{0:T(128)S(1)} %copy-done.4, bf16[64,4096]{1,0:T(8,128)(2,1)S(1)} %bitcast.7), custom_call_target="tpu_custom_call" | custom-call | tf_op jit(solution)/shard_map/own/pallas_call | solution.py:198
  2.8 0.0 collective-permute-done.other_ref
  2.8 0.6 %pick.1 = (bf16[32,4096]{1,0:T(8,128)(2,1)S(1)}, bf16[32,4096]{1,0:T(8,128)(2,1)S(1)}, bf16[32,4096]{1,0:T(8,128)(2,1)S(1)}, bf16[32,4096]{1,0:T(8,128)(2,1)S(1)}) custom-call(s32[48]{0:T(128)S(1)} %copy-done.4, bf16[64,4096]{1,0:T(8,128)(2,1)S(1)} %collective-permute-done.other_ref, bf16[16,4096]{1,0:T(8,128)(2,1)S(1)} %get-tuple-element.20.refs_0_, ...), custom_call_target="tpu_custom_call" | custom-call | tf_op jit(solution)/shard_map/pick/pallas_call | solution.py:206
  3.4 2.6 %collective-permute-start.2 = (bf16[32,4096]{1,0:T(8,128)(2,1)S(1)}, bf16[32,4096]{1,0:T(8,128)(2,1)S(1)}, u32[]{:S(2)}, u32[]{:S(2)}) collective-permute-start(bf16[32,4096]{1,0:T(8,128)(2,1)S(1)} %get-tuple-element.29), channel_id=1, source_target_pairs={{0,2},{1,3},{2,0},{3,1},{4,6},{5,7},{6,4},{7,5},{8,10},{9,11},{10,... | collective-permute-start | bytes 786440 | tf_op jit(solution)/shard_map/ppermute | solution.py:193
  6.0 1.5 %collective-permute-start.3 = (bf16[32,4096]{1,0:T(8,128)(2,1)S(1)}, bf16[32,4096]{1,0:T(8,128)(2,1)S(1)}, u32[]{:S(2)}, u32[]{:S(2)}) collective-permute-start(bf16[32,4096]{1,0:T(8,128)(2,1)S(1)} %get-tuple-element.30), channel_id=1, source_target_pairs={{0,4},{1,5},{2,6},{3,7},{4,0},{5,1},{6,2},{7,3},{8,12},{9,13},{10,... | collective-permute-start | bytes 786440 | tf_op jit(solution)/shard_map/ppermute | solution.py:193
  7.5 0.0 copy-start.2
  7.5 0.8 %copy-done.2 = f32[1,64,64]{2,1,0:T(8,128)S(1)} copy-done((f32[1,64,64]{2,1,0:T(8,128)S(1)}, f32[1,64,64]{2,1,0:T(8,128)}, u32[]{:S(2)}) %copy-start.2) | copy-done | bytes 16408
  8.2 0.0 copy-start.3
  8.3 0.8 %copy-done.3 = f32[1,64,64]{2,1,0:T(8,128)S(1)} copy-done((f32[1,64,64]{2,1,0:T(8,128)S(1)}, f32[1,64,64]{2,1,0:T(8,128)}, u32[]{:S(2)}) %copy-start.3) | copy-done | bytes 16408
  9.0 3.6 %first.1 = (bf16[2,2,512,1024]{3,2,1,0:T(8,128)(2,1)S(1)}, bf16[2,256,256]{2,1,0:T(8,128)(2,1)S(1)}, bf16[2,16,4096]{2,1,0:T(8,128)(2,1)S(1)}) custom-call(f32[64,64]{1,0:T(8,128)S(1)} %bitcast.8, f32[64,64]{1,0:T(8,128)S(1)} %bitcast.9, bf16[32,4096]{1,0:T(8,128)(2,1)S(1)} %get-tuple-element.24.pair_ref), custom_call_target="tpu_custom_call" | custom-call | tf_op jit(solution)/shard_map/first/pallas_call | solution.py:220
  12.6 0.1 collective-permute-start.1
  12.7 1.9 %near0.1.refs_0_ = bf16[2,16,4096]{2,1,0:T(8,128)(2,1)S(1)} custom-call(bf16[2,2,512,1024]{3,2,1,0:T(8,128)(2,1)S(1)} %get-tuple-element.26.left_ref, bf16[2,256,256]{2,1,0:T(8,128)(2,1)S(1)} %get-tuple-element.27.right_ref, bf16[32,4096]{1,0:T(8,128)(2,1)S(1)} %get-tuple-element.28.refs_0_), custom_call_target="tpu_custom_call" | custom-call | tf_op jit(solution)/shard_map/near0/pallas_call | solution.py:238
  14.6 0.0 collective-permute-done.2.refs_1_
  14.6 1.9 %near1.1.refs_0_ = bf16[4,16,4096]{2,1,0:T(8,128)(2,1)S(1)} custom-call(bf16[2,2,512,1024]{3,2,1,0:T(8,128)(2,1)S(1)} %get-tuple-element.26.left_ref, bf16[2,256,256]{2,1,0:T(8,128)(2,1)S(1)} %get-tuple-element.27.right_ref, bf16[2,16,4096]{2,1,0:T(8,128)(2,1)S(1)} %near0.1.refs_0_, bf16[32,4096]{1,0:T(8,128)(2,1)S(1)} %collective-permute-done.2.refs_1_), custom_call_target="tpu_custom_call" | custom-call | tf_op jit(solution)/shard_map/near1/pallas_call | solution.py:238
  16.4 0.0 copy-start
  16.4 0.0 copy-start.5
  16.5 0.0 collective-permute-done.3.refs_1_
  16.5 1.9 %near2.1.early_ref = bf16[6,16,4096]{2,1,0:T(8,128)(2,1)S(1)} custom-call(bf16[2,2,512,1024]{3,2,1,0:T(8,128)(2,1)S(1)} %get-tuple-element.26.left_ref, bf16[2,256,256]{2,1,0:T(8,128)(2,1)S(1)} %get-tuple-element.27.right_ref, bf16[4,16,4096]{2,1,0:T(8,128)(2,1)S(1)} %near1.1.refs_0_, bf16[32,4096]{1,0:T(8,128)(2,1)S(1)} %collective-permute-done.3.refs_1_), custom_call_target="tpu_custom_call" | custom-call | tf_op jit(solution)/shard_map/near2/pallas_call | solution.py:238
  18.3 3.4 %collective-permute-done.1.late_ref = bf16[2,16,4096]{2,1,0:T(8,128)(2,1)S(1)} collective-permute-done((bf16[2,16,4096]{2,1,0:T(8,128)(2,1)S(1)}, bf16[2,16,4096]{2,1,0:T(8,128)(2,1)S(1)}, u32[]{:S(2)}, u32[]{:S(2)}) %collective-permute-start.1) | collective-permute-done | bytes 262176 | tf_op jit(solution)/shard_map/ppermute | solution.py:193
  21.7 0.0 copy-done
  21.7 0.0 copy-done.5
  21.7 2.1 %last.1 = (f32[24,512]{1,0:T(8,128)S(1)}, bf16[24,512]{1,0:T(8,128)(2,1)S(1)}, bf16[24,512]{1,0:T(8,128)(2,1)S(1)}, bf16[24,512]{1,0:T(8,128)(2,1)S(1)}) custom-call(s32[48]{0:T(128)S(1)} %copy-done.5, bf16[2,16,4096]{2,1,0:T(8,128)(2,1)S(1)} %collective-permute-done.1.late_ref, bf16[6,16,4096]{2,1,0:T(8,128)(2,1)S(1)} %near2.1.early_ref, ...), custom_call_target="tpu_custom_call" | custom-call | tf_op jit(solution)/shard_map/last/pallas_call | solution.py:248
  23.9 1.6 %collective-permute-start.4 = (bf16[24,512]{1,0:T(8,128)(2,1)S(1)}, bf16[24,512]{1,0:T(8,128)(2,1)S(1)}, u32[]{:S(2)}, u32[]{:S(2)}) collective-permute-start(bf16[24,512]{1,0:T(8,128)(2,1)S(1)} %get-tuple-element.32), channel_id=1, source_target_pairs={{0,8},{8,0},{16,24},{24,16},{1,9},{9,1},{17,25},{25,17},{2,10},{10... | collective-permute-start | bytes 73736 | tf_op jit(solution)/shard_map/ppermute | solution.py:260
  25.5 2.6 %collective-permute-start.5 = (bf16[24,512]{1,0:T(8,128)(2,1)S(1)}, bf16[24,512]{1,0:T(8,128)(2,1)S(1)}, u32[]{:S(2)}, u32[]{:S(2)}) collective-permute-start(bf16[24,512]{1,0:T(8,128)(2,1)S(1)} %get-tuple-element.33), channel_id=1, source_target_pairs={{0,16},{8,24},{16,0},{24,8},{1,17},{9,25},{17,1},{25,9},{2,18},{10... | collective-permute-start | bytes 73736 | tf_op jit(solution)/shard_map/ppermute | solution.py:260
  28.1 0.2 collective-permute-start.6
  28.3 0.0 collective-permute-done.4.refs_1_
  28.4 2.1 %collective-permute-done.5.refs_2_ = bf16[24,512]{1,0:T(8,128)(2,1)S(1)} collective-permute-done((bf16[24,512]{1,0:T(8,128)(2,1)S(1)}, bf16[24,512]{1,0:T(8,128)(2,1)S(1)}, u32[]{:S(2)}, u32[]{:S(2)}) %collective-permute-start.5) | collective-permute-done | bytes 24608 | tf_op jit(solution)/shard_map/ppermute | solution.py:260
  30.4 3.3 %collective-permute-done.6.refs_3_ = bf16[24,512]{1,0:T(8,128)(2,1)S(1)} collective-permute-done((bf16[24,512]{1,0:T(8,128)(2,1)S(1)}, bf16[24,512]{1,0:T(8,128)(2,1)S(1)}, u32[]{:S(2)}, u32[]{:S(2)}) %collective-permute-start.6) | collective-permute-done | bytes 24608 | tf_op jit(solution)/shard_map/ppermute | solution.py:260
  33.8 0.6 %finish.1 = f32[6,4,512]{2,1,0:T(4,128)} custom-call(f32[24,512]{1,0:T(8,128)S(1)} %get-tuple-element.31.refs_0_, bf16[24,512]{1,0:T(8,128)(2,1)S(1)} %collective-permute-done.4.refs_1_, bf16[24,512]{1,0:T(8,128)(2,1)S(1)} %collective-permute-done.5.refs_2_, bf16[24,512]{1,0:T(8,128)(2,1)S(1)} %collective-permute-done.6.refs_3_), custom_call_target="tpu_custom_call" | custom-call | tf_op jit(solution)/shard_map/finish/pallas_call | solution.py:262
Async XLA Ops:
  0.0 2.8 %collective-permute-start = (bf16[64,4096]{1,0:T(8,128)(2,1)}, bf16[64,4096]{1,0:T(8,128)(2,1)S(1)}, u32[]{:S(2)}, u32[]{:S(2)}) collective-permute-start(bf16[64,4096]{1,0:T(8,128)(2,1)} %bitcast.6), channel_id=1, source_target_pairs={{0,1},{1,0},{2,3},{3,2},{4,5},{5,4},{6,7},{7,6},{8,9},{9,8},{10,11... | collective-permute-start | bytes 1572872 | tf_op jit(solution)/shard_map/ppermute | solution.py:193
  0.5 1.0 %copy-start.1 = (bf16[64,1,4096]{2,0,1:T(8,128)(2,1)S(1)}, bf16[64,1,4096]{2,0,1:T(8,128)(2,1)}, u32[]{:S(2)}) copy-start(bf16[64,1,4096]{2,0,1:T(8,128)(2,1)} %param.6) | copy-start | bytes 1572868
  1.5 0.7 %copy-start.4 = (s32[48]{0:T(128)S(1)}, s32[48]{0:T(128)}, u32[]{:S(2)}) copy-start(s32[48]{0:T(128)} %pairs_ref.5) | copy-start | bytes 580
  3.4 11.1 %collective-permute-start.2 = (bf16[32,4096]{1,0:T(8,128)(2,1)S(1)}, bf16[32,4096]{1,0:T(8,128)(2,1)S(1)}, u32[]{:S(2)}, u32[]{:S(2)}) collective-permute-start(bf16[32,4096]{1,0:T(8,128)(2,1)S(1)} %get-tuple-element.29), channel_id=1, source_target_pairs={{0,2},{1,3},{2,0},{3,1},{4,6},{5,7},{6,4},{7,5},{8,10},{9,11},{10,... | collective-permute-start | bytes 786440 | tf_op jit(solution)/shard_map/ppermute | solution.py:193
  6.0 10.5 %collective-permute-start.3 = (bf16[32,4096]{1,0:T(8,128)(2,1)S(1)}, bf16[32,4096]{1,0:T(8,128)(2,1)S(1)}, u32[]{:S(2)}, u32[]{:S(2)}) collective-permute-start(bf16[32,4096]{1,0:T(8,128)(2,1)S(1)} %get-tuple-element.30), channel_id=1, source_target_pairs={{0,4},{1,5},{2,6},{3,7},{4,0},{5,1},{6,2},{7,3},{8,12},{9,13},{10,... | collective-permute-start | bytes 786440 | tf_op jit(solution)/shard_map/ppermute | solution.py:193
  7.5 0.8 %copy-start.2 = (f32[1,64,64]{2,1,0:T(8,128)S(1)}, f32[1,64,64]{2,1,0:T(8,128)}, u32[]{:S(2)}) copy-start(f32[1,64,64]{2,1,0:T(8,128)} %param.8) | copy-start | bytes 49156
  8.2 0.8 %copy-start.3 = (f32[1,64,64]{2,1,0:T(8,128)S(1)}, f32[1,64,64]{2,1,0:T(8,128)}, u32[]{:S(2)}) copy-start(f32[1,64,64]{2,1,0:T(8,128)} %param.7) | copy-start | bytes 49156
  12.6 9.1 %collective-permute-start.1 = (bf16[2,16,4096]{2,1,0:T(8,128)(2,1)S(1)}, bf16[2,16,4096]{2,1,0:T(8,128)(2,1)S(1)}, u32[]{:S(2)}, u32[]{:S(2)}) collective-permute-start(bf16[2,16,4096]{2,1,0:T(8,128)(2,1)S(1)} %get-tuple-element.25), channel_id=1, source_target_pairs={{0,6},{1,7},{2,4},{3,5},{4,2},{5,3},{6,0},{7,1},{8,14},{9,15},{10,... | collective-permute-start | bytes 786440 | tf_op jit(solution)/shard_map/ppermute | solution.py:193
  16.4 5.3 %copy-start = (bf16[512,1,4096]{2,0,1:T(8,128)(2,1)S(1)}, bf16[512,1,4096]{2,0,1:T(8,128)(2,1)}, u32[]{:S(2)}) copy-start(bf16[512,1,4096]{2,0,1:T(8,128)(2,1)} %param.5) | copy-start | bytes 12582916
  16.4 5.3 %copy-start.5 = (s32[48]{0:T(128)S(1)}, s32[48]{0:T(128)}, u32[]{:S(2)}) copy-start(s32[48]{0:T(128)} %pairs_ref.5) | copy-start | bytes 580
  23.9 4.5 %collective-permute-start.4 = (bf16[24,512]{1,0:T(8,128)(2,1)S(1)}, bf16[24,512]{1,0:T(8,128)(2,1)S(1)}, u32[]{:S(2)}, u32[]{:S(2)}) collective-permute-start(bf16[24,512]{1,0:T(8,128)(2,1)S(1)} %get-tuple-element.32), channel_id=1, source_target_pairs={{0,8},{8,0},{16,24},{24,16},{1,9},{9,1},{17,25},{25,17},{2,10},{10... | collective-permute-start | bytes 73736 | tf_op jit(solution)/shard_map/ppermute | solution.py:260
  25.5 4.9 %collective-permute-start.5 = (bf16[24,512]{1,0:T(8,128)(2,1)S(1)}, bf16[24,512]{1,0:T(8,128)(2,1)S(1)}, u32[]{:S(2)}, u32[]{:S(2)}) collective-permute-start(bf16[24,512]{1,0:T(8,128)(2,1)S(1)} %get-tuple-element.33), channel_id=1, source_target_pairs={{0,16},{8,24},{16,0},{24,8},{1,17},{9,25},{17,1},{25,9},{2,18},{10... | collective-permute-start | bytes 73736 | tf_op jit(solution)/shard_map/ppermute | solution.py:260
  28.1 5.6 %collective-permute-start.6 = (bf16[24,512]{1,0:T(8,128)(2,1)S(1)}, bf16[24,512]{1,0:T(8,128)(2,1)S(1)}, u32[]{:S(2)}, u32[]{:S(2)}) collective-permute-start(bf16[24,512]{1,0:T(8,128)(2,1)S(1)} %get-tuple-element.34), channel_id=1, source_target_pairs={{0,24},{8,16},{16,8},{24,0},{1,25},{9,17},{17,9},{25,1},{2,26},{10... | collective-permute-start | bytes 73736 | tf_op jit(solution)/shard_map/ppermute | solution.py:260

commit v5 on v4

--- a/solution.py
+++ b/solution.py
@@ -53,19 +53,19 @@
         out_ref[QBLK:] = other_ref[pl.ds(find(pairs_ref, group, 1), QBLK), :]
 
 
-def make_factors(rows, out_ref, in_ref, left_ref, right_ref):
-    width = out_ref.shape[0]
-    in_width = in_ref.shape[0]
+def make_factors(rows, width, factors_ref, left_ref, right_ref):
+    in_width = factors_ref.shape[0] - width
     half = left_ref.shape[2]
     span = right_ref.shape[1]
-    outs = split_bf16(out_ref[...])
-    ins = split_bf16(in_ref[...])
+    outs = split_bf16(factors_ref[:width])
+    ins = split_bf16(factors_ref[width:])
     row = lax.broadcasted_iota(jnp.int32, (half, width), 0) // QBLK
     row_o = lax.broadcasted_iota(jnp.int32, (half, width), 1)
     col = lax.broadcasted_iota(jnp.int32, (width, half), 1) // QBLK
     col_o = lax.broadcasted_iota(jnp.int32, (width, half), 0)
     a = lax.broadcasted_iota(jnp.int32, (half, half), 0) ^ lax.broadcasted_iota(jnp.int32, (half, half), 1)
     same = (a & (QBLK - 1)) == lax.axis_index("layer") * rows
+    zero = jnp.zeros((), BF16)
     for h in range(2):
         for s in range(2):
             pick_rows = (row * 2 + s == row_o).astype(BF16)
@@ -73,7 +73,7 @@
             for t in range(2):
                 pick_cols = (col * 2 + (s ^ t) == col_o).astype(BF16)
                 spread = jnp.dot(rows, pick_cols, preferred_element_type=F32)
-                left_ref[h, s, :, t * half : (t + 1) * half] = jnp.where(same, spread, 0.0).astype(BF16)
+                left_ref[h, s, :, t * half : (t + 1) * half] = jnp.where(same, spread.astype(BF16), zero)
         up = (
             lax.broadcasted_iota(jnp.int32, (span, in_width), 0) % in_width
             == lax.broadcasted_iota(jnp.int32, (span, in_width), 1)
@@ -120,8 +120,8 @@
             ]
 
 
-def first_kernel(rows, out_ref, in_ref, pair_ref, left_ref, right_ref, prep_ref):
-    make_factors(rows, out_ref, in_ref, left_ref, right_ref)
+def first_kernel(rows, width, factors_ref, pair_ref, left_ref, right_ref, prep_ref):
+    make_factors(rows, width, factors_ref, left_ref, right_ref)
     prepare(pair_ref, left_ref, right_ref, prep_ref)
 
 
@@ -134,7 +134,7 @@
 
 
 def last_kernel(order, layer, held, slots, pairs_ref, late_ref, early_ref, train_ref, *refs):
-    outs, rows_ref = refs[:layer], refs[layer]
+    mine_ref, send_ref, rows_ref = refs
     ready = early_ref.shape[0]
     me = lax.axis_index("ex")
     wanted = [pairs_ref[me * slots + slot] for slot in range(slots)]
@@ -162,14 +162,15 @@
         chosen.append(jnp.where(q >= 0, value, jnp.zeros_like(value)))
     for m in range(layer):
         part = jnp.concatenate([value[m * rows : (m + 1) * rows] for value in chosen], axis=0)
-        outs[m][...] = part.astype(outs[m].dtype)
-
-
-def finish_kernel(layer, *refs):
-    parts, out_ref = refs[:layer], refs[layer]
-    total = parts[0][...]
-    for part in parts[1:]:
-        total = total + part[...].astype(F32)
+        if m == 0:
+            mine_ref[...] = part
+        send_ref[lax.axis_index("layer") ^ m] = part.astype(BF16)
+
+
+def finish_kernel(layer, mine_ref, parts_ref, out_ref):
+    total = mine_ref[...]
+    for m in range(1, layer):
+        total = total + parts_ref[lax.axis_index("layer") ^ m].astype(F32)
     rows = out_ref.shape[1]
     for slot in range(out_ref.shape[0]):
         out_ref[slot] = total[slot * rows : (slot + 1) * rows]
@@ -217,18 +218,19 @@
 
     stack = features // LANES * QBLK
     span = 2 * LANES
+    out_factor, in_factor, far_pick = lax.optimization_barrier((out_factor, in_factor, picked[order[-1]]))
     left, right, far = pl.pallas_call(
-        functools.partial(first_kernel, rows),
+        functools.partial(first_kernel, rows, out_factor.shape[0]),
         out_shape=[
             jax.ShapeDtypeStruct((2, 2, stack, 2 * stack), BF16),
             jax.ShapeDtypeStruct((2, span, span), BF16),
             jax.ShapeDtypeStruct((2, QBLK, features), BF16),
         ],
-        in_specs=[VMEM] * 3,
+        in_specs=[VMEM] * 2,
         out_specs=[VMEM] * 3,
         compiler_params=limit,
         name="first",
-    )(out_factor, in_factor, picked[order[-1]])
+    )(jnp.concatenate([out_factor, in_factor], axis=0), far_pick)
     far = from_index(far, 2 * order[-1])
 
     early, done = [], 0
@@ -245,28 +247,28 @@
             )(left, right, *early, *pairs)
         ]
         done += 2 * len(pairs)
-    parts = pl.pallas_call(
+    mine, parts = pl.pallas_call(
         functools.partial(last_kernel, order, layer, held, slots),
-        out_shape=[jax.ShapeDtypeStruct((slots * rows, train_rows), F32)]
-        + [jax.ShapeDtypeStruct((slots * rows, train_rows), BF16)] * (layer - 1),
+        out_shape=[
+            jax.ShapeDtypeStruct((slots * rows, train_rows), F32),
+            jax.ShapeDtypeStruct((layer, slots * rows, train_rows), BF16),
+        ],
         in_specs=[SMEM] + [VMEM] * 3,
-        out_specs=[VMEM] * layer,
+        out_specs=[VMEM] * 2,
         scratch_shapes=[pltpu.VMEM((slots * QBLK, features), BF16)],
         compiler_params=limit,
         name="last",
     )(pair_blocks, far, *early, train)
 
-    terms = [parts[0]] + [
-        lax.ppermute(parts[m], "layer", [(i, i ^ m) for i in range(layer)]) for m in range(1, layer)
-    ]
+    parts = lax.all_to_all(parts, "layer", split_axis=0, concat_axis=0, tiled=True)
     out = pl.pallas_call(
         functools.partial(finish_kernel, layer),
         out_shape=jax.ShapeDtypeStruct((slots, rows, train_rows), F32),
-        in_specs=[VMEM] * layer,
+        in_specs=[VMEM] * 2,
         out_specs=VMEM,
         compiler_params=limit,
         name="finish",
-    )(*terms)
+    )(mine, parts)
     return jnp.transpose(out, (1, 0, 2))
 
 

time: 34.7 us -> 34.5 us (level)
  blocking collectives: 0 us -> 10.5 us
  waiting for transfers between devices: 8.8 us -> 3.39 us
  starting transfers between devices: 9.06 us -> 4.62 us
  local copies, waits for them, and re-layouts: 3.22 us -> 1.71 us
  other arithmetic: 0 us -> 0.78 us
    all_to_all x0 -> x1, blocking collectives: none -> 10.5 us  [shards(): lax.all_to_all(parts, 'layer', split_axis=0, concat_axis=0, tiled=True)]
    ppermute x3 -> x0, waiting for transfers between devices: 5.4 us -> none  [shards(): lax.ppermute(parts[m], 'layer', [(i, i ^ m) for i in range(layer)])]
    ppermute x3 -> x0, starting transfers between devices: 4.45 us -> none  [shards(): lax.ppermute(parts[m], 'layer', [(i, i ^ m) for i in range(layer)])]
    unnamed x12 -> x8, local copies, waits for them, and re-layouts: 3.22 us -> 1.71 us
    concatenate x0 -> x1, other arithmetic: none -> 0.78 us  [shards(): jnp.concatenate([out_factor, in_factor], axis=0)]
  transfers between devices with their start and end apart: 7 -> 4, of which waited for: 3 -> 1; matrix products, arithmetic and copies ran while one was open for 0% -> 2% of each run, Pallas kernels for 28% -> 28%
where the time goes in v5:
time: 34.5 us; the launch traced here: 34.3 us
  Pallas kernels  13.2 us (38%)
  blocking collectives  10.5 us (30%)
  starting transfers between devices  4.62 us (13%)
  waiting for transfers between devices  3.39 us (10%)
  local copies, waits for them, and re-layouts  1.71 us (5%)
  other arithmetic  0.78 us (2%)
    all_to_all x1, blocking collectives, shards(): lax.all_to_all(parts, 'layer', split_axis=0, concat_axis=0, tiled=True)  10.5 us
    pallas_call x3, Pallas kernels, shards(): pl.pallas_call(functools.partial(near_kernel, done), out_shape=jax.ShapeD...  5.58 us
    ppermute x4, starting transfers between devices, from_index(): return lax.ppermute(array, 'ex', [(i, i ^ k) for i in range(ex)])  4.62 us
    pallas_call x1, Pallas kernels, shards(): pl.pallas_call(functools.partial(first_kernel, rows, out_factor.shape[0])...  3.57 us
    ppermute x4, waiting for transfers between devices, from_index(): return lax.ppermute(array, 'ex', [(i, i ^ k) for i in range(ex)])  3.39 us
    pallas_call x1, Pallas kernels, shards(): pl.pallas_call(functools.partial(last_kernel, order, layer, held, slots),...  2.15 us
    unnamed x8, local copies, waits for them, and re-layouts  1.71 us
    concatenate x1, other arithmetic, shards(): jnp.concatenate([out_factor, in_factor], axis=0)  0.78 us
  transfers between devices with their start and end apart: 4, of which 1 were waited for; matrix products, arithmetic and copies ran while one was open for 2% of the time, Pallas kernels for 28%

profile of v5, /device:TPU:0, one launch (start us, length us, event | category | flops | bytes accessed | tf_op | source)
XLA Modules:
  0.0 34.3 jit_solution(2545847847658891937)
XLA Ops:
  0.0 0.5 %collective-permute-start = (bf16[64,4096]{1,0:T(8,128)(2,1)}, bf16[64,4096]{1,0:T(8,128)(2,1)S(1)}, u32[]{:S(2)}, u32[]{:S(2)}) collective-permute-start(bf16[64,4096]{1,0:T(8,128)(2,1)} %bitcast.6), channel_id=1, source_target_pairs={{0,1},{1,0},{2,3},{3,2},{4,5},{5,4},{6,7},{7,6},{8,9},{9,8},{10,11... | collective-permute-start | bytes 1572872 | tf_op jit(solution)/shard_map/ppermute | solution.py:194
  0.5 0.0 copy-start.1
  0.5 1.0 %copy-done.1 = bf16[64,1,4096]{2,0,1:T(8,128)(2,1)S(1)} copy-done((bf16[64,1,4096]{2,0,1:T(8,128)(2,1)S(1)}, bf16[64,1,4096]{2,0,1:T(8,128)(2,1)}, u32[]{:S(2)}) %copy-start.1) | copy-done | bytes 524312
  1.5 0.0 copy-start.2
  1.5 0.7 %copy-done.2 = s32[48]{0:T(128)S(1)} copy-done((s32[48]{0:T(128)S(1)}, s32[48]{0:T(128)}, u32[]{:S(2)}) %copy-start.2) | copy-done | bytes 216
  2.2 0.6 %own.1 = (bf16[16,4096]{1,0:T(8,128)(2,1)S(1)}, bf16[16,4096]{1,0:T(8,128)(2,1)S(1)}, bf16[16,4096]{1,0:T(8,128)(2,1)S(1)}, bf16[16,4096]{1,0:T(8,128)(2,1)S(1)}) custom-call(s32[48]{0:T(128)S(1)} %copy-done.2, bf16[64,4096]{1,0:T(8,128)(2,1)S(1)} %bitcast.7), custom_call_target="tpu_custom_call" | custom-call | tf_op jit(solution)/shard_map/own/pallas_call | solution.py:199
  2.8 0.0 collective-permute-done.other_ref
  2.8 0.6 %pick.1 = (bf16[32,4096]{1,0:T(8,128)(2,1)S(1)}, bf16[32,4096]{1,0:T(8,128)(2,1)S(1)}, bf16[32,4096]{1,0:T(8,128)(2,1)S(1)}, bf16[32,4096]{1,0:T(8,128)(2,1)S(1)}) custom-call(s32[48]{0:T(128)S(1)} %copy-done.2, bf16[64,4096]{1,0:T(8,128)(2,1)S(1)} %collective-permute-done.other_ref, bf16[16,4096]{1,0:T(8,128)(2,1)S(1)} %get-tuple-element.21.refs_0_, ...), custom_call_target="tpu_custom_call" | custom-call | tf_op jit(solution)/shard_map/pick/pallas_call | solution.py:207
  3.4 2.6 %collective-permute-start.2 = (bf16[32,4096]{1,0:T(8,128)(2,1)S(1)}, bf16[32,4096]{1,0:T(8,128)(2,1)S(1)}, u32[]{:S(2)}, u32[]{:S(2)}) collective-permute-start(bf16[32,4096]{1,0:T(8,128)(2,1)S(1)} %get-tuple-element.33), channel_id=1, source_target_pairs={{0,2},{1,3},{2,0},{3,1},{4,6},{5,7},{6,4},{7,5},{8,10},{9,11},{10,... | collective-permute-start | bytes 786440 | tf_op jit(solution)/shard_map/ppermute | solution.py:194
  6.0 1.5 %collective-permute-start.3 = (bf16[32,4096]{1,0:T(8,128)(2,1)S(1)}, bf16[32,4096]{1,0:T(8,128)(2,1)S(1)}, u32[]{:S(2)}, u32[]{:S(2)}) collective-permute-start(bf16[32,4096]{1,0:T(8,128)(2,1)S(1)} %get-tuple-element.34), channel_id=1, source_target_pairs={{0,4},{1,5},{2,6},{3,7},{4,0},{5,1},{6,2},{7,3},{8,12},{9,13},{10,... | collective-permute-start | bytes 786440 | tf_op jit(solution)/shard_map/ppermute | solution.py:194
  7.5 0.8 %pad_maximum_fusion.factors_ref = f32[128,64]{1,0:T(8,128)S(1)} fusion(f32[64,64]{1,0:T(8,128)} %bitcast.8, f32[64,64]{1,0:T(8,128)} %bitcast.9), kind=kLoop, calls=%fused_computation | loop fusion | flops 8192 | bytes 65536 | tf_op jit(solution)/shard_map/concatenate | solution.py:233
  8.3 3.6 %first.1 = (bf16[2,2,512,1024]{3,2,1,0:T(8,128)(2,1)S(1)}, bf16[2,256,256]{2,1,0:T(8,128)(2,1)S(1)}, bf16[2,16,4096]{2,1,0:T(8,128)(2,1)S(1)}) custom-call(f32[128,64]{1,0:T(8,128)S(1)} %pad_maximum_fusion.factors_ref, bf16[32,4096]{1,0:T(8,128)(2,1)S(1)} %get-tuple-element.28.pair_ref), custom_call_target="tpu_custom_call" | custom-call | tf_op jit(solution)/shard_map/first/pallas_call | solution.py:222
  11.9 0.1 collective-permute-start.1
  11.9 1.9 %near0.1.refs_0_ = bf16[2,16,4096]{2,1,0:T(8,128)(2,1)S(1)} custom-call(bf16[2,2,512,1024]{3,2,1,0:T(8,128)(2,1)S(1)} %get-tuple-element.30.left_ref, bf16[2,256,256]{2,1,0:T(8,128)(2,1)S(1)} %get-tuple-element.31.right_ref, bf16[32,4096]{1,0:T(8,128)(2,1)S(1)} %get-tuple-element.32.refs_0_), custom_call_target="tpu_custom_call" | custom-call | tf_op jit(solution)/shard_map/near0/pallas_call | solution.py:240
  13.8 0.0 collective-permute-done.2.refs_1_
  13.8 1.9 %near1.1.refs_0_ = bf16[4,16,4096]{2,1,0:T(8,128)(2,1)S(1)} custom-call(bf16[2,2,512,1024]{3,2,1,0:T(8,128)(2,1)S(1)} %get-tuple-element.30.left_ref, bf16[2,256,256]{2,1,0:T(8,128)(2,1)S(1)} %get-tuple-element.31.right_ref, bf16[2,16,4096]{2,1,0:T(8,128)(2,1)S(1)} %near0.1.refs_0_, bf16[32,4096]{1,0:T(8,128)(2,1)S(1)} %collective-permute-done.2.refs_1_), custom_call_target="tpu_custom_call" | custom-call | tf_op jit(solution)/shard_map/near1/pallas_call | solution.py:240
  15.7 0.0 copy-start
  15.7 0.0 copy-start.3
  15.7 0.0 collective-permute-done.3.refs_1_
  15.7 1.9 %near2.1.early_ref = bf16[6,16,4096]{2,1,0:T(8,128)(2,1)S(1)} custom-call(bf16[2,2,512,1024]{3,2,1,0:T(8,128)(2,1)S(1)} %get-tuple-element.30.left_ref, bf16[2,256,256]{2,1,0:T(8,128)(2,1)S(1)} %get-tuple-element.31.right_ref, bf16[4,16,4096]{2,1,0:T(8,128)(2,1)S(1)} %near1.1.refs_0_, bf16[32,4096]{1,0:T(8,128)(2,1)S(1)} %collective-permute-done.3.refs_1_), custom_call_target="tpu_custom_call" | custom-call | tf_op jit(solution)/shard_map/near2/pallas_call | solution.py:240
  17.6 3.4 %collective-permute-done.1.late_ref = bf16[2,16,4096]{2,1,0:T(8,128)(2,1)S(1)} collective-permute-done((bf16[2,16,4096]{2,1,0:T(8,128)(2,1)S(1)}, bf16[2,16,4096]{2,1,0:T(8,128)(2,1)S(1)}, u32[]{:S(2)}, u32[]{:S(2)}) %collective-permute-start.1) | collective-permute-done | bytes 262176 | tf_op jit(solution)/shard_map/ppermute | solution.py:194
  21.0 0.0 copy-done
  21.0 0.0 copy-done.3
  21.0 2.1 %last.1 = (f32[24,512]{1,0:T(8,128)S(1)}, bf16[4,24,512]{2,1,0:T(8,128)(2,1)S(1)}) custom-call(s32[48]{0:T(128)S(1)} %copy-done.3, bf16[2,16,4096]{2,1,0:T(8,128)(2,1)S(1)} %collective-permute-done.1.late_ref, bf16[6,16,4096]{2,1,0:T(8,128)(2,1)S(1)} %near2.1.early_ref, bf16[512,4096]{1,0:T(8,128)(2,1)S(1)} %bitcast.5), custom_call_target="tpu_custom_call" | custom-call | tf_op jit(solution)/shard_map/last/pallas_call | solution.py:250
  23.1 10.5 %all_to_all.5.parts_ref = bf16[4,24,512]{2,1,0:T(8,128)(2,1)S(1)} all-to-all(bf16[4,24,512]{2,1,0:T(8,128)(2,1)S(1)} %get-tuple-element.36), channel_id=1, replica_groups=mesh['layer'=4,'ex'=8] {'layer'}, dimensions={0} | all-to-all | bytes 196608 | tf_op jit(solution)/shard_map/all_to_all | solution.py:263
  33.6 0.6 %finish.1 = f32[6,4,512]{2,1,0:T(4,128)} custom-call(f32[24,512]{1,0:T(8,128)S(1)} %get-tuple-element.35.mine_ref, bf16[4,24,512]{2,1,0:T(8,128)(2,1)S(1)} %all_to_all.5.parts_ref), custom_call_target="tpu_custom_call" | custom-call | tf_op jit(solution)/shard_map/finish/pallas_call | solution.py:264
Async XLA Ops:
  0.0 2.8 %collective-permute-start = (bf16[64,4096]{1,0:T(8,128)(2,1)}, bf16[64,4096]{1,0:T(8,128)(2,1)S(1)}, u32[]{:S(2)}, u32[]{:S(2)}) collective-permute-start(bf16[64,4096]{1,0:T(8,128)(2,1)} %bitcast.6), channel_id=1, source_target_pairs={{0,1},{1,0},{2,3},{3,2},{4,5},{5,4},{6,7},{7,6},{8,9},{9,8},{10,11... | collective-permute-start | bytes 1572872 | tf_op jit(solution)/shard_map/ppermute | solution.py:194
  0.5 1.0 %copy-start.1 = (bf16[64,1,4096]{2,0,1:T(8,128)(2,1)S(1)}, bf16[64,1,4096]{2,0,1:T(8,128)(2,1)}, u32[]{:S(2)}) copy-start(bf16[64,1,4096]{2,0,1:T(8,128)(2,1)} %param.6) | copy-start | bytes 1572868
  1.5 0.7 %copy-start.2 = (s32[48]{0:T(128)S(1)}, s32[48]{0:T(128)}, u32[]{:S(2)}) copy-start(s32[48]{0:T(128)} %pairs_ref.5) | copy-start | bytes 580
  3.4 10.4 %collective-permute-start.2 = (bf16[32,4096]{1,0:T(8,128)(2,1)S(1)}, bf16[32,4096]{1,0:T(8,128)(2,1)S(1)}, u32[]{:S(2)}, u32[]{:S(2)}) collective-permute-start(bf16[32,4096]{1,0:T(8,128)(2,1)S(1)} %get-tuple-element.33), channel_id=1, source_target_pairs={{0,2},{1,3},{2,0},{3,1},{4,6},{5,7},{6,4},{7,5},{8,10},{9,11},{10,... | collective-permute-start | bytes 786440 | tf_op jit(solution)/shard_map/ppermute | solution.py:194
  6.0 9.7 %collective-permute-start.3 = (bf16[32,4096]{1,0:T(8,128)(2,1)S(1)}, bf16[32,4096]{1,0:T(8,128)(2,1)S(1)}, u32[]{:S(2)}, u32[]{:S(2)}) collective-permute-start(bf16[32,4096]{1,0:T(8,128)(2,1)S(1)} %get-tuple-element.34), channel_id=1, source_target_pairs={{0,4},{1,5},{2,6},{3,7},{4,0},{5,1},{6,2},{7,3},{8,12},{9,13},{10,... | collective-permute-start | bytes 786440 | tf_op jit(solution)/shard_map/ppermute | solution.py:194
  11.9 9.1 %collective-permute-start.1 = (bf16[2,16,4096]{2,1,0:T(8,128)(2,1)S(1)}, bf16[2,16,4096]{2,1,0:T(8,128)(2,1)S(1)}, u32[]{:S(2)}, u32[]{:S(2)}) collective-permute-start(bf16[2,16,4096]{2,1,0:T(8,128)(2,1)S(1)} %get-tuple-element.29), channel_id=1, source_target_pairs={{0,6},{1,7},{2,4},{3,5},{4,2},{5,3},{6,0},{7,1},{8,14},{9,15},{10,... | collective-permute-start | bytes 786440 | tf_op jit(solution)/shard_map/ppermute | solution.py:194
  15.7 5.3 %copy-start = (bf16[512,1,4096]{2,0,1:T(8,128)(2,1)S(1)}, bf16[512,1,4096]{2,0,1:T(8,128)(2,1)}, u32[]{:S(2)}) copy-start(bf16[512,1,4096]{2,0,1:T(8,128)(2,1)} %param.5) | copy-start | bytes 12582916
  15.7 5.3 %copy-start.3 = (s32[48]{0:T(128)S(1)}, s32[48]{0:T(128)}, u32[]{:S(2)}) copy-start(s32[48]{0:T(128)} %pairs_ref.5) | copy-start | bytes 580

commit v6 on v4

--- a/solution.py
+++ b/solution.py
@@ -29,9 +29,22 @@
     return init
 
 
-def wanted_block(ex, held, slots, pairs_ref, group, side):
+def ring_chip(place):
+    return place ^ (place >> 1)
+
+
+def ring_place(chip, chips):
+    place, shift = chip, 1
+    while shift < chips:
+        place, shift = place ^ (place >> shift), 2 * shift
+    return place
+
+
+def wanted_block(ex, held, slots, pairs_ref, step, side):
     me = lax.axis_index("ex")
-    first = (me ^ (2 * group)) * slots
+    chips = ex // 2
+    target = ring_chip((ring_place(me >> 1, chips) + step) & (chips - 1))
+    first = (2 * target + (me & 1)) * slots
     base = (me ^ side) * held
 
     def body(slot, block):
@@ -53,19 +66,19 @@
         out_ref[QBLK:] = other_ref[pl.ds(find(pairs_ref, group, 1), QBLK), :]
 
 
-def make_factors(rows, out_ref, in_ref, left_ref, right_ref):
-    width = out_ref.shape[0]
-    in_width = in_ref.shape[0]
+def make_factors(rows, width, factors_ref, left_ref, right_ref):
+    in_width = factors_ref.shape[0] - width
     half = left_ref.shape[2]
     span = right_ref.shape[1]
-    outs = split_bf16(out_ref[...])
-    ins = split_bf16(in_ref[...])
+    outs = split_bf16(factors_ref[:width])
+    ins = split_bf16(factors_ref[width:])
     row = lax.broadcasted_iota(jnp.int32, (half, width), 0) // QBLK
     row_o = lax.broadcasted_iota(jnp.int32, (half, width), 1)
     col = lax.broadcasted_iota(jnp.int32, (width, half), 1) // QBLK
     col_o = lax.broadcasted_iota(jnp.int32, (width, half), 0)
-    a = lax.broadcasted_iota(jnp.int32, (half, half), 0) ^ lax.broadcasted_iota(jnp.int32, (half, half), 1)
+    a = lax.broadcasted_iota(jnp.int32, (half, half), 1) - lax.broadcasted_iota(jnp.int32, (half, half), 0)
     same = (a & (QBLK - 1)) == lax.axis_index("layer") * rows
+    zero = jnp.zeros((), BF16)
     for h in range(2):
         for s in range(2):
             pick_rows = (row * 2 + s == row_o).astype(BF16)
@@ -73,7 +86,7 @@
             for t in range(2):
                 pick_cols = (col * 2 + (s ^ t) == col_o).astype(BF16)
                 spread = jnp.dot(rows, pick_cols, preferred_element_type=F32)
-                left_ref[h, s, :, t * half : (t + 1) * half] = jnp.where(same, spread, 0.0).astype(BF16)
+                left_ref[h, s, :, t * half : (t + 1) * half] = jnp.where(same, spread.astype(BF16), zero)
         up = (
             lax.broadcasted_iota(jnp.int32, (span, in_width), 0) % in_width
             == lax.broadcasted_iota(jnp.int32, (span, in_width), 1)
@@ -120,8 +133,8 @@
             ]
 
 
-def first_kernel(rows, out_ref, in_ref, pair_ref, left_ref, right_ref, prep_ref):
-    make_factors(rows, out_ref, in_ref, left_ref, right_ref)
+def first_kernel(rows, width, factors_ref, pair_ref, left_ref, right_ref, prep_ref):
+    make_factors(rows, width, factors_ref, left_ref, right_ref)
     prepare(pair_ref, left_ref, right_ref, prep_ref)
 
 
@@ -134,15 +147,17 @@
 
 
 def last_kernel(order, layer, held, slots, pairs_ref, late_ref, early_ref, train_ref, *refs):
-    outs, rows_ref = refs[:layer], refs[layer]
+    outs, rows_ref = refs[:-1], refs[-1]
+    chips = len(order)
     ready = early_ref.shape[0]
     me = lax.axis_index("ex")
     wanted = [pairs_ref[me * slots + slot] for slot in range(slots)]
     for slot, q in enumerate(wanted):
-        k = (jnp.maximum(q, 0) // held) ^ me
-        place = jnp.int32(0)
-        for index, group in enumerate(order):
-            place = jnp.where(k // 2 == group, 2 * index + k % 2, place)
+        source = jnp.maximum(q, 0) // held
+        step = (ring_place(me >> 1, chips) - ring_place(source >> 1, chips)) & (chips - 1)
+        place = (source ^ me) & 1
+        for index, taken in enumerate(order):
+            place = jnp.where(step == taken, 2 * index, 0) + place
 
         @pl.when(place < ready)
         def _():
@@ -189,12 +204,14 @@
     out_factor = out_precond.reshape(out_precond.shape[1:])
     limit = pltpu.CompilerParams(vmem_limit_bytes=24 * 2**20)
 
-    def from_index(array, k):
-        return lax.ppermute(array, "ex", [(i, i ^ k) for i in range(ex)])
+    def pass_on(array, step):
+        ring = [ring_chip(place) for place in range(ex // 2)]
+        moves = zip(ring, ring[step:] + ring[:step])
+        return lax.ppermute(array, "ex", [(2 * a + c, 2 * b + c) for a, b in moves for c in range(2)])
 
     groups = ex // 2
     find = functools.partial(wanted_block, ex, held, slots)
-    other = from_index(query, 1)
+    other = lax.ppermute(query, "ex", [(i, i ^ 1) for i in range(ex)])
     own = pl.pallas_call(
         functools.partial(own_kernel, find),
         out_shape=[jax.ShapeDtypeStruct((QBLK, features), BF16)] * groups,
@@ -212,24 +229,25 @@
         name="pick",
     )(pair_blocks, other, *own)
 
-    order = sorted(range(groups), key=lambda group: (bin(group).count("1"), group))
-    raw = [from_index(picked[group], 2 * group) for group in order[1:-1]]
+    order = sorted(range(groups), key=lambda step: min(step, groups - step))
+    raw = [pass_on(picked[step], step) for step in order[1:-1]]
 
     stack = features // LANES * QBLK
     span = 2 * LANES
+    out_factor, in_factor, far_pick = lax.optimization_barrier((out_factor, in_factor, picked[order[-1]]))
     left, right, far = pl.pallas_call(
-        functools.partial(first_kernel, rows),
+        functools.partial(first_kernel, rows, out_factor.shape[0]),
         out_shape=[
             jax.ShapeDtypeStruct((2, 2, stack, 2 * stack), BF16),
             jax.ShapeDtypeStruct((2, span, span), BF16),
             jax.ShapeDtypeStruct((2, QBLK, features), BF16),
         ],
-        in_specs=[VMEM] * 3,
+        in_specs=[VMEM] * 2,
         out_specs=[VMEM] * 3,
         compiler_params=limit,
         name="first",
-    )(out_factor, in_factor, picked[order[-1]])
-    far = from_index(far, 2 * order[-1])
+    )(jnp.concatenate([out_factor, in_factor], axis=0), far_pick)
+    far = pass_on(far, order[-1])
 
     early, done = [], 0
     half = len(raw) // 2
@@ -257,7 +275,7 @@
     )(pair_blocks, far, *early, train)
 
     terms = [parts[0]] + [
-        lax.ppermute(parts[m], "layer", [(i, i ^ m) for i in range(layer)]) for m in range(1, layer)
+        lax.ppermute(parts[m], "layer", [(i, (i + m) % layer) for i in range(layer)]) for m in range(1, layer)
     ]
     out = pl.pallas_call(
         functools.partial(finish_kernel, layer),

time: 34.7 us -> 31 us (0.89)
  waiting for transfers between devices: 8.8 us -> 3.28 us
  starting transfers between devices: 9.06 us -> 11.8 us
  local copies, waits for them, and re-layouts: 3.22 us -> 1.71 us
  other arithmetic: 0 us -> 0.78 us
    ppermute x7, waiting for transfers between devices: 8.8 us -> 3.28 us  [the longest x3 2.48 us: shards(): lax.ppermute(parts[m], 'layer', [(i, (i + m) % layer) for i in range(laye...]
    ppermute x7, starting transfers between devices: 9.06 us -> 11.8 us  [the longest x3 5.73 us: shards(): lax.ppermute(parts[m], 'layer', [(i, (i + m) % layer) for i in range(laye...]
    unnamed x12 -> x8, local copies, waits for them, and re-layouts: 3.22 us -> 1.71 us
    concatenate x0 -> x1, other arithmetic: none -> 0.78 us  [shards(): jnp.concatenate([out_factor, in_factor], axis=0)]
  transfers between devices with their start and end apart: 7 -> 7, of which waited for: 3 -> 4; matrix products, arithmetic and copies ran while one was open for 0% -> 3% of each run, Pallas kernels for 28% -> 32%
where the time goes in v6:
time: 31 us; the launch traced here: 30.8 us
  Pallas kernels  13.2 us (43%)
  starting transfers between devices  11.8 us (38%)
  waiting for transfers between devices  3.28 us (11%)
  local copies, waits for them, and re-layouts  1.71 us (6%)
  other arithmetic  0.78 us (3%)
    ppermute x3, starting transfers between devices, shards(): lax.ppermute(parts[m], 'layer', [(i, (i + m) % layer) for i in range(laye...  5.73 us
    ppermute x3, starting transfers between devices, pass_on(): lax.ppermute(array, 'ex', [(2 * a + c, 2 * b + c) for a, b in moves for c...  5.59 us
    pallas_call x3, Pallas kernels, shards(): pl.pallas_call(functools.partial(near_kernel, done), out_shape=jax.ShapeD...  5.58 us
    pallas_call x1, Pallas kernels, shards(): pl.pallas_call(functools.partial(first_kernel, rows, out_factor.shape[0])...  3.57 us
    ppermute x3, waiting for transfers between devices, shards(): lax.ppermute(parts[m], 'layer', [(i, (i + m) % layer) for i in range(laye...  2.48 us
    pallas_call x1, Pallas kernels, shards(): pl.pallas_call(functools.partial(last_kernel, order, layer, held, slots),...  2.13 us
    unnamed x8, local copies, waits for them, and re-layouts  1.71 us
    ppermute x3, waiting for transfers between devices, pass_on(): lax.ppermute(array, 'ex', [(2 * a + c, 2 * b + c) for a, b in moves for c...  0.8 us
  transfers between devices with their start and end apart: 7, of which 4 were waited for; matrix products, arithmetic and copies ran while one was open for 3% of the time, Pallas kernels for 32%

profile of v6, /device:TPU:0, one launch (start us, length us, event | category | flops | bytes accessed | tf_op | source)
XLA Modules:
  0.0 30.8 jit_solution(6599653984363296335)
XLA Ops:
  0.0 0.5 %collective-permute-start = (bf16[64,4096]{1,0:T(8,128)(2,1)}, bf16[64,4096]{1,0:T(8,128)(2,1)S(1)}, u32[]{:S(2)}, u32[]{:S(2)}) collective-permute-start(bf16[64,4096]{1,0:T(8,128)(2,1)} %bitcast.6), channel_id=1, source_target_pairs={{0,1},{1,0},{2,3},{3,2},{4,5},{5,4},{6,7},{7,6},{8,9},{9,8},{10,11... | collective-permute-start | bytes 1572872 | tf_op jit(solution)/shard_map/ppermute | solution.py:214
  0.5 0.0 copy-start.1
  0.5 1.0 %copy-done.1 = bf16[64,1,4096]{2,0,1:T(8,128)(2,1)S(1)} copy-done((bf16[64,1,4096]{2,0,1:T(8,128)(2,1)S(1)}, bf16[64,1,4096]{2,0,1:T(8,128)(2,1)}, u32[]{:S(2)}) %copy-start.1) | copy-done | bytes 524312
  1.5 0.0 copy-start.2
  1.5 0.7 %copy-done.2 = s32[48]{0:T(128)S(1)} copy-done((s32[48]{0:T(128)S(1)}, s32[48]{0:T(128)}, u32[]{:S(2)}) %copy-start.2) | copy-done | bytes 216
  2.2 0.6 %own.1 = (bf16[16,4096]{1,0:T(8,128)(2,1)S(1)}, bf16[16,4096]{1,0:T(8,128)(2,1)S(1)}, bf16[16,4096]{1,0:T(8,128)(2,1)S(1)}, bf16[16,4096]{1,0:T(8,128)(2,1)S(1)}) custom-call(s32[48]{0:T(128)S(1)} %copy-done.2, bf16[64,4096]{1,0:T(8,128)(2,1)S(1)} %bitcast.7), custom_call_target="tpu_custom_call" | custom-call | tf_op jit(solution)/shard_map/own/pallas_call | solution.py:215
  2.8 0.0 collective-permute-done.other_ref
  2.8 0.6 %pick.1 = (bf16[32,4096]{1,0:T(8,128)(2,1)S(1)}, bf16[32,4096]{1,0:T(8,128)(2,1)S(1)}, bf16[32,4096]{1,0:T(8,128)(2,1)S(1)}, bf16[32,4096]{1,0:T(8,128)(2,1)S(1)}) custom-call(s32[48]{0:T(128)S(1)} %copy-done.2, bf16[64,4096]{1,0:T(8,128)(2,1)S(1)} %collective-permute-done.other_ref, bf16[16,4096]{1,0:T(8,128)(2,1)S(1)} %get-tuple-element.23.refs_0_, ...), custom_call_target="tpu_custom_call" | custom-call | tf_op jit(solution)/shard_map/pick/pallas_call | solution.py:223
  3.4 2.5 %collective-permute-start.2 = (bf16[32,4096]{1,0:T(8,128)(2,1)S(1)}, bf16[32,4096]{1,0:T(8,128)(2,1)S(1)}, u32[]{:S(2)}, u32[]{:S(2)}) collective-permute-start(bf16[32,4096]{1,0:T(8,128)(2,1)S(1)} %get-tuple-element.35), channel_id=1, source_target_pairs={{0,2},{1,3},{2,6},{3,7},{6,4},{7,5},{4,0},{5,1},{8,10},{9,11},{10,... | collective-permute-start | bytes 786440 | tf_op jit(solution)/shard_map/ppermute | solution.py:210
  6.0 0.1 collective-permute-start.3
  6.1 0.8 %pad_maximum_fusion.factors_ref = f32[128,64]{1,0:T(8,128)S(1)} fusion(f32[64,64]{1,0:T(8,128)} %bitcast.8, f32[64,64]{1,0:T(8,128)} %bitcast.9), kind=kLoop, calls=%fused_computation | loop fusion | flops 8192 | bytes 65536 | tf_op jit(solution)/shard_map/concatenate | solution.py:249
  6.8 3.6 %first.1 = (bf16[2,2,512,1024]{3,2,1,0:T(8,128)(2,1)S(1)}, bf16[2,256,256]{2,1,0:T(8,128)(2,1)S(1)}, bf16[2,16,4096]{2,1,0:T(8,128)(2,1)S(1)}) custom-call(f32[128,64]{1,0:T(8,128)S(1)} %pad_maximum_fusion.factors_ref, bf16[32,4096]{1,0:T(8,128)(2,1)S(1)} %get-tuple-element.30.pair_ref), custom_call_target="tpu_custom_call" | custom-call | tf_op jit(solution)/shard_map/first/pallas_call | solution.py:238
  10.4 3.0 %collective-permute-start.1 = (bf16[2,16,4096]{2,1,0:T(8,128)(2,1)S(1)}, bf16[2,16,4096]{2,1,0:T(8,128)(2,1)S(1)}, u32[]{:S(2)}, u32[]{:S(2)}) collective-permute-start(bf16[2,16,4096]{2,1,0:T(8,128)(2,1)S(1)} %get-tuple-element.31), channel_id=1, source_target_pairs={{0,6},{1,7},{2,4},{3,5},{6,0},{7,1},{4,2},{5,3},{8,14},{9,15},{10,... | collective-permute-start | bytes 786440 | tf_op jit(solution)/shard_map/ppermute | solution.py:210
  13.4 1.9 %near0.1.refs_0_ = bf16[2,16,4096]{2,1,0:T(8,128)(2,1)S(1)} custom-call(bf16[2,2,512,1024]{3,2,1,0:T(8,128)(2,1)S(1)} %get-tuple-element.32.left_ref, bf16[2,256,256]{2,1,0:T(8,128)(2,1)S(1)} %get-tuple-element.33.right_ref, bf16[32,4096]{1,0:T(8,128)(2,1)S(1)} %get-tuple-element.34.refs_0_), custom_call_target="tpu_custom_call" | custom-call | tf_op jit(solution)/shard_map/near0/pallas_call | solution.py:256
  15.2 0.0 collective-permute-done.2.refs_1_
  15.2 1.9 %near1.1.refs_0_ = bf16[4,16,4096]{2,1,0:T(8,128)(2,1)S(1)} custom-call(bf16[2,2,512,1024]{3,2,1,0:T(8,128)(2,1)S(1)} %get-tuple-element.32.left_ref, bf16[2,256,256]{2,1,0:T(8,128)(2,1)S(1)} %get-tuple-element.33.right_ref, bf16[2,16,4096]{2,1,0:T(8,128)(2,1)S(1)} %near0.1.refs_0_, bf16[32,4096]{1,0:T(8,128)(2,1)S(1)} %collective-permute-done.2.refs_1_), custom_call_target="tpu_custom_call" | custom-call | tf_op jit(solution)/shard_map/near1/pallas_call | solution.py:256
  17.1 0.0 copy-start
  17.1 0.0 copy-start.3
  17.1 0.0 collective-permute-done.3.refs_1_
  17.1 1.9 %near2.1.early_ref = bf16[6,16,4096]{2,1,0:T(8,128)(2,1)S(1)} custom-call(bf16[2,2,512,1024]{3,2,1,0:T(8,128)(2,1)S(1)} %get-tuple-element.32.left_ref, bf16[2,256,256]{2,1,0:T(8,128)(2,1)S(1)} %get-tuple-element.33.right_ref, bf16[4,16,4096]{2,1,0:T(8,128)(2,1)S(1)} %near1.1.refs_0_, bf16[32,4096]{1,0:T(8,128)(2,1)S(1)} %collective-permute-done.3.refs_1_), custom_call_target="tpu_custom_call" | custom-call | tf_op jit(solution)/shard_map/near2/pallas_call | solution.py:256
  19.0 0.8 %collective-permute-done.1.late_ref = bf16[2,16,4096]{2,1,0:T(8,128)(2,1)S(1)} collective-permute-done((bf16[2,16,4096]{2,1,0:T(8,128)(2,1)S(1)}, bf16[2,16,4096]{2,1,0:T(8,128)(2,1)S(1)}, u32[]{:S(2)}, u32[]{:S(2)}) %collective-permute-start.1) | collective-permute-done | bytes 262176 | tf_op jit(solution)/shard_map/ppermute | solution.py:210
  19.8 0.0 copy-done
  19.8 0.0 copy-done.3
  19.8 2.1 %last.1 = (f32[24,512]{1,0:T(8,128)S(1)}, bf16[24,512]{1,0:T(8,128)(2,1)S(1)}, bf16[24,512]{1,0:T(8,128)(2,1)S(1)}, bf16[24,512]{1,0:T(8,128)(2,1)S(1)}) custom-call(s32[48]{0:T(128)S(1)} %copy-done.3, bf16[2,16,4096]{2,1,0:T(8,128)(2,1)S(1)} %collective-permute-done.1.late_ref, bf16[6,16,4096]{2,1,0:T(8,128)(2,1)S(1)} %near2.1.early_ref, ...), custom_call_target="tpu_custom_call" | custom-call | tf_op jit(solution)/shard_map/last/pallas_call | solution.py:266
  22.0 1.8 %collective-permute-start.4 = (bf16[24,512]{1,0:T(8,128)(2,1)S(1)}, bf16[24,512]{1,0:T(8,128)(2,1)S(1)}, u32[]{:S(2)}, u32[]{:S(2)}) collective-permute-start(bf16[24,512]{1,0:T(8,128)(2,1)S(1)} %get-tuple-element.38), channel_id=1, source_target_pairs={{0,8},{8,16},{16,24},{24,0},{1,9},{9,17},{17,25},{25,1},{2,10},{10... | collective-permute-start | bytes 73736 | tf_op jit(solution)/shard_map/ppermute | solution.py:278
  23.8 2.6 %collective-permute-start.5 = (bf16[24,512]{1,0:T(8,128)(2,1)S(1)}, bf16[24,512]{1,0:T(8,128)(2,1)S(1)}, u32[]{:S(2)}, u32[]{:S(2)}) collective-permute-start(bf16[24,512]{1,0:T(8,128)(2,1)S(1)} %get-tuple-element.39), channel_id=1, source_target_pairs={{0,16},{8,24},{16,0},{24,8},{1,17},{9,25},{17,1},{25,9},{2,18},{10... | collective-permute-start | bytes 73736 | tf_op jit(solution)/shard_map/ppermute | solution.py:278
  26.3 1.3 %collective-permute-start.6 = (bf16[24,512]{1,0:T(8,128)(2,1)S(1)}, bf16[24,512]{1,0:T(8,128)(2,1)S(1)}, u32[]{:S(2)}, u32[]{:S(2)}) collective-permute-start(bf16[24,512]{1,0:T(8,128)(2,1)S(1)} %get-tuple-element.40), channel_id=1, source_target_pairs={{0,24},{8,0},{16,8},{24,16},{1,25},{9,1},{17,9},{25,17},{2,26},{10... | collective-permute-start | bytes 73736 | tf_op jit(solution)/shard_map/ppermute | solution.py:278
  27.7 0.3 collective-permute-done.4.refs_1_
  28.0 0.5 %collective-permute-done.5.refs_2_ = bf16[24,512]{1,0:T(8,128)(2,1)S(1)} collective-permute-done((bf16[24,512]{1,0:T(8,128)(2,1)S(1)}, bf16[24,512]{1,0:T(8,128)(2,1)S(1)}, u32[]{:S(2)}, u32[]{:S(2)}) %collective-permute-start.5) | collective-permute-done | bytes 24608 | tf_op jit(solution)/shard_map/ppermute | solution.py:278
  28.5 1.7 %collective-permute-done.6.refs_3_ = bf16[24,512]{1,0:T(8,128)(2,1)S(1)} collective-permute-done((bf16[24,512]{1,0:T(8,128)(2,1)S(1)}, bf16[24,512]{1,0:T(8,128)(2,1)S(1)}, u32[]{:S(2)}, u32[]{:S(2)}) %collective-permute-start.6) | collective-permute-done | bytes 24608 | tf_op jit(solution)/shard_map/ppermute | solution.py:278
  30.2 0.6 %finish.1 = f32[6,4,512]{2,1,0:T(4,128)} custom-call(f32[24,512]{1,0:T(8,128)S(1)} %get-tuple-element.37.refs_0_, bf16[24,512]{1,0:T(8,128)(2,1)S(1)} %collective-permute-done.4.refs_1_, bf16[24,512]{1,0:T(8,128)(2,1)S(1)} %collective-permute-done.5.refs_2_, bf16[24,512]{1,0:T(8,128)(2,1)S(1)} %collective-permute-done.6.refs_3_), custom_call_target="tpu_custom_call" | custom-call | tf_op jit(solution)/shard_map/finish/pallas_call | solution.py:280
Async XLA Ops:
  0.0 2.8 %collective-permute-start = (bf16[64,4096]{1,0:T(8,128)(2,1)}, bf16[64,4096]{1,0:T(8,128)(2,1)S(1)}, u32[]{:S(2)}, u32[]{:S(2)}) collective-permute-start(bf16[64,4096]{1,0:T(8,128)(2,1)} %bitcast.6), channel_id=1, source_target_pairs={{0,1},{1,0},{2,3},{3,2},{4,5},{5,4},{6,7},{7,6},{8,9},{9,8},{10,11... | collective-permute-start | bytes 1572872 | tf_op jit(solution)/shard_map/ppermute | solution.py:214
  0.5 1.0 %copy-start.1 = (bf16[64,1,4096]{2,0,1:T(8,128)(2,1)S(1)}, bf16[64,1,4096]{2,0,1:T(8,128)(2,1)}, u32[]{:S(2)}) copy-start(bf16[64,1,4096]{2,0,1:T(8,128)(2,1)} %param.6) | copy-start | bytes 1572868
  1.5 0.7 %copy-start.2 = (s32[48]{0:T(128)S(1)}, s32[48]{0:T(128)}, u32[]{:S(2)}) copy-start(s32[48]{0:T(128)} %pairs_ref.5) | copy-start | bytes 580
  3.4 11.8 %collective-permute-start.2 = (bf16[32,4096]{1,0:T(8,128)(2,1)S(1)}, bf16[32,4096]{1,0:T(8,128)(2,1)S(1)}, u32[]{:S(2)}, u32[]{:S(2)}) collective-permute-start(bf16[32,4096]{1,0:T(8,128)(2,1)S(1)} %get-tuple-element.35), channel_id=1, source_target_pairs={{0,2},{1,3},{2,6},{3,7},{6,4},{7,5},{4,0},{5,1},{8,10},{9,11},{10,... | collective-permute-start | bytes 786440 | tf_op jit(solution)/shard_map/ppermute | solution.py:210
  6.0 11.2 %collective-permute-start.3 = (bf16[32,4096]{1,0:T(8,128)(2,1)S(1)}, bf16[32,4096]{1,0:T(8,128)(2,1)S(1)}, u32[]{:S(2)}, u32[]{:S(2)}) collective-permute-start(bf16[32,4096]{1,0:T(8,128)(2,1)S(1)} %get-tuple-element.36), channel_id=1, source_target_pairs={{0,4},{1,5},{2,0},{3,1},{6,2},{7,3},{4,6},{5,7},{8,12},{9,13},{10,... | collective-permute-start | bytes 786440 | tf_op jit(solution)/shard_map/ppermute | solution.py:210
  10.4 9.4 %collective-permute-start.1 = (bf16[2,16,4096]{2,1,0:T(8,128)(2,1)S(1)}, bf16[2,16,4096]{2,1,0:T(8,128)(2,1)S(1)}, u32[]{:S(2)}, u32[]{:S(2)}) collective-permute-start(bf16[2,16,4096]{2,1,0:T(8,128)(2,1)S(1)} %get-tuple-element.31), channel_id=1, source_target_pairs={{0,6},{1,7},{2,4},{3,5},{6,0},{7,1},{4,2},{5,3},{8,14},{9,15},{10,... | collective-permute-start | bytes 786440 | tf_op jit(solution)/shard_map/ppermute | solution.py:210
  17.1 2.7 %copy-start = (bf16[512,1,4096]{2,0,1:T(8,128)(2,1)S(1)}, bf16[512,1,4096]{2,0,1:T(8,128)(2,1)}, u32[]{:S(2)}) copy-start(bf16[512,1,4096]{2,0,1:T(8,128)(2,1)} %param.5) | copy-start | bytes 12582916
  17.1 2.7 %copy-start.3 = (s32[48]{0:T(128)S(1)}, s32[48]{0:T(128)}, u32[]{:S(2)}) copy-start(s32[48]{0:T(128)} %pairs_ref.5) | copy-start | bytes 580
  22.0 6.0 %collective-permute-start.4 = (bf16[24,512]{1,0:T(8,128)(2,1)S(1)}, bf16[24,512]{1,0:T(8,128)(2,1)S(1)}, u32[]{:S(2)}, u32[]{:S(2)}) collective-permute-start(bf16[24,512]{1,0:T(8,128)(2,1)S(1)} %get-tuple-element.38), channel_id=1, source_target_pairs={{0,8},{8,16},{16,24},{24,0},{1,9},{9,17},{17,25},{25,1},{2,10},{10... | collective-permute-start | bytes 73736 | tf_op jit(solution)/shard_map/ppermute | solution.py:278
  23.8 4.7 %collective-permute-start.5 = (bf16[24,512]{1,0:T(8,128)(2,1)S(1)}, bf16[24,512]{1,0:T(8,128)(2,1)S(1)}, u32[]{:S(2)}, u32[]{:S(2)}) collective-permute-start(bf16[24,512]{1,0:T(8,128)(2,1)S(1)} %get-tuple-element.39), channel_id=1, source_target_pairs={{0,16},{8,24},{16,0},{24,8},{1,17},{9,25},{17,1},{25,9},{2,18},{10... | collective-permute-start | bytes 73736 | tf_op jit(solution)/shard_map/ppermute | solution.py:278
  26.3 3.8 %collective-permute-start.6 = (bf16[24,512]{1,0:T(8,128)(2,1)S(1)}, bf16[24,512]{1,0:T(8,128)(2,1)S(1)}, u32[]{:S(2)}, u32[]{:S(2)}) collective-permute-start(bf16[24,512]{1,0:T(8,128)(2,1)S(1)} %get-tuple-element.40), channel_id=1, source_target_pairs={{0,24},{8,0},{16,8},{24,16},{1,25},{9,1},{17,9},{25,17},{2,26},{10... | collective-permute-start | bytes 73736 | tf_op jit(solution)/shard_map/ppermute | solution.py:278

commit v7 on v6

--- a/solution.py
+++ b/solution.py
@@ -40,30 +40,21 @@
     return place
 
 
-def wanted_block(ex, held, slots, pairs_ref, step, side):
+def pick_kernel(ex, held, slots, order, pairs_ref, query_ref, *outs):
     me = lax.axis_index("ex")
     chips = ex // 2
-    target = ring_chip((ring_place(me >> 1, chips) + step) & (chips - 1))
-    first = (2 * target + (me & 1)) * slots
-    base = (me ^ side) * held
-
-    def body(slot, block):
-        local = pairs_ref[first + slot] - base
-        return jnp.where((local >= 0) & (local < held), local, block)
-
-    return pl.multiple_of(over_slots(slots, body, jnp.int32(0)) * QBLK, QBLK)
-
-
-def own_kernel(find, pairs_ref, query_ref, *outs):
-    for group, out_ref in enumerate(outs):
-        out_ref[...] = query_ref[pl.ds(find(pairs_ref, group, 0), QBLK), :]
-
-
-def pick_kernel(find, groups, pairs_ref, other_ref, *refs):
-    for group in range(groups):
-        out_ref = refs[groups + group]
-        out_ref[:QBLK] = refs[group][...]
-        out_ref[QBLK:] = other_ref[pl.ds(find(pairs_ref, group, 1), QBLK), :]
+    place = ring_place(me >> 1, chips)
+    self_ref, near_refs, far_ref, swap_ref = outs[0], outs[1:-2], outs[-2], outs[-1]
+    targets = [self_ref, swap_ref.at[pl.ds(0, QBLK)], *near_refs, far_ref, swap_ref.at[pl.ds(QBLK, QBLK)]]
+    for index, out_ref in enumerate(targets):
+        target = 2 * ring_chip((place + order[index // 2]) & (chips - 1)) + ((me & 1) ^ (index % 2))
+
+        def body(slot, block):
+            local = pairs_ref[target * slots + slot] - me * held
+            return jnp.where((local >= 0) & (local < held), local, block)
+
+        block = over_slots(slots, body, jnp.int32(0))
+        out_ref[...] = query_ref[pl.ds(pl.multiple_of(block * QBLK, QBLK), QBLK), :]
 
 
 def make_factors(rows, width, factors_ref, left_ref, right_ref):
@@ -72,13 +63,12 @@
     span = right_ref.shape[1]
     outs = split_bf16(factors_ref[:width])
     ins = split_bf16(factors_ref[width:])
-    row = lax.broadcasted_iota(jnp.int32, (half, width), 0) // QBLK
-    row_o = lax.broadcasted_iota(jnp.int32, (half, width), 1)
+    row = lax.broadcasted_iota(jnp.int32, (half // QBLK, width), 0)
+    row_o = lax.broadcasted_iota(jnp.int32, (half // QBLK, width), 1)
     col = lax.broadcasted_iota(jnp.int32, (width, half), 1) // QBLK
     col_o = lax.broadcasted_iota(jnp.int32, (width, half), 0)
     a = lax.broadcasted_iota(jnp.int32, (half, half), 1) - lax.broadcasted_iota(jnp.int32, (half, half), 0)
     same = (a & (QBLK - 1)) == lax.axis_index("layer") * rows
-    zero = jnp.zeros((), BF16)
     for h in range(2):
         for s in range(2):
             pick_rows = (row * 2 + s == row_o).astype(BF16)
@@ -86,7 +76,8 @@
             for t in range(2):
                 pick_cols = (col * 2 + (s ^ t) == col_o).astype(BF16)
                 spread = jnp.dot(rows, pick_cols, preferred_element_type=F32)
-                left_ref[h, s, :, t * half : (t + 1) * half] = jnp.where(same, spread.astype(BF16), zero)
+                tall = jnp.broadcast_to(spread[:, None, :], (half // QBLK, QBLK, half)).reshape(half, half)
+                left_ref[h, s, :, t * half : (t + 1) * half] = jnp.where(same, tall, 0.0).astype(BF16)
         up = (
             lax.broadcasted_iota(jnp.int32, (span, in_width), 0) % in_width
             == lax.broadcasted_iota(jnp.int32, (span, in_width), 1)
@@ -104,12 +95,11 @@
         right_ref[h] = jnp.where(block, wide, 0.0).astype(BF16)
 
 
-def prepare(pair_ref, left_ref, right_ref, prep_ref):
-    chunks = pair_ref.shape[1] // LANES
+def prepare(blocks, left_ref, right_ref, prep_ref):
+    chunks = blocks[0].shape[1] // LANES
     half = LANES // 2
     stacked = []
-    for side in range(2):
-        block = pair_ref[side * QBLK : (side + 1) * QBLK, :]
+    for block in blocks:
         tall = jnp.concatenate([block[:, c * LANES : (c + 1) * LANES] for c in range(chunks)], axis=0)
         turned = jnp.concatenate([tall[:, half:], tall[:, :half]], axis=1)
         stacked.append(jnp.concatenate([tall, turned], axis=0))
@@ -133,17 +123,18 @@
             ]
 
 
-def first_kernel(rows, width, factors_ref, pair_ref, left_ref, right_ref, prep_ref):
+def first_kernel(rows, width, factors_ref, far_ref, swap_ref, left_ref, right_ref, prep_ref):
     make_factors(rows, width, factors_ref, left_ref, right_ref)
-    prepare(pair_ref, left_ref, right_ref, prep_ref)
+    prepare((far_ref[...], swap_ref[QBLK:]), left_ref, right_ref, prep_ref)
 
 
 def near_kernel(done, left_ref, right_ref, *refs):
     prep_ref = refs[-1]
     if done:
         prep_ref[:done] = refs[0][...]
-    for index, pair_ref in enumerate(refs[min(done, 1) : -1]):
-        prepare(pair_ref, left_ref, right_ref, prep_ref.at[pl.ds(done + 2 * index, 2)])
+    blocks = [ref[:QBLK] for ref in refs[min(done, 1) : -1]]
+    for index in range(0, len(blocks), 2):
+        prepare(blocks[index : index + 2], left_ref, right_ref, prep_ref.at[pl.ds(done + index, 2)])
 
 
 def last_kernel(order, layer, held, slots, pairs_ref, late_ref, early_ref, train_ref, *refs):
@@ -204,37 +195,35 @@
     out_factor = out_precond.reshape(out_precond.shape[1:])
     limit = pltpu.CompilerParams(vmem_limit_bytes=24 * 2**20)
 
-    def pass_on(array, step):
-        ring = [ring_chip(place) for place in range(ex // 2)]
+    work = pl.CostEstimate(flops=2 * 10**9, bytes_accessed=1000, transcendentals=0)
+    groups = ex // 2
+    order = sorted(range(groups), key=lambda step: min(step, groups - step))
+
+    def pass_on(array, step, flip=0):
+        ring = [ring_chip(place) for place in range(groups)]
         moves = zip(ring, ring[step:] + ring[:step])
-        return lax.ppermute(array, "ex", [(2 * a + c, 2 * b + c) for a, b in moves for c in range(2)])
-
-    groups = ex // 2
-    find = functools.partial(wanted_block, ex, held, slots)
-    other = lax.ppermute(query, "ex", [(i, i ^ 1) for i in range(ex)])
-    own = pl.pallas_call(
-        functools.partial(own_kernel, find),
-        out_shape=[jax.ShapeDtypeStruct((QBLK, features), BF16)] * groups,
+        return lax.ppermute(array, "ex", [(2 * a + c, 2 * b + (c ^ flip)) for a, b in moves for c in range(2)])
+
+    block = jax.ShapeDtypeStruct((QBLK, features), BF16)
+    picked = pl.pallas_call(
+        functools.partial(pick_kernel, ex, held, slots, order),
+        out_shape=[block] * (ex - 2) + [jax.ShapeDtypeStruct((2 * QBLK, features), BF16)],
         in_specs=[SMEM, VMEM],
-        out_specs=[VMEM] * groups,
-        compiler_params=limit,
-        name="own",
+        out_specs=[VMEM] * (ex - 1),
+        compiler_params=limit,
+        name="pick",
     )(pair_blocks, query)
-    picked = pl.pallas_call(
-        functools.partial(pick_kernel, find, groups),
-        out_shape=[jax.ShapeDtypeStruct((2 * QBLK, features), BF16)] * groups,
-        in_specs=[SMEM] + [VMEM] * (1 + groups),
-        out_specs=[VMEM] * groups,
-        compiler_params=limit,
-        name="pick",
-    )(pair_blocks, other, *own)
-
-    order = sorted(range(groups), key=lambda step: min(step, groups - step))
-    raw = [pass_on(picked[step], step) for step in order[1:-1]]
+    near = picked[1:-2]
+    raw = [None] * len(near)
+    for flip in range(2):
+        for index in range(flip, len(near), 2):
+            raw[index] = pass_on(near[index], order[1 + index // 2], flip)
+        if flip == 0:
+            swapped = pass_on(picked[-1], 0, 1)
 
     stack = features // LANES * QBLK
     span = 2 * LANES
-    out_factor, in_factor, far_pick = lax.optimization_barrier((out_factor, in_factor, picked[order[-1]]))
+    out_factor, in_factor, far_pick = lax.optimization_barrier((out_factor, in_factor, picked[-2]))
     left, right, far = pl.pallas_call(
         functools.partial(first_kernel, rows, out_factor.shape[0]),
         out_shape=[
@@ -242,27 +231,29 @@
             jax.ShapeDtypeStruct((2, span, span), BF16),
             jax.ShapeDtypeStruct((2, QBLK, features), BF16),
         ],
-        in_specs=[VMEM] * 2,
+        in_specs=[VMEM] * 3,
         out_specs=[VMEM] * 3,
         compiler_params=limit,
         name="first",
-    )(jnp.concatenate([out_factor, in_factor], axis=0), far_pick)
+        cost_estimate=work,
+    )(jnp.concatenate([out_factor, in_factor], axis=0), far_pick, swapped)
     far = pass_on(far, order[-1])
 
     early, done = [], 0
-    half = len(raw) // 2
-    for index, pairs in enumerate(([picked[0]], raw[:half], raw[half:])):
+    half = len(raw) // 4 * 2
+    for index, blocks in enumerate(([picked[0], swapped], raw[:half], raw[half:])):
         early = [
             pl.pallas_call(
                 functools.partial(near_kernel, done),
-                out_shape=jax.ShapeDtypeStruct((done + 2 * len(pairs), QBLK, features), BF16),
-                in_specs=[VMEM] * (2 + len(early) + len(pairs)),
+                out_shape=jax.ShapeDtypeStruct((done + len(blocks), QBLK, features), BF16),
+                in_specs=[VMEM] * (2 + len(early) + len(blocks)),
                 out_specs=VMEM,
                 compiler_params=limit,
                 name=f"near{index}",
-            )(left, right, *early, *pairs)
+                cost_estimate=work,
+            )(left, right, *early, *blocks)
         ]
-        done += 2 * len(pairs)
+        done += len(blocks)
     parts = pl.pallas_call(
         functools.partial(last_kernel, order, layer, held, slots),
         out_shape=[jax.ShapeDtypeStruct((slots * rows, train_rows), F32)]

time: 31 us -> 32.2 us (1.039)
  starting transfers between devices: 11.8 us -> 13.3 us
  Pallas kernels: 13.2 us -> 12.2 us
  waiting for transfers between devices: 3.28 us -> 3.74 us
    ppermute x4 -> x6, starting transfers between devices: 6.04 us -> 7.58 us  [pass_on(): lax.ppermute(array, 'ex', [(2 * a + c, 2 * b + (c ^ flip)) for a, b in mo...]
    pallas_call x2 -> x1, Pallas kernels: 1.24 us -> 0.67 us  [shards(): pl.pallas_call(functools.partial(pick_kernel, ex, held, slots, order), ou...]
    ppermute x4 -> x6, waiting for transfers between devices: 0.81 us -> 1.26 us  [pass_on(): lax.ppermute(array, 'ex', [(2 * a + c, 2 * b + (c ^ flip)) for a, b in mo...]
    pallas_call x1, Pallas kernels: 3.57 us -> 3.22 us  [shards(): pl.pallas_call(functools.partial(first_kernel, rows, out_factor.shape[0])...]
  transfers between devices with their start and end apart: 7 -> 9, of which waited for: 4 -> 3; matrix products, arithmetic and copies ran while one was open for 3% -> 2% of each run, Pallas kernels for 32% -> 28%
where the time goes in v7:
time: 32.2 us; the launch traced here: 31.9 us
  starting transfers between devices  13.3 us (41%)
  Pallas kernels  12.2 us (38%)
  waiting for transfers between devices  3.74 us (12%)
  local copies, waits for them, and re-layouts  1.71 us (5%)
  other arithmetic  0.78 us (2%)
    ppermute x6, starting transfers between devices, pass_on(): lax.ppermute(array, 'ex', [(2 * a + c, 2 * b + (c ^ flip)) for a, b in mo...  7.58 us
    ppermute x3, starting transfers between devices, shards(): lax.ppermute(parts[m], 'layer', [(i, (i + m) % layer) for i in range(laye...  5.76 us
    pallas_call x3, Pallas kernels, shards(): pl.pallas_call(functools.partial(near_kernel, done), out_shape=jax.ShapeD...  5.58 us
    pallas_call x1, Pallas kernels, shards(): pl.pallas_call(functools.partial(first_kernel, rows, out_factor.shape[0])...  3.22 us
    ppermute x3, waiting for transfers between devices, shards(): lax.ppermute(parts[m], 'layer', [(i, (i + m) % layer) for i in range(laye...  2.48 us
    pallas_call x1, Pallas kernels, shards(): pl.pallas_call(functools.partial(last_kernel, order, layer, held, slots),...  2.13 us
    unnamed x8, local copies, waits for them, and re-layouts  1.71 us
    ppermute x6, waiting for transfers between devices, pass_on(): lax.ppermute(array, 'ex', [(2 * a + c, 2 * b + (c ^ flip)) for a, b in mo...  1.26 us
  transfers between devices with their start and end apart: 9, of which 3 were waited for; matrix products, arithmetic and copies ran while one was open for 2% of the time, Pallas kernels for 28%

profile of v7, /device:TPU:0, one launch (start us, length us, event | category | flops | bytes accessed | tf_op | source)
XLA Modules:
  0.0 31.9 jit_solution(2182356633765170706)
XLA Ops:
  0.0 0.0 copy-start.1
  0.0 1.0 %copy-done.1 = bf16[64,1,4096]{2,0,1:T(8,128)(2,1)S(1)} copy-done((bf16[64,1,4096]{2,0,1:T(8,128)(2,1)S(1)}, bf16[64,1,4096]{2,0,1:T(8,128)(2,1)}, u32[]{:S(2)}) %copy-start.1) | copy-done | bytes 524312
  1.0 0.0 copy-start.2
  1.0 0.7 %copy-done.2 = s32[48]{0:T(128)S(1)} copy-done((s32[48]{0:T(128)S(1)}, s32[48]{0:T(128)}, u32[]{:S(2)}) %copy-start.2) | copy-done | bytes 216
  1.7 0.7 %pick.1 = (bf16[16,4096]{1,0:T(8,128)(2,1)S(1)}, bf16[16,4096]{1,0:T(8,128)(2,1)S(1)}, bf16[16,4096]{1,0:T(8,128)(2,1)S(1)}, bf16[16,4096]{1,0:T(8,128)(2,1)S(1)...) custom-call(s32[48]{0:T(128)S(1)} %copy-done.2, ...), custom_call_target="tpu_custom_call" | custom-call | tf_op jit(solution)/shard_map/pick/pallas_call | solution.py:208
  2.4 0.5 %collective-permute-start = (bf16[32,4096]{1,0:T(8,128)(2,1)S(1)}, bf16[32,4096]{1,0:T(8,128)(2,1)S(1)}, u32[]{:S(2)}, u32[]{:S(2)}) collective-permute-start(bf16[32,4096]{1,0:T(8,128)(2,1)S(1)} %get-tuple-element.26), channel_id=1, source_target_pairs={{0,1},{1,0},{2,3},{3,2},{6,7},{7,6},{4,5},{5,4},{8,9},{9,8},{10,11... | collective-permute-start | bytes 786440 | tf_op jit(solution)/shard_map/ppermute | solution.py:205
  2.9 2.6 %collective-permute-start.2 = (bf16[16,4096]{1,0:T(8,128)(2,1)S(1)}, bf16[16,4096]{1,0:T(8,128)(2,1)S(1)}, u32[]{:S(2)}, u32[]{:S(2)}) collective-permute-start(bf16[16,4096]{1,0:T(8,128)(2,1)S(1)} %get-tuple-element.31), channel_id=1, source_target_pairs={{0,2},{1,3},{2,6},{3,7},{6,4},{7,5},{4,0},{5,1},{8,10},{9,11},{10,... | collective-permute-start | bytes 393224 | tf_op jit(solution)/shard_map/ppermute | solution.py:205
  5.4 1.3 %collective-permute-start.3 = (bf16[16,4096]{1,0:T(8,128)(2,1)S(1)}, bf16[16,4096]{1,0:T(8,128)(2,1)S(1)}, u32[]{:S(2)}, u32[]{:S(2)}) collective-permute-start(bf16[16,4096]{1,0:T(8,128)(2,1)S(1)} %get-tuple-element.32), channel_id=1, source_target_pairs={{0,3},{1,2},{2,7},{3,6},{6,5},{7,4},{4,1},{5,0},{8,11},{9,10},{10,... | collective-permute-start | bytes 393224 | tf_op jit(solution)/shard_map/ppermute | solution.py:205
  6.7 0.5 %collective-permute-start.4 = (bf16[16,4096]{1,0:T(8,128)(2,1)S(1)}, bf16[16,4096]{1,0:T(8,128)(2,1)S(1)}, u32[]{:S(2)}, u32[]{:S(2)}) collective-permute-start(bf16[16,4096]{1,0:T(8,128)(2,1)S(1)} %get-tuple-element.33), channel_id=1, source_target_pairs={{0,4},{1,5},{2,0},{3,1},{6,2},{7,3},{4,6},{5,7},{8,12},{9,13},{10,... | collective-permute-start | bytes 393224 | tf_op jit(solution)/shard_map/ppermute | solution.py:205
  7.3 0.0 collective-permute-start.5
  7.3 0.8 %pad_maximum_fusion.factors_ref = f32[128,64]{1,0:T(8,128)S(1)} fusion(f32[64,64]{1,0:T(8,128)} %bitcast.7, f32[64,64]{1,0:T(8,128)} %bitcast.8), kind=kLoop, calls=%fused_computation | loop fusion | flops 8192 | bytes 65536 | tf_op jit(solution)/shard_map/concatenate | solution.py:239
  8.0 0.0 collective-permute-done.swap_ref.refs_1_
  8.0 3.2 %first.1 = (bf16[2,2,512,1024]{3,2,1,0:T(8,128)(2,1)S(1)}, bf16[2,256,256]{2,1,0:T(8,128)(2,1)S(1)}, bf16[2,16,4096]{2,1,0:T(8,128)(2,1)S(1)}) custom-call(f32[128,64]{1,0:T(8,128)S(1)} %pad_maximum_fusion.factors_ref, bf16[16,4096]{1,0:T(8,128)(2,1)S(1)} %get-tuple-element.25.far_ref, bf16[32,4096]{1,0:T(8,128)(2,1)S(1)} %collective-permute-done.swap_ref.refs_1_), custom_call_target="tpu_custom_call" | custom-call | flops 2000000000 | bytes 1000 | tf_op jit(solution)/shard_map/first/pallas_call | solution.py:227
  11.3 2.7 %collective-permute-start.1 = (bf16[2,16,4096]{2,1,0:T(8,128)(2,1)S(1)}, bf16[2,16,4096]{2,1,0:T(8,128)(2,1)S(1)}, u32[]{:S(2)}, u32[]{:S(2)}) collective-permute-start(bf16[2,16,4096]{2,1,0:T(8,128)(2,1)S(1)} %get-tuple-element.27), channel_id=1, source_target_pairs={{0,6},{1,7},{2,4},{3,5},{6,0},{7,1},{4,2},{5,3},{8,14},{9,15},{10,... | collective-permute-start | bytes 786440 | tf_op jit(solution)/shard_map/ppermute | solution.py:205
  14.0 1.9 %near0.1.refs_0_ = bf16[2,16,4096]{2,1,0:T(8,128)(2,1)S(1)} custom-call(bf16[2,2,512,1024]{3,2,1,0:T(8,128)(2,1)S(1)} %get-tuple-element.28.left_ref, bf16[2,256,256]{2,1,0:T(8,128)(2,1)S(1)} %get-tuple-element.29.right_ref, bf16[16,4096]{1,0:T(8,128)(2,1)S(1)} %get-tuple-element.30.refs_0_, bf16[32,4096]{1,0:T(8,128)(2,1)S(1)} %collective-permute-done.swap_ref.refs_1_), custom_call_target="tpu_custom_call" | custom-call | flops 2000000000 | bytes 1000 | tf_op jit(solution)/shard_map/near0/pallas_call | solution.py:246
  15.8 0.0 collective-permute-done.2.refs_1_
  15.8 0.0 collective-permute-done.3.refs_2_
  15.9 1.9 %near1.1.refs_0_ = bf16[4,16,4096]{2,1,0:T(8,128)(2,1)S(1)} custom-call(bf16[2,2,512,1024]{3,2,1,0:T(8,128)(2,1)S(1)} %get-tuple-element.28.left_ref, bf16[2,256,256]{2,1,0:T(8,128)(2,1)S(1)} %get-tuple-element.29.right_ref, bf16[2,16,4096]{2,1,0:T(8,128)(2,1)S(1)} %near0.1.refs_0_, bf16[16,4096]{1,0:T(8,128)(2,1)S(1)} %collective-permute-done.2.refs_1_, ...), custom_call_target="tpu_custom_call" | custom-call | flops 2000000000 | bytes 1000 | tf_op jit(solution)/shard_map/near1/pallas_call | solution.py:246
  17.7 0.0 copy-start
  17.7 0.0 copy-start.3
  17.7 0.0 collective-permute-done.4.refs_1_
  17.8 0.0 collective-permute-done.5.refs_2_
  17.8 1.9 %near2.1.early_ref = bf16[6,16,4096]{2,1,0:T(8,128)(2,1)S(1)} custom-call(bf16[2,2,512,1024]{3,2,1,0:T(8,128)(2,1)S(1)} %get-tuple-element.28.left_ref, bf16[2,256,256]{2,1,0:T(8,128)(2,1)S(1)} %get-tuple-element.29.right_ref, bf16[4,16,4096]{2,1,0:T(8,128)(2,1)S(1)} %near1.1.refs_0_, bf16[16,4096]{1,0:T(8,128)(2,1)S(1)} %collective-permute-done.4.refs_1_, ...), custom_call_target="tpu_custom_call" | custom-call | flops 2000000000 | bytes 1000 | tf_op jit(solution)/shard_map/near2/pallas_call | solution.py:246
  19.6 1.2 %collective-permute-done.1.late_ref = bf16[2,16,4096]{2,1,0:T(8,128)(2,1)S(1)} collective-permute-done((bf16[2,16,4096]{2,1,0:T(8,128)(2,1)S(1)}, bf16[2,16,4096]{2,1,0:T(8,128)(2,1)S(1)}, u32[]{:S(2)}, u32[]{:S(2)}) %collective-permute-start.1) | collective-permute-done | bytes 262176 | tf_op jit(solution)/shard_map/ppermute | solution.py:205
  20.9 0.0 copy-done
  20.9 0.0 copy-done.3
  20.9 2.1 %last.1 = (f32[24,512]{1,0:T(8,128)S(1)}, bf16[24,512]{1,0:T(8,128)(2,1)S(1)}, bf16[24,512]{1,0:T(8,128)(2,1)S(1)}, bf16[24,512]{1,0:T(8,128)(2,1)S(1)}) custom-call(s32[48]{0:T(128)S(1)} %copy-done.3, bf16[2,16,4096]{2,1,0:T(8,128)(2,1)S(1)} %collective-permute-done.1.late_ref, bf16[6,16,4096]{2,1,0:T(8,128)(2,1)S(1)} %near2.1.early_ref, ...), custom_call_target="tpu_custom_call" | custom-call | tf_op jit(solution)/shard_map/last/pallas_call | solution.py:257
  23.0 1.8 %collective-permute-start.6 = (bf16[24,512]{1,0:T(8,128)(2,1)S(1)}, bf16[24,512]{1,0:T(8,128)(2,1)S(1)}, u32[]{:S(2)}, u32[]{:S(2)}) collective-permute-start(bf16[24,512]{1,0:T(8,128)(2,1)S(1)} %get-tuple-element.36), channel_id=1, source_target_pairs={{0,8},{8,16},{16,24},{24,0},{1,9},{9,17},{17,25},{25,1},{2,10},{10... | collective-permute-start | bytes 73736 | tf_op jit(solution)/shard_map/ppermute | solution.py:269
  24.9 2.6 %collective-permute-start.7 = (bf16[24,512]{1,0:T(8,128)(2,1)S(1)}, bf16[24,512]{1,0:T(8,128)(2,1)S(1)}, u32[]{:S(2)}, u32[]{:S(2)}) collective-permute-start(bf16[24,512]{1,0:T(8,128)(2,1)S(1)} %get-tuple-element.37), channel_id=1, source_target_pairs={{0,16},{8,24},{16,0},{24,8},{1,17},{9,25},{17,1},{25,9},{2,18},{10... | collective-permute-start | bytes 73736 | tf_op jit(solution)/shard_map/ppermute | solution.py:269
  27.5 1.3 %collective-permute-start.8 = (bf16[24,512]{1,0:T(8,128)(2,1)S(1)}, bf16[24,512]{1,0:T(8,128)(2,1)S(1)}, u32[]{:S(2)}, u32[]{:S(2)}) collective-permute-start(bf16[24,512]{1,0:T(8,128)(2,1)S(1)} %get-tuple-element.38), channel_id=1, source_target_pairs={{0,24},{8,0},{16,8},{24,16},{1,25},{9,1},{17,9},{25,17},{2,26},{10... | collective-permute-start | bytes 73736 | tf_op jit(solution)/shard_map/ppermute | solution.py:269
  28.8 0.0 collective-permute-done.6.refs_1_
  28.8 0.9 %collective-permute-done.7.refs_2_ = bf16[24,512]{1,0:T(8,128)(2,1)S(1)} collective-permute-done((bf16[24,512]{1,0:T(8,128)(2,1)S(1)}, bf16[24,512]{1,0:T(8,128)(2,1)S(1)}, u32[]{:S(2)}, u32[]{:S(2)}) %collective-permute-start.7) | collective-permute-done | bytes 24608 | tf_op jit(solution)/shard_map/ppermute | solution.py:269
  29.7 1.6 %collective-permute-done.8.refs_3_ = bf16[24,512]{1,0:T(8,128)(2,1)S(1)} collective-permute-done((bf16[24,512]{1,0:T(8,128)(2,1)S(1)}, bf16[24,512]{1,0:T(8,128)(2,1)S(1)}, u32[]{:S(2)}, u32[]{:S(2)}) %collective-permute-start.8) | collective-permute-done | bytes 24608 | tf_op jit(solution)/shard_map/ppermute | solution.py:269
  31.3 0.6 %finish.1 = f32[6,4,512]{2,1,0:T(4,128)} custom-call(f32[24,512]{1,0:T(8,128)S(1)} %get-tuple-element.35.refs_0_, bf16[24,512]{1,0:T(8,128)(2,1)S(1)} %collective-permute-done.6.refs_1_, bf16[24,512]{1,0:T(8,128)(2,1)S(1)} %collective-permute-done.7.refs_2_, bf16[24,512]{1,0:T(8,128)(2,1)S(1)} %collective-permute-done.8.refs_3_), custom_call_target="tpu_custom_call" | custom-call | tf_op jit(solution)/shard_map/finish/pallas_call | solution.py:271
Async XLA Ops:
  0.0 1.0 %copy-start.1 = (bf16[64,1,4096]{2,0,1:T(8,128)(2,1)S(1)}, bf16[64,1,4096]{2,0,1:T(8,128)(2,1)}, u32[]{:S(2)}) copy-start(bf16[64,1,4096]{2,0,1:T(8,128)(2,1)} %param.6) | copy-start | bytes 1572868
  1.0 0.7 %copy-start.2 = (s32[48]{0:T(128)S(1)}, s32[48]{0:T(128)}, u32[]{:S(2)}) copy-start(s32[48]{0:T(128)} %pairs_ref.3) | copy-start | bytes 580
  2.4 5.7 %collective-permute-start = (bf16[32,4096]{1,0:T(8,128)(2,1)S(1)}, bf16[32,4096]{1,0:T(8,128)(2,1)S(1)}, u32[]{:S(2)}, u32[]{:S(2)}) collective-permute-start(bf16[32,4096]{1,0:T(8,128)(2,1)S(1)} %get-tuple-element.26), channel_id=1, source_target_pairs={{0,1},{1,0},{2,3},{3,2},{6,7},{7,6},{4,5},{5,4},{8,9},{9,8},{10,11... | collective-permute-start | bytes 786440 | tf_op jit(solution)/shard_map/ppermute | solution.py:205
  2.9 12.9 %collective-permute-start.2 = (bf16[16,4096]{1,0:T(8,128)(2,1)S(1)}, bf16[16,4096]{1,0:T(8,128)(2,1)S(1)}, u32[]{:S(2)}, u32[]{:S(2)}) collective-permute-start(bf16[16,4096]{1,0:T(8,128)(2,1)S(1)} %get-tuple-element.31), channel_id=1, source_target_pairs={{0,2},{1,3},{2,6},{3,7},{6,4},{7,5},{4,0},{5,1},{8,10},{9,11},{10,... | collective-permute-start | bytes 393224 | tf_op jit(solution)/shard_map/ppermute | solution.py:205
  5.4 10.4 %collective-permute-start.3 = (bf16[16,4096]{1,0:T(8,128)(2,1)S(1)}, bf16[16,4096]{1,0:T(8,128)(2,1)S(1)}, u32[]{:S(2)}, u32[]{:S(2)}) collective-permute-start(bf16[16,4096]{1,0:T(8,128)(2,1)S(1)} %get-tuple-element.32), channel_id=1, source_target_pairs={{0,3},{1,2},{2,7},{3,6},{6,5},{7,4},{4,1},{5,0},{8,11},{9,10},{10,... | collective-permute-start | bytes 393224 | tf_op jit(solution)/shard_map/ppermute | solution.py:205
  6.7 11.0 %collective-permute-start.4 = (bf16[16,4096]{1,0:T(8,128)(2,1)S(1)}, bf16[16,4096]{1,0:T(8,128)(2,1)S(1)}, u32[]{:S(2)}, u32[]{:S(2)}) collective-permute-start(bf16[16,4096]{1,0:T(8,128)(2,1)S(1)} %get-tuple-element.33), channel_id=1, source_target_pairs={{0,4},{1,5},{2,0},{3,1},{6,2},{7,3},{4,6},{5,7},{8,12},{9,13},{10,... | collective-permute-start | bytes 393224 | tf_op jit(solution)/shard_map/ppermute | solution.py:205
  7.3 10.5 %collective-permute-start.5 = (bf16[16,4096]{1,0:T(8,128)(2,1)S(1)}, bf16[16,4096]{1,0:T(8,128)(2,1)S(1)}, u32[]{:S(2)}, u32[]{:S(2)}) collective-permute-start(bf16[16,4096]{1,0:T(8,128)(2,1)S(1)} %get-tuple-element.34), channel_id=1, source_target_pairs={{0,5},{1,4},{2,1},{3,0},{6,3},{7,2},{4,7},{5,6},{8,13},{9,12},{10,... | collective-permute-start | bytes 393224 | tf_op jit(solution)/shard_map/ppermute | solution.py:205
  11.3 9.6 %collective-permute-start.1 = (bf16[2,16,4096]{2,1,0:T(8,128)(2,1)S(1)}, bf16[2,16,4096]{2,1,0:T(8,128)(2,1)S(1)}, u32[]{:S(2)}, u32[]{:S(2)}) collective-permute-start(bf16[2,16,4096]{2,1,0:T(8,128)(2,1)S(1)} %get-tuple-element.27), channel_id=1, source_target_pairs={{0,6},{1,7},{2,4},{3,5},{6,0},{7,1},{4,2},{5,3},{8,14},{9,15},{10,... | collective-permute-start | bytes 786440 | tf_op jit(solution)/shard_map/ppermute | solution.py:205
  17.7 3.2 %copy-start = (bf16[512,1,4096]{2,0,1:T(8,128)(2,1)S(1)}, bf16[512,1,4096]{2,0,1:T(8,128)(2,1)}, u32[]{:S(2)}) copy-start(bf16[512,1,4096]{2,0,1:T(8,128)(2,1)} %param.5) | copy-start | bytes 12582916
  17.7 3.2 %copy-start.3 = (s32[48]{0:T(128)S(1)}, s32[48]{0:T(128)}, u32[]{:S(2)}) copy-start(s32[48]{0:T(128)} %pairs_ref.3) | copy-start | bytes 580
  23.0 5.8 %collective-permute-start.6 = (bf16[24,512]{1,0:T(8,128)(2,1)S(1)}, bf16[24,512]{1,0:T(8,128)(2,1)S(1)}, u32[]{:S(2)}, u32[]{:S(2)}) collective-permute-start(bf16[24,512]{1,0:T(8,128)(2,1)S(1)} %get-tuple-element.36), channel_id=1, source_target_pairs={{0,8},{8,16},{16,24},{24,0},{1,9},{9,17},{17,25},{25,1},{2,10},{10... | collective-permute-start | bytes 73736 | tf_op jit(solution)/shard_map/ppermute | solution.py:269
  24.9 4.8 %collective-permute-start.7 = (bf16[24,512]{1,0:T(8,128)(2,1)S(1)}, bf16[24,512]{1,0:T(8,128)(2,1)S(1)}, u32[]{:S(2)}, u32[]{:S(2)}) collective-permute-start(bf16[24,512]{1,0:T(8,128)(2,1)S(1)} %get-tuple-element.37), channel_id=1, source_target_pairs={{0,16},{8,24},{16,0},{24,8},{1,17},{9,25},{17,1},{25,9},{2,18},{10... | collective-permute-start | bytes 73736 | tf_op jit(solution)/shard_map/ppermute | solution.py:269
  27.5 3.8 %collective-permute-start.8 = (bf16[24,512]{1,0:T(8,128)(2,1)S(1)}, bf16[24,512]{1,0:T(8,128)(2,1)S(1)}, u32[]{:S(2)}, u32[]{:S(2)}) collective-permute-start(bf16[24,512]{1,0:T(8,128)(2,1)S(1)} %get-tuple-element.38), channel_id=1, source_target_pairs={{0,24},{8,0},{16,8},{24,16},{1,25},{9,1},{17,9},{25,17},{2,26},{10... | collective-permute-start | bytes 73736 | tf_op jit(solution)/shard_map/ppermute | solution.py:269

commit v8 on v6

--- a/solution.py
+++ b/solution.py
@@ -68,40 +68,45 @@
 
 def make_factors(rows, width, factors_ref, left_ref, right_ref):
     in_width = factors_ref.shape[0] - width
-    half = left_ref.shape[2]
+    half = left_ref.shape[1] // 2
     span = right_ref.shape[1]
     outs = split_bf16(factors_ref[:width])
     ins = split_bf16(factors_ref[width:])
-    row = lax.broadcasted_iota(jnp.int32, (half, width), 0) // QBLK
-    row_o = lax.broadcasted_iota(jnp.int32, (half, width), 1)
+    row = lax.broadcasted_iota(jnp.int32, (half // QBLK, width), 0)
+    row_o = lax.broadcasted_iota(jnp.int32, (half // QBLK, width), 1)
     col = lax.broadcasted_iota(jnp.int32, (width, half), 1) // QBLK
     col_o = lax.broadcasted_iota(jnp.int32, (width, half), 0)
     a = lax.broadcasted_iota(jnp.int32, (half, half), 1) - lax.broadcasted_iota(jnp.int32, (half, half), 0)
     same = (a & (QBLK - 1)) == lax.axis_index("layer") * rows
-    zero = jnp.zeros((), BF16)
     for h in range(2):
         for s in range(2):
             pick_rows = (row * 2 + s == row_o).astype(BF16)
-            rows = jnp.dot(pick_rows, outs[h], preferred_element_type=F32).astype(BF16)
+            part = jnp.dot(pick_rows, outs[h], preferred_element_type=F32).astype(BF16)
+            start = (2 * h + s) * half
             for t in range(2):
                 pick_cols = (col * 2 + (s ^ t) == col_o).astype(BF16)
-                spread = jnp.dot(rows, pick_cols, preferred_element_type=F32)
-                left_ref[h, s, :, t * half : (t + 1) * half] = jnp.where(same, spread.astype(BF16), zero)
-        up = (
-            lax.broadcasted_iota(jnp.int32, (span, in_width), 0) % in_width
-            == lax.broadcasted_iota(jnp.int32, (span, in_width), 1)
-        ).astype(BF16)
-        down = (
-            lax.broadcasted_iota(jnp.int32, (in_width, span), 1) % in_width
-            == lax.broadcasted_iota(jnp.int32, (in_width, span), 0)
-        ).astype(BF16)
+                spread = jnp.dot(part, pick_cols, preferred_element_type=F32)
+                tall = jnp.broadcast_to(spread[:, None, :], (half // QBLK, QBLK, half)).reshape(half, half)
+                left_ref[start : start + half, t * half : (t + 1) * half] = jnp.where(same, tall, 0.0).astype(BF16)
+    up = (
+        lax.broadcasted_iota(jnp.int32, (span, in_width), 0) % in_width
+        == lax.broadcasted_iota(jnp.int32, (span, in_width), 1)
+    ).astype(BF16)
+    down = (
+        lax.broadcasted_iota(jnp.int32, (in_width, span), 1) % in_width
+        == lax.broadcasted_iota(jnp.int32, (in_width, span), 0)
+    ).astype(BF16)
+    block = (lax.broadcasted_iota(jnp.int32, (span, span), 0) // in_width) == (
+        lax.broadcasted_iota(jnp.int32, (span, span), 1) // in_width
+    )
+    for h in range(2):
         wide = jnp.dot(
             jnp.dot(up, ins[h], preferred_element_type=F32).astype(BF16), down, preferred_element_type=F32
         )
-        block = (lax.broadcasted_iota(jnp.int32, (span, span), 0) // in_width) == (
-            lax.broadcasted_iota(jnp.int32, (span, span), 1) // in_width
-        )
-        right_ref[h] = jnp.where(block, wide, 0.0).astype(BF16)
+        wide = jnp.where(block, wide, 0.0).astype(BF16)
+        right_ref[h * span : (h + 1) * span] = wide
+        if h == 0:
+            right_ref[2 * span :] = wide
 
 
 def prepare(pair_ref, left_ref, right_ref, prep_ref):
@@ -114,17 +119,13 @@
         turned = jnp.concatenate([tall[:, half:], tall[:, :half]], axis=1)
         stacked.append(jnp.concatenate([tall, turned], axis=0))
     stacked = jnp.concatenate(stacked, axis=1)
-    parts = [
-        jnp.dot(left_ref[0, s], stacked, preferred_element_type=F32)
-        + jnp.dot(left_ref[1, s], stacked, preferred_element_type=F32)
-        for s in range(2)
-    ]
+    tall = jnp.dot(left_ref[...], stacked, preferred_element_type=F32)
+    quarter = tall.shape[0] // 4
+    parts = [tall[s * quarter : (s + 1) * quarter] + tall[(2 + s) * quarter : (3 + s) * quarter] for s in range(2)]
     lane = lax.broadcasted_iota(jnp.int32, parts[0].shape, 1) % LANES
     high, low = split_bf16(jnp.where(lane < half, parts[0], parts[1]))
-    done = (
-        jnp.dot(high, right_ref[0], preferred_element_type=F32)
-        + jnp.dot(low, right_ref[0], preferred_element_type=F32)
-        + jnp.dot(high, right_ref[1], preferred_element_type=F32)
+    done = jnp.dot(
+        jnp.concatenate([high, high, low], axis=1), right_ref[...], preferred_element_type=F32
     ).astype(BF16)
     for side in range(2):
         for c in range(chunks):
@@ -236,10 +237,10 @@
     span = 2 * LANES
     out_factor, in_factor, far_pick = lax.optimization_barrier((out_factor, in_factor, picked[order[-1]]))
     left, right, far = pl.pallas_call(
-        functools.partial(first_kernel, rows, out_factor.shape[0]),
+        functools.partial(first_kernel, rows, out_precond.shape[-1]),
         out_shape=[
-            jax.ShapeDtypeStruct((2, 2, stack, 2 * stack), BF16),
-            jax.ShapeDtypeStruct((2, span, span), BF16),
+            jax.ShapeDtypeStruct((4 * stack, 2 * stack), BF16),
+            jax.ShapeDtypeStruct((3 * span, span), BF16),
             jax.ShapeDtypeStruct((2, QBLK, features), BF16),
         ],
         in_specs=[VMEM] * 2,

time: 31 us -> 30.8 us (level)
  Pallas kernels: 13.2 us -> 12.7 us
  waiting for transfers between devices: 3.28 us -> 3.67 us
    pallas_call x1, Pallas kernels: 3.57 us -> 3.16 us  [shards(): pl.pallas_call(functools.partial(first_kernel, rows, out_precond.shape[-1...]
    ppermute x3, waiting for transfers between devices: 0.8 us -> 1.19 us  [pass_on(): lax.ppermute(array, 'ex', [(2 * a + c, 2 * b + c) for a, b in moves for c...]
    unnamed x8 -> x6, local copies, waits for them, and re-layouts: 1.71 us -> 1.7 us
  transfers between devices with their start and end apart: 7 -> 7, of which waited for: 4 -> 4; matrix products, arithmetic and copies ran while one was open for 3% -> 3% of each run, Pallas kernels for 32% -> 31%
where the time goes in v8:
time: 30.8 us; the launch traced here: 30.6 us
  Pallas kernels  12.7 us (41%)
  starting transfers between devices  11.6 us (38%)
  waiting for transfers between devices  3.67 us (12%)
  local copies, waits for them, and re-layouts  1.7 us (6%)
  other arithmetic  0.78 us (3%)
    ppermute x3, starting transfers between devices, pass_on(): lax.ppermute(array, 'ex', [(2 * a + c, 2 * b + c) for a, b in moves for c...  5.59 us
    pallas_call x3, Pallas kernels, shards(): pl.pallas_call(functools.partial(near_kernel, done), out_shape=jax.ShapeD...  5.57 us
    ppermute x3, starting transfers between devices, shards(): lax.ppermute(parts[m], 'layer', [(i, (i + m) % layer) for i in range(laye...  5.57 us
    pallas_call x1, Pallas kernels, shards(): pl.pallas_call(functools.partial(first_kernel, rows, out_precond.shape[-1...  3.16 us
    ppermute x3, waiting for transfers between devices, shards(): lax.ppermute(parts[m], 'layer', [(i, (i + m) % layer) for i in range(laye...  2.48 us
    pallas_call x1, Pallas kernels, shards(): pl.pallas_call(functools.partial(last_kernel, order, layer, held, slots),...  2.13 us
    unnamed x6, local copies, waits for them, and re-layouts  1.7 us
    ppermute x3, waiting for transfers between devices, pass_on(): lax.ppermute(array, 'ex', [(2 * a + c, 2 * b + c) for a, b in moves for c...  1.19 us
  transfers between devices with their start and end apart: 7, of which 4 were waited for; matrix products, arithmetic and copies ran while one was open for 3% of the time, Pallas kernels for 31%

profile of v8, /device:TPU:0, one launch (start us, length us, event | category | flops | bytes accessed | tf_op | source)
XLA Modules:
  0.0 30.6 jit_solution(8783590127719495993)
XLA Ops:
  0.0 0.5 %collective-permute-start = (bf16[64,4096]{1,0:T(8,128)(2,1)}, bf16[64,4096]{1,0:T(8,128)(2,1)S(1)}, u32[]{:S(2)}, u32[]{:S(2)}) collective-permute-start(bf16[64,4096]{1,0:T(8,128)(2,1)} %bitcast.6), channel_id=1, source_target_pairs={{0,1},{1,0},{2,3},{3,2},{4,5},{5,4},{6,7},{7,6},{8,9},{9,8},{10,11... | collective-permute-start | bytes 1572872 | tf_op jit(solution)/shard_map/ppermute | solution.py:215
  0.5 0.0 copy-start.1
  0.5 1.0 %copy-done.1 = bf16[64,1,4096]{2,0,1:T(8,128)(2,1)S(1)} copy-done((bf16[64,1,4096]{2,0,1:T(8,128)(2,1)S(1)}, bf16[64,1,4096]{2,0,1:T(8,128)(2,1)}, u32[]{:S(2)}) %copy-start.1) | copy-done | bytes 524312
  1.5 0.0 copy-start.2
  1.5 0.7 %copy-done.2 = s32[48]{0:T(128)S(1)} copy-done((s32[48]{0:T(128)S(1)}, s32[48]{0:T(128)}, u32[]{:S(2)}) %copy-start.2) | copy-done | bytes 216
  2.2 0.6 %own.1 = (bf16[16,4096]{1,0:T(8,128)(2,1)S(1)}, bf16[16,4096]{1,0:T(8,128)(2,1)S(1)}, bf16[16,4096]{1,0:T(8,128)(2,1)S(1)}, bf16[16,4096]{1,0:T(8,128)(2,1)S(1)}) custom-call(s32[48]{0:T(128)S(1)} %copy-done.2, bf16[64,4096]{1,0:T(8,128)(2,1)S(1)} %bitcast.7), custom_call_target="tpu_custom_call" | custom-call | tf_op jit(solution)/shard_map/own/pallas_call | solution.py:216
  2.8 0.0 collective-permute-done.other_ref
  2.8 0.6 %pick.1 = (bf16[32,4096]{1,0:T(8,128)(2,1)S(1)}, bf16[32,4096]{1,0:T(8,128)(2,1)S(1)}, bf16[32,4096]{1,0:T(8,128)(2,1)S(1)}, bf16[32,4096]{1,0:T(8,128)(2,1)S(1)}) custom-call(s32[48]{0:T(128)S(1)} %copy-done.2, bf16[64,4096]{1,0:T(8,128)(2,1)S(1)} %collective-permute-done.other_ref, bf16[16,4096]{1,0:T(8,128)(2,1)S(1)} %get-tuple-element.23.refs_0_, ...), custom_call_target="tpu_custom_call" | custom-call | tf_op jit(solution)/shard_map/pick/pallas_call | solution.py:224
  3.4 2.5 %collective-permute-start.2 = (bf16[32,4096]{1,0:T(8,128)(2,1)S(1)}, bf16[32,4096]{1,0:T(8,128)(2,1)S(1)}, u32[]{:S(2)}, u32[]{:S(2)}) collective-permute-start(bf16[32,4096]{1,0:T(8,128)(2,1)S(1)} %get-tuple-element.35), channel_id=1, source_target_pairs={{0,2},{1,3},{2,6},{3,7},{6,4},{7,5},{4,0},{5,1},{8,10},{9,11},{10,... | collective-permute-start | bytes 786440 | tf_op jit(solution)/shard_map/ppermute | solution.py:211
  6.0 0.1 collective-permute-start.3
  6.1 0.8 %pad_maximum_fusion.factors_ref = f32[128,64]{1,0:T(8,128)S(1)} fusion(f32[64,64]{1,0:T(8,128)} %bitcast.8, f32[64,64]{1,0:T(8,128)} %bitcast.9), kind=kLoop, calls=%fused_computation | loop fusion | flops 8192 | bytes 65536 | tf_op jit(solution)/shard_map/concatenate | solution.py:250
  6.8 3.2 %first.1 = (bf16[2048,1024]{1,0:T(8,128)(2,1)S(1)}, bf16[768,256]{1,0:T(8,128)(2,1)S(1)}, bf16[2,16,4096]{2,1,0:T(8,128)(2,1)S(1)}) custom-call(f32[128,64]{1,0:T(8,128)S(1)} %pad_maximum_fusion.factors_ref, bf16[32,4096]{1,0:T(8,128)(2,1)S(1)} %get-tuple-element.30.pair_ref), custom_call_target="tpu_custom_call" | custom-call | tf_op jit(solution)/shard_map/first/pallas_call | solution.py:239
  10.0 3.0 %collective-permute-start.1 = (bf16[2,16,4096]{2,1,0:T(8,128)(2,1)S(1)}, bf16[2,16,4096]{2,1,0:T(8,128)(2,1)S(1)}, u32[]{:S(2)}, u32[]{:S(2)}) collective-permute-start(bf16[2,16,4096]{2,1,0:T(8,128)(2,1)S(1)} %get-tuple-element.31), channel_id=1, source_target_pairs={{0,6},{1,7},{2,4},{3,5},{6,0},{7,1},{4,2},{5,3},{8,14},{9,15},{10,... | collective-permute-start | bytes 786440 | tf_op jit(solution)/shard_map/ppermute | solution.py:211
  13.0 1.9 %near0.1.refs_0_ = bf16[2,16,4096]{2,1,0:T(8,128)(2,1)S(1)} custom-call(bf16[2048,1024]{1,0:T(8,128)(2,1)S(1)} %get-tuple-element.32.left_ref, bf16[768,256]{1,0:T(8,128)(2,1)S(1)} %get-tuple-element.33.right_ref, bf16[32,4096]{1,0:T(8,128)(2,1)S(1)} %get-tuple-element.34.refs_0_), custom_call_target="tpu_custom_call" | custom-call | tf_op jit(solution)/shard_map/near0/pallas_call | solution.py:257
  14.8 0.0 collective-permute-done.2.refs_1_
  14.8 1.9 %near1.1.refs_0_ = bf16[4,16,4096]{2,1,0:T(8,128)(2,1)S(1)} custom-call(bf16[2048,1024]{1,0:T(8,128)(2,1)S(1)} %get-tuple-element.32.left_ref, bf16[768,256]{1,0:T(8,128)(2,1)S(1)} %get-tuple-element.33.right_ref, bf16[2,16,4096]{2,1,0:T(8,128)(2,1)S(1)} %near0.1.refs_0_, bf16[32,4096]{1,0:T(8,128)(2,1)S(1)} %collective-permute-done.2.refs_1_), custom_call_target="tpu_custom_call" | custom-call | tf_op jit(solution)/shard_map/near1/pallas_call | solution.py:257
  16.7 0.0 copy-start
  16.7 0.0 collective-permute-done.3.refs_1_
  16.7 1.9 %near2.1.early_ref = bf16[6,16,4096]{2,1,0:T(8,128)(2,1)S(1)} custom-call(bf16[2048,1024]{1,0:T(8,128)(2,1)S(1)} %get-tuple-element.32.left_ref, bf16[768,256]{1,0:T(8,128)(2,1)S(1)} %get-tuple-element.33.right_ref, bf16[4,16,4096]{2,1,0:T(8,128)(2,1)S(1)} %near1.1.refs_0_, bf16[32,4096]{1,0:T(8,128)(2,1)S(1)} %collective-permute-done.3.refs_1_), custom_call_target="tpu_custom_call" | custom-call | tf_op jit(solution)/shard_map/near2/pallas_call | solution.py:257
  18.6 1.2 %collective-permute-done.1.late_ref = bf16[2,16,4096]{2,1,0:T(8,128)(2,1)S(1)} collective-permute-done((bf16[2,16,4096]{2,1,0:T(8,128)(2,1)S(1)}, bf16[2,16,4096]{2,1,0:T(8,128)(2,1)S(1)}, u32[]{:S(2)}, u32[]{:S(2)}) %collective-permute-start.1) | collective-permute-done | bytes 262176 | tf_op jit(solution)/shard_map/ppermute | solution.py:211
  19.8 0.0 copy-done
  19.8 2.1 %last.1 = (f32[24,512]{1,0:T(8,128)S(1)}, bf16[24,512]{1,0:T(8,128)(2,1)S(1)}, bf16[24,512]{1,0:T(8,128)(2,1)S(1)}, bf16[24,512]{1,0:T(8,128)(2,1)S(1)}) custom-call(s32[48]{0:T(128)S(1)} %copy-done.2, bf16[2,16,4096]{2,1,0:T(8,128)(2,1)S(1)} %collective-permute-done.1.late_ref, bf16[6,16,4096]{2,1,0:T(8,128)(2,1)S(1)} %near2.1.early_ref, ...), custom_call_target="tpu_custom_call" | custom-call | tf_op jit(solution)/shard_map/last/pallas_call | solution.py:267
  21.9 1.6 %collective-permute-start.4 = (bf16[24,512]{1,0:T(8,128)(2,1)S(1)}, bf16[24,512]{1,0:T(8,128)(2,1)S(1)}, u32[]{:S(2)}, u32[]{:S(2)}) collective-permute-start(bf16[24,512]{1,0:T(8,128)(2,1)S(1)} %get-tuple-element.38), channel_id=1, source_target_pairs={{0,8},{8,16},{16,24},{24,0},{1,9},{9,17},{17,25},{25,1},{2,10},{10... | collective-permute-start | bytes 73736 | tf_op jit(solution)/shard_map/ppermute | solution.py:279
  23.5 2.6 %collective-permute-start.5 = (bf16[24,512]{1,0:T(8,128)(2,1)S(1)}, bf16[24,512]{1,0:T(8,128)(2,1)S(1)}, u32[]{:S(2)}, u32[]{:S(2)}) collective-permute-start(bf16[24,512]{1,0:T(8,128)(2,1)S(1)} %get-tuple-element.39), channel_id=1, source_target_pairs={{0,16},{8,24},{16,0},{24,8},{1,17},{9,25},{17,1},{25,9},{2,18},{10... | collective-permute-start | bytes 73736 | tf_op jit(solution)/shard_map/ppermute | solution.py:279
  26.1 1.4 %collective-permute-start.6 = (bf16[24,512]{1,0:T(8,128)(2,1)S(1)}, bf16[24,512]{1,0:T(8,128)(2,1)S(1)}, u32[]{:S(2)}, u32[]{:S(2)}) collective-permute-start(bf16[24,512]{1,0:T(8,128)(2,1)S(1)} %get-tuple-element.40), channel_id=1, source_target_pairs={{0,24},{8,0},{16,8},{24,16},{1,25},{9,1},{17,9},{25,17},{2,26},{10... | collective-permute-start | bytes 73736 | tf_op jit(solution)/shard_map/ppermute | solution.py:279
  27.5 0.4 %collective-permute-done.4.refs_1_ = bf16[24,512]{1,0:T(8,128)(2,1)S(1)} collective-permute-done((bf16[24,512]{1,0:T(8,128)(2,1)S(1)}, bf16[24,512]{1,0:T(8,128)(2,1)S(1)}, u32[]{:S(2)}, u32[]{:S(2)}) %collective-permute-start.4) | collective-permute-done | bytes 24608 | tf_op jit(solution)/shard_map/ppermute | solution.py:279
  27.8 0.4 %collective-permute-done.5.refs_2_ = bf16[24,512]{1,0:T(8,128)(2,1)S(1)} collective-permute-done((bf16[24,512]{1,0:T(8,128)(2,1)S(1)}, bf16[24,512]{1,0:T(8,128)(2,1)S(1)}, u32[]{:S(2)}, u32[]{:S(2)}) %collective-permute-start.5) | collective-permute-done | bytes 24608 | tf_op jit(solution)/shard_map/ppermute | solution.py:279
  28.3 1.7 %collective-permute-done.6.refs_3_ = bf16[24,512]{1,0:T(8,128)(2,1)S(1)} collective-permute-done((bf16[24,512]{1,0:T(8,128)(2,1)S(1)}, bf16[24,512]{1,0:T(8,128)(2,1)S(1)}, u32[]{:S(2)}, u32[]{:S(2)}) %collective-permute-start.6) | collective-permute-done | bytes 24608 | tf_op jit(solution)/shard_map/ppermute | solution.py:279
  30.0 0.6 %finish.1 = f32[6,4,512]{2,1,0:T(4,128)} custom-call(f32[24,512]{1,0:T(8,128)S(1)} %get-tuple-element.37.refs_0_, bf16[24,512]{1,0:T(8,128)(2,1)S(1)} %collective-permute-done.4.refs_1_, bf16[24,512]{1,0:T(8,128)(2,1)S(1)} %collective-permute-done.5.refs_2_, bf16[24,512]{1,0:T(8,128)(2,1)S(1)} %collective-permute-done.6.refs_3_), custom_call_target="tpu_custom_call" | custom-call | tf_op jit(solution)/shard_map/finish/pallas_call | solution.py:281
Async XLA Ops:
  0.0 2.8 %collective-permute-start = (bf16[64,4096]{1,0:T(8,128)(2,1)}, bf16[64,4096]{1,0:T(8,128)(2,1)S(1)}, u32[]{:S(2)}, u32[]{:S(2)}) collective-permute-start(bf16[64,4096]{1,0:T(8,128)(2,1)} %bitcast.6), channel_id=1, source_target_pairs={{0,1},{1,0},{2,3},{3,2},{4,5},{5,4},{6,7},{7,6},{8,9},{9,8},{10,11... | collective-permute-start | bytes 1572872 | tf_op jit(solution)/shard_map/ppermute | solution.py:215
  0.5 1.0 %copy-start.1 = (bf16[64,1,4096]{2,0,1:T(8,128)(2,1)S(1)}, bf16[64,1,4096]{2,0,1:T(8,128)(2,1)}, u32[]{:S(2)}) copy-start(bf16[64,1,4096]{2,0,1:T(8,128)(2,1)} %param.6) | copy-start | bytes 1572868
  1.5 0.7 %copy-start.2 = (s32[48]{0:T(128)S(1)}, s32[48]{0:T(128)}, u32[]{:S(2)}) copy-start(s32[48]{0:T(128)} %pairs_ref.5) | copy-start | bytes 580
  3.4 11.4 %collective-permute-start.2 = (bf16[32,4096]{1,0:T(8,128)(2,1)S(1)}, bf16[32,4096]{1,0:T(8,128)(2,1)S(1)}, u32[]{:S(2)}, u32[]{:S(2)}) collective-permute-start(bf16[32,4096]{1,0:T(8,128)(2,1)S(1)} %get-tuple-element.35), channel_id=1, source_target_pairs={{0,2},{1,3},{2,6},{3,7},{6,4},{7,5},{4,0},{5,1},{8,10},{9,11},{10,... | collective-permute-start | bytes 786440 | tf_op jit(solution)/shard_map/ppermute | solution.py:211
  6.0 10.7 %collective-permute-start.3 = (bf16[32,4096]{1,0:T(8,128)(2,1)S(1)}, bf16[32,4096]{1,0:T(8,128)(2,1)S(1)}, u32[]{:S(2)}, u32[]{:S(2)}) collective-permute-start(bf16[32,4096]{1,0:T(8,128)(2,1)S(1)} %get-tuple-element.36), channel_id=1, source_target_pairs={{0,4},{1,5},{2,0},{3,1},{6,2},{7,3},{4,6},{5,7},{8,12},{9,13},{10,... | collective-permute-start | bytes 786440 | tf_op jit(solution)/shard_map/ppermute | solution.py:211
  10.0 9.8 %collective-permute-start.1 = (bf16[2,16,4096]{2,1,0:T(8,128)(2,1)S(1)}, bf16[2,16,4096]{2,1,0:T(8,128)(2,1)S(1)}, u32[]{:S(2)}, u32[]{:S(2)}) collective-permute-start(bf16[2,16,4096]{2,1,0:T(8,128)(2,1)S(1)} %get-tuple-element.31), channel_id=1, source_target_pairs={{0,6},{1,7},{2,4},{3,5},{6,0},{7,1},{4,2},{5,3},{8,14},{9,15},{10,... | collective-permute-start | bytes 786440 | tf_op jit(solution)/shard_map/ppermute | solution.py:211
  16.7 3.1 %copy-start = (bf16[512,1,4096]{2,0,1:T(8,128)(2,1)S(1)}, bf16[512,1,4096]{2,0,1:T(8,128)(2,1)}, u32[]{:S(2)}) copy-start(bf16[512,1,4096]{2,0,1:T(8,128)(2,1)} %param.5) | copy-start | bytes 12582916
  21.9 5.9 %collective-permute-start.4 = (bf16[24,512]{1,0:T(8,128)(2,1)S(1)}, bf16[24,512]{1,0:T(8,128)(2,1)S(1)}, u32[]{:S(2)}, u32[]{:S(2)}) collective-permute-start(bf16[24,512]{1,0:T(8,128)(2,1)S(1)} %get-tuple-element.38), channel_id=1, source_target_pairs={{0,8},{8,16},{16,24},{24,0},{1,9},{9,17},{17,25},{25,1},{2,10},{10... | collective-permute-start | bytes 73736 | tf_op jit(solution)/shard_map/ppermute | solution.py:279
  23.5 4.7 %collective-permute-start.5 = (bf16[24,512]{1,0:T(8,128)(2,1)S(1)}, bf16[24,512]{1,0:T(8,128)(2,1)S(1)}, u32[]{:S(2)}, u32[]{:S(2)}) collective-permute-start(bf16[24,512]{1,0:T(8,128)(2,1)S(1)} %get-tuple-element.39), channel_id=1, source_target_pairs={{0,16},{8,24},{16,0},{24,8},{1,17},{9,25},{17,1},{25,9},{2,18},{10... | collective-permute-start | bytes 73736 | tf_op jit(solution)/shard_map/ppermute | solution.py:279
  26.1 3.8 %collective-permute-start.6 = (bf16[24,512]{1,0:T(8,128)(2,1)S(1)}, bf16[24,512]{1,0:T(8,128)(2,1)S(1)}, u32[]{:S(2)}, u32[]{:S(2)}) collective-permute-start(bf16[24,512]{1,0:T(8,128)(2,1)S(1)} %get-tuple-element.40), channel_id=1, source_target_pairs={{0,24},{8,0},{16,8},{24,16},{1,25},{9,1},{17,9},{25,17},{2,26},{10... | collective-permute-start | bytes 73736 | tf_op jit(solution)/shard_map/ppermute | solution.py:279

commit v9 on v8

--- a/solution.py
+++ b/solution.py
@@ -68,7 +68,7 @@
 
 def make_factors(rows, width, factors_ref, left_ref, right_ref):
     in_width = factors_ref.shape[0] - width
-    half = left_ref.shape[1] // 2
+    half = left_ref.shape[0] // 2
     span = right_ref.shape[1]
     outs = split_bf16(factors_ref[:width])
     ins = split_bf16(factors_ref[width:])
@@ -82,12 +82,12 @@
         for s in range(2):
             pick_rows = (row * 2 + s == row_o).astype(BF16)
             part = jnp.dot(pick_rows, outs[h], preferred_element_type=F32).astype(BF16)
-            start = (2 * h + s) * half
             for t in range(2):
-                pick_cols = (col * 2 + (s ^ t) == col_o).astype(BF16)
+                pick_cols = (col * 2 + t == col_o).astype(BF16)
                 spread = jnp.dot(part, pick_cols, preferred_element_type=F32)
                 tall = jnp.broadcast_to(spread[:, None, :], (half // QBLK, QBLK, half)).reshape(half, half)
-                left_ref[start : start + half, t * half : (t + 1) * half] = jnp.where(same, tall, 0.0).astype(BF16)
+                start = (2 * h + t) * half
+                left_ref[s * half : (s + 1) * half, start : start + half] = jnp.where(same, tall, 0.0).astype(BF16)
     up = (
         lax.broadcasted_iota(jnp.int32, (span, in_width), 0) % in_width
         == lax.broadcasted_iota(jnp.int32, (span, in_width), 1)
@@ -109,42 +109,62 @@
             right_ref[2 * span :] = wide
 
 
-def prepare(pair_ref, left_ref, right_ref, prep_ref):
-    chunks = pair_ref.shape[1] // LANES
-    half = LANES // 2
+def swap_halves(x):
+    half = x.shape[1] // 2
+    return jnp.concatenate([x[:, half:], x[:, :half]], axis=1)
+
+
+def prepare(blocks, left_ref, right_ref, targets):
+    chunks = blocks[0].shape[1] // LANES
+    half = chunks * QBLK
+    lower = lax.broadcasted_iota(jnp.int32, (half, LANES), 1) < LANES // 2
+    talls = [
+        jnp.concatenate([block[:, c * LANES : (c + 1) * LANES] for c in range(chunks)], axis=0) for block in blocks
+    ]
     stacked = []
-    for side in range(2):
-        block = pair_ref[side * QBLK : (side + 1) * QBLK, :]
-        tall = jnp.concatenate([block[:, c * LANES : (c + 1) * LANES] for c in range(chunks)], axis=0)
-        turned = jnp.concatenate([tall[:, half:], tall[:, :half]], axis=1)
-        stacked.append(jnp.concatenate([tall, turned], axis=0))
+    for one, two in (talls[:2], talls[2:]):
+        stacked.append(
+            jnp.concatenate(
+                [jnp.where(lower, one, swap_halves(two)), jnp.where(lower, swap_halves(one), two)], axis=0
+            )
+        )
     stacked = jnp.concatenate(stacked, axis=1)
-    tall = jnp.dot(left_ref[...], stacked, preferred_element_type=F32)
-    quarter = tall.shape[0] // 4
-    parts = [tall[s * quarter : (s + 1) * quarter] + tall[(2 + s) * quarter : (3 + s) * quarter] for s in range(2)]
-    lane = lax.broadcasted_iota(jnp.int32, parts[0].shape, 1) % LANES
-    high, low = split_bf16(jnp.where(lane < half, parts[0], parts[1]))
+    high, low = split_bf16(
+        jnp.dot(left_ref[...], jnp.concatenate([stacked, stacked], axis=0), preferred_element_type=F32)
+    )
     done = jnp.dot(
         jnp.concatenate([high, high, low], axis=1), right_ref[...], preferred_element_type=F32
     ).astype(BF16)
-    for side in range(2):
-        for c in range(chunks):
-            prep_ref[side, :, c * LANES : (c + 1) * LANES] = done[
-                c * QBLK : (c + 1) * QBLK, side * LANES : (side + 1) * LANES
-            ]
-
-
-def first_kernel(rows, width, factors_ref, pair_ref, left_ref, right_ref, prep_ref):
+    for pair in range(2):
+        even = done[:half, pair * LANES : (pair + 1) * LANES]
+        odd = done[half:, pair * LANES : (pair + 1) * LANES]
+        for value, (ref, index) in zip(
+            (jnp.where(lower, even, swap_halves(odd)), jnp.where(lower, swap_halves(even), odd)),
+            targets[2 * pair : 2 * pair + 2],
+        ):
+            for c in range(chunks):
+                ref[index, :, c * LANES : (c + 1) * LANES] = value[c * QBLK : (c + 1) * QBLK]
+
+
+def halves(refs):
+    return [ref[side * QBLK : (side + 1) * QBLK] for ref in refs for side in range(2)]
+
+
+def first_kernel(rows, width, factors_ref, far_pair_ref, self_pair_ref, left_ref, right_ref, far_ref, self_ref):
     make_factors(rows, width, factors_ref, left_ref, right_ref)
-    prepare(pair_ref, left_ref, right_ref, prep_ref)
-
-
-def near_kernel(done, left_ref, right_ref, *refs):
+    targets = [(far_ref, 0), (far_ref, 1), (self_ref, 0), (self_ref, 1)]
+    prepare(halves((far_pair_ref, self_pair_ref)), left_ref, right_ref, targets)
+
+
+def near_kernel(left_ref, right_ref, self_ref, *refs):
     prep_ref = refs[-1]
-    if done:
-        prep_ref[:done] = refs[0][...]
-    for index, pair_ref in enumerate(refs[min(done, 1) : -1]):
-        prepare(pair_ref, left_ref, right_ref, prep_ref.at[pl.ds(done + 2 * index, 2)])
+    prep_ref[:2] = self_ref[...]
+    blocks = halves(refs[:-1])
+    targets = [(prep_ref, 2 + index) for index in range(len(blocks))]
+    for start in range(0, len(blocks), 4):
+        pick = slice(start, start + 4) if start + 4 <= len(blocks) else slice(-2, None)
+        times = 1 if start + 4 <= len(blocks) else 2
+        prepare(blocks[pick] * times, left_ref, right_ref, targets[pick] * times)
 
 
 def last_kernel(order, layer, held, slots, pairs_ref, late_ref, early_ref, train_ref, *refs):
@@ -236,34 +256,29 @@
     stack = features // LANES * QBLK
     span = 2 * LANES
     out_factor, in_factor, far_pick = lax.optimization_barrier((out_factor, in_factor, picked[order[-1]]))
-    left, right, far = pl.pallas_call(
+    left, right, far, self_pair = pl.pallas_call(
         functools.partial(first_kernel, rows, out_precond.shape[-1]),
         out_shape=[
-            jax.ShapeDtypeStruct((4 * stack, 2 * stack), BF16),
+            jax.ShapeDtypeStruct((2 * stack, 4 * stack), BF16),
             jax.ShapeDtypeStruct((3 * span, span), BF16),
             jax.ShapeDtypeStruct((2, QBLK, features), BF16),
+            jax.ShapeDtypeStruct((2, QBLK, features), BF16),
         ],
-        in_specs=[VMEM] * 2,
-        out_specs=[VMEM] * 3,
+        in_specs=[VMEM] * 3,
+        out_specs=[VMEM] * 4,
         compiler_params=limit,
         name="first",
-    )(jnp.concatenate([out_factor, in_factor], axis=0), far_pick)
+    )(jnp.concatenate([out_factor, in_factor], axis=0), far_pick, picked[0])
     far = pass_on(far, order[-1])
 
-    early, done = [], 0
-    half = len(raw) // 2
-    for index, pairs in enumerate(([picked[0]], raw[:half], raw[half:])):
-        early = [
-            pl.pallas_call(
-                functools.partial(near_kernel, done),
-                out_shape=jax.ShapeDtypeStruct((done + 2 * len(pairs), QBLK, features), BF16),
-                in_specs=[VMEM] * (2 + len(early) + len(pairs)),
-                out_specs=VMEM,
-                compiler_params=limit,
-                name=f"near{index}",
-            )(left, right, *early, *pairs)
-        ]
-        done += 2 * len(pairs)
+    early = pl.pallas_call(
+        near_kernel,
+        out_shape=jax.ShapeDtypeStruct((ex - 2, QBLK, features), BF16),
+        in_specs=[VMEM] * (3 + len(raw)),
+        out_specs=VMEM,
+        compiler_params=limit,
+        name="near",
+    )(left, right, self_pair, *raw)
     parts = pl.pallas_call(
         functools.partial(last_kernel, order, layer, held, slots),
         out_shape=[jax.ShapeDtypeStruct((slots * rows, train_rows), F32)]
@@ -273,7 +288,7 @@
         scratch_shapes=[pltpu.VMEM((slots * QBLK, features), BF16)],
         compiler_params=limit,
         name="last",
-    )(pair_blocks, far, *early, train)
+    )(pair_blocks, far, early, train)
 
     terms = [parts[0]] + [
         lax.ppermute(parts[m], "layer", [(i, (i + m) % layer) for i in range(layer)]) for m in range(1, layer)

time: 30.8 us -> 31.5 us (1.023)
  waiting for transfers between devices: 3.67 us -> 6.43 us
  Pallas kernels: 12.7 us -> 10.2 us
    pallas_call x3 -> x1, Pallas kernels: 5.57 us -> 2.45 us  [shards(): pl.pallas_call(near_kernel, out_shape=jax.ShapeDtypeStruct((ex - 2, QBLK,...]
    ppermute x3, waiting for transfers between devices: 1.19 us -> 3.95 us  [pass_on(): lax.ppermute(array, 'ex', [(2 * a + c, 2 * b + c) for a, b in moves for c...]
    pallas_call x1, Pallas kernels: 3.16 us -> 3.75 us  [shards(): pl.pallas_call(functools.partial(first_kernel, rows, out_precond.shape[-1...]
  transfers between devices with their start and end apart: 7 -> 7, of which waited for: 4 -> 5; matrix products, arithmetic and copies ran while one was open for 3% -> 2% of each run, Pallas kernels for 31% -> 22%
where the time goes in v9:
time: 31.5 us; the launch traced here: 31.3 us
  starting transfers between devices  11.9 us (38%)
  Pallas kernels  10.2 us (32%)
  waiting for transfers between devices  6.43 us (20%)
  local copies, waits for them, and re-layouts  1.93 us (6%)
  other arithmetic  0.78 us (2%)
    ppermute x3, starting transfers between devices, pass_on(): lax.ppermute(array, 'ex', [(2 * a + c, 2 * b + c) for a, b in moves for c...  5.73 us
    ppermute x3, starting transfers between devices, shards(): lax.ppermute(parts[m], 'layer', [(i, (i + m) % layer) for i in range(laye...  5.73 us
    ppermute x3, waiting for transfers between devices, pass_on(): lax.ppermute(array, 'ex', [(2 * a + c, 2 * b + c) for a, b in moves for c...  3.95 us
    pallas_call x1, Pallas kernels, shards(): pl.pallas_call(functools.partial(first_kernel, rows, out_precond.shape[-1...  3.75 us
    ppermute x3, waiting for transfers between devices, shards(): lax.ppermute(parts[m], 'layer', [(i, (i + m) % layer) for i in range(laye...  2.48 us
    pallas_call x1, Pallas kernels, shards(): pl.pallas_call(near_kernel, out_shape=jax.ShapeDtypeStruct((ex - 2, QBLK,...  2.45 us
    pallas_call x1, Pallas kernels, shards(): pl.pallas_call(functools.partial(last_kernel, order, layer, held, slots),...  2.13 us
    unnamed x6, local copies, waits for them, and re-layouts  1.93 us
  transfers between devices with their start and end apart: 7, of which 5 were waited for; matrix products, arithmetic and copies ran while one was open for 2% of the time, Pallas kernels for 22%

profile of v9, /device:TPU:0, one launch (start us, length us, event | category | flops | bytes accessed | tf_op | source)
XLA Modules:
  0.0 31.3 jit_solution(8494833066370202206)
XLA Ops:
  0.0 0.0 copy-start
  0.0 0.5 %collective-permute-start = (bf16[64,4096]{1,0:T(8,128)(2,1)}, bf16[64,4096]{1,0:T(8,128)(2,1)S(1)}, u32[]{:S(2)}, u32[]{:S(2)}) collective-permute-start(bf16[64,4096]{1,0:T(8,128)(2,1)} %bitcast.6), channel_id=1, source_target_pairs={{0,1},{1,0},{2,3},{3,2},{4,5},{5,4},{6,7},{7,6},{8,9},{9,8},{10,11... | collective-permute-start | bytes 1572872 | tf_op jit(solution)/shard_map/ppermute | solution.py:235
  0.5 0.0 copy-start.1
  0.5 1.3 %copy-done.1 = bf16[64,1,4096]{2,0,1:T(8,128)(2,1)S(1)} copy-done((bf16[64,1,4096]{2,0,1:T(8,128)(2,1)S(1)}, bf16[64,1,4096]{2,0,1:T(8,128)(2,1)}, u32[]{:S(2)}) %copy-start.1) | copy-done | bytes 524312
  1.7 0.0 copy-start.2
  1.7 0.7 %copy-done.2 = s32[48]{0:T(128)S(1)} copy-done((s32[48]{0:T(128)S(1)}, s32[48]{0:T(128)}, u32[]{:S(2)}) %copy-start.2) | copy-done | bytes 216
  2.4 0.6 %own.1 = (bf16[16,4096]{1,0:T(8,128)(2,1)S(1)}, bf16[16,4096]{1,0:T(8,128)(2,1)S(1)}, bf16[16,4096]{1,0:T(8,128)(2,1)S(1)}, bf16[16,4096]{1,0:T(8,128)(2,1)S(1)}) custom-call(s32[48]{0:T(128)S(1)} %copy-done.2, bf16[64,4096]{1,0:T(8,128)(2,1)S(1)} %bitcast.7), custom_call_target="tpu_custom_call" | custom-call | tf_op jit(solution)/shard_map/own/pallas_call | solution.py:236
  3.0 0.0 collective-permute-done.other_ref
  3.0 0.6 %pick.1 = (bf16[32,4096]{1,0:T(8,128)(2,1)S(1)}, bf16[32,4096]{1,0:T(8,128)(2,1)S(1)}, bf16[32,4096]{1,0:T(8,128)(2,1)S(1)}, bf16[32,4096]{1,0:T(8,128)(2,1)S(1)}) custom-call(s32[48]{0:T(128)S(1)} %copy-done.2, bf16[64,4096]{1,0:T(8,128)(2,1)S(1)} %collective-permute-done.other_ref, bf16[16,4096]{1,0:T(8,128)(2,1)S(1)} %get-tuple-element.24.refs_0_, ...), custom_call_target="tpu_custom_call" | custom-call | tf_op jit(solution)/shard_map/pick/pallas_call | solution.py:244
  3.6 2.7 %collective-permute-start.2 = (bf16[32,4096]{1,0:T(8,128)(2,1)S(1)}, bf16[32,4096]{1,0:T(8,128)(2,1)S(1)}, u32[]{:S(2)}, u32[]{:S(2)}) collective-permute-start(bf16[32,4096]{1,0:T(8,128)(2,1)S(1)} %get-tuple-element.37), channel_id=1, source_target_pairs={{0,2},{1,3},{2,6},{3,7},{6,4},{7,5},{4,0},{5,1},{8,10},{9,11},{10,... | collective-permute-start | bytes 786440 | tf_op jit(solution)/shard_map/ppermute | solution.py:231
  6.3 0.1 collective-permute-start.3
  6.4 0.8 %pad_maximum_fusion.factors_ref = f32[128,64]{1,0:T(8,128)S(1)} fusion(f32[64,64]{1,0:T(8,128)} %bitcast.8, f32[64,64]{1,0:T(8,128)} %bitcast.9), kind=kLoop, calls=%fused_computation | loop fusion | flops 8192 | bytes 65536 | tf_op jit(solution)/shard_map/concatenate | solution.py:271
  7.2 3.8 %first.1 = (bf16[1024,2048]{1,0:T(8,128)(2,1)S(1)}, bf16[768,256]{1,0:T(8,128)(2,1)S(1)}, bf16[2,16,4096]{2,1,0:T(8,128)(2,1)S(1)}, bf16[2,16,4096]{2,1,0:T(8,128)(2,1)S(1)}) custom-call(f32[128,64]{1,0:T(8,128)S(1)} %pad_maximum_fusion.factors_ref, bf16[32,4096]{1,0:T(8,128)(2,1)S(1)} %get-tuple-element.31.far_pair_ref, ...), custom_call_target="tpu_custom_call" | custom-call | tf_op jit(solution)/shard_map/first/pallas_call | solution.py:259
  11.0 3.0 %collective-permute-start.1 = (bf16[2,16,4096]{2,1,0:T(8,128)(2,1)S(1)}, bf16[2,16,4096]{2,1,0:T(8,128)(2,1)S(1)}, u32[]{:S(2)}, u32[]{:S(2)}) collective-permute-start(bf16[2,16,4096]{2,1,0:T(8,128)(2,1)S(1)} %get-tuple-element.33), channel_id=1, source_target_pairs={{0,6},{1,7},{2,4},{3,5},{6,0},{7,1},{4,2},{5,3},{8,14},{9,15},{10,... | collective-permute-start | bytes 786440 | tf_op jit(solution)/shard_map/ppermute | solution.py:231
  13.9 0.0 collective-permute-done.2.refs_0_
  13.9 0.8 %collective-permute-done.3.refs_1_ = bf16[32,4096]{1,0:T(8,128)(2,1)S(1)} collective-permute-done((bf16[32,4096]{1,0:T(8,128)(2,1)S(1)}, bf16[32,4096]{1,0:T(8,128)(2,1)S(1)}, u32[]{:S(2)}, u32[]{:S(2)}) %collective-permute-start.3) | collective-permute-done | bytes 262176 | tf_op jit(solution)/shard_map/ppermute | solution.py:231
  14.7 2.5 %near.1.early_ref = bf16[6,16,4096]{2,1,0:T(8,128)(2,1)S(1)} custom-call(bf16[1024,2048]{1,0:T(8,128)(2,1)S(1)} %get-tuple-element.34.left_ref, bf16[768,256]{1,0:T(8,128)(2,1)S(1)} %get-tuple-element.35.right_ref, bf16[2,16,4096]{2,1,0:T(8,128)(2,1)S(1)} %get-tuple-element.36.self_ref, bf16[32,4096]{1,0:T(8,128)(2,1)S(1)} %collective-permute-done.2.refs_0_, ...), custom_call_target="tpu_custom_call" | custom-call | tf_op jit(solution)/shard_map/near/pallas_call | solution.py:274
  17.2 3.1 %collective-permute-done.1.late_ref = bf16[2,16,4096]{2,1,0:T(8,128)(2,1)S(1)} collective-permute-done((bf16[2,16,4096]{2,1,0:T(8,128)(2,1)S(1)}, bf16[2,16,4096]{2,1,0:T(8,128)(2,1)S(1)}, u32[]{:S(2)}, u32[]{:S(2)}) %collective-permute-start.1) | collective-permute-done | bytes 262176 | tf_op jit(solution)/shard_map/ppermute | solution.py:231
  20.3 0.0 copy-done
  20.3 2.1 %last.1 = (f32[24,512]{1,0:T(8,128)S(1)}, bf16[24,512]{1,0:T(8,128)(2,1)S(1)}, bf16[24,512]{1,0:T(8,128)(2,1)S(1)}, bf16[24,512]{1,0:T(8,128)(2,1)S(1)}) custom-call(s32[48]{0:T(128)S(1)} %copy-done.2, bf16[2,16,4096]{2,1,0:T(8,128)(2,1)S(1)} %collective-permute-done.1.late_ref, bf16[6,16,4096]{2,1,0:T(8,128)(2,1)S(1)} %near.1.early_ref, ...), custom_call_target="tpu_custom_call" | custom-call | tf_op jit(solution)/shard_map/last/pallas_call | solution.py:282
  22.5 1.8 %collective-permute-start.4 = (bf16[24,512]{1,0:T(8,128)(2,1)S(1)}, bf16[24,512]{1,0:T(8,128)(2,1)S(1)}, u32[]{:S(2)}, u32[]{:S(2)}) collective-permute-start(bf16[24,512]{1,0:T(8,128)(2,1)S(1)} %get-tuple-element.40), channel_id=1, source_target_pairs={{0,8},{8,16},{16,24},{24,0},{1,9},{9,17},{17,25},{25,1},{2,10},{10... | collective-permute-start | bytes 73736 | tf_op jit(solution)/shard_map/ppermute | solution.py:294
  24.3 2.6 %collective-permute-start.5 = (bf16[24,512]{1,0:T(8,128)(2,1)S(1)}, bf16[24,512]{1,0:T(8,128)(2,1)S(1)}, u32[]{:S(2)}, u32[]{:S(2)}) collective-permute-start(bf16[24,512]{1,0:T(8,128)(2,1)S(1)} %get-tuple-element.41), channel_id=1, source_target_pairs={{0,16},{8,24},{16,0},{24,8},{1,17},{9,25},{17,1},{25,9},{2,18},{10... | collective-permute-start | bytes 73736 | tf_op jit(solution)/shard_map/ppermute | solution.py:294
  26.9 1.3 %collective-permute-start.6 = (bf16[24,512]{1,0:T(8,128)(2,1)S(1)}, bf16[24,512]{1,0:T(8,128)(2,1)S(1)}, u32[]{:S(2)}, u32[]{:S(2)}) collective-permute-start(bf16[24,512]{1,0:T(8,128)(2,1)S(1)} %get-tuple-element.42), channel_id=1, source_target_pairs={{0,24},{8,0},{16,8},{24,16},{1,25},{9,1},{17,9},{25,17},{2,26},{10... | collective-permute-start | bytes 73736 | tf_op jit(solution)/shard_map/ppermute | solution.py:294
  28.2 0.1 collective-permute-done.4.refs_1_
  28.3 0.7 %collective-permute-done.5.refs_2_ = bf16[24,512]{1,0:T(8,128)(2,1)S(1)} collective-permute-done((bf16[24,512]{1,0:T(8,128)(2,1)S(1)}, bf16[24,512]{1,0:T(8,128)(2,1)S(1)}, u32[]{:S(2)}, u32[]{:S(2)}) %collective-permute-start.5) | collective-permute-done | bytes 24608 | tf_op jit(solution)/shard_map/ppermute | solution.py:294
  29.0 1.7 %collective-permute-done.6.refs_3_ = bf16[24,512]{1,0:T(8,128)(2,1)S(1)} collective-permute-done((bf16[24,512]{1,0:T(8,128)(2,1)S(1)}, bf16[24,512]{1,0:T(8,128)(2,1)S(1)}, u32[]{:S(2)}, u32[]{:S(2)}) %collective-permute-start.6) | collective-permute-done | bytes 24608 | tf_op jit(solution)/shard_map/ppermute | solution.py:294
  30.7 0.6 %finish.1 = f32[6,4,512]{2,1,0:T(4,128)} custom-call(f32[24,512]{1,0:T(8,128)S(1)} %get-tuple-element.39.refs_0_, bf16[24,512]{1,0:T(8,128)(2,1)S(1)} %collective-permute-done.4.refs_1_, bf16[24,512]{1,0:T(8,128)(2,1)S(1)} %collective-permute-done.5.refs_2_, bf16[24,512]{1,0:T(8,128)(2,1)S(1)} %collective-permute-done.6.refs_3_), custom_call_target="tpu_custom_call" | custom-call | tf_op jit(solution)/shard_map/finish/pallas_call | solution.py:296
Async XLA Ops:
  0.0 20.3 %copy-start = (bf16[512,1,4096]{2,0,1:T(8,128)(2,1)S(1)}, bf16[512,1,4096]{2,0,1:T(8,128)(2,1)}, u32[]{:S(2)}) copy-start(bf16[512,1,4096]{2,0,1:T(8,128)(2,1)} %param.5) | copy-start | bytes 12582916
  0.0 3.0 %collective-permute-start = (bf16[64,4096]{1,0:T(8,128)(2,1)}, bf16[64,4096]{1,0:T(8,128)(2,1)S(1)}, u32[]{:S(2)}, u32[]{:S(2)}) collective-permute-start(bf16[64,4096]{1,0:T(8,128)(2,1)} %bitcast.6), channel_id=1, source_target_pairs={{0,1},{1,0},{2,3},{3,2},{4,5},{5,4},{6,7},{7,6},{8,9},{9,8},{10,11... | collective-permute-start | bytes 1572872 | tf_op jit(solution)/shard_map/ppermute | solution.py:235
  0.5 1.3 %copy-start.1 = (bf16[64,1,4096]{2,0,1:T(8,128)(2,1)S(1)}, bf16[64,1,4096]{2,0,1:T(8,128)(2,1)}, u32[]{:S(2)}) copy-start(bf16[64,1,4096]{2,0,1:T(8,128)(2,1)} %param.6) | copy-start | bytes 1572868
  1.7 0.7 %copy-start.2 = (s32[48]{0:T(128)S(1)}, s32[48]{0:T(128)}, u32[]{:S(2)}) copy-start(s32[48]{0:T(128)} %pairs_ref.5) | copy-start | bytes 580
  3.6 10.3 %collective-permute-start.2 = (bf16[32,4096]{1,0:T(8,128)(2,1)S(1)}, bf16[32,4096]{1,0:T(8,128)(2,1)S(1)}, u32[]{:S(2)}, u32[]{:S(2)}) collective-permute-start(bf16[32,4096]{1,0:T(8,128)(2,1)S(1)} %get-tuple-element.37), channel_id=1, source_target_pairs={{0,2},{1,3},{2,6},{3,7},{6,4},{7,5},{4,0},{5,1},{8,10},{9,11},{10,... | collective-permute-start | bytes 786440 | tf_op jit(solution)/shard_map/ppermute | solution.py:231
  6.3 8.4 %collective-permute-start.3 = (bf16[32,4096]{1,0:T(8,128)(2,1)S(1)}, bf16[32,4096]{1,0:T(8,128)(2,1)S(1)}, u32[]{:S(2)}, u32[]{:S(2)}) collective-permute-start(bf16[32,4096]{1,0:T(8,128)(2,1)S(1)} %get-tuple-element.38), channel_id=1, source_target_pairs={{0,4},{1,5},{2,0},{3,1},{6,2},{7,3},{4,6},{5,7},{8,12},{9,13},{10,... | collective-permute-start | bytes 786440 | tf_op jit(solution)/shard_map/ppermute | solution.py:231
  11.0 9.4 %collective-permute-start.1 = (bf16[2,16,4096]{2,1,0:T(8,128)(2,1)S(1)}, bf16[2,16,4096]{2,1,0:T(8,128)(2,1)S(1)}, u32[]{:S(2)}, u32[]{:S(2)}) collective-permute-start(bf16[2,16,4096]{2,1,0:T(8,128)(2,1)S(1)} %get-tuple-element.33), channel_id=1, source_target_pairs={{0,6},{1,7},{2,4},{3,5},{6,0},{7,1},{4,2},{5,3},{8,14},{9,15},{10,... | collective-permute-start | bytes 786440 | tf_op jit(solution)/shard_map/ppermute | solution.py:231
  22.5 5.8 %collective-permute-start.4 = (bf16[24,512]{1,0:T(8,128)(2,1)S(1)}, bf16[24,512]{1,0:T(8,128)(2,1)S(1)}, u32[]{:S(2)}, u32[]{:S(2)}) collective-permute-start(bf16[24,512]{1,0:T(8,128)(2,1)S(1)} %get-tuple-element.40), channel_id=1, source_target_pairs={{0,8},{8,16},{16,24},{24,0},{1,9},{9,17},{17,25},{25,1},{2,10},{10... | collective-permute-start | bytes 73736 | tf_op jit(solution)/shard_map/ppermute | solution.py:294
  24.3 4.7 %collective-permute-start.5 = (bf16[24,512]{1,0:T(8,128)(2,1)S(1)}, bf16[24,512]{1,0:T(8,128)(2,1)S(1)}, u32[]{:S(2)}, u32[]{:S(2)}) collective-permute-start(bf16[24,512]{1,0:T(8,128)(2,1)S(1)} %get-tuple-element.41), channel_id=1, source_target_pairs={{0,16},{8,24},{16,0},{24,8},{1,17},{9,25},{17,1},{25,9},{2,18},{10... | collective-permute-start | bytes 73736 | tf_op jit(solution)/shard_map/ppermute | solution.py:294
  26.9 3.8 %collective-permute-start.6 = (bf16[24,512]{1,0:T(8,128)(2,1)S(1)}, bf16[24,512]{1,0:T(8,128)(2,1)S(1)}, u32[]{:S(2)}, u32[]{:S(2)}) collective-permute-start(bf16[24,512]{1,0:T(8,128)(2,1)S(1)} %get-tuple-element.42), channel_id=1, source_target_pairs={{0,24},{8,0},{16,8},{24,16},{1,25},{9,1},{17,9},{25,17},{2,26},{10... | collective-permute-start | bytes 73736 | tf_op jit(solution)/shard_map/ppermute | solution.py:294

commit v10 on v8

--- a/solution.py
+++ b/solution.py
@@ -40,30 +40,29 @@
     return place
 
 
-def wanted_block(ex, held, slots, pairs_ref, step, side):
+def pick_kernel(ex, held, slots, order, pairs_ref, query_ref, self_ref, far_ref, swap_ref, *near_refs):
     me = lax.axis_index("ex")
     chips = ex // 2
-    target = ring_chip((ring_place(me >> 1, chips) + step) & (chips - 1))
-    first = (2 * target + (me & 1)) * slots
-    base = (me ^ side) * held
-
-    def body(slot, block):
-        local = pairs_ref[first + slot] - base
-        return jnp.where((local >= 0) & (local < held), local, block)
-
-    return pl.multiple_of(over_slots(slots, body, jnp.int32(0)) * QBLK, QBLK)
-
-
-def own_kernel(find, pairs_ref, query_ref, *outs):
-    for group, out_ref in enumerate(outs):
-        out_ref[...] = query_ref[pl.ds(find(pairs_ref, group, 0), QBLK), :]
-
-
-def pick_kernel(find, groups, pairs_ref, other_ref, *refs):
-    for group in range(groups):
-        out_ref = refs[groups + group]
-        out_ref[:QBLK] = refs[group][...]
-        out_ref[QBLK:] = other_ref[pl.ds(find(pairs_ref, group, 1), QBLK), :]
+    place = ring_place(me >> 1, chips)
+    targets = [self_ref, swap_ref.at[pl.ds(0, QBLK)]]
+    for ref in near_refs:
+        targets += [ref.at[pl.ds(0, QBLK)], ref.at[pl.ds(QBLK, QBLK)]]
+    targets += [far_ref, swap_ref.at[pl.ds(QBLK, QBLK)]]
+    for index, out_ref in enumerate(targets):
+        target = 2 * ring_chip((place + order[index // 2]) & (chips - 1)) + ((me & 1) ^ (index % 2))
+
+        def body(slot, block):
+            local = pairs_ref[target * slots + slot] - me * held
+            return jnp.where((local >= 0) & (local < held), local, block)
+
+        block = over_slots(slots, body, jnp.int32(0))
+        out_ref[...] = query_ref[pl.ds(pl.multiple_of(block * QBLK, QBLK), QBLK), :]
+
+
+def cross_kernel(*refs):
+    count = len(refs) // 2
+    for ref, out_ref in zip(refs[:count], refs[count:]):
+        out_ref[...] = ref[QBLK:]
 
 
 def make_factors(rows, width, factors_ref, left_ref, right_ref):
@@ -109,12 +108,11 @@
             right_ref[2 * span :] = wide
 
 
-def prepare(pair_ref, left_ref, right_ref, prep_ref):
-    chunks = pair_ref.shape[1] // LANES
+def prepare(blocks, left_ref, right_ref, prep_ref):
+    chunks = blocks[0].shape[1] // LANES
     half = LANES // 2
     stacked = []
-    for side in range(2):
-        block = pair_ref[side * QBLK : (side + 1) * QBLK, :]
+    for block in blocks:
         tall = jnp.concatenate([block[:, c * LANES : (c + 1) * LANES] for c in range(chunks)], axis=0)
         turned = jnp.concatenate([tall[:, half:], tall[:, :half]], axis=1)
         stacked.append(jnp.concatenate([tall, turned], axis=0))
@@ -134,17 +132,22 @@
             ]
 
 
-def first_kernel(rows, width, factors_ref, pair_ref, left_ref, right_ref, prep_ref):
+def first_kernel(rows, width, factors_ref, far_ref, swap_ref, left_ref, right_ref, prep_ref):
     make_factors(rows, width, factors_ref, left_ref, right_ref)
-    prepare(pair_ref, left_ref, right_ref, prep_ref)
-
-
-def near_kernel(done, left_ref, right_ref, *refs):
+    prepare((far_ref[...], swap_ref[QBLK:]), left_ref, right_ref, prep_ref)
+
+
+def self_kernel(left_ref, right_ref, self_ref, swap_ref, prep_ref):
+    prepare((self_ref[...], swap_ref[:QBLK]), left_ref, right_ref, prep_ref)
+
+
+def near_kernel(left_ref, right_ref, done_ref, *refs):
     prep_ref = refs[-1]
-    if done:
-        prep_ref[:done] = refs[0][...]
-    for index, pair_ref in enumerate(refs[min(done, 1) : -1]):
-        prepare(pair_ref, left_ref, right_ref, prep_ref.at[pl.ds(done + 2 * index, 2)])
+    done = done_ref.shape[0]
+    prep_ref[:done] = done_ref[...]
+    blocks = [ref[:QBLK] for ref in refs[:-1]]
+    for index in range(0, len(blocks), 2):
+        prepare(blocks[index : index + 2], left_ref, right_ref, prep_ref.at[pl.ds(done + index, 2)])
 
 
 def last_kernel(order, layer, held, slots, pairs_ref, late_ref, early_ref, train_ref, *refs):
@@ -156,9 +159,10 @@
     for slot, q in enumerate(wanted):
         source = jnp.maximum(q, 0) // held
         step = (ring_place(me >> 1, chips) - ring_place(source >> 1, chips)) & (chips - 1)
-        place = (source ^ me) & 1
-        for index, taken in enumerate(order):
-            place = jnp.where(step == taken, 2 * index, 0) + place
+        side = (source ^ me) & 1
+        place = jnp.where(step == order[-1], ready, 0) + side
+        for index, taken in enumerate(order[1:-1]):
+            place = jnp.where(step == taken, 2 + side * (chips - 2) + index, place)
 
         @pl.when(place < ready)
         def _():
@@ -205,37 +209,31 @@
     out_factor = out_precond.reshape(out_precond.shape[1:])
     limit = pltpu.CompilerParams(vmem_limit_bytes=24 * 2**20)
 
-    def pass_on(array, step):
-        ring = [ring_chip(place) for place in range(ex // 2)]
+    groups = ex // 2
+    order = sorted(range(groups), key=lambda step: min(step, groups - step))
+
+    def pass_on(array, step, flip=0):
+        ring = [ring_chip(place) for place in range(groups)]
         moves = zip(ring, ring[step:] + ring[:step])
-        return lax.ppermute(array, "ex", [(2 * a + c, 2 * b + c) for a, b in moves for c in range(2)])
-
-    groups = ex // 2
-    find = functools.partial(wanted_block, ex, held, slots)
-    other = lax.ppermute(query, "ex", [(i, i ^ 1) for i in range(ex)])
-    own = pl.pallas_call(
-        functools.partial(own_kernel, find),
-        out_shape=[jax.ShapeDtypeStruct((QBLK, features), BF16)] * groups,
+        return lax.ppermute(array, "ex", [(2 * a + c, 2 * b + (c ^ flip)) for a, b in moves for c in range(2)])
+
+    one = jax.ShapeDtypeStruct((QBLK, features), BF16)
+    two = jax.ShapeDtypeStruct((2 * QBLK, features), BF16)
+    self_block, far_block, swap, *near = pl.pallas_call(
+        functools.partial(pick_kernel, ex, held, slots, order),
+        out_shape=[one, one, two] + [two] * (groups - 2),
         in_specs=[SMEM, VMEM],
-        out_specs=[VMEM] * groups,
-        compiler_params=limit,
-        name="own",
+        out_specs=[VMEM] * (groups + 1),
+        compiler_params=limit,
+        name="pick",
     )(pair_blocks, query)
-    picked = pl.pallas_call(
-        functools.partial(pick_kernel, find, groups),
-        out_shape=[jax.ShapeDtypeStruct((2 * QBLK, features), BF16)] * groups,
-        in_specs=[SMEM] + [VMEM] * (1 + groups),
-        out_specs=[VMEM] * groups,
-        compiler_params=limit,
-        name="pick",
-    )(pair_blocks, other, *own)
-
-    order = sorted(range(groups), key=lambda step: min(step, groups - step))
-    raw = [pass_on(picked[step], step) for step in order[1:-1]]
-
+    raw = [pass_on(array, step) for array, step in zip(near, order[1:])]
+    swap = pass_on(swap, 0, 1)
+
+    brief = pl.CostEstimate(flops=1000, bytes_accessed=1000, transcendentals=0)
     stack = features // LANES * QBLK
     span = 2 * LANES
-    out_factor, in_factor, far_pick = lax.optimization_barrier((out_factor, in_factor, picked[order[-1]]))
+    out_factor, in_factor, far_pick = lax.optimization_barrier((out_factor, in_factor, far_block))
     left, right, far = pl.pallas_call(
         functools.partial(first_kernel, rows, out_precond.shape[-1]),
         out_shape=[
@@ -243,27 +241,46 @@
             jax.ShapeDtypeStruct((3 * span, span), BF16),
             jax.ShapeDtypeStruct((2, QBLK, features), BF16),
         ],
-        in_specs=[VMEM] * 2,
+        in_specs=[VMEM] * 3,
         out_specs=[VMEM] * 3,
         compiler_params=limit,
         name="first",
-    )(jnp.concatenate([out_factor, in_factor], axis=0), far_pick)
+        cost_estimate=brief,
+    )(jnp.concatenate([out_factor, in_factor], axis=0), far_pick, swap)
     far = pass_on(far, order[-1])
 
-    early, done = [], 0
-    half = len(raw) // 2
-    for index, pairs in enumerate(([picked[0]], raw[:half], raw[half:])):
-        early = [
-            pl.pallas_call(
-                functools.partial(near_kernel, done),
-                out_shape=jax.ShapeDtypeStruct((done + 2 * len(pairs), QBLK, features), BF16),
-                in_specs=[VMEM] * (2 + len(early) + len(pairs)),
-                out_specs=VMEM,
-                compiler_params=limit,
-                name=f"near{index}",
-            )(left, right, *early, *pairs)
-        ]
-        done += 2 * len(pairs)
+    def prepared(count):
+        return jax.ShapeDtypeStruct((count, QBLK, features), BF16)
+
+    early = pl.pallas_call(
+        self_kernel,
+        out_shape=prepared(2),
+        in_specs=[VMEM] * 4,
+        out_specs=VMEM,
+        compiler_params=limit,
+        name="self",
+        cost_estimate=brief,
+    )(left, right, self_block, swap)
+    _, *ready = lax.optimization_barrier((early, *raw))
+    crossed = pl.pallas_call(
+        cross_kernel,
+        out_shape=[one] * len(raw),
+        in_specs=[VMEM] * len(raw),
+        out_specs=[VMEM] * len(raw),
+        compiler_params=limit,
+        name="cross",
+    )(*ready)
+    crossed = [pass_on(array, 0, 1) for array in crossed]
+    for name, blocks in (("near", raw), ("crossed", crossed)):
+        early = pl.pallas_call(
+            near_kernel,
+            out_shape=prepared(early.shape[0] + len(raw)),
+            in_specs=[VMEM] * (3 + len(blocks)),
+            out_specs=VMEM,
+            compiler_params=limit,
+            name=name,
+            cost_estimate=brief,
+        )(left, right, early, *blocks)
     parts = pl.pallas_call(
         functools.partial(last_kernel, order, layer, held, slots),
         out_shape=[jax.ShapeDtypeStruct((slots * rows, train_rows), F32)]
@@ -273,7 +290,7 @@
         scratch_shapes=[pltpu.VMEM((slots * QBLK, features), BF16)],
         compiler_params=limit,
         name="last",
-    )(pair_blocks, far, *early, train)
+    )(pair_blocks, far, early, train)
 
     terms = [parts[0]] + [
         lax.ppermute(parts[m], "layer", [(i, (i + m) % layer) for i in range(layer)]) for m in range(1, layer)

time: 30.8 us -> 30.2 us (0.981)
  waiting for transfers between devices: 3.67 us -> 2.97 us
  starting transfers between devices: 11.6 us -> 12.2 us
  Pallas kernels: 12.7 us -> 12.2 us
    ppermute x4 -> x6, waiting for transfers between devices: 1.19 us -> 0.49 us  [pass_on(): lax.ppermute(array, 'ex', [(2 * a + c, 2 * b + (c ^ flip)) for a, b in mo...]
    ppermute x4 -> x6, starting transfers between devices: 6.04 us -> 6.68 us  [pass_on(): lax.ppermute(array, 'ex', [(2 * a + c, 2 * b + (c ^ flip)) for a, b in mo...]
    pallas_call x5, Pallas kernels: 6.81 us -> 6.26 us  [the longest x2 3.72 us: shards(): pl.pallas_call(near_kernel, out_shape=prepared(early.shape[0] + len(raw))...]
    unnamed x6 -> x8, local copies, waits for them, and re-layouts: 1.7 us -> 1.71 us
  transfers between devices with their start and end apart: 7 -> 9, of which waited for: 4 -> 4; matrix products, arithmetic and copies ran while one was open for 3% -> 3% of each run, Pallas kernels for 31% -> 29%
where the time goes in v10:
time: 30.2 us; the launch traced here: 30 us
  Pallas kernels  12.2 us (40%)
  starting transfers between devices  12.2 us (40%)
  waiting for transfers between devices  2.97 us (10%)
  local copies, waits for them, and re-layouts  1.71 us (6%)
  other arithmetic  0.78 us (3%)
    ppermute x6, starting transfers between devices, pass_on(): lax.ppermute(array, 'ex', [(2 * a + c, 2 * b + (c ^ flip)) for a, b in mo...  6.68 us
    ppermute x3, starting transfers between devices, shards(): lax.ppermute(parts[m], 'layer', [(i, (i + m) % layer) for i in range(laye...  5.57 us
    pallas_call x2, Pallas kernels, shards(): pl.pallas_call(near_kernel, out_shape=prepared(early.shape[0] + len(raw))...  3.72 us
    pallas_call x1, Pallas kernels, shards(): pl.pallas_call(functools.partial(first_kernel, rows, out_precond.shape[-1...  3.16 us
    ppermute x3, waiting for transfers between devices, shards(): lax.ppermute(parts[m], 'layer', [(i, (i + m) % layer) for i in range(laye...  2.48 us
    pallas_call x1, Pallas kernels, shards(): pl.pallas_call(functools.partial(last_kernel, order, layer, held, slots),...  2.13 us
    pallas_call x1, Pallas kernels, shards(): pl.pallas_call(self_kernel, out_shape=prepared(2), in_specs=[VMEM] * 4, o...  1.85 us
    unnamed x8, local copies, waits for them, and re-layouts  1.71 us
  transfers between devices with their start and end apart: 9, of which 4 were waited for; matrix products, arithmetic and copies ran while one was open for 3% of the time, Pallas kernels for 29%

profile of v10, /device:TPU:0, one launch (start us, length us, event | category | flops | bytes accessed | tf_op | source)
XLA Modules:
  0.0 30.0 jit_solution(8974496737688927189)
XLA Ops:
  0.0 0.0 copy-start.1
  0.0 1.0 %copy-done.1 = bf16[64,1,4096]{2,0,1:T(8,128)(2,1)S(1)} copy-done((bf16[64,1,4096]{2,0,1:T(8,128)(2,1)S(1)}, bf16[64,1,4096]{2,0,1:T(8,128)(2,1)}, u32[]{:S(2)}) %copy-start.1) | copy-done | bytes 524312
  1.0 0.0 copy-start.2
  1.0 0.7 %copy-done.2 = s32[48]{0:T(128)S(1)} copy-done((s32[48]{0:T(128)S(1)}, s32[48]{0:T(128)}, u32[]{:S(2)}) %copy-start.2) | copy-done | bytes 216
  1.7 0.7 %pick.1 = (bf16[16,4096]{1,0:T(8,128)(2,1)S(1)}, bf16[16,4096]{1,0:T(8,128)(2,1)S(1)}, bf16[32,4096]{1,0:T(8,128)(2,1)S(1)}, bf16[32,4096]{1,0:T(8,128)(2,1)S(1)}, bf16[32,4096]{1,0:T(8,128)(2,1)S(1)}) custom-call(s32[48]{0:T(128)S(1)} %copy-done.2, bf16[64,4096]{1,0:T(8,128)(2,1)S(1)} %bitcast.6), custom_call_target="tpu_custom_call" | custom-call | tf_op jit(solution)/shard_map/pick/pallas_call | solution.py:222
  2.4 0.5 %collective-permute-start = (bf16[32,4096]{1,0:T(8,128)(2,1)S(1)}, bf16[32,4096]{1,0:T(8,128)(2,1)S(1)}, u32[]{:S(2)}, u32[]{:S(2)}) collective-permute-start(bf16[32,4096]{1,0:T(8,128)(2,1)S(1)} %get-tuple-element.28), channel_id=1, source_target_pairs={{0,1},{1,0},{2,3},{3,2},{6,7},{7,6},{4,5},{5,4},{8,9},{9,8},{10,11... | collective-permute-start | bytes 786440 | tf_op jit(solution)/shard_map/ppermute | solution.py:218
  2.9 2.6 %collective-permute-start.2 = (bf16[32,4096]{1,0:T(8,128)(2,1)S(1)}, bf16[32,4096]{1,0:T(8,128)(2,1)S(1)}, u32[]{:S(2)}, u32[]{:S(2)}) collective-permute-start(bf16[32,4096]{1,0:T(8,128)(2,1)S(1)} %get-tuple-element.33), channel_id=1, source_target_pairs={{0,2},{1,3},{2,6},{3,7},{6,4},{7,5},{4,0},{5,1},{8,10},{9,11},{10,... | collective-permute-start | bytes 786440 | tf_op jit(solution)/shard_map/ppermute | solution.py:218
  5.4 0.1 collective-permute-start.3
  5.6 0.8 %pad_maximum_fusion.factors_ref = f32[128,64]{1,0:T(8,128)S(1)} fusion(f32[64,64]{1,0:T(8,128)} %bitcast.7, f32[64,64]{1,0:T(8,128)} %bitcast.8), kind=kLoop, calls=%fused_computation | loop fusion | flops 8192 | bytes 65536 | tf_op jit(solution)/shard_map/concatenate | solution.py:249
  6.3 0.0 collective-permute-done.swap_ref
  6.3 3.2 %first.1 = (bf16[2048,1024]{1,0:T(8,128)(2,1)S(1)}, bf16[768,256]{1,0:T(8,128)(2,1)S(1)}, bf16[2,16,4096]{2,1,0:T(8,128)(2,1)S(1)}) custom-call(f32[128,64]{1,0:T(8,128)S(1)} %pad_maximum_fusion.factors_ref, bf16[16,4096]{1,0:T(8,128)(2,1)S(1)} %get-tuple-element.27.far_ref, bf16[32,4096]{1,0:T(8,128)(2,1)S(1)} %collective-permute-done.swap_ref), custom_call_target="tpu_custom_call" | custom-call | flops 1000 | bytes 1000 | tf_op jit(solution)/shard_map/first/pallas_call | solution.py:237
  9.5 2.9 %collective-permute-start.1 = (bf16[2,16,4096]{2,1,0:T(8,128)(2,1)S(1)}, bf16[2,16,4096]{2,1,0:T(8,128)(2,1)S(1)}, u32[]{:S(2)}, u32[]{:S(2)}) collective-permute-start(bf16[2,16,4096]{2,1,0:T(8,128)(2,1)S(1)} %get-tuple-element.29), channel_id=1, source_target_pairs={{0,6},{1,7},{2,4},{3,5},{6,0},{7,1},{4,2},{5,3},{8,14},{9,15},{10,... | collective-permute-start | bytes 786440 | tf_op jit(solution)/shard_map/ppermute | solution.py:218
  12.4 1.8 %self.1.done_ref = bf16[2,16,4096]{2,1,0:T(8,128)(2,1)S(1)} custom-call(bf16[2048,1024]{1,0:T(8,128)(2,1)S(1)} %get-tuple-element.30.left_ref, bf16[768,256]{1,0:T(8,128)(2,1)S(1)} %get-tuple-element.31.right_ref, bf16[16,4096]{1,0:T(8,128)(2,1)S(1)} %get-tuple-element.32.self_ref, bf16[32,4096]{1,0:T(8,128)(2,1)S(1)} %collective-permute-done.swap_ref), custom_call_target="tpu_custom_call" | custom-call | flops 1000 | bytes 1000 | tf_op jit(solution)/shard_map/self/pallas_call | solution.py:255
  14.3 0.0 collective-permute-done.2.refs_0_
  14.3 0.0 collective-permute-done.3.refs_1_
  14.4 0.1 collective-permute-start.4
  14.4 0.5 %collective-permute-start.5 = (bf16[16,4096]{1,0:T(8,128)(2,1)S(1)}, bf16[16,4096]{1,0:T(8,128)(2,1)S(1)}, u32[]{:S(2)}, u32[]{:S(2)}) collective-permute-start(bf16[16,4096]{1,0:T(8,128)(2,1)S(1)} %get-tuple-element.38), channel_id=1, source_target_pairs={{0,1},{1,0},{2,3},{3,2},{6,7},{7,6},{4,5},{5,4},{8,9},{9,8},{10,11... | collective-permute-start | bytes 393224 | tf_op jit(solution)/shard_map/ppermute | solution.py:218
  14.9 1.9 %near.1.done_ref = bf16[4,16,4096]{2,1,0:T(8,128)(2,1)S(1)} custom-call(bf16[2048,1024]{1,0:T(8,128)(2,1)S(1)} %get-tuple-element.30.left_ref, bf16[768,256]{1,0:T(8,128)(2,1)S(1)} %get-tuple-element.31.right_ref, bf16[2,16,4096]{2,1,0:T(8,128)(2,1)S(1)} %self.1.done_ref, bf16[32,4096]{1,0:T(8,128)(2,1)S(1)} %collective-permute-done.2.refs_0_, ...), custom_call_target="tpu_custom_call" | custom-call | flops 1000 | bytes 1000 | tf_op jit(solution)/shard_map/near/pallas_call | solution.py:275
  16.8 0.0 copy-start
  16.8 0.0 copy-start.3
  16.8 0.0 collective-permute-done.4.refs_0_
  16.8 0.0 collective-permute-done.5.refs_1_
  16.8 1.9 %crossed.1.early_ref = bf16[6,16,4096]{2,1,0:T(8,128)(2,1)S(1)} custom-call(bf16[2048,1024]{1,0:T(8,128)(2,1)S(1)} %get-tuple-element.30.left_ref, bf16[768,256]{1,0:T(8,128)(2,1)S(1)} %get-tuple-element.31.right_ref, bf16[4,16,4096]{2,1,0:T(8,128)(2,1)S(1)} %near.1.done_ref, bf16[16,4096]{1,0:T(8,128)(2,1)S(1)} %collective-permute-done.4.refs_0_, ...), custom_call_target="tpu_custom_call" | custom-call | flops 1000 | bytes 1000 | tf_op jit(solution)/shard_map/crossed/pallas_call | solution.py:275
  18.7 0.5 %collective-permute-done.1.late_ref = bf16[2,16,4096]{2,1,0:T(8,128)(2,1)S(1)} collective-permute-done((bf16[2,16,4096]{2,1,0:T(8,128)(2,1)S(1)}, bf16[2,16,4096]{2,1,0:T(8,128)(2,1)S(1)}, u32[]{:S(2)}, u32[]{:S(2)}) %collective-permute-start.1) | collective-permute-done | bytes 262176 | tf_op jit(solution)/shard_map/ppermute | solution.py:218
  19.2 0.0 copy-done
  19.2 0.0 copy-done.3
  19.2 2.1 %last.1 = (f32[24,512]{1,0:T(8,128)S(1)}, bf16[24,512]{1,0:T(8,128)(2,1)S(1)}, bf16[24,512]{1,0:T(8,128)(2,1)S(1)}, bf16[24,512]{1,0:T(8,128)(2,1)S(1)}) custom-call(s32[48]{0:T(128)S(1)} %copy-done.3, bf16[2,16,4096]{2,1,0:T(8,128)(2,1)S(1)} %collective-permute-done.1.late_ref, bf16[6,16,4096]{2,1,0:T(8,128)(2,1)S(1)} %crossed.1.early_ref, ...), custom_call_target="tpu_custom_call" | custom-call | tf_op jit(solution)/shard_map/last/pallas_call | solution.py:284
  21.3 1.6 %collective-permute-start.6 = (bf16[24,512]{1,0:T(8,128)(2,1)S(1)}, bf16[24,512]{1,0:T(8,128)(2,1)S(1)}, u32[]{:S(2)}, u32[]{:S(2)}) collective-permute-start(bf16[24,512]{1,0:T(8,128)(2,1)S(1)} %get-tuple-element.40), channel_id=1, source_target_pairs={{0,8},{8,16},{16,24},{24,0},{1,9},{9,17},{17,25},{25,1},{2,10},{10... | collective-permute-start | bytes 73736 | tf_op jit(solution)/shard_map/ppermute | solution.py:296
  23.0 2.6 %collective-permute-start.7 = (bf16[24,512]{1,0:T(8,128)(2,1)S(1)}, bf16[24,512]{1,0:T(8,128)(2,1)S(1)}, u32[]{:S(2)}, u32[]{:S(2)}) collective-permute-start(bf16[24,512]{1,0:T(8,128)(2,1)S(1)} %get-tuple-element.41), channel_id=1, source_target_pairs={{0,16},{8,24},{16,0},{24,8},{1,17},{9,25},{17,1},{25,9},{2,18},{10... | collective-permute-start | bytes 73736 | tf_op jit(solution)/shard_map/ppermute | solution.py:296
  25.5 1.3 %collective-permute-start.8 = (bf16[24,512]{1,0:T(8,128)(2,1)S(1)}, bf16[24,512]{1,0:T(8,128)(2,1)S(1)}, u32[]{:S(2)}, u32[]{:S(2)}) collective-permute-start(bf16[24,512]{1,0:T(8,128)(2,1)S(1)} %get-tuple-element.42), channel_id=1, source_target_pairs={{0,24},{8,0},{16,8},{24,16},{1,25},{9,1},{17,9},{25,17},{2,26},{10... | collective-permute-start | bytes 73736 | tf_op jit(solution)/shard_map/ppermute | solution.py:296
  26.9 0.1 collective-permute-done.6.refs_1_
  27.0 0.9 %collective-permute-done.7.refs_2_ = bf16[24,512]{1,0:T(8,128)(2,1)S(1)} collective-permute-done((bf16[24,512]{1,0:T(8,128)(2,1)S(1)}, bf16[24,512]{1,0:T(8,128)(2,1)S(1)}, u32[]{:S(2)}, u32[]{:S(2)}) %collective-permute-start.7) | collective-permute-done | bytes 24608 | tf_op jit(solution)/shard_map/ppermute | solution.py:296
  27.9 1.4 %collective-permute-done.8.refs_3_ = bf16[24,512]{1,0:T(8,128)(2,1)S(1)} collective-permute-done((bf16[24,512]{1,0:T(8,128)(2,1)S(1)}, bf16[24,512]{1,0:T(8,128)(2,1)S(1)}, u32[]{:S(2)}, u32[]{:S(2)}) %collective-permute-start.8) | collective-permute-done | bytes 24608 | tf_op jit(solution)/shard_map/ppermute | solution.py:296
  29.4 0.6 %finish.1 = f32[6,4,512]{2,1,0:T(4,128)} custom-call(f32[24,512]{1,0:T(8,128)S(1)} %get-tuple-element.39.refs_0_, bf16[24,512]{1,0:T(8,128)(2,1)S(1)} %collective-permute-done.6.refs_1_, bf16[24,512]{1,0:T(8,128)(2,1)S(1)} %collective-permute-done.7.refs_2_, bf16[24,512]{1,0:T(8,128)(2,1)S(1)} %collective-permute-done.8.refs_3_), custom_call_target="tpu_custom_call" | custom-call | tf_op jit(solution)/shard_map/finish/pallas_call | solution.py:298
  (1 shorter events, 0.0 us)
Async XLA Ops:
  0.0 1.0 %copy-start.1 = (bf16[64,1,4096]{2,0,1:T(8,128)(2,1)S(1)}, bf16[64,1,4096]{2,0,1:T(8,128)(2,1)}, u32[]{:S(2)}) copy-start(bf16[64,1,4096]{2,0,1:T(8,128)(2,1)} %param.6) | copy-start | bytes 1572868
  1.0 0.7 %copy-start.2 = (s32[48]{0:T(128)S(1)}, s32[48]{0:T(128)}, u32[]{:S(2)}) copy-start(s32[48]{0:T(128)} %pairs_ref.3) | copy-start | bytes 580
  2.4 4.0 %collective-permute-start = (bf16[32,4096]{1,0:T(8,128)(2,1)S(1)}, bf16[32,4096]{1,0:T(8,128)(2,1)S(1)}, u32[]{:S(2)}, u32[]{:S(2)}) collective-permute-start(bf16[32,4096]{1,0:T(8,128)(2,1)S(1)} %get-tuple-element.28), channel_id=1, source_target_pairs={{0,1},{1,0},{2,3},{3,2},{6,7},{7,6},{4,5},{5,4},{8,9},{9,8},{10,11... | collective-permute-start | bytes 786440 | tf_op jit(solution)/shard_map/ppermute | solution.py:218
  2.9 11.4 %collective-permute-start.2 = (bf16[32,4096]{1,0:T(8,128)(2,1)S(1)}, bf16[32,4096]{1,0:T(8,128)(2,1)S(1)}, u32[]{:S(2)}, u32[]{:S(2)}) collective-permute-start(bf16[32,4096]{1,0:T(8,128)(2,1)S(1)} %get-tuple-element.33), channel_id=1, source_target_pairs={{0,2},{1,3},{2,6},{3,7},{6,4},{7,5},{4,0},{5,1},{8,10},{9,11},{10,... | collective-permute-start | bytes 786440 | tf_op jit(solution)/shard_map/ppermute | solution.py:218
  5.4 8.9 %collective-permute-start.3 = (bf16[32,4096]{1,0:T(8,128)(2,1)S(1)}, bf16[32,4096]{1,0:T(8,128)(2,1)S(1)}, u32[]{:S(2)}, u32[]{:S(2)}) collective-permute-start(bf16[32,4096]{1,0:T(8,128)(2,1)S(1)} %get-tuple-element.34), channel_id=1, source_target_pairs={{0,4},{1,5},{2,0},{3,1},{6,2},{7,3},{4,6},{5,7},{8,12},{9,13},{10,... | collective-permute-start | bytes 786440 | tf_op jit(solution)/shard_map/ppermute | solution.py:218
  9.5 9.7 %collective-permute-start.1 = (bf16[2,16,4096]{2,1,0:T(8,128)(2,1)S(1)}, bf16[2,16,4096]{2,1,0:T(8,128)(2,1)S(1)}, u32[]{:S(2)}, u32[]{:S(2)}) collective-permute-start(bf16[2,16,4096]{2,1,0:T(8,128)(2,1)S(1)} %get-tuple-element.29), channel_id=1, source_target_pairs={{0,6},{1,7},{2,4},{3,5},{6,0},{7,1},{4,2},{5,3},{8,14},{9,15},{10,... | collective-permute-start | bytes 786440 | tf_op jit(solution)/shard_map/ppermute | solution.py:218
  14.4 2.5 %collective-permute-start.4 = (bf16[16,4096]{1,0:T(8,128)(2,1)S(1)}, bf16[16,4096]{1,0:T(8,128)(2,1)S(1)}, u32[]{:S(2)}, u32[]{:S(2)}) collective-permute-start(bf16[16,4096]{1,0:T(8,128)(2,1)S(1)} %get-tuple-element.37), channel_id=1, source_target_pairs={{0,1},{1,0},{2,3},{3,2},{6,7},{7,6},{4,5},{5,4},{8,9},{9,8},{10,11... | collective-permute-start | bytes 393224 | tf_op jit(solution)/shard_map/ppermute | solution.py:218
  14.4 2.4 %collective-permute-start.5 = (bf16[16,4096]{1,0:T(8,128)(2,1)S(1)}, bf16[16,4096]{1,0:T(8,128)(2,1)S(1)}, u32[]{:S(2)}, u32[]{:S(2)}) collective-permute-start(bf16[16,4096]{1,0:T(8,128)(2,1)S(1)} %get-tuple-element.38), channel_id=1, source_target_pairs={{0,1},{1,0},{2,3},{3,2},{6,7},{7,6},{4,5},{5,4},{8,9},{9,8},{10,11... | collective-permute-start | bytes 393224 | tf_op jit(solution)/shard_map/ppermute | solution.py:218
  16.8 2.4 %copy-start = (bf16[512,1,4096]{2,0,1:T(8,128)(2,1)S(1)}, bf16[512,1,4096]{2,0,1:T(8,128)(2,1)}, u32[]{:S(2)}) copy-start(bf16[512,1,4096]{2,0,1:T(8,128)(2,1)} %param.5) | copy-start | bytes 12582916
  16.8 2.4 %copy-start.3 = (s32[48]{0:T(128)S(1)}, s32[48]{0:T(128)}, u32[]{:S(2)}) copy-start(s32[48]{0:T(128)} %pairs_ref.3) | copy-start | bytes 580
  21.3 5.7 %collective-permute-start.6 = (bf16[24,512]{1,0:T(8,128)(2,1)S(1)}, bf16[24,512]{1,0:T(8,128)(2,1)S(1)}, u32[]{:S(2)}, u32[]{:S(2)}) collective-permute-start(bf16[24,512]{1,0:T(8,128)(2,1)S(1)} %get-tuple-element.40), channel_id=1, source_target_pairs={{0,8},{8,16},{16,24},{24,0},{1,9},{9,17},{17,25},{25,1},{2,10},{10... | collective-permute-start | bytes 73736 | tf_op jit(solution)/shard_map/ppermute | solution.py:296
  23.0 5.0 %collective-permute-start.7 = (bf16[24,512]{1,0:T(8,128)(2,1)S(1)}, bf16[24,512]{1,0:T(8,128)(2,1)S(1)}, u32[]{:S(2)}, u32[]{:S(2)}) collective-permute-start(bf16[24,512]{1,0:T(8,128)(2,1)S(1)} %get-tuple-element.41), channel_id=1, source_target_pairs={{0,16},{8,24},{16,0},{24,8},{1,17},{9,25},{17,1},{25,9},{2,18},{10... | collective-permute-start | bytes 73736 | tf_op jit(solution)/shard_map/ppermute | solution.py:296
  25.5 3.8 %collective-permute-start.8 = (bf16[24,512]{1,0:T(8,128)(2,1)S(1)}, bf16[24,512]{1,0:T(8,128)(2,1)S(1)}, u32[]{:S(2)}, u32[]{:S(2)}) collective-permute-start(bf16[24,512]{1,0:T(8,128)(2,1)S(1)} %get-tuple-element.42), channel_id=1, source_target_pairs={{0,24},{8,0},{16,8},{24,16},{1,25},{9,1},{17,9},{25,17},{2,26},{10... | collective-permute-start | bytes 73736 | tf_op jit(solution)/shard_map/ppermute | solution.py:296

commit v11 on v10

--- a/solution.py
+++ b/solution.py
@@ -76,7 +76,7 @@
     col = lax.broadcasted_iota(jnp.int32, (width, half), 1) // QBLK
     col_o = lax.broadcasted_iota(jnp.int32, (width, half), 0)
     a = lax.broadcasted_iota(jnp.int32, (half, half), 1) - lax.broadcasted_iota(jnp.int32, (half, half), 0)
-    same = (a & (QBLK - 1)) == lax.axis_index("layer") * rows
+    same = jnp.where((a & (QBLK - 1)) == lax.axis_index("layer") * rows, 1.0, 0.0).astype(BF16)
     for h in range(2):
         for s in range(2):
             pick_rows = (row * 2 + s == row_o).astype(BF16)
@@ -84,9 +84,9 @@
             start = (2 * h + s) * half
             for t in range(2):
                 pick_cols = (col * 2 + (s ^ t) == col_o).astype(BF16)
-                spread = jnp.dot(part, pick_cols, preferred_element_type=F32)
+                spread = jnp.dot(part, pick_cols, preferred_element_type=F32).astype(BF16)
                 tall = jnp.broadcast_to(spread[:, None, :], (half // QBLK, QBLK, half)).reshape(half, half)
-                left_ref[start : start + half, t * half : (t + 1) * half] = jnp.where(same, tall, 0.0).astype(BF16)
+                left_ref[start : start + half, t * half : (t + 1) * half] = tall * same
     up = (
         lax.broadcasted_iota(jnp.int32, (span, in_width), 0) % in_width
         == lax.broadcasted_iota(jnp.int32, (span, in_width), 1)
@@ -173,8 +173,8 @@
             rows_ref[slot * QBLK : (slot + 1) * QBLK, :] = late_ref[jnp.maximum(place - ready, 0)]
 
     tile = lax.dot_general(
-        rows_ref[...], train_ref[...], (((1,), (1,)), ((), ())), preferred_element_type=F32
-    )
+        train_ref[...], rows_ref[...], (((1,), (1,)), ((), ())), preferred_element_type=F32
+    ).T
     rows = QBLK // layer
     chosen = []
     for slot, q in enumerate(wanted):

time: 30.2 us -> 30.1 us (level)
  transfers between devices with their start and end apart: 9 -> 9, of which waited for: 4 -> 4; matrix products, arithmetic and copies ran while one was open for 3% -> 3% of each run, Pallas kernels for 29% -> 30%
where the time goes in v11:
time: 30.1 us; the launch traced here: 29.9 us
  Pallas kernels  12.3 us (41%)
  starting transfers between devices  12.3 us (41%)
  waiting for transfers between devices  2.78 us (9%)
  local copies, waits for them, and re-layouts  1.71 us (6%)
  other arithmetic  0.78 us (3%)
    ppermute x6, starting transfers between devices, pass_on(): lax.ppermute(array, 'ex', [(2 * a + c, 2 * b + (c ^ flip)) for a, b in mo...  6.68 us
    ppermute x3, starting transfers between devices, shards(): lax.ppermute(parts[m], 'layer', [(i, (i + m) % layer) for i in range(laye...  5.57 us
    pallas_call x2, Pallas kernels, shards(): pl.pallas_call(near_kernel, out_shape=prepared(early.shape[0] + len(raw))...  3.72 us
    pallas_call x1, Pallas kernels, shards(): pl.pallas_call(functools.partial(first_kernel, rows, out_precond.shape[-1...  3.34 us
    ppermute x3, waiting for transfers between devices, shards(): lax.ppermute(parts[m], 'layer', [(i, (i + m) % layer) for i in range(laye...  2.48 us
    pallas_call x1, Pallas kernels, shards(): pl.pallas_call(functools.partial(last_kernel, order, layer, held, slots),...  2.03 us
    pallas_call x1, Pallas kernels, shards(): pl.pallas_call(self_kernel, out_shape=prepared(2), in_specs=[VMEM] * 4, o...  1.85 us
    unnamed x8, local copies, waits for them, and re-layouts  1.71 us
  transfers between devices with their start and end apart: 9, of which 4 were waited for; matrix products, arithmetic and copies ran while one was open for 3% of the time, Pallas kernels for 30%

profile of v11, /device:TPU:0, one launch (start us, length us, event | category | flops | bytes accessed | tf_op | source)
XLA Modules:
  0.0 29.9 jit_solution(16984529709091809584)
XLA Ops:
  0.0 0.0 copy-start.1
  0.0 1.0 %copy-done.1 = bf16[64,1,4096]{2,0,1:T(8,128)(2,1)S(1)} copy-done((bf16[64,1,4096]{2,0,1:T(8,128)(2,1)S(1)}, bf16[64,1,4096]{2,0,1:T(8,128)(2,1)}, u32[]{:S(2)}) %copy-start.1) | copy-done | bytes 524312
  1.0 0.0 copy-start.2
  1.0 0.7 %copy-done.2 = s32[48]{0:T(128)S(1)} copy-done((s32[48]{0:T(128)S(1)}, s32[48]{0:T(128)}, u32[]{:S(2)}) %copy-start.2) | copy-done | bytes 216
  1.7 0.7 %pick.1 = (bf16[16,4096]{1,0:T(8,128)(2,1)S(1)}, bf16[16,4096]{1,0:T(8,128)(2,1)S(1)}, bf16[32,4096]{1,0:T(8,128)(2,1)S(1)}, bf16[32,4096]{1,0:T(8,128)(2,1)S(1)}, bf16[32,4096]{1,0:T(8,128)(2,1)S(1)}) custom-call(s32[48]{0:T(128)S(1)} %copy-done.2, bf16[64,4096]{1,0:T(8,128)(2,1)S(1)} %bitcast.6), custom_call_target="tpu_custom_call" | custom-call | tf_op jit(solution)/shard_map/pick/pallas_call | solution.py:222
  2.4 0.5 %collective-permute-start = (bf16[32,4096]{1,0:T(8,128)(2,1)S(1)}, bf16[32,4096]{1,0:T(8,128)(2,1)S(1)}, u32[]{:S(2)}, u32[]{:S(2)}) collective-permute-start(bf16[32,4096]{1,0:T(8,128)(2,1)S(1)} %get-tuple-element.28), channel_id=1, source_target_pairs={{0,1},{1,0},{2,3},{3,2},{6,7},{7,6},{4,5},{5,4},{8,9},{9,8},{10,11... | collective-permute-start | bytes 786440 | tf_op jit(solution)/shard_map/ppermute | solution.py:218
  2.9 2.6 %collective-permute-start.2 = (bf16[32,4096]{1,0:T(8,128)(2,1)S(1)}, bf16[32,4096]{1,0:T(8,128)(2,1)S(1)}, u32[]{:S(2)}, u32[]{:S(2)}) collective-permute-start(bf16[32,4096]{1,0:T(8,128)(2,1)S(1)} %get-tuple-element.33), channel_id=1, source_target_pairs={{0,2},{1,3},{2,6},{3,7},{6,4},{7,5},{4,0},{5,1},{8,10},{9,11},{10,... | collective-permute-start | bytes 786440 | tf_op jit(solution)/shard_map/ppermute | solution.py:218
  5.4 0.1 collective-permute-start.3
  5.6 0.8 %pad_maximum_fusion.factors_ref = f32[128,64]{1,0:T(8,128)S(1)} fusion(f32[64,64]{1,0:T(8,128)} %bitcast.7, f32[64,64]{1,0:T(8,128)} %bitcast.8), kind=kLoop, calls=%fused_computation | loop fusion | flops 8192 | bytes 65536 | tf_op jit(solution)/shard_map/concatenate | solution.py:249
  6.3 0.0 collective-permute-done.swap_ref
  6.3 3.3 %first.1 = (bf16[2048,1024]{1,0:T(8,128)(2,1)S(1)}, bf16[768,256]{1,0:T(8,128)(2,1)S(1)}, bf16[2,16,4096]{2,1,0:T(8,128)(2,1)S(1)}) custom-call(f32[128,64]{1,0:T(8,128)S(1)} %pad_maximum_fusion.factors_ref, bf16[16,4096]{1,0:T(8,128)(2,1)S(1)} %get-tuple-element.27.far_ref, bf16[32,4096]{1,0:T(8,128)(2,1)S(1)} %collective-permute-done.swap_ref), custom_call_target="tpu_custom_call" | custom-call | flops 1000 | bytes 1000 | tf_op jit(solution)/shard_map/first/pallas_call | solution.py:237
  9.7 2.9 %collective-permute-start.1 = (bf16[2,16,4096]{2,1,0:T(8,128)(2,1)S(1)}, bf16[2,16,4096]{2,1,0:T(8,128)(2,1)S(1)}, u32[]{:S(2)}, u32[]{:S(2)}) collective-permute-start(bf16[2,16,4096]{2,1,0:T(8,128)(2,1)S(1)} %get-tuple-element.29), channel_id=1, source_target_pairs={{0,6},{1,7},{2,4},{3,5},{6,0},{7,1},{4,2},{5,3},{8,14},{9,15},{10,... | collective-permute-start | bytes 786440 | tf_op jit(solution)/shard_map/ppermute | solution.py:218
  12.6 1.9 %self.1.done_ref = bf16[2,16,4096]{2,1,0:T(8,128)(2,1)S(1)} custom-call(bf16[2048,1024]{1,0:T(8,128)(2,1)S(1)} %get-tuple-element.30.left_ref, bf16[768,256]{1,0:T(8,128)(2,1)S(1)} %get-tuple-element.31.right_ref, bf16[16,4096]{1,0:T(8,128)(2,1)S(1)} %get-tuple-element.32.self_ref, bf16[32,4096]{1,0:T(8,128)(2,1)S(1)} %collective-permute-done.swap_ref), custom_call_target="tpu_custom_call" | custom-call | flops 1000 | bytes 1000 | tf_op jit(solution)/shard_map/self/pallas_call | solution.py:255
  14.5 0.0 collective-permute-done.2.refs_0_
  14.5 0.0 collective-permute-done.3.refs_1_
  14.5 0.1 collective-permute-start.4
  14.6 0.5 %collective-permute-start.5 = (bf16[16,4096]{1,0:T(8,128)(2,1)S(1)}, bf16[16,4096]{1,0:T(8,128)(2,1)S(1)}, u32[]{:S(2)}, u32[]{:S(2)}) collective-permute-start(bf16[16,4096]{1,0:T(8,128)(2,1)S(1)} %get-tuple-element.38), channel_id=1, source_target_pairs={{0,1},{1,0},{2,3},{3,2},{6,7},{7,6},{4,5},{5,4},{8,9},{9,8},{10,11... | collective-permute-start | bytes 393224 | tf_op jit(solution)/shard_map/ppermute | solution.py:218
  15.1 1.9 %near.1.done_ref = bf16[4,16,4096]{2,1,0:T(8,128)(2,1)S(1)} custom-call(bf16[2048,1024]{1,0:T(8,128)(2,1)S(1)} %get-tuple-element.30.left_ref, bf16[768,256]{1,0:T(8,128)(2,1)S(1)} %get-tuple-element.31.right_ref, bf16[2,16,4096]{2,1,0:T(8,128)(2,1)S(1)} %self.1.done_ref, bf16[32,4096]{1,0:T(8,128)(2,1)S(1)} %collective-permute-done.2.refs_0_, ...), custom_call_target="tpu_custom_call" | custom-call | flops 1000 | bytes 1000 | tf_op jit(solution)/shard_map/near/pallas_call | solution.py:275
  17.0 0.0 copy-start
  17.0 0.0 copy-start.3
  17.0 0.0 collective-permute-done.4.refs_0_
  17.0 0.0 collective-permute-done.5.refs_1_
  17.0 1.9 %crossed.1.early_ref = bf16[6,16,4096]{2,1,0:T(8,128)(2,1)S(1)} custom-call(bf16[2048,1024]{1,0:T(8,128)(2,1)S(1)} %get-tuple-element.30.left_ref, bf16[768,256]{1,0:T(8,128)(2,1)S(1)} %get-tuple-element.31.right_ref, bf16[4,16,4096]{2,1,0:T(8,128)(2,1)S(1)} %near.1.done_ref, bf16[16,4096]{1,0:T(8,128)(2,1)S(1)} %collective-permute-done.4.refs_0_, ...), custom_call_target="tpu_custom_call" | custom-call | flops 1000 | bytes 1000 | tf_op jit(solution)/shard_map/crossed/pallas_call | solution.py:275
  18.9 0.3 collective-permute-done.1.late_ref
  19.2 0.0 copy-done
  19.2 0.0 copy-done.3
  19.2 2.0 %last.1 = (f32[24,512]{1,0:T(8,128)S(1)}, bf16[24,512]{1,0:T(8,128)(2,1)S(1)}, bf16[24,512]{1,0:T(8,128)(2,1)S(1)}, bf16[24,512]{1,0:T(8,128)(2,1)S(1)}) custom-call(s32[48]{0:T(128)S(1)} %copy-done.3, bf16[2,16,4096]{2,1,0:T(8,128)(2,1)S(1)} %collective-permute-done.1.late_ref, bf16[6,16,4096]{2,1,0:T(8,128)(2,1)S(1)} %crossed.1.early_ref, ...), custom_call_target="tpu_custom_call" | custom-call | tf_op jit(solution)/shard_map/last/pallas_call | solution.py:284
  21.2 1.6 %collective-permute-start.6 = (bf16[24,512]{1,0:T(8,128)(2,1)S(1)}, bf16[24,512]{1,0:T(8,128)(2,1)S(1)}, u32[]{:S(2)}, u32[]{:S(2)}) collective-permute-start(bf16[24,512]{1,0:T(8,128)(2,1)S(1)} %get-tuple-element.40), channel_id=1, source_target_pairs={{0,8},{8,16},{16,24},{24,0},{1,9},{9,17},{17,25},{25,1},{2,10},{10... | collective-permute-start | bytes 73736 | tf_op jit(solution)/shard_map/ppermute | solution.py:296
  22.9 2.6 %collective-permute-start.7 = (bf16[24,512]{1,0:T(8,128)(2,1)S(1)}, bf16[24,512]{1,0:T(8,128)(2,1)S(1)}, u32[]{:S(2)}, u32[]{:S(2)}) collective-permute-start(bf16[24,512]{1,0:T(8,128)(2,1)S(1)} %get-tuple-element.41), channel_id=1, source_target_pairs={{0,16},{8,24},{16,0},{24,8},{1,17},{9,25},{17,1},{25,9},{2,18},{10... | collective-permute-start | bytes 73736 | tf_op jit(solution)/shard_map/ppermute | solution.py:296
  25.4 1.3 %collective-permute-start.8 = (bf16[24,512]{1,0:T(8,128)(2,1)S(1)}, bf16[24,512]{1,0:T(8,128)(2,1)S(1)}, u32[]{:S(2)}, u32[]{:S(2)}) collective-permute-start(bf16[24,512]{1,0:T(8,128)(2,1)S(1)} %get-tuple-element.42), channel_id=1, source_target_pairs={{0,24},{8,0},{16,8},{24,16},{1,25},{9,1},{17,9},{25,17},{2,26},{10... | collective-permute-start | bytes 73736 | tf_op jit(solution)/shard_map/ppermute | solution.py:296
  26.8 0.1 collective-permute-done.6.refs_1_
  26.9 1.0 %collective-permute-done.7.refs_2_ = bf16[24,512]{1,0:T(8,128)(2,1)S(1)} collective-permute-done((bf16[24,512]{1,0:T(8,128)(2,1)S(1)}, bf16[24,512]{1,0:T(8,128)(2,1)S(1)}, u32[]{:S(2)}, u32[]{:S(2)}) %collective-permute-start.7) | collective-permute-done | bytes 24608 | tf_op jit(solution)/shard_map/ppermute | solution.py:296
  27.9 1.3 %collective-permute-done.8.refs_3_ = bf16[24,512]{1,0:T(8,128)(2,1)S(1)} collective-permute-done((bf16[24,512]{1,0:T(8,128)(2,1)S(1)}, bf16[24,512]{1,0:T(8,128)(2,1)S(1)}, u32[]{:S(2)}, u32[]{:S(2)}) %collective-permute-start.8) | collective-permute-done | bytes 24608 | tf_op jit(solution)/shard_map/ppermute | solution.py:296
  29.3 0.6 %finish.1 = f32[6,4,512]{2,1,0:T(4,128)} custom-call(f32[24,512]{1,0:T(8,128)S(1)} %get-tuple-element.39.refs_0_, bf16[24,512]{1,0:T(8,128)(2,1)S(1)} %collective-permute-done.6.refs_1_, bf16[24,512]{1,0:T(8,128)(2,1)S(1)} %collective-permute-done.7.refs_2_, bf16[24,512]{1,0:T(8,128)(2,1)S(1)} %collective-permute-done.8.refs_3_), custom_call_target="tpu_custom_call" | custom-call | tf_op jit(solution)/shard_map/finish/pallas_call | solution.py:298
  (1 shorter events, 0.0 us)
Async XLA Ops:
  0.0 1.0 %copy-start.1 = (bf16[64,1,4096]{2,0,1:T(8,128)(2,1)S(1)}, bf16[64,1,4096]{2,0,1:T(8,128)(2,1)}, u32[]{:S(2)}) copy-start(bf16[64,1,4096]{2,0,1:T(8,128)(2,1)} %param.6) | copy-start | bytes 1572868
  1.0 0.7 %copy-start.2 = (s32[48]{0:T(128)S(1)}, s32[48]{0:T(128)}, u32[]{:S(2)}) copy-start(s32[48]{0:T(128)} %pairs_ref.3) | copy-start | bytes 580
  2.4 4.0 %collective-permute-start = (bf16[32,4096]{1,0:T(8,128)(2,1)S(1)}, bf16[32,4096]{1,0:T(8,128)(2,1)S(1)}, u32[]{:S(2)}, u32[]{:S(2)}) collective-permute-start(bf16[32,4096]{1,0:T(8,128)(2,1)S(1)} %get-tuple-element.28), channel_id=1, source_target_pairs={{0,1},{1,0},{2,3},{3,2},{6,7},{7,6},{4,5},{5,4},{8,9},{9,8},{10,11... | collective-permute-start | bytes 786440 | tf_op jit(solution)/shard_map/ppermute | solution.py:218
  2.9 11.6 %collective-permute-start.2 = (bf16[32,4096]{1,0:T(8,128)(2,1)S(1)}, bf16[32,4096]{1,0:T(8,128)(2,1)S(1)}, u32[]{:S(2)}, u32[]{:S(2)}) collective-permute-start(bf16[32,4096]{1,0:T(8,128)(2,1)S(1)} %get-tuple-element.33), channel_id=1, source_target_pairs={{0,2},{1,3},{2,6},{3,7},{6,4},{7,5},{4,0},{5,1},{8,10},{9,11},{10,... | collective-permute-start | bytes 786440 | tf_op jit(solution)/shard_map/ppermute | solution.py:218
  5.4 9.1 %collective-permute-start.3 = (bf16[32,4096]{1,0:T(8,128)(2,1)S(1)}, bf16[32,4096]{1,0:T(8,128)(2,1)S(1)}, u32[]{:S(2)}, u32[]{:S(2)}) collective-permute-start(bf16[32,4096]{1,0:T(8,128)(2,1)S(1)} %get-tuple-element.34), channel_id=1, source_target_pairs={{0,4},{1,5},{2,0},{3,1},{6,2},{7,3},{4,6},{5,7},{8,12},{9,13},{10,... | collective-permute-start | bytes 786440 | tf_op jit(solution)/shard_map/ppermute | solution.py:218
  9.7 9.5 %collective-permute-start.1 = (bf16[2,16,4096]{2,1,0:T(8,128)(2,1)S(1)}, bf16[2,16,4096]{2,1,0:T(8,128)(2,1)S(1)}, u32[]{:S(2)}, u32[]{:S(2)}) collective-permute-start(bf16[2,16,4096]{2,1,0:T(8,128)(2,1)S(1)} %get-tuple-element.29), channel_id=1, source_target_pairs={{0,6},{1,7},{2,4},{3,5},{6,0},{7,1},{4,2},{5,3},{8,14},{9,15},{10,... | collective-permute-start | bytes 786440 | tf_op jit(solution)/shard_map/ppermute | solution.py:218
  14.5 2.5 %collective-permute-start.4 = (bf16[16,4096]{1,0:T(8,128)(2,1)S(1)}, bf16[16,4096]{1,0:T(8,128)(2,1)S(1)}, u32[]{:S(2)}, u32[]{:S(2)}) collective-permute-start(bf16[16,4096]{1,0:T(8,128)(2,1)S(1)} %get-tuple-element.37), channel_id=1, source_target_pairs={{0,1},{1,0},{2,3},{3,2},{6,7},{7,6},{4,5},{5,4},{8,9},{9,8},{10,11... | collective-permute-start | bytes 393224 | tf_op jit(solution)/shard_map/ppermute | solution.py:218
  14.6 2.4 %collective-permute-start.5 = (bf16[16,4096]{1,0:T(8,128)(2,1)S(1)}, bf16[16,4096]{1,0:T(8,128)(2,1)S(1)}, u32[]{:S(2)}, u32[]{:S(2)}) collective-permute-start(bf16[16,4096]{1,0:T(8,128)(2,1)S(1)} %get-tuple-element.38), channel_id=1, source_target_pairs={{0,1},{1,0},{2,3},{3,2},{6,7},{7,6},{4,5},{5,4},{8,9},{9,8},{10,11... | collective-permute-start | bytes 393224 | tf_op jit(solution)/shard_map/ppermute | solution.py:218
  17.0 2.2 %copy-start = (bf16[512,1,4096]{2,0,1:T(8,128)(2,1)S(1)}, bf16[512,1,4096]{2,0,1:T(8,128)(2,1)}, u32[]{:S(2)}) copy-start(bf16[512,1,4096]{2,0,1:T(8,128)(2,1)} %param.5) | copy-start | bytes 12582916
  17.0 2.2 %copy-start.3 = (s32[48]{0:T(128)S(1)}, s32[48]{0:T(128)}, u32[]{:S(2)}) copy-start(s32[48]{0:T(128)} %pairs_ref.3) | copy-start | bytes 580
  21.2 5.7 %collective-permute-start.6 = (bf16[24,512]{1,0:T(8,128)(2,1)S(1)}, bf16[24,512]{1,0:T(8,128)(2,1)S(1)}, u32[]{:S(2)}, u32[]{:S(2)}) collective-permute-start(bf16[24,512]{1,0:T(8,128)(2,1)S(1)} %get-tuple-element.40), channel_id=1, source_target_pairs={{0,8},{8,16},{16,24},{24,0},{1,9},{9,17},{17,25},{25,1},{2,10},{10... | collective-permute-start | bytes 73736 | tf_op jit(solution)/shard_map/ppermute | solution.py:296
  22.9 5.1 %collective-permute-start.7 = (bf16[24,512]{1,0:T(8,128)(2,1)S(1)}, bf16[24,512]{1,0:T(8,128)(2,1)S(1)}, u32[]{:S(2)}, u32[]{:S(2)}) collective-permute-start(bf16[24,512]{1,0:T(8,128)(2,1)S(1)} %get-tuple-element.41), channel_id=1, source_target_pairs={{0,16},{8,24},{16,0},{24,8},{1,17},{9,25},{17,1},{25,9},{2,18},{10... | collective-permute-start | bytes 73736 | tf_op jit(solution)/shard_map/ppermute | solution.py:296
  25.4 3.8 %collective-permute-start.8 = (bf16[24,512]{1,0:T(8,128)(2,1)S(1)}, bf16[24,512]{1,0:T(8,128)(2,1)S(1)}, u32[]{:S(2)}, u32[]{:S(2)}) collective-permute-start(bf16[24,512]{1,0:T(8,128)(2,1)S(1)} %get-tuple-element.42), channel_id=1, source_target_pairs={{0,24},{8,0},{16,8},{24,16},{1,25},{9,1},{17,9},{25,17},{2,26},{10... | collective-permute-start | bytes 73736 | tf_op jit(solution)/shard_map/ppermute | solution.py:296

commit v12 on v10

--- a/solution.py
+++ b/solution.py
@@ -173,8 +173,8 @@
             rows_ref[slot * QBLK : (slot + 1) * QBLK, :] = late_ref[jnp.maximum(place - ready, 0)]
 
     tile = lax.dot_general(
-        rows_ref[...], train_ref[...], (((1,), (1,)), ((), ())), preferred_element_type=F32
-    )
+        train_ref[...], rows_ref[...], (((1,), (1,)), ((), ())), preferred_element_type=F32
+    ).T
     rows = QBLK // layer
     chosen = []
     for slot, q in enumerate(wanted):
@@ -292,8 +292,9 @@
         name="last",
     )(pair_blocks, far, early, train)
 
+    shifts = sorted(range(1, layer), key=lambda m: (min(m, layer - m), m))
     terms = [parts[0]] + [
-        lax.ppermute(parts[m], "layer", [(i, (i + m) % layer) for i in range(layer)]) for m in range(1, layer)
+        lax.ppermute(parts[m], "layer", [(i, (i + m) % layer) for i in range(layer)]) for m in shifts
     ]
     out = pl.pallas_call(
         functools.partial(finish_kernel, layer),

time: 30.2 us -> 30.7 us (1.017)
  waiting for transfers between devices: 2.97 us -> 4.43 us
  starting transfers between devices: 12.2 us -> 11.4 us
    ppermute x3, waiting for transfers between devices: 2.48 us -> 3.93 us  [shards(): lax.ppermute(parts[m], 'layer', [(i, (i + m) % layer) for i in range(laye...]
    ppermute x3, starting transfers between devices: 5.57 us -> 4.67 us  [shards(): lax.ppermute(parts[m], 'layer', [(i, (i + m) % layer) for i in range(laye...]
  transfers between devices with their start and end apart: 9 -> 9, of which waited for: 4 -> 3; matrix products, arithmetic and copies ran while one was open for 3% -> 3% of each run, Pallas kernels for 29% -> 29%
where the time goes in v12:
time: 30.7 us; the launch traced here: 30.5 us
  Pallas kernels  12.1 us (39%)
  starting transfers between devices  11.4 us (37%)
  waiting for transfers between devices  4.43 us (14%)
  local copies, waits for them, and re-layouts  1.71 us (6%)
  other arithmetic  0.78 us (3%)
    ppermute x6, starting transfers between devices, pass_on(): lax.ppermute(array, 'ex', [(2 * a + c, 2 * b + (c ^ flip)) for a, b in mo...  6.68 us
    ppermute x3, starting transfers between devices, shards(): lax.ppermute(parts[m], 'layer', [(i, (i + m) % layer) for i in range(laye...  4.67 us
    ppermute x3, waiting for transfers between devices, shards(): lax.ppermute(parts[m], 'layer', [(i, (i + m) % layer) for i in range(laye...  3.93 us
    pallas_call x2, Pallas kernels, shards(): pl.pallas_call(near_kernel, out_shape=prepared(early.shape[0] + len(raw))...  3.72 us
    pallas_call x1, Pallas kernels, shards(): pl.pallas_call(functools.partial(first_kernel, rows, out_precond.shape[-1...  3.16 us
    pallas_call x1, Pallas kernels, shards(): pl.pallas_call(functools.partial(last_kernel, order, layer, held, slots),...  2.03 us
    pallas_call x1, Pallas kernels, shards(): pl.pallas_call(self_kernel, out_shape=prepared(2), in_specs=[VMEM] * 4, o...  1.85 us
    unnamed x8, local copies, waits for them, and re-layouts  1.71 us
  transfers between devices with their start and end apart: 9, of which 3 were waited for; matrix products, arithmetic and copies ran while one was open for 3% of the time, Pallas kernels for 29%

profile of v12, /device:TPU:0, one launch (start us, length us, event | category | flops | bytes accessed | tf_op | source)
XLA Modules:
  0.0 30.5 jit_solution(9494098713839460367)
XLA Ops:
  0.0 0.0 copy-start.1
  0.0 1.0 %copy-done.1 = bf16[64,1,4096]{2,0,1:T(8,128)(2,1)S(1)} copy-done((bf16[64,1,4096]{2,0,1:T(8,128)(2,1)S(1)}, bf16[64,1,4096]{2,0,1:T(8,128)(2,1)}, u32[]{:S(2)}) %copy-start.1) | copy-done | bytes 524312
  1.0 0.0 copy-start.2
  1.0 0.7 %copy-done.2 = s32[48]{0:T(128)S(1)} copy-done((s32[48]{0:T(128)S(1)}, s32[48]{0:T(128)}, u32[]{:S(2)}) %copy-start.2) | copy-done | bytes 216
  1.7 0.7 %pick.1 = (bf16[16,4096]{1,0:T(8,128)(2,1)S(1)}, bf16[16,4096]{1,0:T(8,128)(2,1)S(1)}, bf16[32,4096]{1,0:T(8,128)(2,1)S(1)}, bf16[32,4096]{1,0:T(8,128)(2,1)S(1)}, bf16[32,4096]{1,0:T(8,128)(2,1)S(1)}) custom-call(s32[48]{0:T(128)S(1)} %copy-done.2, bf16[64,4096]{1,0:T(8,128)(2,1)S(1)} %bitcast.6), custom_call_target="tpu_custom_call" | custom-call | tf_op jit(solution)/shard_map/pick/pallas_call | solution.py:222
  2.4 0.5 %collective-permute-start = (bf16[32,4096]{1,0:T(8,128)(2,1)S(1)}, bf16[32,4096]{1,0:T(8,128)(2,1)S(1)}, u32[]{:S(2)}, u32[]{:S(2)}) collective-permute-start(bf16[32,4096]{1,0:T(8,128)(2,1)S(1)} %get-tuple-element.28), channel_id=1, source_target_pairs={{0,1},{1,0},{2,3},{3,2},{6,7},{7,6},{4,5},{5,4},{8,9},{9,8},{10,11... | collective-permute-start | bytes 786440 | tf_op jit(solution)/shard_map/ppermute | solution.py:218
  2.9 2.6 %collective-permute-start.2 = (bf16[32,4096]{1,0:T(8,128)(2,1)S(1)}, bf16[32,4096]{1,0:T(8,128)(2,1)S(1)}, u32[]{:S(2)}, u32[]{:S(2)}) collective-permute-start(bf16[32,4096]{1,0:T(8,128)(2,1)S(1)} %get-tuple-element.33), channel_id=1, source_target_pairs={{0,2},{1,3},{2,6},{3,7},{6,4},{7,5},{4,0},{5,1},{8,10},{9,11},{10,... | collective-permute-start | bytes 786440 | tf_op jit(solution)/shard_map/ppermute | solution.py:218
  5.4 0.1 collective-permute-start.3
  5.6 0.8 %pad_maximum_fusion.factors_ref = f32[128,64]{1,0:T(8,128)S(1)} fusion(f32[64,64]{1,0:T(8,128)} %bitcast.7, f32[64,64]{1,0:T(8,128)} %bitcast.8), kind=kLoop, calls=%fused_computation | loop fusion | flops 8192 | bytes 65536 | tf_op jit(solution)/shard_map/concatenate | solution.py:249
  6.3 0.0 collective-permute-done.swap_ref
  6.3 3.2 %first.1 = (bf16[2048,1024]{1,0:T(8,128)(2,1)S(1)}, bf16[768,256]{1,0:T(8,128)(2,1)S(1)}, bf16[2,16,4096]{2,1,0:T(8,128)(2,1)S(1)}) custom-call(f32[128,64]{1,0:T(8,128)S(1)} %pad_maximum_fusion.factors_ref, bf16[16,4096]{1,0:T(8,128)(2,1)S(1)} %get-tuple-element.27.far_ref, bf16[32,4096]{1,0:T(8,128)(2,1)S(1)} %collective-permute-done.swap_ref), custom_call_target="tpu_custom_call" | custom-call | flops 1000 | bytes 1000 | tf_op jit(solution)/shard_map/first/pallas_call | solution.py:237
  9.5 2.9 %collective-permute-start.1 = (bf16[2,16,4096]{2,1,0:T(8,128)(2,1)S(1)}, bf16[2,16,4096]{2,1,0:T(8,128)(2,1)S(1)}, u32[]{:S(2)}, u32[]{:S(2)}) collective-permute-start(bf16[2,16,4096]{2,1,0:T(8,128)(2,1)S(1)} %get-tuple-element.29), channel_id=1, source_target_pairs={{0,6},{1,7},{2,4},{3,5},{6,0},{7,1},{4,2},{5,3},{8,14},{9,15},{10,... | collective-permute-start | bytes 786440 | tf_op jit(solution)/shard_map/ppermute | solution.py:218
  12.4 1.8 %self.1.done_ref = bf16[2,16,4096]{2,1,0:T(8,128)(2,1)S(1)} custom-call(bf16[2048,1024]{1,0:T(8,128)(2,1)S(1)} %get-tuple-element.30.left_ref, bf16[768,256]{1,0:T(8,128)(2,1)S(1)} %get-tuple-element.31.right_ref, bf16[16,4096]{1,0:T(8,128)(2,1)S(1)} %get-tuple-element.32.self_ref, bf16[32,4096]{1,0:T(8,128)(2,1)S(1)} %collective-permute-done.swap_ref), custom_call_target="tpu_custom_call" | custom-call | flops 1000 | bytes 1000 | tf_op jit(solution)/shard_map/self/pallas_call | solution.py:255
  14.3 0.0 collective-permute-done.2.refs_0_
  14.3 0.0 collective-permute-done.3.refs_1_
  14.4 0.1 collective-permute-start.4
  14.4 0.5 %collective-permute-start.5 = (bf16[16,4096]{1,0:T(8,128)(2,1)S(1)}, bf16[16,4096]{1,0:T(8,128)(2,1)S(1)}, u32[]{:S(2)}, u32[]{:S(2)}) collective-permute-start(bf16[16,4096]{1,0:T(8,128)(2,1)S(1)} %get-tuple-element.38), channel_id=1, source_target_pairs={{0,1},{1,0},{2,3},{3,2},{6,7},{7,6},{4,5},{5,4},{8,9},{9,8},{10,11... | collective-permute-start | bytes 393224 | tf_op jit(solution)/shard_map/ppermute | solution.py:218
  14.9 1.9 %near.1.done_ref = bf16[4,16,4096]{2,1,0:T(8,128)(2,1)S(1)} custom-call(bf16[2048,1024]{1,0:T(8,128)(2,1)S(1)} %get-tuple-element.30.left_ref, bf16[768,256]{1,0:T(8,128)(2,1)S(1)} %get-tuple-element.31.right_ref, bf16[2,16,4096]{2,1,0:T(8,128)(2,1)S(1)} %self.1.done_ref, bf16[32,4096]{1,0:T(8,128)(2,1)S(1)} %collective-permute-done.2.refs_0_, ...), custom_call_target="tpu_custom_call" | custom-call | flops 1000 | bytes 1000 | tf_op jit(solution)/shard_map/near/pallas_call | solution.py:275
  16.8 0.0 copy-start
  16.8 0.0 copy-start.3
  16.8 0.0 collective-permute-done.4.refs_0_
  16.8 0.0 collective-permute-done.5.refs_1_
  16.8 1.9 %crossed.1.early_ref = bf16[6,16,4096]{2,1,0:T(8,128)(2,1)S(1)} custom-call(bf16[2048,1024]{1,0:T(8,128)(2,1)S(1)} %get-tuple-element.30.left_ref, bf16[768,256]{1,0:T(8,128)(2,1)S(1)} %get-tuple-element.31.right_ref, bf16[4,16,4096]{2,1,0:T(8,128)(2,1)S(1)} %near.1.done_ref, bf16[16,4096]{1,0:T(8,128)(2,1)S(1)} %collective-permute-done.4.refs_0_, ...), custom_call_target="tpu_custom_call" | custom-call | flops 1000 | bytes 1000 | tf_op jit(solution)/shard_map/crossed/pallas_call | solution.py:275
  18.7 0.5 %collective-permute-done.1.late_ref = bf16[2,16,4096]{2,1,0:T(8,128)(2,1)S(1)} collective-permute-done((bf16[2,16,4096]{2,1,0:T(8,128)(2,1)S(1)}, bf16[2,16,4096]{2,1,0:T(8,128)(2,1)S(1)}, u32[]{:S(2)}, u32[]{:S(2)}) %collective-permute-start.1) | collective-permute-done | bytes 262176 | tf_op jit(solution)/shard_map/ppermute | solution.py:218
  19.2 0.0 copy-done
  19.2 0.0 copy-done.3
  19.2 2.0 %last.1 = (f32[24,512]{1,0:T(8,128)S(1)}, bf16[24,512]{1,0:T(8,128)(2,1)S(1)}, bf16[24,512]{1,0:T(8,128)(2,1)S(1)}, bf16[24,512]{1,0:T(8,128)(2,1)S(1)}) custom-call(s32[48]{0:T(128)S(1)} %copy-done.3, bf16[2,16,4096]{2,1,0:T(8,128)(2,1)S(1)} %collective-permute-done.1.late_ref, bf16[6,16,4096]{2,1,0:T(8,128)(2,1)S(1)} %crossed.1.early_ref, ...), custom_call_target="tpu_custom_call" | custom-call | tf_op jit(solution)/shard_map/last/pallas_call | solution.py:284
  21.2 1.6 %collective-permute-start.6 = (bf16[24,512]{1,0:T(8,128)(2,1)S(1)}, bf16[24,512]{1,0:T(8,128)(2,1)S(1)}, u32[]{:S(2)}, u32[]{:S(2)}) collective-permute-start(bf16[24,512]{1,0:T(8,128)(2,1)S(1)} %get-tuple-element.40), channel_id=1, source_target_pairs={{0,8},{8,16},{16,24},{24,0},{1,9},{9,17},{17,25},{25,1},{2,10},{10... | collective-permute-start | bytes 73736 | tf_op jit(solution)/shard_map/ppermute | solution.py:297
  22.9 2.2 %collective-permute-start.7 = (bf16[24,512]{1,0:T(8,128)(2,1)S(1)}, bf16[24,512]{1,0:T(8,128)(2,1)S(1)}, u32[]{:S(2)}, u32[]{:S(2)}) collective-permute-start(bf16[24,512]{1,0:T(8,128)(2,1)S(1)} %get-tuple-element.41), channel_id=1, source_target_pairs={{0,24},{8,0},{16,8},{24,16},{1,25},{9,1},{17,9},{25,17},{2,26},{10... | collective-permute-start | bytes 73736 | tf_op jit(solution)/shard_map/ppermute | solution.py:297
  25.1 0.8 %collective-permute-start.8 = (bf16[24,512]{1,0:T(8,128)(2,1)S(1)}, bf16[24,512]{1,0:T(8,128)(2,1)S(1)}, u32[]{:S(2)}, u32[]{:S(2)}) collective-permute-start(bf16[24,512]{1,0:T(8,128)(2,1)S(1)} %get-tuple-element.42), channel_id=1, source_target_pairs={{0,16},{8,24},{16,0},{24,8},{1,17},{9,25},{17,1},{25,9},{2,18},{10... | collective-permute-start | bytes 73736 | tf_op jit(solution)/shard_map/ppermute | solution.py:297
  25.9 1.1 %collective-permute-done.6.refs_1_ = bf16[24,512]{1,0:T(8,128)(2,1)S(1)} collective-permute-done((bf16[24,512]{1,0:T(8,128)(2,1)S(1)}, bf16[24,512]{1,0:T(8,128)(2,1)S(1)}, u32[]{:S(2)}, u32[]{:S(2)}) %collective-permute-start.6) | collective-permute-done | bytes 24608 | tf_op jit(solution)/shard_map/ppermute | solution.py:297
  26.9 0.0 collective-permute-done.7.refs_2_
  26.9 2.9 %collective-permute-done.8.refs_3_ = bf16[24,512]{1,0:T(8,128)(2,1)S(1)} collective-permute-done((bf16[24,512]{1,0:T(8,128)(2,1)S(1)}, bf16[24,512]{1,0:T(8,128)(2,1)S(1)}, u32[]{:S(2)}, u32[]{:S(2)}) %collective-permute-start.8) | collective-permute-done | bytes 24608 | tf_op jit(solution)/shard_map/ppermute | solution.py:297
  29.8 0.6 %finish.1 = f32[6,4,512]{2,1,0:T(4,128)} custom-call(f32[24,512]{1,0:T(8,128)S(1)} %get-tuple-element.39.refs_0_, bf16[24,512]{1,0:T(8,128)(2,1)S(1)} %collective-permute-done.6.refs_1_, bf16[24,512]{1,0:T(8,128)(2,1)S(1)} %collective-permute-done.7.refs_2_, bf16[24,512]{1,0:T(8,128)(2,1)S(1)} %collective-permute-done.8.refs_3_), custom_call_target="tpu_custom_call" | custom-call | tf_op jit(solution)/shard_map/finish/pallas_call | solution.py:299
  (1 shorter events, 0.0 us)
Async XLA Ops:
  0.0 1.0 %copy-start.1 = (bf16[64,1,4096]{2,0,1:T(8,128)(2,1)S(1)}, bf16[64,1,4096]{2,0,1:T(8,128)(2,1)}, u32[]{:S(2)}) copy-start(bf16[64,1,4096]{2,0,1:T(8,128)(2,1)} %param.6) | copy-start | bytes 1572868
  1.0 0.7 %copy-start.2 = (s32[48]{0:T(128)S(1)}, s32[48]{0:T(128)}, u32[]{:S(2)}) copy-start(s32[48]{0:T(128)} %pairs_ref.3) | copy-start | bytes 580
  2.4 4.0 %collective-permute-start = (bf16[32,4096]{1,0:T(8,128)(2,1)S(1)}, bf16[32,4096]{1,0:T(8,128)(2,1)S(1)}, u32[]{:S(2)}, u32[]{:S(2)}) collective-permute-start(bf16[32,4096]{1,0:T(8,128)(2,1)S(1)} %get-tuple-element.28), channel_id=1, source_target_pairs={{0,1},{1,0},{2,3},{3,2},{6,7},{7,6},{4,5},{5,4},{8,9},{9,8},{10,11... | collective-permute-start | bytes 786440 | tf_op jit(solution)/shard_map/ppermute | solution.py:218
  2.9 11.4 %collective-permute-start.2 = (bf16[32,4096]{1,0:T(8,128)(2,1)S(1)}, bf16[32,4096]{1,0:T(8,128)(2,1)S(1)}, u32[]{:S(2)}, u32[]{:S(2)}) collective-permute-start(bf16[32,4096]{1,0:T(8,128)(2,1)S(1)} %get-tuple-element.33), channel_id=1, source_target_pairs={{0,2},{1,3},{2,6},{3,7},{6,4},{7,5},{4,0},{5,1},{8,10},{9,11},{10,... | collective-permute-start | bytes 786440 | tf_op jit(solution)/shard_map/ppermute | solution.py:218
  5.4 8.9 %collective-permute-start.3 = (bf16[32,4096]{1,0:T(8,128)(2,1)S(1)}, bf16[32,4096]{1,0:T(8,128)(2,1)S(1)}, u32[]{:S(2)}, u32[]{:S(2)}) collective-permute-start(bf16[32,4096]{1,0:T(8,128)(2,1)S(1)} %get-tuple-element.34), channel_id=1, source_target_pairs={{0,4},{1,5},{2,0},{3,1},{6,2},{7,3},{4,6},{5,7},{8,12},{9,13},{10,... | collective-permute-start | bytes 786440 | tf_op jit(solution)/shard_map/ppermute | solution.py:218
  9.5 9.7 %collective-permute-start.1 = (bf16[2,16,4096]{2,1,0:T(8,128)(2,1)S(1)}, bf16[2,16,4096]{2,1,0:T(8,128)(2,1)S(1)}, u32[]{:S(2)}, u32[]{:S(2)}) collective-permute-start(bf16[2,16,4096]{2,1,0:T(8,128)(2,1)S(1)} %get-tuple-element.29), channel_id=1, source_target_pairs={{0,6},{1,7},{2,4},{3,5},{6,0},{7,1},{4,2},{5,3},{8,14},{9,15},{10,... | collective-permute-start | bytes 786440 | tf_op jit(solution)/shard_map/ppermute | solution.py:218
  14.4 2.5 %collective-permute-start.4 = (bf16[16,4096]{1,0:T(8,128)(2,1)S(1)}, bf16[16,4096]{1,0:T(8,128)(2,1)S(1)}, u32[]{:S(2)}, u32[]{:S(2)}) collective-permute-start(bf16[16,4096]{1,0:T(8,128)(2,1)S(1)} %get-tuple-element.37), channel_id=1, source_target_pairs={{0,1},{1,0},{2,3},{3,2},{6,7},{7,6},{4,5},{5,4},{8,9},{9,8},{10,11... | collective-permute-start | bytes 393224 | tf_op jit(solution)/shard_map/ppermute | solution.py:218
  14.4 2.4 %collective-permute-start.5 = (bf16[16,4096]{1,0:T(8,128)(2,1)S(1)}, bf16[16,4096]{1,0:T(8,128)(2,1)S(1)}, u32[]{:S(2)}, u32[]{:S(2)}) collective-permute-start(bf16[16,4096]{1,0:T(8,128)(2,1)S(1)} %get-tuple-element.38), channel_id=1, source_target_pairs={{0,1},{1,0},{2,3},{3,2},{6,7},{7,6},{4,5},{5,4},{8,9},{9,8},{10,11... | collective-permute-start | bytes 393224 | tf_op jit(solution)/shard_map/ppermute | solution.py:218
  16.8 2.4 %copy-start = (bf16[512,1,4096]{2,0,1:T(8,128)(2,1)S(1)}, bf16[512,1,4096]{2,0,1:T(8,128)(2,1)}, u32[]{:S(2)}) copy-start(bf16[512,1,4096]{2,0,1:T(8,128)(2,1)} %param.5) | copy-start | bytes 12582916
  16.8 2.4 %copy-start.3 = (s32[48]{0:T(128)S(1)}, s32[48]{0:T(128)}, u32[]{:S(2)}) copy-start(s32[48]{0:T(128)} %pairs_ref.3) | copy-start | bytes 580
  21.2 5.7 %collective-permute-start.6 = (bf16[24,512]{1,0:T(8,128)(2,1)S(1)}, bf16[24,512]{1,0:T(8,128)(2,1)S(1)}, u32[]{:S(2)}, u32[]{:S(2)}) collective-permute-start(bf16[24,512]{1,0:T(8,128)(2,1)S(1)} %get-tuple-element.40), channel_id=1, source_target_pairs={{0,8},{8,16},{16,24},{24,0},{1,9},{9,17},{17,25},{25,1},{2,10},{10... | collective-permute-start | bytes 73736 | tf_op jit(solution)/shard_map/ppermute | solution.py:297
  22.9 4.1 %collective-permute-start.7 = (bf16[24,512]{1,0:T(8,128)(2,1)S(1)}, bf16[24,512]{1,0:T(8,128)(2,1)S(1)}, u32[]{:S(2)}, u32[]{:S(2)}) collective-permute-start(bf16[24,512]{1,0:T(8,128)(2,1)S(1)} %get-tuple-element.41), channel_id=1, source_target_pairs={{0,24},{8,0},{16,8},{24,16},{1,25},{9,1},{17,9},{25,17},{2,26},{10... | collective-permute-start | bytes 73736 | tf_op jit(solution)/shard_map/ppermute | solution.py:297
  25.1 4.7 %collective-permute-start.8 = (bf16[24,512]{1,0:T(8,128)(2,1)S(1)}, bf16[24,512]{1,0:T(8,128)(2,1)S(1)}, u32[]{:S(2)}, u32[]{:S(2)}) collective-permute-start(bf16[24,512]{1,0:T(8,128)(2,1)S(1)} %get-tuple-element.42), channel_id=1, source_target_pairs={{0,16},{8,24},{16,0},{24,8},{1,17},{9,25},{17,1},{25,9},{2,18},{10... | collective-permute-start | bytes 73736 | tf_op jit(solution)/shard_map/ppermute | solution.py:297

commit v13 on v12

--- a/solution.py
+++ b/solution.py
@@ -65,12 +65,12 @@
         out_ref[...] = ref[QBLK:]
 
 
-def make_factors(rows, width, factors_ref, left_ref, right_ref):
-    in_width = factors_ref.shape[0] - width
+def make_factors(rows, out_ref, in_ref, left_ref, right_ref):
+    width, in_width = out_ref.shape[0], in_ref.shape[0]
     half = left_ref.shape[1] // 2
     span = right_ref.shape[1]
-    outs = split_bf16(factors_ref[:width])
-    ins = split_bf16(factors_ref[width:])
+    outs = split_bf16(out_ref[...])
+    ins = split_bf16(in_ref[...])
     row = lax.broadcasted_iota(jnp.int32, (half // QBLK, width), 0)
     row_o = lax.broadcasted_iota(jnp.int32, (half // QBLK, width), 1)
     col = lax.broadcasted_iota(jnp.int32, (width, half), 1) // QBLK
@@ -132,8 +132,8 @@
             ]
 
 
-def first_kernel(rows, width, factors_ref, far_ref, swap_ref, left_ref, right_ref, prep_ref):
-    make_factors(rows, width, factors_ref, left_ref, right_ref)
+def first_kernel(rows, out_ref, in_ref, far_ref, swap_ref, left_ref, right_ref, prep_ref):
+    make_factors(rows, out_ref, in_ref, left_ref, right_ref)
     prepare((far_ref[...], swap_ref[QBLK:]), left_ref, right_ref, prep_ref)
 
 
@@ -226,6 +226,7 @@
         out_specs=[VMEM] * (groups + 1),
         compiler_params=limit,
         name="pick",
+        cost_estimate=pl.CostEstimate(flops=2 * 10**9, bytes_accessed=1000, transcendentals=0),
     )(pair_blocks, query)
     raw = [pass_on(array, step) for array, step in zip(near, order[1:])]
     swap = pass_on(swap, 0, 1)
@@ -233,20 +234,19 @@
     brief = pl.CostEstimate(flops=1000, bytes_accessed=1000, transcendentals=0)
     stack = features // LANES * QBLK
     span = 2 * LANES
-    out_factor, in_factor, far_pick = lax.optimization_barrier((out_factor, in_factor, far_block))
     left, right, far = pl.pallas_call(
-        functools.partial(first_kernel, rows, out_precond.shape[-1]),
+        functools.partial(first_kernel, rows),
         out_shape=[
             jax.ShapeDtypeStruct((4 * stack, 2 * stack), BF16),
             jax.ShapeDtypeStruct((3 * span, span), BF16),
             jax.ShapeDtypeStruct((2, QBLK, features), BF16),
         ],
-        in_specs=[VMEM] * 3,
+        in_specs=[VMEM] * 4,
         out_specs=[VMEM] * 3,
         compiler_params=limit,
         name="first",
         cost_estimate=brief,
-    )(jnp.concatenate([out_factor, in_factor], axis=0), far_pick, swap)
+    )(out_factor, in_factor, far_block, swap)
     far = pass_on(far, order[-1])
 
     def prepared(count):
@@ -292,9 +292,8 @@
         name="last",
     )(pair_blocks, far, early, train)
 
-    shifts = sorted(range(1, layer), key=lambda m: (min(m, layer - m), m))
     terms = [parts[0]] + [
-        lax.ppermute(parts[m], "layer", [(i, (i + m) % layer) for i in range(layer)]) for m in shifts
+        lax.ppermute(parts[m], "layer", [(i, (i + m) % layer) for i in range(layer)]) for m in range(1, layer)
     ]
     out = pl.pallas_call(
         functools.partial(finish_kernel, layer),

time: 30.7 us -> 30.2 us (0.984)
  starting transfers between devices: 11.4 us -> 12.2 us
  other arithmetic: 0.78 us -> 0 us
  waiting for transfers between devices: 4.43 us -> 3.76 us
    ppermute x3, waiting for transfers between devices: 3.93 us -> 2.48 us  [shards(): lax.ppermute(parts[m], 'layer', [(i, (i + m) % layer) for i in range(laye...]
    ppermute x3, starting transfers between devices: 4.67 us -> 5.56 us  [shards(): lax.ppermute(parts[m], 'layer', [(i, (i + m) % layer) for i in range(laye...]
    ppermute x6, waiting for transfers between devices: 0.49 us -> 1.28 us  [pass_on(): lax.ppermute(array, 'ex', [(2 * a + c, 2 * b + (c ^ flip)) for a, b in mo...]
    concatenate x1 -> x0, other arithmetic: 0.78 us -> none  [shards(): jnp.concatenate([out_factor, in_factor], axis=0)]
    unnamed x8 -> x12, local copies, waits for them, and re-layouts: 1.71 us -> 1.78 us
  transfers between devices with their start and end apart: 9 -> 9, of which waited for: 3 -> 5; matrix products, arithmetic and copies ran while one was open for 3% -> 0% of each run, Pallas kernels for 29% -> 29%
where the time goes in v13:
time: 30.2 us; the launch traced here: 30 us
  starting transfers between devices  12.2 us (40%)
  Pallas kernels  12.1 us (40%)
  waiting for transfers between devices  3.76 us (12%)
  local copies, waits for them, and re-layouts  1.78 us (6%)
    ppermute x6, starting transfers between devices, pass_on(): lax.ppermute(array, 'ex', [(2 * a + c, 2 * b + (c ^ flip)) for a, b in mo...  6.68 us
    ppermute x3, starting transfers between devices, shards(): lax.ppermute(parts[m], 'layer', [(i, (i + m) % layer) for i in range(laye...  5.56 us
    pallas_call x2, Pallas kernels, shards(): pl.pallas_call(near_kernel, out_shape=prepared(early.shape[0] + len(raw))...  3.72 us
    pallas_call x1, Pallas kernels, shards(): pl.pallas_call(functools.partial(first_kernel, rows), out_shape=[jax.Shap...  3.16 us
    ppermute x3, waiting for transfers between devices, shards(): lax.ppermute(parts[m], 'layer', [(i, (i + m) % layer) for i in range(laye...  2.48 us
    pallas_call x1, Pallas kernels, shards(): pl.pallas_call(functools.partial(last_kernel, order, layer, held, slots),...  2.03 us
    pallas_call x1, Pallas kernels, shards(): pl.pallas_call(self_kernel, out_shape=prepared(2), in_specs=[VMEM] * 4, o...  1.85 us
    unnamed x12, local copies, waits for them, and re-layouts  1.78 us
  transfers between devices with their start and end apart: 9, of which 5 were waited for; matrix products, arithmetic and copies ran while one was open for 0% of the time, Pallas kernels for 29%

profile of v13, /device:TPU:0, one launch (start us, length us, event | category | flops | bytes accessed | tf_op | source)
XLA Modules:
  0.0 30.0 jit_solution(3468662908118367947)
XLA Ops:
  0.0 0.0 copy-start.1
  0.0 0.0 copy-start.2
  0.0 0.0 copy-start.3
  0.0 0.7 %copy-done.3 = s32[48]{0:T(128)S(1)} copy-done((s32[48]{0:T(128)S(1)}, s32[48]{0:T(128)}, u32[]{:S(2)}) %copy-start.3) | copy-done | bytes 216
  0.7 0.0 copy-start.5
  0.7 1.0 %copy-done.5 = bf16[64,1,4096]{2,0,1:T(8,128)(2,1)S(1)} copy-done((bf16[64,1,4096]{2,0,1:T(8,128)(2,1)S(1)}, bf16[64,1,4096]{2,0,1:T(8,128)(2,1)}, u32[]{:S(2)}) %copy-start.5) | copy-done | bytes 524312
  1.7 0.7 %pick.1 = (bf16[16,4096]{1,0:T(8,128)(2,1)S(1)}, bf16[16,4096]{1,0:T(8,128)(2,1)S(1)}, bf16[32,4096]{1,0:T(8,128)(2,1)S(1)}, bf16[32,4096]{1,0:T(8,128)(2,1)S(1)}, bf16[32,4096]{1,0:T(8,128)(2,1)S(1)}) custom-call(s32[48]{0:T(128)S(1)} %copy-done.3, bf16[64,4096]{1,0:T(8,128)(2,1)S(1)} %bitcast.8), custom_call_target="tpu_custom_call" | custom-call | flops 2000000000 | bytes 1000 | tf_op jit(solution)/shard_map/pick/pallas_call | solution.py:222
  2.4 0.5 %collective-permute-start = (bf16[32,4096]{1,0:T(8,128)(2,1)S(1)}, bf16[32,4096]{1,0:T(8,128)(2,1)S(1)}, u32[]{:S(2)}, u32[]{:S(2)}) collective-permute-start(bf16[32,4096]{1,0:T(8,128)(2,1)S(1)} %get-tuple-element.22), channel_id=1, source_target_pairs={{0,1},{1,0},{2,3},{3,2},{6,7},{7,6},{4,5},{5,4},{8,9},{9,8},{10,11... | collective-permute-start | bytes 786440 | tf_op jit(solution)/shard_map/ppermute | solution.py:218
  2.9 2.6 %collective-permute-start.2 = (bf16[32,4096]{1,0:T(8,128)(2,1)S(1)}, bf16[32,4096]{1,0:T(8,128)(2,1)S(1)}, u32[]{:S(2)}, u32[]{:S(2)}) collective-permute-start(bf16[32,4096]{1,0:T(8,128)(2,1)S(1)} %get-tuple-element.27), channel_id=1, source_target_pairs={{0,2},{1,3},{2,6},{3,7},{6,4},{7,5},{4,0},{5,1},{8,10},{9,11},{10,... | collective-permute-start | bytes 786440 | tf_op jit(solution)/shard_map/ppermute | solution.py:218
  5.5 0.1 collective-permute-start.3
  5.6 0.0 collective-permute-done.swap_ref
  5.6 0.0 copy-done.1
  5.6 0.0 copy-done.2
  5.6 3.2 %first.1 = (bf16[2048,1024]{1,0:T(8,128)(2,1)S(1)}, bf16[768,256]{1,0:T(8,128)(2,1)S(1)}, bf16[2,16,4096]{2,1,0:T(8,128)(2,1)S(1)}) custom-call(f32[64,64]{1,0:T(8,128)S(1)} %bitcast.6, f32[64,64]{1,0:T(8,128)S(1)} %bitcast.7, bf16[16,4096]{1,0:T(8,128)(2,1)S(1)} %get-tuple-element.21.far_ref, bf16[32,4096]{1,0:T(8,128)(2,1)S(1)} %collective-permute-done.swap_ref), custom_call_target="tpu_custom_call" | custom-call | flops 1000 | bytes 1000 | tf_op jit(solution)/shard_map/first/pallas_call | solution.py:237
  8.7 2.9 %collective-permute-start.1 = (bf16[2,16,4096]{2,1,0:T(8,128)(2,1)S(1)}, bf16[2,16,4096]{2,1,0:T(8,128)(2,1)S(1)}, u32[]{:S(2)}, u32[]{:S(2)}) collective-permute-start(bf16[2,16,4096]{2,1,0:T(8,128)(2,1)S(1)} %get-tuple-element.23), channel_id=1, source_target_pairs={{0,6},{1,7},{2,4},{3,5},{6,0},{7,1},{4,2},{5,3},{8,14},{9,15},{10,... | collective-permute-start | bytes 786440 | tf_op jit(solution)/shard_map/ppermute | solution.py:218
  11.7 1.8 %self.1.done_ref = bf16[2,16,4096]{2,1,0:T(8,128)(2,1)S(1)} custom-call(bf16[2048,1024]{1,0:T(8,128)(2,1)S(1)} %get-tuple-element.24.left_ref, bf16[768,256]{1,0:T(8,128)(2,1)S(1)} %get-tuple-element.25.right_ref, bf16[16,4096]{1,0:T(8,128)(2,1)S(1)} %get-tuple-element.26.self_ref, bf16[32,4096]{1,0:T(8,128)(2,1)S(1)} %collective-permute-done.swap_ref), custom_call_target="tpu_custom_call" | custom-call | flops 1000 | bytes 1000 | tf_op jit(solution)/shard_map/self/pallas_call | solution.py:255
  13.5 0.0 collective-permute-done.2.refs_0_
  13.5 1.1 %collective-permute-done.3.refs_1_ = bf16[32,4096]{1,0:T(8,128)(2,1)S(1)} collective-permute-done((bf16[32,4096]{1,0:T(8,128)(2,1)S(1)}, bf16[32,4096]{1,0:T(8,128)(2,1)S(1)}, u32[]{:S(2)}, u32[]{:S(2)}) %collective-permute-start.3) | collective-permute-done | bytes 262176 | tf_op jit(solution)/shard_map/ppermute | solution.py:218
  14.6 0.1 collective-permute-start.4
  14.7 0.5 %collective-permute-start.5 = (bf16[16,4096]{1,0:T(8,128)(2,1)S(1)}, bf16[16,4096]{1,0:T(8,128)(2,1)S(1)}, u32[]{:S(2)}, u32[]{:S(2)}) collective-permute-start(bf16[16,4096]{1,0:T(8,128)(2,1)S(1)} %get-tuple-element.32), channel_id=1, source_target_pairs={{0,1},{1,0},{2,3},{3,2},{6,7},{7,6},{4,5},{5,4},{8,9},{9,8},{10,11... | collective-permute-start | bytes 393224 | tf_op jit(solution)/shard_map/ppermute | solution.py:218
  15.2 1.9 %near.1.done_ref = bf16[4,16,4096]{2,1,0:T(8,128)(2,1)S(1)} custom-call(bf16[2048,1024]{1,0:T(8,128)(2,1)S(1)} %get-tuple-element.24.left_ref, bf16[768,256]{1,0:T(8,128)(2,1)S(1)} %get-tuple-element.25.right_ref, bf16[2,16,4096]{2,1,0:T(8,128)(2,1)S(1)} %self.1.done_ref, bf16[32,4096]{1,0:T(8,128)(2,1)S(1)} %collective-permute-done.2.refs_0_, ...), custom_call_target="tpu_custom_call" | custom-call | flops 1000 | bytes 1000 | tf_op jit(solution)/shard_map/near/pallas_call | solution.py:275
  17.1 0.0 copy-start
  17.1 0.0 copy-start.4
  17.1 0.0 collective-permute-done.4.refs_0_
  17.1 0.0 collective-permute-done.5.refs_1_
  17.1 1.9 %crossed.1.early_ref = bf16[6,16,4096]{2,1,0:T(8,128)(2,1)S(1)} custom-call(bf16[2048,1024]{1,0:T(8,128)(2,1)S(1)} %get-tuple-element.24.left_ref, bf16[768,256]{1,0:T(8,128)(2,1)S(1)} %get-tuple-element.25.right_ref, bf16[4,16,4096]{2,1,0:T(8,128)(2,1)S(1)} %near.1.done_ref, bf16[16,4096]{1,0:T(8,128)(2,1)S(1)} %collective-permute-done.4.refs_0_, ...), custom_call_target="tpu_custom_call" | custom-call | flops 1000 | bytes 1000 | tf_op jit(solution)/shard_map/crossed/pallas_call | solution.py:275
  19.0 0.2 collective-permute-done.1.late_ref
  19.2 0.1 copy-done
  19.3 0.0 copy-done.4
  19.3 2.0 %last.1 = (f32[24,512]{1,0:T(8,128)S(1)}, bf16[24,512]{1,0:T(8,128)(2,1)S(1)}, bf16[24,512]{1,0:T(8,128)(2,1)S(1)}, bf16[24,512]{1,0:T(8,128)(2,1)S(1)}) custom-call(s32[48]{0:T(128)S(1)} %copy-done.4, bf16[2,16,4096]{2,1,0:T(8,128)(2,1)S(1)} %collective-permute-done.1.late_ref, bf16[6,16,4096]{2,1,0:T(8,128)(2,1)S(1)} %crossed.1.early_ref, ...), custom_call_target="tpu_custom_call" | custom-call | tf_op jit(solution)/shard_map/last/pallas_call | solution.py:284
  21.3 1.6 %collective-permute-start.6 = (bf16[24,512]{1,0:T(8,128)(2,1)S(1)}, bf16[24,512]{1,0:T(8,128)(2,1)S(1)}, u32[]{:S(2)}, u32[]{:S(2)}) collective-permute-start(bf16[24,512]{1,0:T(8,128)(2,1)S(1)} %get-tuple-element.34), channel_id=1, source_target_pairs={{0,8},{8,16},{16,24},{24,0},{1,9},{9,17},{17,25},{25,1},{2,10},{10... | collective-permute-start | bytes 73736 | tf_op jit(solution)/shard_map/ppermute | solution.py:296
  22.9 2.6 %collective-permute-start.7 = (bf16[24,512]{1,0:T(8,128)(2,1)S(1)}, bf16[24,512]{1,0:T(8,128)(2,1)S(1)}, u32[]{:S(2)}, u32[]{:S(2)}) collective-permute-start(bf16[24,512]{1,0:T(8,128)(2,1)S(1)} %get-tuple-element.35), channel_id=1, source_target_pairs={{0,16},{8,24},{16,0},{24,8},{1,17},{9,25},{17,1},{25,9},{2,18},{10... | collective-permute-start | bytes 73736 | tf_op jit(solution)/shard_map/ppermute | solution.py:296
  25.5 1.3 %collective-permute-start.8 = (bf16[24,512]{1,0:T(8,128)(2,1)S(1)}, bf16[24,512]{1,0:T(8,128)(2,1)S(1)}, u32[]{:S(2)}, u32[]{:S(2)}) collective-permute-start(bf16[24,512]{1,0:T(8,128)(2,1)S(1)} %get-tuple-element.36), channel_id=1, source_target_pairs={{0,24},{8,0},{16,8},{24,16},{1,25},{9,1},{17,9},{25,17},{2,26},{10... | collective-permute-start | bytes 73736 | tf_op jit(solution)/shard_map/ppermute | solution.py:296
  26.9 0.1 collective-permute-done.6.refs_1_
  27.0 1.0 %collective-permute-done.7.refs_2_ = bf16[24,512]{1,0:T(8,128)(2,1)S(1)} collective-permute-done((bf16[24,512]{1,0:T(8,128)(2,1)S(1)}, bf16[24,512]{1,0:T(8,128)(2,1)S(1)}, u32[]{:S(2)}, u32[]{:S(2)}) %collective-permute-start.7) | collective-permute-done | bytes 24608 | tf_op jit(solution)/shard_map/ppermute | solution.py:296
  28.0 1.3 %collective-permute-done.8.refs_3_ = bf16[24,512]{1,0:T(8,128)(2,1)S(1)} collective-permute-done((bf16[24,512]{1,0:T(8,128)(2,1)S(1)}, bf16[24,512]{1,0:T(8,128)(2,1)S(1)}, u32[]{:S(2)}, u32[]{:S(2)}) %collective-permute-start.8) | collective-permute-done | bytes 24608 | tf_op jit(solution)/shard_map/ppermute | solution.py:296
  29.3 0.6 %finish.1 = f32[6,4,512]{2,1,0:T(4,128)} custom-call(f32[24,512]{1,0:T(8,128)S(1)} %get-tuple-element.33.refs_0_, bf16[24,512]{1,0:T(8,128)(2,1)S(1)} %collective-permute-done.6.refs_1_, bf16[24,512]{1,0:T(8,128)(2,1)S(1)} %collective-permute-done.7.refs_2_, bf16[24,512]{1,0:T(8,128)(2,1)S(1)} %collective-permute-done.8.refs_3_), custom_call_target="tpu_custom_call" | custom-call | tf_op jit(solution)/shard_map/finish/pallas_call | solution.py:298
  (1 shorter events, 0.0 us)
Async XLA Ops:
  0.0 5.6 %copy-start.1 = (f32[1,64,64]{2,1,0:T(8,128)S(1)}, f32[1,64,64]{2,1,0:T(8,128)}, u32[]{:S(2)}) copy-start(f32[1,64,64]{2,1,0:T(8,128)} %param.8) | copy-start | bytes 49156
  0.0 5.6 %copy-start.2 = (f32[1,64,64]{2,1,0:T(8,128)S(1)}, f32[1,64,64]{2,1,0:T(8,128)}, u32[]{:S(2)}) copy-start(f32[1,64,64]{2,1,0:T(8,128)} %param.7) | copy-start | bytes 49156
  0.0 0.7 %copy-start.3 = (s32[48]{0:T(128)S(1)}, s32[48]{0:T(128)}, u32[]{:S(2)}) copy-start(s32[48]{0:T(128)} %pairs_ref.3) | copy-start | bytes 580
  0.7 1.0 %copy-start.5 = (bf16[64,1,4096]{2,0,1:T(8,128)(2,1)S(1)}, bf16[64,1,4096]{2,0,1:T(8,128)(2,1)}, u32[]{:S(2)}) copy-start(bf16[64,1,4096]{2,0,1:T(8,128)(2,1)} %param.6) | copy-start | bytes 1572868
  2.4 3.2 %collective-permute-start = (bf16[32,4096]{1,0:T(8,128)(2,1)S(1)}, bf16[32,4096]{1,0:T(8,128)(2,1)S(1)}, u32[]{:S(2)}, u32[]{:S(2)}) collective-permute-start(bf16[32,4096]{1,0:T(8,128)(2,1)S(1)} %get-tuple-element.22), channel_id=1, source_target_pairs={{0,1},{1,0},{2,3},{3,2},{6,7},{7,6},{4,5},{5,4},{8,9},{9,8},{10,11... | collective-permute-start | bytes 786440 | tf_op jit(solution)/shard_map/ppermute | solution.py:218
  2.9 10.6 %collective-permute-start.2 = (bf16[32,4096]{1,0:T(8,128)(2,1)S(1)}, bf16[32,4096]{1,0:T(8,128)(2,1)S(1)}, u32[]{:S(2)}, u32[]{:S(2)}) collective-permute-start(bf16[32,4096]{1,0:T(8,128)(2,1)S(1)} %get-tuple-element.27), channel_id=1, source_target_pairs={{0,2},{1,3},{2,6},{3,7},{6,4},{7,5},{4,0},{5,1},{8,10},{9,11},{10,... | collective-permute-start | bytes 786440 | tf_op jit(solution)/shard_map/ppermute | solution.py:218
  5.5 9.1 %collective-permute-start.3 = (bf16[32,4096]{1,0:T(8,128)(2,1)S(1)}, bf16[32,4096]{1,0:T(8,128)(2,1)S(1)}, u32[]{:S(2)}, u32[]{:S(2)}) collective-permute-start(bf16[32,4096]{1,0:T(8,128)(2,1)S(1)} %get-tuple-element.28), channel_id=1, source_target_pairs={{0,4},{1,5},{2,0},{3,1},{6,2},{7,3},{4,6},{5,7},{8,12},{9,13},{10,... | collective-permute-start | bytes 786440 | tf_op jit(solution)/shard_map/ppermute | solution.py:218
  8.7 10.4 %collective-permute-start.1 = (bf16[2,16,4096]{2,1,0:T(8,128)(2,1)S(1)}, bf16[2,16,4096]{2,1,0:T(8,128)(2,1)S(1)}, u32[]{:S(2)}, u32[]{:S(2)}) collective-permute-start(bf16[2,16,4096]{2,1,0:T(8,128)(2,1)S(1)} %get-tuple-element.23), channel_id=1, source_target_pairs={{0,6},{1,7},{2,4},{3,5},{6,0},{7,1},{4,2},{5,3},{8,14},{9,15},{10,... | collective-permute-start | bytes 786440 | tf_op jit(solution)/shard_map/ppermute | solution.py:218
  14.6 2.5 %collective-permute-start.4 = (bf16[16,4096]{1,0:T(8,128)(2,1)S(1)}, bf16[16,4096]{1,0:T(8,128)(2,1)S(1)}, u32[]{:S(2)}, u32[]{:S(2)}) collective-permute-start(bf16[16,4096]{1,0:T(8,128)(2,1)S(1)} %get-tuple-element.31), channel_id=1, source_target_pairs={{0,1},{1,0},{2,3},{3,2},{6,7},{7,6},{4,5},{5,4},{8,9},{9,8},{10,11... | collective-permute-start | bytes 393224 | tf_op jit(solution)/shard_map/ppermute | solution.py:218
  14.7 2.4 %collective-permute-start.5 = (bf16[16,4096]{1,0:T(8,128)(2,1)S(1)}, bf16[16,4096]{1,0:T(8,128)(2,1)S(1)}, u32[]{:S(2)}, u32[]{:S(2)}) collective-permute-start(bf16[16,4096]{1,0:T(8,128)(2,1)S(1)} %get-tuple-element.32), channel_id=1, source_target_pairs={{0,1},{1,0},{2,3},{3,2},{6,7},{7,6},{4,5},{5,4},{8,9},{9,8},{10,11... | collective-permute-start | bytes 393224 | tf_op jit(solution)/shard_map/ppermute | solution.py:218
  17.1 2.2 %copy-start = (bf16[512,1,4096]{2,0,1:T(8,128)(2,1)S(1)}, bf16[512,1,4096]{2,0,1:T(8,128)(2,1)}, u32[]{:S(2)}) copy-start(bf16[512,1,4096]{2,0,1:T(8,128)(2,1)} %param.5) | copy-start | bytes 12582916
  17.1 2.2 %copy-start.4 = (s32[48]{0:T(128)S(1)}, s32[48]{0:T(128)}, u32[]{:S(2)}) copy-start(s32[48]{0:T(128)} %pairs_ref.3) | copy-start | bytes 580
  21.3 5.7 %collective-permute-start.6 = (bf16[24,512]{1,0:T(8,128)(2,1)S(1)}, bf16[24,512]{1,0:T(8,128)(2,1)S(1)}, u32[]{:S(2)}, u32[]{:S(2)}) collective-permute-start(bf16[24,512]{1,0:T(8,128)(2,1)S(1)} %get-tuple-element.34), channel_id=1, source_target_pairs={{0,8},{8,16},{16,24},{24,0},{1,9},{9,17},{17,25},{25,1},{2,10},{10... | collective-permute-start | bytes 73736 | tf_op jit(solution)/shard_map/ppermute | solution.py:296
  22.9 5.1 %collective-permute-start.7 = (bf16[24,512]{1,0:T(8,128)(2,1)S(1)}, bf16[24,512]{1,0:T(8,128)(2,1)S(1)}, u32[]{:S(2)}, u32[]{:S(2)}) collective-permute-start(bf16[24,512]{1,0:T(8,128)(2,1)S(1)} %get-tuple-element.35), channel_id=1, source_target_pairs={{0,16},{8,24},{16,0},{24,8},{1,17},{9,25},{17,1},{25,9},{2,18},{10... | collective-permute-start | bytes 73736 | tf_op jit(solution)/shard_map/ppermute | solution.py:296
  25.5 3.8 %collective-permute-start.8 = (bf16[24,512]{1,0:T(8,128)(2,1)S(1)}, bf16[24,512]{1,0:T(8,128)(2,1)S(1)}, u32[]{:S(2)}, u32[]{:S(2)}) collective-permute-start(bf16[24,512]{1,0:T(8,128)(2,1)S(1)} %get-tuple-element.36), channel_id=1, source_target_pairs={{0,24},{8,0},{16,8},{24,16},{1,25},{9,1},{17,9},{25,17},{2,26},{10... | collective-permute-start | bytes 73736 | tf_op jit(solution)/shard_map/ppermute | solution.py:296

commit v14 on v13

--- a/solution.py
+++ b/solution.py
@@ -67,7 +67,7 @@
 
 def make_factors(rows, out_ref, in_ref, left_ref, right_ref):
     width, in_width = out_ref.shape[0], in_ref.shape[0]
-    half = left_ref.shape[1] // 2
+    half = left_ref.shape[0] // 2
     span = right_ref.shape[1]
     outs = split_bf16(out_ref[...])
     ins = split_bf16(in_ref[...])
@@ -81,12 +81,12 @@
         for s in range(2):
             pick_rows = (row * 2 + s == row_o).astype(BF16)
             part = jnp.dot(pick_rows, outs[h], preferred_element_type=F32).astype(BF16)
-            start = (2 * h + s) * half
             for t in range(2):
-                pick_cols = (col * 2 + (s ^ t) == col_o).astype(BF16)
+                pick_cols = (col * 2 + t == col_o).astype(BF16)
                 spread = jnp.dot(part, pick_cols, preferred_element_type=F32)
                 tall = jnp.broadcast_to(spread[:, None, :], (half // QBLK, QBLK, half)).reshape(half, half)
-                left_ref[start : start + half, t * half : (t + 1) * half] = jnp.where(same, tall, 0.0).astype(BF16)
+                start = (2 * h + t) * half
+                left_ref[s * half : (s + 1) * half, start : start + half] = jnp.where(same, tall, 0.0).astype(BF16)
     up = (
         lax.broadcasted_iota(jnp.int32, (span, in_width), 0) % in_width
         == lax.broadcasted_iota(jnp.int32, (span, in_width), 1)
@@ -108,46 +108,58 @@
             right_ref[2 * span :] = wide
 
 
-def prepare(blocks, left_ref, right_ref, prep_ref):
+def swap_halves(x):
+    half = x.shape[1] // 2
+    return jnp.concatenate([x[:, half:], x[:, :half]], axis=1)
+
+
+def prepare(blocks, left_ref, right_ref, targets):
     chunks = blocks[0].shape[1] // LANES
-    half = LANES // 2
+    half = chunks * QBLK
+    lower = lax.broadcasted_iota(jnp.int32, (half, LANES), 1) < LANES // 2
+    talls = [
+        jnp.concatenate([block[:, c * LANES : (c + 1) * LANES] for c in range(chunks)], axis=0) for block in blocks
+    ]
     stacked = []
-    for block in blocks:
-        tall = jnp.concatenate([block[:, c * LANES : (c + 1) * LANES] for c in range(chunks)], axis=0)
-        turned = jnp.concatenate([tall[:, half:], tall[:, :half]], axis=1)
-        stacked.append(jnp.concatenate([tall, turned], axis=0))
+    for one, two in (talls[:2], talls[2:]):
+        stacked.append(
+            jnp.concatenate(
+                [jnp.where(lower, one, swap_halves(two)), jnp.where(lower, swap_halves(one), two)], axis=0
+            )
+        )
     stacked = jnp.concatenate(stacked, axis=1)
-    tall = jnp.dot(left_ref[...], stacked, preferred_element_type=F32)
-    quarter = tall.shape[0] // 4
-    parts = [tall[s * quarter : (s + 1) * quarter] + tall[(2 + s) * quarter : (3 + s) * quarter] for s in range(2)]
-    lane = lax.broadcasted_iota(jnp.int32, parts[0].shape, 1) % LANES
-    high, low = split_bf16(jnp.where(lane < half, parts[0], parts[1]))
+    high, low = split_bf16(
+        jnp.dot(left_ref[...], jnp.concatenate([stacked, stacked], axis=0), preferred_element_type=F32)
+    )
     done = jnp.dot(
         jnp.concatenate([high, high, low], axis=1), right_ref[...], preferred_element_type=F32
     ).astype(BF16)
-    for side in range(2):
-        for c in range(chunks):
-            prep_ref[side, :, c * LANES : (c + 1) * LANES] = done[
-                c * QBLK : (c + 1) * QBLK, side * LANES : (side + 1) * LANES
-            ]
-
-
-def first_kernel(rows, out_ref, in_ref, far_ref, swap_ref, left_ref, right_ref, prep_ref):
+    for pair in range(2):
+        even = done[:half, pair * LANES : (pair + 1) * LANES]
+        odd = done[half:, pair * LANES : (pair + 1) * LANES]
+        for value, (ref, index) in zip(
+            (jnp.where(lower, even, swap_halves(odd)), jnp.where(lower, swap_halves(even), odd)),
+            targets[2 * pair : 2 * pair + 2],
+        ):
+            for c in range(chunks):
+                ref[index, :, c * LANES : (c + 1) * LANES] = value[c * QBLK : (c + 1) * QBLK]
+
+
+def first_kernel(rows, out_ref, in_ref, own_far_ref, own_ref, swap_ref, left_ref, right_ref, far_ref, self_ref):
     make_factors(rows, out_ref, in_ref, left_ref, right_ref)
-    prepare((far_ref[...], swap_ref[QBLK:]), left_ref, right_ref, prep_ref)
-
-
-def self_kernel(left_ref, right_ref, self_ref, swap_ref, prep_ref):
-    prepare((self_ref[...], swap_ref[:QBLK]), left_ref, right_ref, prep_ref)
-
-
-def near_kernel(left_ref, right_ref, done_ref, *refs):
+    blocks = [own_far_ref[...], swap_ref[QBLK:], own_ref[...], swap_ref[:QBLK]]
+    prepare(blocks, left_ref, right_ref, [(far_ref, 0), (far_ref, 1), (self_ref, 0), (self_ref, 1)])
+
+
+def near_kernel(left_ref, right_ref, self_ref, *refs):
     prep_ref = refs[-1]
-    done = done_ref.shape[0]
-    prep_ref[:done] = done_ref[...]
+    prep_ref[:2] = self_ref[...]
     blocks = [ref[:QBLK] for ref in refs[:-1]]
-    for index in range(0, len(blocks), 2):
-        prepare(blocks[index : index + 2], left_ref, right_ref, prep_ref.at[pl.ds(done + index, 2)])
+    targets = [(prep_ref, 2 + index) for index in range(len(blocks))]
+    for start in range(0, len(blocks), 4):
+        pick = slice(start, start + 4) if start + 4 <= len(blocks) else slice(-2, None)
+        times = 1 if start + 4 <= len(blocks) else 2
+        prepare(blocks[pick] * times, left_ref, right_ref, targets[pick] * times)
 
 
 def last_kernel(order, layer, held, slots, pairs_ref, late_ref, early_ref, train_ref, *refs):
@@ -234,33 +246,25 @@
     brief = pl.CostEstimate(flops=1000, bytes_accessed=1000, transcendentals=0)
     stack = features // LANES * QBLK
     span = 2 * LANES
-    left, right, far = pl.pallas_call(
+    def prepared(count):
+        return jax.ShapeDtypeStruct((count, QBLK, features), BF16)
+
+    left, right, far, early = pl.pallas_call(
         functools.partial(first_kernel, rows),
         out_shape=[
-            jax.ShapeDtypeStruct((4 * stack, 2 * stack), BF16),
+            jax.ShapeDtypeStruct((2 * stack, 4 * stack), BF16),
             jax.ShapeDtypeStruct((3 * span, span), BF16),
-            jax.ShapeDtypeStruct((2, QBLK, features), BF16),
+            prepared(2),
+            prepared(2),
         ],
-        in_specs=[VMEM] * 4,
-        out_specs=[VMEM] * 3,
+        in_specs=[VMEM] * 5,
+        out_specs=[VMEM] * 4,
         compiler_params=limit,
         name="first",
         cost_estimate=brief,
-    )(out_factor, in_factor, far_block, swap)
+    )(out_factor, in_factor, far_block, self_block, swap)
     far = pass_on(far, order[-1])
 
-    def prepared(count):
-        return jax.ShapeDtypeStruct((count, QBLK, features), BF16)
-
-    early = pl.pallas_call(
-        self_kernel,
-        out_shape=prepared(2),
-        in_specs=[VMEM] * 4,
-        out_specs=VMEM,
-        compiler_params=limit,
-        name="self",
-        cost_estimate=brief,
-    )(left, right, self_block, swap)
     _, *ready = lax.optimization_barrier((early, *raw))
     crossed = pl.pallas_call(
         cross_kernel,
@@ -271,16 +275,15 @@
         name="cross",
     )(*ready)
     crossed = [pass_on(array, 0, 1) for array in crossed]
-    for name, blocks in (("near", raw), ("crossed", crossed)):
-        early = pl.pallas_call(
-            near_kernel,
-            out_shape=prepared(early.shape[0] + len(raw)),
-            in_specs=[VMEM] * (3 + len(blocks)),
-            out_specs=VMEM,
-            compiler_params=limit,
-            name=name,
-            cost_estimate=brief,
-        )(left, right, early, *blocks)
+    early = pl.pallas_call(
+        near_kernel,
+        out_shape=prepared(ex - 2),
+        in_specs=[VMEM] * (3 + 2 * len(raw)),
+        out_specs=VMEM,
+        compiler_params=limit,
+        name="near",
+        cost_estimate=brief,
+    )(left, right, early, *raw, *crossed)
     parts = pl.pallas_call(
         functools.partial(last_kernel, order, layer, held, slots),
         out_shape=[jax.ShapeDtypeStruct((slots * rows, train_rows), F32)]

time: 30.2 us -> 30.1 us (level)
  waiting for transfers between devices: 3.76 us -> 6.34 us
  Pallas kernels: 12.1 us -> 9.56 us
    pallas_call x3 -> x1, Pallas kernels: 5.57 us -> 2.45 us  [shards(): pl.pallas_call(near_kernel, out_shape=prepared(ex - 2), in_specs=[VMEM] *...]
    ppermute x6, waiting for transfers between devices: 1.28 us -> 3.86 us  [pass_on(): lax.ppermute(array, 'ex', [(2 * a + c, 2 * b + (c ^ flip)) for a, b in mo...]
    pallas_call x1, Pallas kernels: 3.16 us -> 3.76 us  [shards(): pl.pallas_call(functools.partial(first_kernel, rows), out_shape=[jax.Shap...]
    unnamed x12 -> x10, local copies, waits for them, and re-layouts: 1.78 us -> 1.72 us
  transfers between devices with their start and end apart: 9 -> 9, of which waited for: 5 -> 8; matrix products, arithmetic and copies ran while one was open for 0% -> 0% of each run, Pallas kernels for 29% -> 21%
where the time goes in v14:
time: 30.1 us; the launch traced here: 29.9 us
  starting transfers between devices  12.3 us (41%)
  Pallas kernels  9.56 us (32%)
  waiting for transfers between devices  6.34 us (21%)
  local copies, waits for them, and re-layouts  1.72 us (6%)
    ppermute x6, starting transfers between devices, pass_on(): lax.ppermute(array, 'ex', [(2 * a + c, 2 * b + (c ^ flip)) for a, b in mo...  6.69 us
    ppermute x3, starting transfers between devices, shards(): lax.ppermute(parts[m], 'layer', [(i, (i + m) % layer) for i in range(laye...  5.56 us
    ppermute x6, waiting for transfers between devices, pass_on(): lax.ppermute(array, 'ex', [(2 * a + c, 2 * b + (c ^ flip)) for a, b in mo...  3.86 us
    pallas_call x1, Pallas kernels, shards(): pl.pallas_call(functools.partial(first_kernel, rows), out_shape=[jax.Shap...  3.76 us
    ppermute x3, waiting for transfers between devices, shards(): lax.ppermute(parts[m], 'layer', [(i, (i + m) % layer) for i in range(laye...  2.48 us
    pallas_call x1, Pallas kernels, shards(): pl.pallas_call(near_kernel, out_shape=prepared(ex - 2), in_specs=[VMEM] *...  2.45 us
    pallas_call x1, Pallas kernels, shards(): pl.pallas_call(functools.partial(last_kernel, order, layer, held, slots),...  2.03 us
    unnamed x10, local copies, waits for them, and re-layouts  1.72 us
  transfers between devices with their start and end apart: 9, of which 8 were waited for; matrix products, arithmetic and copies ran while one was open for 0% of the time, Pallas kernels for 21%

profile of v14, /device:TPU:0, one launch (start us, length us, event | category | flops | bytes accessed | tf_op | source)
XLA Modules:
  0.0 29.9 jit_solution(12679770701099600584)
XLA Ops:
  0.0 0.0 copy-start.1
  0.0 0.0 copy-start.2
  0.0 0.0 copy-start.3
  0.0 0.7 %copy-done.3 = s32[48]{0:T(128)S(1)} copy-done((s32[48]{0:T(128)S(1)}, s32[48]{0:T(128)}, u32[]{:S(2)}) %copy-start.3) | copy-done | bytes 216
  0.7 0.0 copy-start.4
  0.7 1.0 %copy-done.4 = bf16[64,1,4096]{2,0,1:T(8,128)(2,1)S(1)} copy-done((bf16[64,1,4096]{2,0,1:T(8,128)(2,1)S(1)}, bf16[64,1,4096]{2,0,1:T(8,128)(2,1)}, u32[]{:S(2)}) %copy-start.4) | copy-done | bytes 524312
  1.7 0.7 %pick.1 = (bf16[16,4096]{1,0:T(8,128)(2,1)S(1)}, bf16[16,4096]{1,0:T(8,128)(2,1)S(1)}, bf16[32,4096]{1,0:T(8,128)(2,1)S(1)}, bf16[32,4096]{1,0:T(8,128)(2,1)S(1)}, bf16[32,4096]{1,0:T(8,128)(2,1)S(1)}) custom-call(s32[48]{0:T(128)S(1)} %copy-done.3, bf16[64,4096]{1,0:T(8,128)(2,1)S(1)} %bitcast.8), custom_call_target="tpu_custom_call" | custom-call | flops 2000000000 | bytes 1000 | tf_op jit(solution)/shard_map/pick/pallas_call | solution.py:234
  2.4 0.0 copy-start
  2.4 0.5 %collective-permute-start = (bf16[32,4096]{1,0:T(8,128)(2,1)S(1)}, bf16[32,4096]{1,0:T(8,128)(2,1)S(1)}, u32[]{:S(2)}, u32[]{:S(2)}) collective-permute-start(bf16[32,4096]{1,0:T(8,128)(2,1)S(1)} %get-tuple-element.24), channel_id=1, source_target_pairs={{0,1},{1,0},{2,3},{3,2},{6,7},{7,6},{4,5},{5,4},{8,9},{9,8},{10,11... | collective-permute-start | bytes 786440 | tf_op jit(solution)/shard_map/ppermute | solution.py:230
  2.9 2.6 %collective-permute-start.2 = (bf16[32,4096]{1,0:T(8,128)(2,1)S(1)}, bf16[32,4096]{1,0:T(8,128)(2,1)S(1)}, u32[]{:S(2)}, u32[]{:S(2)}) collective-permute-start(bf16[32,4096]{1,0:T(8,128)(2,1)S(1)} %get-tuple-element.29), channel_id=1, source_target_pairs={{0,2},{1,3},{2,6},{3,7},{6,4},{7,5},{4,0},{5,1},{8,10},{9,11},{10,... | collective-permute-start | bytes 786440 | tf_op jit(solution)/shard_map/ppermute | solution.py:230
  5.5 0.1 collective-permute-start.3
  5.6 0.0 collective-permute-done.swap_ref
  5.6 0.0 copy-done.1
  5.6 0.0 copy-done.2
  5.6 3.8 %first.1 = (bf16[1024,2048]{1,0:T(8,128)(2,1)S(1)}, bf16[768,256]{1,0:T(8,128)(2,1)S(1)}, bf16[2,16,4096]{2,1,0:T(8,128)(2,1)S(1)}, bf16[2,16,4096]{2,1,0:T(8,128)(2,1)S(1)}) custom-call(f32[64,64]{1,0:T(8,128)S(1)} %bitcast.6, f32[64,64]{1,0:T(8,128)S(1)} %bitcast.7, bf16[16,4096]{1,0:T(8,128)(2,1)S(1)} %get-tuple-element.22.own_far_ref, ...), custom_call_target="tpu_custom_call" | custom-call | flops 1000 | bytes 1000 | tf_op jit(solution)/shard_map/first/pallas_call | solution.py:252
  9.4 2.9 %collective-permute-start.1 = (bf16[2,16,4096]{2,1,0:T(8,128)(2,1)S(1)}, bf16[2,16,4096]{2,1,0:T(8,128)(2,1)S(1)}, u32[]{:S(2)}, u32[]{:S(2)}) collective-permute-start(bf16[2,16,4096]{2,1,0:T(8,128)(2,1)S(1)} %get-tuple-element.25), channel_id=1, source_target_pairs={{0,6},{1,7},{2,4},{3,5},{6,0},{7,1},{4,2},{5,3},{8,14},{9,15},{10,... | collective-permute-start | bytes 786440 | tf_op jit(solution)/shard_map/ppermute | solution.py:230
  12.3 0.1 collective-permute-done.2.refs_0_
  12.4 1.9 %collective-permute-done.3.refs_1_ = bf16[32,4096]{1,0:T(8,128)(2,1)S(1)} collective-permute-done((bf16[32,4096]{1,0:T(8,128)(2,1)S(1)}, bf16[32,4096]{1,0:T(8,128)(2,1)S(1)}, u32[]{:S(2)}, u32[]{:S(2)}) %collective-permute-start.3) | collective-permute-done | bytes 262176 | tf_op jit(solution)/shard_map/ppermute | solution.py:230
  14.4 0.1 collective-permute-start.4
  14.4 0.5 %collective-permute-start.5 = (bf16[16,4096]{1,0:T(8,128)(2,1)S(1)}, bf16[16,4096]{1,0:T(8,128)(2,1)S(1)}, u32[]{:S(2)}, u32[]{:S(2)}) collective-permute-start(bf16[16,4096]{1,0:T(8,128)(2,1)S(1)} %get-tuple-element.34), channel_id=1, source_target_pairs={{0,1},{1,0},{2,3},{3,2},{6,7},{7,6},{4,5},{5,4},{8,9},{9,8},{10,11... | collective-permute-start | bytes 393224 | tf_op jit(solution)/shard_map/ppermute | solution.py:230
  14.9 0.8 %collective-permute-done.4.refs_2_ = bf16[16,4096]{1,0:T(8,128)(2,1)S(1)} collective-permute-done((bf16[16,4096]{1,0:T(8,128)(2,1)S(1)}, bf16[16,4096]{1,0:T(8,128)(2,1)S(1)}, u32[]{:S(2)}, u32[]{:S(2)}) %collective-permute-start.4) | collective-permute-done | bytes 131104 | tf_op jit(solution)/shard_map/ppermute | solution.py:230
  15.8 0.2 collective-permute-done.5.refs_3_
  16.0 2.4 %near.1.early_ref = bf16[6,16,4096]{2,1,0:T(8,128)(2,1)S(1)} custom-call(bf16[1024,2048]{1,0:T(8,128)(2,1)S(1)} %get-tuple-element.26.left_ref, bf16[768,256]{1,0:T(8,128)(2,1)S(1)} %get-tuple-element.27.right_ref, bf16[2,16,4096]{2,1,0:T(8,128)(2,1)S(1)} %get-tuple-element.28.self_ref, bf16[32,4096]{1,0:T(8,128)(2,1)S(1)} %collective-permute-done.2.refs_0_, ...), custom_call_target="tpu_custom_call" | custom-call | flops 1000 | bytes 1000 | tf_op jit(solution)/shard_map/near/pallas_call | solution.py:278
  18.4 0.8 %collective-permute-done.1.late_ref = bf16[2,16,4096]{2,1,0:T(8,128)(2,1)S(1)} collective-permute-done((bf16[2,16,4096]{2,1,0:T(8,128)(2,1)S(1)}, bf16[2,16,4096]{2,1,0:T(8,128)(2,1)S(1)}, u32[]{:S(2)}, u32[]{:S(2)}) %collective-permute-start.1) | collective-permute-done | bytes 262176 | tf_op jit(solution)/shard_map/ppermute | solution.py:230
  19.2 0.0 copy-done
  19.2 2.0 %last.1 = (f32[24,512]{1,0:T(8,128)S(1)}, bf16[24,512]{1,0:T(8,128)(2,1)S(1)}, bf16[24,512]{1,0:T(8,128)(2,1)S(1)}, bf16[24,512]{1,0:T(8,128)(2,1)S(1)}) custom-call(s32[48]{0:T(128)S(1)} %copy-done.3, bf16[2,16,4096]{2,1,0:T(8,128)(2,1)S(1)} %collective-permute-done.1.late_ref, bf16[6,16,4096]{2,1,0:T(8,128)(2,1)S(1)} %near.1.early_ref, ...), custom_call_target="tpu_custom_call" | custom-call | tf_op jit(solution)/shard_map/last/pallas_call | solution.py:287
  21.2 1.6 %collective-permute-start.6 = (bf16[24,512]{1,0:T(8,128)(2,1)S(1)}, bf16[24,512]{1,0:T(8,128)(2,1)S(1)}, u32[]{:S(2)}, u32[]{:S(2)}) collective-permute-start(bf16[24,512]{1,0:T(8,128)(2,1)S(1)} %get-tuple-element.36), channel_id=1, source_target_pairs={{0,8},{8,16},{16,24},{24,0},{1,9},{9,17},{17,25},{25,1},{2,10},{10... | collective-permute-start | bytes 73736 | tf_op jit(solution)/shard_map/ppermute | solution.py:299
  22.9 2.6 %collective-permute-start.7 = (bf16[24,512]{1,0:T(8,128)(2,1)S(1)}, bf16[24,512]{1,0:T(8,128)(2,1)S(1)}, u32[]{:S(2)}, u32[]{:S(2)}) collective-permute-start(bf16[24,512]{1,0:T(8,128)(2,1)S(1)} %get-tuple-element.37), channel_id=1, source_target_pairs={{0,16},{8,24},{16,0},{24,8},{1,17},{9,25},{17,1},{25,9},{2,18},{10... | collective-permute-start | bytes 73736 | tf_op jit(solution)/shard_map/ppermute | solution.py:299
  25.5 1.3 %collective-permute-start.8 = (bf16[24,512]{1,0:T(8,128)(2,1)S(1)}, bf16[24,512]{1,0:T(8,128)(2,1)S(1)}, u32[]{:S(2)}, u32[]{:S(2)}) collective-permute-start(bf16[24,512]{1,0:T(8,128)(2,1)S(1)} %get-tuple-element.38), channel_id=1, source_target_pairs={{0,24},{8,0},{16,8},{24,16},{1,25},{9,1},{17,9},{25,17},{2,26},{10... | collective-permute-start | bytes 73736 | tf_op jit(solution)/shard_map/ppermute | solution.py:299
  26.8 0.4 %collective-permute-done.6.refs_1_ = bf16[24,512]{1,0:T(8,128)(2,1)S(1)} collective-permute-done((bf16[24,512]{1,0:T(8,128)(2,1)S(1)}, bf16[24,512]{1,0:T(8,128)(2,1)S(1)}, u32[]{:S(2)}, u32[]{:S(2)}) %collective-permute-start.6) | collective-permute-done | bytes 24608 | tf_op jit(solution)/shard_map/ppermute | solution.py:299
  27.2 0.5 %collective-permute-done.7.refs_2_ = bf16[24,512]{1,0:T(8,128)(2,1)S(1)} collective-permute-done((bf16[24,512]{1,0:T(8,128)(2,1)S(1)}, bf16[24,512]{1,0:T(8,128)(2,1)S(1)}, u32[]{:S(2)}, u32[]{:S(2)}) %collective-permute-start.7) | collective-permute-done | bytes 24608 | tf_op jit(solution)/shard_map/ppermute | solution.py:299
  27.7 1.6 %collective-permute-done.8.refs_3_ = bf16[24,512]{1,0:T(8,128)(2,1)S(1)} collective-permute-done((bf16[24,512]{1,0:T(8,128)(2,1)S(1)}, bf16[24,512]{1,0:T(8,128)(2,1)S(1)}, u32[]{:S(2)}, u32[]{:S(2)}) %collective-permute-start.8) | collective-permute-done | bytes 24608 | tf_op jit(solution)/shard_map/ppermute | solution.py:299
  29.3 0.6 %finish.1 = f32[6,4,512]{2,1,0:T(4,128)} custom-call(f32[24,512]{1,0:T(8,128)S(1)} %get-tuple-element.35.refs_0_, bf16[24,512]{1,0:T(8,128)(2,1)S(1)} %collective-permute-done.6.refs_1_, bf16[24,512]{1,0:T(8,128)(2,1)S(1)} %collective-permute-done.7.refs_2_, bf16[24,512]{1,0:T(8,128)(2,1)S(1)} %collective-permute-done.8.refs_3_), custom_call_target="tpu_custom_call" | custom-call | tf_op jit(solution)/shard_map/finish/pallas_call | solution.py:301
  (1 shorter events, 0.0 us)
Async XLA Ops:
  0.0 5.6 %copy-start.1 = (f32[1,64,64]{2,1,0:T(8,128)S(1)}, f32[1,64,64]{2,1,0:T(8,128)}, u32[]{:S(2)}) copy-start(f32[1,64,64]{2,1,0:T(8,128)} %param.8) | copy-start | bytes 49156
  0.0 5.6 %copy-start.2 = (f32[1,64,64]{2,1,0:T(8,128)S(1)}, f32[1,64,64]{2,1,0:T(8,128)}, u32[]{:S(2)}) copy-start(f32[1,64,64]{2,1,0:T(8,128)} %param.7) | copy-start | bytes 49156
  0.0 0.7 %copy-start.3 = (s32[48]{0:T(128)S(1)}, s32[48]{0:T(128)}, u32[]{:S(2)}) copy-start(s32[48]{0:T(128)} %pairs_ref.3) | copy-start | bytes 580
  0.7 1.0 %copy-start.4 = (bf16[64,1,4096]{2,0,1:T(8,128)(2,1)S(1)}, bf16[64,1,4096]{2,0,1:T(8,128)(2,1)}, u32[]{:S(2)}) copy-start(bf16[64,1,4096]{2,0,1:T(8,128)(2,1)} %param.6) | copy-start | bytes 1572868
  2.4 16.8 %copy-start = (bf16[512,1,4096]{2,0,1:T(8,128)(2,1)S(1)}, bf16[512,1,4096]{2,0,1:T(8,128)(2,1)}, u32[]{:S(2)}) copy-start(bf16[512,1,4096]{2,0,1:T(8,128)(2,1)} %param.5) | copy-start | bytes 12582916
  2.4 3.2 %collective-permute-start = (bf16[32,4096]{1,0:T(8,128)(2,1)S(1)}, bf16[32,4096]{1,0:T(8,128)(2,1)S(1)}, u32[]{:S(2)}, u32[]{:S(2)}) collective-permute-start(bf16[32,4096]{1,0:T(8,128)(2,1)S(1)} %get-tuple-element.24), channel_id=1, source_target_pairs={{0,1},{1,0},{2,3},{3,2},{6,7},{7,6},{4,5},{5,4},{8,9},{9,8},{10,11... | collective-permute-start | bytes 786440 | tf_op jit(solution)/shard_map/ppermute | solution.py:230
  2.9 9.5 %collective-permute-start.2 = (bf16[32,4096]{1,0:T(8,128)(2,1)S(1)}, bf16[32,4096]{1,0:T(8,128)(2,1)S(1)}, u32[]{:S(2)}, u32[]{:S(2)}) collective-permute-start(bf16[32,4096]{1,0:T(8,128)(2,1)S(1)} %get-tuple-element.29), channel_id=1, source_target_pairs={{0,2},{1,3},{2,6},{3,7},{6,4},{7,5},{4,0},{5,1},{8,10},{9,11},{10,... | collective-permute-start | bytes 786440 | tf_op jit(solution)/shard_map/ppermute | solution.py:230
  5.5 8.9 %collective-permute-start.3 = (bf16[32,4096]{1,0:T(8,128)(2,1)S(1)}, bf16[32,4096]{1,0:T(8,128)(2,1)S(1)}, u32[]{:S(2)}, u32[]{:S(2)}) collective-permute-start(bf16[32,4096]{1,0:T(8,128)(2,1)S(1)} %get-tuple-element.30), channel_id=1, source_target_pairs={{0,4},{1,5},{2,0},{3,1},{6,2},{7,3},{4,6},{5,7},{8,12},{9,13},{10,... | collective-permute-start | bytes 786440 | tf_op jit(solution)/shard_map/ppermute | solution.py:230
  9.4 9.9 %collective-permute-start.1 = (bf16[2,16,4096]{2,1,0:T(8,128)(2,1)S(1)}, bf16[2,16,4096]{2,1,0:T(8,128)(2,1)S(1)}, u32[]{:S(2)}, u32[]{:S(2)}) collective-permute-start(bf16[2,16,4096]{2,1,0:T(8,128)(2,1)S(1)} %get-tuple-element.25), channel_id=1, source_target_pairs={{0,6},{1,7},{2,4},{3,5},{6,0},{7,1},{4,2},{5,3},{8,14},{9,15},{10,... | collective-permute-start | bytes 786440 | tf_op jit(solution)/shard_map/ppermute | solution.py:230
  14.4 1.4 %collective-permute-start.4 = (bf16[16,4096]{1,0:T(8,128)(2,1)S(1)}, bf16[16,4096]{1,0:T(8,128)(2,1)S(1)}, u32[]{:S(2)}, u32[]{:S(2)}) collective-permute-start(bf16[16,4096]{1,0:T(8,128)(2,1)S(1)} %get-tuple-element.33), channel_id=1, source_target_pairs={{0,1},{1,0},{2,3},{3,2},{6,7},{7,6},{4,5},{5,4},{8,9},{9,8},{10,11... | collective-permute-start | bytes 393224 | tf_op jit(solution)/shard_map/ppermute | solution.py:230
  14.4 1.5 %collective-permute-start.5 = (bf16[16,4096]{1,0:T(8,128)(2,1)S(1)}, bf16[16,4096]{1,0:T(8,128)(2,1)S(1)}, u32[]{:S(2)}, u32[]{:S(2)}) collective-permute-start(bf16[16,4096]{1,0:T(8,128)(2,1)S(1)} %get-tuple-element.34), channel_id=1, source_target_pairs={{0,1},{1,0},{2,3},{3,2},{6,7},{7,6},{4,5},{5,4},{8,9},{9,8},{10,11... | collective-permute-start | bytes 393224 | tf_op jit(solution)/shard_map/ppermute | solution.py:230
  21.2 6.0 %collective-permute-start.6 = (bf16[24,512]{1,0:T(8,128)(2,1)S(1)}, bf16[24,512]{1,0:T(8,128)(2,1)S(1)}, u32[]{:S(2)}, u32[]{:S(2)}) collective-permute-start(bf16[24,512]{1,0:T(8,128)(2,1)S(1)} %get-tuple-element.36), channel_id=1, source_target_pairs={{0,8},{8,16},{16,24},{24,0},{1,9},{9,17},{17,25},{25,1},{2,10},{10... | collective-permute-start | bytes 73736 | tf_op jit(solution)/shard_map/ppermute | solution.py:299
  22.9 4.8 %collective-permute-start.7 = (bf16[24,512]{1,0:T(8,128)(2,1)S(1)}, bf16[24,512]{1,0:T(8,128)(2,1)S(1)}, u32[]{:S(2)}, u32[]{:S(2)}) collective-permute-start(bf16[24,512]{1,0:T(8,128)(2,1)S(1)} %get-tuple-element.37), channel_id=1, source_target_pairs={{0,16},{8,24},{16,0},{24,8},{1,17},{9,25},{17,1},{25,9},{2,18},{10... | collective-permute-start | bytes 73736 | tf_op jit(solution)/shard_map/ppermute | solution.py:299
  25.5 3.8 %collective-permute-start.8 = (bf16[24,512]{1,0:T(8,128)(2,1)S(1)}, bf16[24,512]{1,0:T(8,128)(2,1)S(1)}, u32[]{:S(2)}, u32[]{:S(2)}) collective-permute-start(bf16[24,512]{1,0:T(8,128)(2,1)S(1)} %get-tuple-element.38), channel_id=1, source_target_pairs={{0,24},{8,0},{16,8},{24,16},{1,25},{9,1},{17,9},{25,17},{2,26},{10... | collective-permute-start | bytes 73736 | tf_op jit(solution)/shard_map/ppermute | solution.py:299

commit v15 on v13

--- a/solution.py
+++ b/solution.py
@@ -261,6 +261,18 @@
         name="self",
         cost_estimate=brief,
     )(left, right, self_block, swap)
+    def near_work(name, early, blocks):
+        return pl.pallas_call(
+            near_kernel,
+            out_shape=prepared(early.shape[0] + len(blocks)),
+            in_specs=[VMEM] * (3 + len(blocks)),
+            out_specs=VMEM,
+            compiler_params=limit,
+            name=name,
+            cost_estimate=brief,
+        )(left, right, early, *blocks)
+
+    early = near_work("near", early, raw)
     _, *ready = lax.optimization_barrier((early, *raw))
     crossed = pl.pallas_call(
         cross_kernel,
@@ -271,16 +283,7 @@
         name="cross",
     )(*ready)
     crossed = [pass_on(array, 0, 1) for array in crossed]
-    for name, blocks in (("near", raw), ("crossed", crossed)):
-        early = pl.pallas_call(
-            near_kernel,
-            out_shape=prepared(early.shape[0] + len(raw)),
-            in_specs=[VMEM] * (3 + len(blocks)),
-            out_specs=VMEM,
-            compiler_params=limit,
-            name=name,
-            cost_estimate=brief,
-        )(left, right, early, *blocks)
+    early = near_work("crossed", early, crossed)
     parts = pl.pallas_call(
         functools.partial(last_kernel, order, layer, held, slots),
         out_shape=[jax.ShapeDtypeStruct((slots * rows, train_rows), F32)]

time: 30.2 us -> 30.9 us (1.023)
  waiting for transfers between devices: 3.76 us -> 4.55 us
    ppermute x6, waiting for transfers between devices: 1.28 us -> 2.08 us  [pass_on(): lax.ppermute(array, 'ex', [(2 * a + c, 2 * b + (c ^ flip)) for a, b in mo...]
  transfers between devices with their start and end apart: 9 -> 9, of which waited for: 5 -> 6; matrix products, arithmetic and copies ran while one was open for 0% -> 0% of each run, Pallas kernels for 29% -> 29%
where the time goes in v15:
time: 30.9 us; the launch traced here: 30.7 us
  starting transfers between devices  12.2 us (39%)
  Pallas kernels  12.1 us (39%)
  waiting for transfers between devices  4.55 us (15%)
  local copies, waits for them, and re-layouts  1.72 us (6%)
    ppermute x6, starting transfers between devices, pass_on(): lax.ppermute(array, 'ex', [(2 * a + c, 2 * b + (c ^ flip)) for a, b in mo...  6.68 us
    ppermute x3, starting transfers between devices, shards(): lax.ppermute(parts[m], 'layer', [(i, (i + m) % layer) for i in range(laye...  5.56 us
    pallas_call x2, Pallas kernels, near_work(): pl.pallas_call(near_kernel, out_shape=prepared(early.shape[0] + len(block...  3.72 us
    pallas_call x1, Pallas kernels, shards(): pl.pallas_call(functools.partial(first_kernel, rows), out_shape=[jax.Shap...  3.16 us
    ppermute x3, waiting for transfers between devices, shards(): lax.ppermute(parts[m], 'layer', [(i, (i + m) % layer) for i in range(laye...  2.48 us
    ppermute x6, waiting for transfers between devices, pass_on(): lax.ppermute(array, 'ex', [(2 * a + c, 2 * b + (c ^ flip)) for a, b in mo...  2.08 us
    pallas_call x1, Pallas kernels, shards(): pl.pallas_call(functools.partial(last_kernel, order, layer, held, slots),...  2.03 us
    pallas_call x1, Pallas kernels, shards(): pl.pallas_call(self_kernel, out_shape=prepared(2), in_specs=[VMEM] * 4, o...  1.86 us
  transfers between devices with their start and end apart: 9, of which 6 were waited for; matrix products, arithmetic and copies ran while one was open for 0% of the time, Pallas kernels for 29%

profile of v15, /device:TPU:0, one launch (start us, length us, event | category | flops | bytes accessed | tf_op | source)
XLA Modules:
  0.0 30.7 jit_solution(6404888619268926400)
XLA Ops:
  0.0 0.0 copy-start.1
  0.0 0.0 copy-start.2
  0.0 0.0 copy-start.3
  0.0 0.7 %copy-done.3 = s32[48]{0:T(128)S(1)} copy-done((s32[48]{0:T(128)S(1)}, s32[48]{0:T(128)}, u32[]{:S(2)}) %copy-start.3) | copy-done | bytes 216
  0.7 0.0 copy-start.5
  0.7 1.0 %copy-done.5 = bf16[64,1,4096]{2,0,1:T(8,128)(2,1)S(1)} copy-done((bf16[64,1,4096]{2,0,1:T(8,128)(2,1)S(1)}, bf16[64,1,4096]{2,0,1:T(8,128)(2,1)}, u32[]{:S(2)}) %copy-start.5) | copy-done | bytes 524312
  1.7 0.7 %pick.1 = (bf16[16,4096]{1,0:T(8,128)(2,1)S(1)}, bf16[16,4096]{1,0:T(8,128)(2,1)S(1)}, bf16[32,4096]{1,0:T(8,128)(2,1)S(1)}, bf16[32,4096]{1,0:T(8,128)(2,1)S(1)}, bf16[32,4096]{1,0:T(8,128)(2,1)S(1)}) custom-call(s32[48]{0:T(128)S(1)} %copy-done.3, bf16[64,4096]{1,0:T(8,128)(2,1)S(1)} %bitcast.8), custom_call_target="tpu_custom_call" | custom-call | flops 2000000000 | bytes 1000 | tf_op jit(solution)/shard_map/pick/pallas_call | solution.py:222
  2.4 0.5 %collective-permute-start = (bf16[32,4096]{1,0:T(8,128)(2,1)S(1)}, bf16[32,4096]{1,0:T(8,128)(2,1)S(1)}, u32[]{:S(2)}, u32[]{:S(2)}) collective-permute-start(bf16[32,4096]{1,0:T(8,128)(2,1)S(1)} %get-tuple-element.22), channel_id=1, source_target_pairs={{0,1},{1,0},{2,3},{3,2},{6,7},{7,6},{4,5},{5,4},{8,9},{9,8},{10,11... | collective-permute-start | bytes 786440 | tf_op jit(solution)/shard_map/ppermute | solution.py:218
  2.9 2.6 %collective-permute-start.2 = (bf16[32,4096]{1,0:T(8,128)(2,1)S(1)}, bf16[32,4096]{1,0:T(8,128)(2,1)S(1)}, u32[]{:S(2)}, u32[]{:S(2)}) collective-permute-start(bf16[32,4096]{1,0:T(8,128)(2,1)S(1)} %get-tuple-element.27), channel_id=1, source_target_pairs={{0,2},{1,3},{2,6},{3,7},{6,4},{7,5},{4,0},{5,1},{8,10},{9,11},{10,... | collective-permute-start | bytes 786440 | tf_op jit(solution)/shard_map/ppermute | solution.py:218
  5.5 0.1 collective-permute-start.3
  5.6 0.0 collective-permute-done.swap_ref
  5.6 0.0 copy-done.1
  5.6 0.0 copy-done.2
  5.6 3.2 %first.1 = (bf16[2048,1024]{1,0:T(8,128)(2,1)S(1)}, bf16[768,256]{1,0:T(8,128)(2,1)S(1)}, bf16[2,16,4096]{2,1,0:T(8,128)(2,1)S(1)}) custom-call(f32[64,64]{1,0:T(8,128)S(1)} %bitcast.6, f32[64,64]{1,0:T(8,128)S(1)} %bitcast.7, bf16[16,4096]{1,0:T(8,128)(2,1)S(1)} %get-tuple-element.21.far_ref, bf16[32,4096]{1,0:T(8,128)(2,1)S(1)} %collective-permute-done.swap_ref), custom_call_target="tpu_custom_call" | custom-call | flops 1000 | bytes 1000 | tf_op jit(solution)/shard_map/first/pallas_call | solution.py:237
  8.8 2.9 %collective-permute-start.1 = (bf16[2,16,4096]{2,1,0:T(8,128)(2,1)S(1)}, bf16[2,16,4096]{2,1,0:T(8,128)(2,1)S(1)}, u32[]{:S(2)}, u32[]{:S(2)}) collective-permute-start(bf16[2,16,4096]{2,1,0:T(8,128)(2,1)S(1)} %get-tuple-element.23), channel_id=1, source_target_pairs={{0,6},{1,7},{2,4},{3,5},{6,0},{7,1},{4,2},{5,3},{8,14},{9,15},{10,... | collective-permute-start | bytes 786440 | tf_op jit(solution)/shard_map/ppermute | solution.py:218
  11.7 1.9 %self.1.done_ref = bf16[2,16,4096]{2,1,0:T(8,128)(2,1)S(1)} custom-call(bf16[2048,1024]{1,0:T(8,128)(2,1)S(1)} %get-tuple-element.24.left_ref, bf16[768,256]{1,0:T(8,128)(2,1)S(1)} %get-tuple-element.25.right_ref, bf16[16,4096]{1,0:T(8,128)(2,1)S(1)} %get-tuple-element.26.self_ref, bf16[32,4096]{1,0:T(8,128)(2,1)S(1)} %collective-permute-done.swap_ref), custom_call_target="tpu_custom_call" | custom-call | flops 1000 | bytes 1000 | tf_op jit(solution)/shard_map/self/pallas_call | solution.py:255
  13.6 0.0 collective-permute-done.2.refs_0_
  13.6 1.0 %collective-permute-done.3.refs_1_ = bf16[32,4096]{1,0:T(8,128)(2,1)S(1)} collective-permute-done((bf16[32,4096]{1,0:T(8,128)(2,1)S(1)}, bf16[32,4096]{1,0:T(8,128)(2,1)S(1)}, u32[]{:S(2)}, u32[]{:S(2)}) %collective-permute-start.3) | collective-permute-done | bytes 262176 | tf_op jit(solution)/shard_map/ppermute | solution.py:218
  14.6 1.9 %near.1.done_ref = bf16[4,16,4096]{2,1,0:T(8,128)(2,1)S(1)} custom-call(bf16[2048,1024]{1,0:T(8,128)(2,1)S(1)} %get-tuple-element.24.left_ref, bf16[768,256]{1,0:T(8,128)(2,1)S(1)} %get-tuple-element.25.right_ref, bf16[2,16,4096]{2,1,0:T(8,128)(2,1)S(1)} %self.1.done_ref, bf16[32,4096]{1,0:T(8,128)(2,1)S(1)} %collective-permute-done.2.refs_0_, ...), custom_call_target="tpu_custom_call" | custom-call | flops 1000 | bytes 1000 | tf_op jit(solution)/shard_map/near/pallas_call | solution.py:265
  16.5 0.0 copy-start
  16.5 0.0 copy-start.4
  16.5 0.1 collective-permute-start.4
  16.6 0.5 %collective-permute-start.5 = (bf16[16,4096]{1,0:T(8,128)(2,1)S(1)}, bf16[16,4096]{1,0:T(8,128)(2,1)S(1)}, u32[]{:S(2)}, u32[]{:S(2)}) collective-permute-start(bf16[16,4096]{1,0:T(8,128)(2,1)S(1)} %get-tuple-element.32), channel_id=1, source_target_pairs={{0,1},{1,0},{2,3},{3,2},{6,7},{7,6},{4,5},{5,4},{8,9},{9,8},{10,11... | collective-permute-start | bytes 393224 | tf_op jit(solution)/shard_map/ppermute | solution.py:218
  17.1 0.8 %collective-permute-done.4.refs_0_ = bf16[16,4096]{1,0:T(8,128)(2,1)S(1)} collective-permute-done((bf16[16,4096]{1,0:T(8,128)(2,1)S(1)}, bf16[16,4096]{1,0:T(8,128)(2,1)S(1)}, u32[]{:S(2)}, u32[]{:S(2)}) %collective-permute-start.4) | collective-permute-done | bytes 131104 | tf_op jit(solution)/shard_map/ppermute | solution.py:218
  17.9 0.2 collective-permute-done.5.refs_1_
  18.1 1.9 %crossed.1.early_ref = bf16[6,16,4096]{2,1,0:T(8,128)(2,1)S(1)} custom-call(bf16[2048,1024]{1,0:T(8,128)(2,1)S(1)} %get-tuple-element.24.left_ref, bf16[768,256]{1,0:T(8,128)(2,1)S(1)} %get-tuple-element.25.right_ref, bf16[4,16,4096]{2,1,0:T(8,128)(2,1)S(1)} %near.1.done_ref, bf16[16,4096]{1,0:T(8,128)(2,1)S(1)} %collective-permute-done.4.refs_0_, ...), custom_call_target="tpu_custom_call" | custom-call | flops 1000 | bytes 1000 | tf_op jit(solution)/shard_map/crossed/pallas_call | solution.py:265
  20.0 0.0 collective-permute-done.1.late_ref
  20.0 0.0 copy-done
  20.0 0.0 copy-done.4
  20.0 2.0 %last.1 = (f32[24,512]{1,0:T(8,128)S(1)}, bf16[24,512]{1,0:T(8,128)(2,1)S(1)}, bf16[24,512]{1,0:T(8,128)(2,1)S(1)}, bf16[24,512]{1,0:T(8,128)(2,1)S(1)}) custom-call(s32[48]{0:T(128)S(1)} %copy-done.4, bf16[2,16,4096]{2,1,0:T(8,128)(2,1)S(1)} %collective-permute-done.1.late_ref, bf16[6,16,4096]{2,1,0:T(8,128)(2,1)S(1)} %crossed.1.early_ref, ...), custom_call_target="tpu_custom_call" | custom-call | tf_op jit(solution)/shard_map/last/pallas_call | solution.py:287
  22.1 1.6 %collective-permute-start.6 = (bf16[24,512]{1,0:T(8,128)(2,1)S(1)}, bf16[24,512]{1,0:T(8,128)(2,1)S(1)}, u32[]{:S(2)}, u32[]{:S(2)}) collective-permute-start(bf16[24,512]{1,0:T(8,128)(2,1)S(1)} %get-tuple-element.34), channel_id=1, source_target_pairs={{0,8},{8,16},{16,24},{24,0},{1,9},{9,17},{17,25},{25,1},{2,10},{10... | collective-permute-start | bytes 73736 | tf_op jit(solution)/shard_map/ppermute | solution.py:299
  23.7 2.6 %collective-permute-start.7 = (bf16[24,512]{1,0:T(8,128)(2,1)S(1)}, bf16[24,512]{1,0:T(8,128)(2,1)S(1)}, u32[]{:S(2)}, u32[]{:S(2)}) collective-permute-start(bf16[24,512]{1,0:T(8,128)(2,1)S(1)} %get-tuple-element.35), channel_id=1, source_target_pairs={{0,16},{8,24},{16,0},{24,8},{1,17},{9,25},{17,1},{25,9},{2,18},{10... | collective-permute-start | bytes 73736 | tf_op jit(solution)/shard_map/ppermute | solution.py:299
  26.3 1.3 %collective-permute-start.8 = (bf16[24,512]{1,0:T(8,128)(2,1)S(1)}, bf16[24,512]{1,0:T(8,128)(2,1)S(1)}, u32[]{:S(2)}, u32[]{:S(2)}) collective-permute-start(bf16[24,512]{1,0:T(8,128)(2,1)S(1)} %get-tuple-element.36), channel_id=1, source_target_pairs={{0,24},{8,0},{16,8},{24,16},{1,25},{9,1},{17,9},{25,17},{2,26},{10... | collective-permute-start | bytes 73736 | tf_op jit(solution)/shard_map/ppermute | solution.py:299
  27.6 0.1 collective-permute-done.6.refs_1_
  27.7 1.0 %collective-permute-done.7.refs_2_ = bf16[24,512]{1,0:T(8,128)(2,1)S(1)} collective-permute-done((bf16[24,512]{1,0:T(8,128)(2,1)S(1)}, bf16[24,512]{1,0:T(8,128)(2,1)S(1)}, u32[]{:S(2)}, u32[]{:S(2)}) %collective-permute-start.7) | collective-permute-done | bytes 24608 | tf_op jit(solution)/shard_map/ppermute | solution.py:299
  28.8 1.3 %collective-permute-done.8.refs_3_ = bf16[24,512]{1,0:T(8,128)(2,1)S(1)} collective-permute-done((bf16[24,512]{1,0:T(8,128)(2,1)S(1)}, bf16[24,512]{1,0:T(8,128)(2,1)S(1)}, u32[]{:S(2)}, u32[]{:S(2)}) %collective-permute-start.8) | collective-permute-done | bytes 24608 | tf_op jit(solution)/shard_map/ppermute | solution.py:299
  30.1 0.6 %finish.1 = f32[6,4,512]{2,1,0:T(4,128)} custom-call(f32[24,512]{1,0:T(8,128)S(1)} %get-tuple-element.33.refs_0_, bf16[24,512]{1,0:T(8,128)(2,1)S(1)} %collective-permute-done.6.refs_1_, bf16[24,512]{1,0:T(8,128)(2,1)S(1)} %collective-permute-done.7.refs_2_, bf16[24,512]{1,0:T(8,128)(2,1)S(1)} %collective-permute-done.8.refs_3_), custom_call_target="tpu_custom_call" | custom-call | tf_op jit(solution)/shard_map/finish/pallas_call | solution.py:301
  (1 shorter events, 0.0 us)
Async XLA Ops:
  0.0 5.6 %copy-start.1 = (f32[1,64,64]{2,1,0:T(8,128)S(1)}, f32[1,64,64]{2,1,0:T(8,128)}, u32[]{:S(2)}) copy-start(f32[1,64,64]{2,1,0:T(8,128)} %param.8) | copy-start | bytes 49156
  0.0 5.6 %copy-start.2 = (f32[1,64,64]{2,1,0:T(8,128)S(1)}, f32[1,64,64]{2,1,0:T(8,128)}, u32[]{:S(2)}) copy-start(f32[1,64,64]{2,1,0:T(8,128)} %param.7) | copy-start | bytes 49156
  0.0 0.7 %copy-start.3 = (s32[48]{0:T(128)S(1)}, s32[48]{0:T(128)}, u32[]{:S(2)}) copy-start(s32[48]{0:T(128)} %pairs_ref.3) | copy-start | bytes 580
  0.7 1.0 %copy-start.5 = (bf16[64,1,4096]{2,0,1:T(8,128)(2,1)S(1)}, bf16[64,1,4096]{2,0,1:T(8,128)(2,1)}, u32[]{:S(2)}) copy-start(bf16[64,1,4096]{2,0,1:T(8,128)(2,1)} %param.6) | copy-start | bytes 1572868
  2.4 3.2 %collective-permute-start = (bf16[32,4096]{1,0:T(8,128)(2,1)S(1)}, bf16[32,4096]{1,0:T(8,128)(2,1)S(1)}, u32[]{:S(2)}, u32[]{:S(2)}) collective-permute-start(bf16[32,4096]{1,0:T(8,128)(2,1)S(1)} %get-tuple-element.22), channel_id=1, source_target_pairs={{0,1},{1,0},{2,3},{3,2},{6,7},{7,6},{4,5},{5,4},{8,9},{9,8},{10,11... | collective-permute-start | bytes 786440 | tf_op jit(solution)/shard_map/ppermute | solution.py:218
  2.9 10.6 %collective-permute-start.2 = (bf16[32,4096]{1,0:T(8,128)(2,1)S(1)}, bf16[32,4096]{1,0:T(8,128)(2,1)S(1)}, u32[]{:S(2)}, u32[]{:S(2)}) collective-permute-start(bf16[32,4096]{1,0:T(8,128)(2,1)S(1)} %get-tuple-element.27), channel_id=1, source_target_pairs={{0,2},{1,3},{2,6},{3,7},{6,4},{7,5},{4,0},{5,1},{8,10},{9,11},{10,... | collective-permute-start | bytes 786440 | tf_op jit(solution)/shard_map/ppermute | solution.py:218
  5.5 9.1 %collective-permute-start.3 = (bf16[32,4096]{1,0:T(8,128)(2,1)S(1)}, bf16[32,4096]{1,0:T(8,128)(2,1)S(1)}, u32[]{:S(2)}, u32[]{:S(2)}) collective-permute-start(bf16[32,4096]{1,0:T(8,128)(2,1)S(1)} %get-tuple-element.28), channel_id=1, source_target_pairs={{0,4},{1,5},{2,0},{3,1},{6,2},{7,3},{4,6},{5,7},{8,12},{9,13},{10,... | collective-permute-start | bytes 786440 | tf_op jit(solution)/shard_map/ppermute | solution.py:218
  8.8 11.2 %collective-permute-start.1 = (bf16[2,16,4096]{2,1,0:T(8,128)(2,1)S(1)}, bf16[2,16,4096]{2,1,0:T(8,128)(2,1)S(1)}, u32[]{:S(2)}, u32[]{:S(2)}) collective-permute-start(bf16[2,16,4096]{2,1,0:T(8,128)(2,1)S(1)} %get-tuple-element.23), channel_id=1, source_target_pairs={{0,6},{1,7},{2,4},{3,5},{6,0},{7,1},{4,2},{5,3},{8,14},{9,15},{10,... | collective-permute-start | bytes 786440 | tf_op jit(solution)/shard_map/ppermute | solution.py:218
  16.5 3.5 %copy-start = (bf16[512,1,4096]{2,0,1:T(8,128)(2,1)S(1)}, bf16[512,1,4096]{2,0,1:T(8,128)(2,1)}, u32[]{:S(2)}) copy-start(bf16[512,1,4096]{2,0,1:T(8,128)(2,1)} %param.5) | copy-start | bytes 12582916
  16.5 3.5 %copy-start.4 = (s32[48]{0:T(128)S(1)}, s32[48]{0:T(128)}, u32[]{:S(2)}) copy-start(s32[48]{0:T(128)} %pairs_ref.3) | copy-start | bytes 580
  16.5 1.4 %collective-permute-start.4 = (bf16[16,4096]{1,0:T(8,128)(2,1)S(1)}, bf16[16,4096]{1,0:T(8,128)(2,1)S(1)}, u32[]{:S(2)}, u32[]{:S(2)}) collective-permute-start(bf16[16,4096]{1,0:T(8,128)(2,1)S(1)} %get-tuple-element.31), channel_id=1, source_target_pairs={{0,1},{1,0},{2,3},{3,2},{6,7},{7,6},{4,5},{5,4},{8,9},{9,8},{10,11... | collective-permute-start | bytes 393224 | tf_op jit(solution)/shard_map/ppermute | solution.py:218
  16.6 1.5 %collective-permute-start.5 = (bf16[16,4096]{1,0:T(8,128)(2,1)S(1)}, bf16[16,4096]{1,0:T(8,128)(2,1)S(1)}, u32[]{:S(2)}, u32[]{:S(2)}) collective-permute-start(bf16[16,4096]{1,0:T(8,128)(2,1)S(1)} %get-tuple-element.32), channel_id=1, source_target_pairs={{0,1},{1,0},{2,3},{3,2},{6,7},{7,6},{4,5},{5,4},{8,9},{9,8},{10,11... | collective-permute-start | bytes 393224 | tf_op jit(solution)/shard_map/ppermute | solution.py:218
  22.1 5.7 %collective-permute-start.6 = (bf16[24,512]{1,0:T(8,128)(2,1)S(1)}, bf16[24,512]{1,0:T(8,128)(2,1)S(1)}, u32[]{:S(2)}, u32[]{:S(2)}) collective-permute-start(bf16[24,512]{1,0:T(8,128)(2,1)S(1)} %get-tuple-element.34), channel_id=1, source_target_pairs={{0,8},{8,16},{16,24},{24,0},{1,9},{9,17},{17,25},{25,1},{2,10},{10... | collective-permute-start | bytes 73736 | tf_op jit(solution)/shard_map/ppermute | solution.py:299
  23.7 5.1 %collective-permute-start.7 = (bf16[24,512]{1,0:T(8,128)(2,1)S(1)}, bf16[24,512]{1,0:T(8,128)(2,1)S(1)}, u32[]{:S(2)}, u32[]{:S(2)}) collective-permute-start(bf16[24,512]{1,0:T(8,128)(2,1)S(1)} %get-tuple-element.35), channel_id=1, source_target_pairs={{0,16},{8,24},{16,0},{24,8},{1,17},{9,25},{17,1},{25,9},{2,18},{10... | collective-permute-start | bytes 73736 | tf_op jit(solution)/shard_map/ppermute | solution.py:299
  26.3 3.8 %collective-permute-start.8 = (bf16[24,512]{1,0:T(8,128)(2,1)S(1)}, bf16[24,512]{1,0:T(8,128)(2,1)S(1)}, u32[]{:S(2)}, u32[]{:S(2)}) collective-permute-start(bf16[24,512]{1,0:T(8,128)(2,1)S(1)} %get-tuple-element.36), channel_id=1, source_target_pairs={{0,24},{8,0},{16,8},{24,16},{1,25},{9,1},{17,9},{25,17},{2,26},{10... | collective-permute-start | bytes 73736 | tf_op jit(solution)/shard_map/ppermute | solution.py:299

commit v16 on v12

--- a/solution.py
+++ b/solution.py
@@ -292,9 +292,8 @@
         name="last",
     )(pair_blocks, far, early, train)
 
-    shifts = sorted(range(1, layer), key=lambda m: (min(m, layer - m), m))
     terms = [parts[0]] + [
-        lax.ppermute(parts[m], "layer", [(i, (i + m) % layer) for i in range(layer)]) for m in shifts
+        lax.ppermute(parts[m], "layer", [(i, (i + m) % layer) for i in range(layer)]) for m in range(1, layer)
     ]
     out = pl.pallas_call(
         functools.partial(finish_kernel, layer),

time: 30.7 us -> 30.1 us (0.980)
  waiting for transfers between devices: 4.43 us -> 2.97 us
  starting transfers between devices: 11.4 us -> 12.2 us
    ppermute x3, waiting for transfers between devices: 3.93 us -> 2.48 us  [shards(): lax.ppermute(parts[m], 'layer', [(i, (i + m) % layer) for i in range(laye...]
    ppermute x3, starting transfers between devices: 4.67 us -> 5.57 us  [shards(): lax.ppermute(parts[m], 'layer', [(i, (i + m) % layer) for i in range(laye...]
  transfers between devices with their start and end apart: 9 -> 9, of which waited for: 3 -> 4; matrix products, arithmetic and copies ran while one was open for 3% -> 3% of each run, Pallas kernels for 29% -> 29%
where the time goes in v16:
time: 30.1 us; the launch traced here: 29.9 us
  starting transfers between devices  12.2 us (41%)
  Pallas kernels  12.1 us (40%)
  waiting for transfers between devices  2.97 us (10%)
  local copies, waits for them, and re-layouts  1.71 us (6%)
  other arithmetic  0.78 us (3%)
    ppermute x6, starting transfers between devices, pass_on(): lax.ppermute(array, 'ex', [(2 * a + c, 2 * b + (c ^ flip)) for a, b in mo...  6.68 us
    ppermute x3, starting transfers between devices, shards(): lax.ppermute(parts[m], 'layer', [(i, (i + m) % layer) for i in range(laye...  5.57 us
    pallas_call x2, Pallas kernels, shards(): pl.pallas_call(near_kernel, out_shape=prepared(early.shape[0] + len(raw))...  3.72 us
    pallas_call x1, Pallas kernels, shards(): pl.pallas_call(functools.partial(first_kernel, rows, out_precond.shape[-1...  3.16 us
    ppermute x3, waiting for transfers between devices, shards(): lax.ppermute(parts[m], 'layer', [(i, (i + m) % layer) for i in range(laye...  2.48 us
    pallas_call x1, Pallas kernels, shards(): pl.pallas_call(functools.partial(last_kernel, order, layer, held, slots),...  2.03 us
    pallas_call x1, Pallas kernels, shards(): pl.pallas_call(self_kernel, out_shape=prepared(2), in_specs=[VMEM] * 4, o...  1.85 us
    unnamed x8, local copies, waits for them, and re-layouts  1.71 us
  transfers between devices with their start and end apart: 9, of which 4 were waited for; matrix products, arithmetic and copies ran while one was open for 3% of the time, Pallas kernels for 29%

profile of v16, /device:TPU:0, one launch (start us, length us, event | category | flops | bytes accessed | tf_op | source)
XLA Modules:
  0.0 29.9 jit_solution(12368416383934831542)
XLA Ops:
  0.0 0.0 copy-start.1
  0.0 1.0 %copy-done.1 = bf16[64,1,4096]{2,0,1:T(8,128)(2,1)S(1)} copy-done((bf16[64,1,4096]{2,0,1:T(8,128)(2,1)S(1)}, bf16[64,1,4096]{2,0,1:T(8,128)(2,1)}, u32[]{:S(2)}) %copy-start.1) | copy-done | bytes 524312
  1.0 0.0 copy-start.2
  1.0 0.7 %copy-done.2 = s32[48]{0:T(128)S(1)} copy-done((s32[48]{0:T(128)S(1)}, s32[48]{0:T(128)}, u32[]{:S(2)}) %copy-start.2) | copy-done | bytes 216
  1.7 0.7 %pick.1 = (bf16[16,4096]{1,0:T(8,128)(2,1)S(1)}, bf16[16,4096]{1,0:T(8,128)(2,1)S(1)}, bf16[32,4096]{1,0:T(8,128)(2,1)S(1)}, bf16[32,4096]{1,0:T(8,128)(2,1)S(1)}, bf16[32,4096]{1,0:T(8,128)(2,1)S(1)}) custom-call(s32[48]{0:T(128)S(1)} %copy-done.2, bf16[64,4096]{1,0:T(8,128)(2,1)S(1)} %bitcast.6), custom_call_target="tpu_custom_call" | custom-call | tf_op jit(solution)/shard_map/pick/pallas_call | solution.py:222
  2.4 0.5 %collective-permute-start = (bf16[32,4096]{1,0:T(8,128)(2,1)S(1)}, bf16[32,4096]{1,0:T(8,128)(2,1)S(1)}, u32[]{:S(2)}, u32[]{:S(2)}) collective-permute-start(bf16[32,4096]{1,0:T(8,128)(2,1)S(1)} %get-tuple-element.28), channel_id=1, source_target_pairs={{0,1},{1,0},{2,3},{3,2},{6,7},{7,6},{4,5},{5,4},{8,9},{9,8},{10,11... | collective-permute-start | bytes 786440 | tf_op jit(solution)/shard_map/ppermute | solution.py:218
  2.9 2.6 %collective-permute-start.2 = (bf16[32,4096]{1,0:T(8,128)(2,1)S(1)}, bf16[32,4096]{1,0:T(8,128)(2,1)S(1)}, u32[]{:S(2)}, u32[]{:S(2)}) collective-permute-start(bf16[32,4096]{1,0:T(8,128)(2,1)S(1)} %get-tuple-element.33), channel_id=1, source_target_pairs={{0,2},{1,3},{2,6},{3,7},{6,4},{7,5},{4,0},{5,1},{8,10},{9,11},{10,... | collective-permute-start | bytes 786440 | tf_op jit(solution)/shard_map/ppermute | solution.py:218
  5.4 0.1 collective-permute-start.3
  5.6 0.8 %pad_maximum_fusion.factors_ref = f32[128,64]{1,0:T(8,128)S(1)} fusion(f32[64,64]{1,0:T(8,128)} %bitcast.7, f32[64,64]{1,0:T(8,128)} %bitcast.8), kind=kLoop, calls=%fused_computation | loop fusion | flops 8192 | bytes 65536 | tf_op jit(solution)/shard_map/concatenate | solution.py:249
  6.3 0.0 collective-permute-done.swap_ref
  6.3 3.2 %first.1 = (bf16[2048,1024]{1,0:T(8,128)(2,1)S(1)}, bf16[768,256]{1,0:T(8,128)(2,1)S(1)}, bf16[2,16,4096]{2,1,0:T(8,128)(2,1)S(1)}) custom-call(f32[128,64]{1,0:T(8,128)S(1)} %pad_maximum_fusion.factors_ref, bf16[16,4096]{1,0:T(8,128)(2,1)S(1)} %get-tuple-element.27.far_ref, bf16[32,4096]{1,0:T(8,128)(2,1)S(1)} %collective-permute-done.swap_ref), custom_call_target="tpu_custom_call" | custom-call | flops 1000 | bytes 1000 | tf_op jit(solution)/shard_map/first/pallas_call | solution.py:237
  9.5 2.9 %collective-permute-start.1 = (bf16[2,16,4096]{2,1,0:T(8,128)(2,1)S(1)}, bf16[2,16,4096]{2,1,0:T(8,128)(2,1)S(1)}, u32[]{:S(2)}, u32[]{:S(2)}) collective-permute-start(bf16[2,16,4096]{2,1,0:T(8,128)(2,1)S(1)} %get-tuple-element.29), channel_id=1, source_target_pairs={{0,6},{1,7},{2,4},{3,5},{6,0},{7,1},{4,2},{5,3},{8,14},{9,15},{10,... | collective-permute-start | bytes 786440 | tf_op jit(solution)/shard_map/ppermute | solution.py:218
  12.4 1.8 %self.1.done_ref = bf16[2,16,4096]{2,1,0:T(8,128)(2,1)S(1)} custom-call(bf16[2048,1024]{1,0:T(8,128)(2,1)S(1)} %get-tuple-element.30.left_ref, bf16[768,256]{1,0:T(8,128)(2,1)S(1)} %get-tuple-element.31.right_ref, bf16[16,4096]{1,0:T(8,128)(2,1)S(1)} %get-tuple-element.32.self_ref, bf16[32,4096]{1,0:T(8,128)(2,1)S(1)} %collective-permute-done.swap_ref), custom_call_target="tpu_custom_call" | custom-call | flops 1000 | bytes 1000 | tf_op jit(solution)/shard_map/self/pallas_call | solution.py:255
  14.3 0.0 collective-permute-done.2.refs_0_
  14.3 0.0 collective-permute-done.3.refs_1_
  14.4 0.1 collective-permute-start.4
  14.4 0.5 %collective-permute-start.5 = (bf16[16,4096]{1,0:T(8,128)(2,1)S(1)}, bf16[16,4096]{1,0:T(8,128)(2,1)S(1)}, u32[]{:S(2)}, u32[]{:S(2)}) collective-permute-start(bf16[16,4096]{1,0:T(8,128)(2,1)S(1)} %get-tuple-element.38), channel_id=1, source_target_pairs={{0,1},{1,0},{2,3},{3,2},{6,7},{7,6},{4,5},{5,4},{8,9},{9,8},{10,11... | collective-permute-start | bytes 393224 | tf_op jit(solution)/shard_map/ppermute | solution.py:218
  14.9 1.9 %near.1.done_ref = bf16[4,16,4096]{2,1,0:T(8,128)(2,1)S(1)} custom-call(bf16[2048,1024]{1,0:T(8,128)(2,1)S(1)} %get-tuple-element.30.left_ref, bf16[768,256]{1,0:T(8,128)(2,1)S(1)} %get-tuple-element.31.right_ref, bf16[2,16,4096]{2,1,0:T(8,128)(2,1)S(1)} %self.1.done_ref, bf16[32,4096]{1,0:T(8,128)(2,1)S(1)} %collective-permute-done.2.refs_0_, ...), custom_call_target="tpu_custom_call" | custom-call | flops 1000 | bytes 1000 | tf_op jit(solution)/shard_map/near/pallas_call | solution.py:275
  16.8 0.0 copy-start
  16.8 0.0 copy-start.3
  16.8 0.0 collective-permute-done.4.refs_0_
  16.8 0.0 collective-permute-done.5.refs_1_
  16.8 1.9 %crossed.1.early_ref = bf16[6,16,4096]{2,1,0:T(8,128)(2,1)S(1)} custom-call(bf16[2048,1024]{1,0:T(8,128)(2,1)S(1)} %get-tuple-element.30.left_ref, bf16[768,256]{1,0:T(8,128)(2,1)S(1)} %get-tuple-element.31.right_ref, bf16[4,16,4096]{2,1,0:T(8,128)(2,1)S(1)} %near.1.done_ref, bf16[16,4096]{1,0:T(8,128)(2,1)S(1)} %collective-permute-done.4.refs_0_, ...), custom_call_target="tpu_custom_call" | custom-call | flops 1000 | bytes 1000 | tf_op jit(solution)/shard_map/crossed/pallas_call | solution.py:275
  18.7 0.5 %collective-permute-done.1.late_ref = bf16[2,16,4096]{2,1,0:T(8,128)(2,1)S(1)} collective-permute-done((bf16[2,16,4096]{2,1,0:T(8,128)(2,1)S(1)}, bf16[2,16,4096]{2,1,0:T(8,128)(2,1)S(1)}, u32[]{:S(2)}, u32[]{:S(2)}) %collective-permute-start.1) | collective-permute-done | bytes 262176 | tf_op jit(solution)/shard_map/ppermute | solution.py:218
  19.2 0.0 copy-done
  19.2 0.0 copy-done.3
  19.2 2.0 %last.1 = (f32[24,512]{1,0:T(8,128)S(1)}, bf16[24,512]{1,0:T(8,128)(2,1)S(1)}, bf16[24,512]{1,0:T(8,128)(2,1)S(1)}, bf16[24,512]{1,0:T(8,128)(2,1)S(1)}) custom-call(s32[48]{0:T(128)S(1)} %copy-done.3, bf16[2,16,4096]{2,1,0:T(8,128)(2,1)S(1)} %collective-permute-done.1.late_ref, bf16[6,16,4096]{2,1,0:T(8,128)(2,1)S(1)} %crossed.1.early_ref, ...), custom_call_target="tpu_custom_call" | custom-call | tf_op jit(solution)/shard_map/last/pallas_call | solution.py:284
  21.2 1.6 %collective-permute-start.6 = (bf16[24,512]{1,0:T(8,128)(2,1)S(1)}, bf16[24,512]{1,0:T(8,128)(2,1)S(1)}, u32[]{:S(2)}, u32[]{:S(2)}) collective-permute-start(bf16[24,512]{1,0:T(8,128)(2,1)S(1)} %get-tuple-element.40), channel_id=1, source_target_pairs={{0,8},{8,16},{16,24},{24,0},{1,9},{9,17},{17,25},{25,1},{2,10},{10... | collective-permute-start | bytes 73736 | tf_op jit(solution)/shard_map/ppermute | solution.py:296
  22.9 2.6 %collective-permute-start.7 = (bf16[24,512]{1,0:T(8,128)(2,1)S(1)}, bf16[24,512]{1,0:T(8,128)(2,1)S(1)}, u32[]{:S(2)}, u32[]{:S(2)}) collective-permute-start(bf16[24,512]{1,0:T(8,128)(2,1)S(1)} %get-tuple-element.41), channel_id=1, source_target_pairs={{0,16},{8,24},{16,0},{24,8},{1,17},{9,25},{17,1},{25,9},{2,18},{10... | collective-permute-start | bytes 73736 | tf_op jit(solution)/shard_map/ppermute | solution.py:296
  25.4 1.3 %collective-permute-start.8 = (bf16[24,512]{1,0:T(8,128)(2,1)S(1)}, bf16[24,512]{1,0:T(8,128)(2,1)S(1)}, u32[]{:S(2)}, u32[]{:S(2)}) collective-permute-start(bf16[24,512]{1,0:T(8,128)(2,1)S(1)} %get-tuple-element.42), channel_id=1, source_target_pairs={{0,24},{8,0},{16,8},{24,16},{1,25},{9,1},{17,9},{25,17},{2,26},{10... | collective-permute-start | bytes 73736 | tf_op jit(solution)/shard_map/ppermute | solution.py:296
  26.8 0.1 collective-permute-done.6.refs_1_
  26.9 0.9 %collective-permute-done.7.refs_2_ = bf16[24,512]{1,0:T(8,128)(2,1)S(1)} collective-permute-done((bf16[24,512]{1,0:T(8,128)(2,1)S(1)}, bf16[24,512]{1,0:T(8,128)(2,1)S(1)}, u32[]{:S(2)}, u32[]{:S(2)}) %collective-permute-start.7) | collective-permute-done | bytes 24608 | tf_op jit(solution)/shard_map/ppermute | solution.py:296
  27.8 1.4 %collective-permute-done.8.refs_3_ = bf16[24,512]{1,0:T(8,128)(2,1)S(1)} collective-permute-done((bf16[24,512]{1,0:T(8,128)(2,1)S(1)}, bf16[24,512]{1,0:T(8,128)(2,1)S(1)}, u32[]{:S(2)}, u32[]{:S(2)}) %collective-permute-start.8) | collective-permute-done | bytes 24608 | tf_op jit(solution)/shard_map/ppermute | solution.py:296
  29.3 0.6 %finish.1 = f32[6,4,512]{2,1,0:T(4,128)} custom-call(f32[24,512]{1,0:T(8,128)S(1)} %get-tuple-element.39.refs_0_, bf16[24,512]{1,0:T(8,128)(2,1)S(1)} %collective-permute-done.6.refs_1_, bf16[24,512]{1,0:T(8,128)(2,1)S(1)} %collective-permute-done.7.refs_2_, bf16[24,512]{1,0:T(8,128)(2,1)S(1)} %collective-permute-done.8.refs_3_), custom_call_target="tpu_custom_call" | custom-call | tf_op jit(solution)/shard_map/finish/pallas_call | solution.py:298
  (1 shorter events, 0.0 us)
Async XLA Ops:
  0.0 1.0 %copy-start.1 = (bf16[64,1,4096]{2,0,1:T(8,128)(2,1)S(1)}, bf16[64,1,4096]{2,0,1:T(8,128)(2,1)}, u32[]{:S(2)}) copy-start(bf16[64,1,4096]{2,0,1:T(8,128)(2,1)} %param.6) | copy-start | bytes 1572868
  1.0 0.7 %copy-start.2 = (s32[48]{0:T(128)S(1)}, s32[48]{0:T(128)}, u32[]{:S(2)}) copy-start(s32[48]{0:T(128)} %pairs_ref.3) | copy-start | bytes 580
  2.4 4.0 %collective-permute-start = (bf16[32,4096]{1,0:T(8,128)(2,1)S(1)}, bf16[32,4096]{1,0:T(8,128)(2,1)S(1)}, u32[]{:S(2)}, u32[]{:S(2)}) collective-permute-start(bf16[32,4096]{1,0:T(8,128)(2,1)S(1)} %get-tuple-element.28), channel_id=1, source_target_pairs={{0,1},{1,0},{2,3},{3,2},{6,7},{7,6},{4,5},{5,4},{8,9},{9,8},{10,11... | collective-permute-start | bytes 786440 | tf_op jit(solution)/shard_map/ppermute | solution.py:218
  2.9 11.4 %collective-permute-start.2 = (bf16[32,4096]{1,0:T(8,128)(2,1)S(1)}, bf16[32,4096]{1,0:T(8,128)(2,1)S(1)}, u32[]{:S(2)}, u32[]{:S(2)}) collective-permute-start(bf16[32,4096]{1,0:T(8,128)(2,1)S(1)} %get-tuple-element.33), channel_id=1, source_target_pairs={{0,2},{1,3},{2,6},{3,7},{6,4},{7,5},{4,0},{5,1},{8,10},{9,11},{10,... | collective-permute-start | bytes 786440 | tf_op jit(solution)/shard_map/ppermute | solution.py:218
  5.4 8.9 %collective-permute-start.3 = (bf16[32,4096]{1,0:T(8,128)(2,1)S(1)}, bf16[32,4096]{1,0:T(8,128)(2,1)S(1)}, u32[]{:S(2)}, u32[]{:S(2)}) collective-permute-start(bf16[32,4096]{1,0:T(8,128)(2,1)S(1)} %get-tuple-element.34), channel_id=1, source_target_pairs={{0,4},{1,5},{2,0},{3,1},{6,2},{7,3},{4,6},{5,7},{8,12},{9,13},{10,... | collective-permute-start | bytes 786440 | tf_op jit(solution)/shard_map/ppermute | solution.py:218
  9.5 9.7 %collective-permute-start.1 = (bf16[2,16,4096]{2,1,0:T(8,128)(2,1)S(1)}, bf16[2,16,4096]{2,1,0:T(8,128)(2,1)S(1)}, u32[]{:S(2)}, u32[]{:S(2)}) collective-permute-start(bf16[2,16,4096]{2,1,0:T(8,128)(2,1)S(1)} %get-tuple-element.29), channel_id=1, source_target_pairs={{0,6},{1,7},{2,4},{3,5},{6,0},{7,1},{4,2},{5,3},{8,14},{9,15},{10,... | collective-permute-start | bytes 786440 | tf_op jit(solution)/shard_map/ppermute | solution.py:218
  14.4 2.5 %collective-permute-start.4 = (bf16[16,4096]{1,0:T(8,128)(2,1)S(1)}, bf16[16,4096]{1,0:T(8,128)(2,1)S(1)}, u32[]{:S(2)}, u32[]{:S(2)}) collective-permute-start(bf16[16,4096]{1,0:T(8,128)(2,1)S(1)} %get-tuple-element.37), channel_id=1, source_target_pairs={{0,1},{1,0},{2,3},{3,2},{6,7},{7,6},{4,5},{5,4},{8,9},{9,8},{10,11... | collective-permute-start | bytes 393224 | tf_op jit(solution)/shard_map/ppermute | solution.py:218
  14.4 2.4 %collective-permute-start.5 = (bf16[16,4096]{1,0:T(8,128)(2,1)S(1)}, bf16[16,4096]{1,0:T(8,128)(2,1)S(1)}, u32[]{:S(2)}, u32[]{:S(2)}) collective-permute-start(bf16[16,4096]{1,0:T(8,128)(2,1)S(1)} %get-tuple-element.38), channel_id=1, source_target_pairs={{0,1},{1,0},{2,3},{3,2},{6,7},{7,6},{4,5},{5,4},{8,9},{9,8},{10,11... | collective-permute-start | bytes 393224 | tf_op jit(solution)/shard_map/ppermute | solution.py:218
  16.8 2.4 %copy-start = (bf16[512,1,4096]{2,0,1:T(8,128)(2,1)S(1)}, bf16[512,1,4096]{2,0,1:T(8,128)(2,1)}, u32[]{:S(2)}) copy-start(bf16[512,1,4096]{2,0,1:T(8,128)(2,1)} %param.5) | copy-start | bytes 12582916
  16.8 2.4 %copy-start.3 = (s32[48]{0:T(128)S(1)}, s32[48]{0:T(128)}, u32[]{:S(2)}) copy-start(s32[48]{0:T(128)} %pairs_ref.3) | copy-start | bytes 580
  21.2 5.7 %collective-permute-start.6 = (bf16[24,512]{1,0:T(8,128)(2,1)S(1)}, bf16[24,512]{1,0:T(8,128)(2,1)S(1)}, u32[]{:S(2)}, u32[]{:S(2)}) collective-permute-start(bf16[24,512]{1,0:T(8,128)(2,1)S(1)} %get-tuple-element.40), channel_id=1, source_target_pairs={{0,8},{8,16},{16,24},{24,0},{1,9},{9,17},{17,25},{25,1},{2,10},{10... | collective-permute-start | bytes 73736 | tf_op jit(solution)/shard_map/ppermute | solution.py:296
  22.9 5.0 %collective-permute-start.7 = (bf16[24,512]{1,0:T(8,128)(2,1)S(1)}, bf16[24,512]{1,0:T(8,128)(2,1)S(1)}, u32[]{:S(2)}, u32[]{:S(2)}) collective-permute-start(bf16[24,512]{1,0:T(8,128)(2,1)S(1)} %get-tuple-element.41), channel_id=1, source_target_pairs={{0,16},{8,24},{16,0},{24,8},{1,17},{9,25},{17,1},{25,9},{2,18},{10... | collective-permute-start | bytes 73736 | tf_op jit(solution)/shard_map/ppermute | solution.py:296
  25.4 3.8 %collective-permute-start.8 = (bf16[24,512]{1,0:T(8,128)(2,1)S(1)}, bf16[24,512]{1,0:T(8,128)(2,1)S(1)}, u32[]{:S(2)}, u32[]{:S(2)}) collective-permute-start(bf16[24,512]{1,0:T(8,128)(2,1)S(1)} %get-tuple-element.42), channel_id=1, source_target_pairs={{0,24},{8,0},{16,8},{24,16},{1,25},{9,1},{17,9},{25,17},{2,26},{10... | collective-permute-start | bytes 73736 | tf_op jit(solution)/shard_map/ppermute | solution.py:296

commit v17 on v11

--- a/solution.py
+++ b/solution.py
@@ -210,7 +210,7 @@
     limit = pltpu.CompilerParams(vmem_limit_bytes=24 * 2**20)
 
     groups = ex // 2
-    order = sorted(range(groups), key=lambda step: min(step, groups - step))
+    order = sorted(range(groups), key=lambda step: (min(step, groups - step), -step))
 
     def pass_on(array, step, flip=0):
         ring = [ring_chip(place) for place in range(groups)]

time: 30.1 us -> 31.4 us (1.043)
  waiting for transfers between devices: 2.78 us -> 3.99 us
    ppermute x6, waiting for transfers between devices: 0.31 us -> 1.52 us  [pass_on(): lax.ppermute(array, 'ex', [(2 * a + c, 2 * b + (c ^ flip)) for a, b in mo...]
  transfers between devices with their start and end apart: 9 -> 9, of which waited for: 4 -> 4; matrix products, arithmetic and copies ran while one was open for 3% -> 3% of each run, Pallas kernels for 30% -> 29%
where the time goes in v17:
time: 31.4 us; the launch traced here: 31.1 us
  Pallas kernels  12.3 us (39%)
  starting transfers between devices  12.3 us (39%)
  waiting for transfers between devices  3.99 us (13%)
  local copies, waits for them, and re-layouts  1.71 us (5%)
  other arithmetic  0.78 us (2%)
    ppermute x6, starting transfers between devices, pass_on(): lax.ppermute(array, 'ex', [(2 * a + c, 2 * b + (c ^ flip)) for a, b in mo...  6.69 us
    ppermute x3, starting transfers between devices, shards(): lax.ppermute(parts[m], 'layer', [(i, (i + m) % layer) for i in range(laye...  5.57 us
    pallas_call x2, Pallas kernels, shards(): pl.pallas_call(near_kernel, out_shape=prepared(early.shape[0] + len(raw))...  3.72 us
    pallas_call x1, Pallas kernels, shards(): pl.pallas_call(functools.partial(first_kernel, rows, out_precond.shape[-1...  3.34 us
    ppermute x3, waiting for transfers between devices, shards(): lax.ppermute(parts[m], 'layer', [(i, (i + m) % layer) for i in range(laye...  2.48 us
    pallas_call x1, Pallas kernels, shards(): pl.pallas_call(functools.partial(last_kernel, order, layer, held, slots),...  2.03 us
    pallas_call x1, Pallas kernels, shards(): pl.pallas_call(self_kernel, out_shape=prepared(2), in_specs=[VMEM] * 4, o...  1.85 us
    unnamed x8, local copies, waits for them, and re-layouts  1.71 us
  transfers between devices with their start and end apart: 9, of which 4 were waited for; matrix products, arithmetic and copies ran while one was open for 3% of the time, Pallas kernels for 29%

profile of v17, /device:TPU:0, one launch (start us, length us, event | category | flops | bytes accessed | tf_op | source)
XLA Modules:
  0.0 31.1 jit_solution(15035238454598762253)
XLA Ops:
  0.0 0.0 copy-start.1
  0.0 1.0 %copy-done.1 = bf16[64,1,4096]{2,0,1:T(8,128)(2,1)S(1)} copy-done((bf16[64,1,4096]{2,0,1:T(8,128)(2,1)S(1)}, bf16[64,1,4096]{2,0,1:T(8,128)(2,1)}, u32[]{:S(2)}) %copy-start.1) | copy-done | bytes 524312
  1.0 0.0 copy-start.2
  1.0 0.7 %copy-done.2 = s32[48]{0:T(128)S(1)} copy-done((s32[48]{0:T(128)S(1)}, s32[48]{0:T(128)}, u32[]{:S(2)}) %copy-start.2) | copy-done | bytes 216
  1.7 0.7 %pick.1 = (bf16[16,4096]{1,0:T(8,128)(2,1)S(1)}, bf16[16,4096]{1,0:T(8,128)(2,1)S(1)}, bf16[32,4096]{1,0:T(8,128)(2,1)S(1)}, bf16[32,4096]{1,0:T(8,128)(2,1)S(1)}, bf16[32,4096]{1,0:T(8,128)(2,1)S(1)}) custom-call(s32[48]{0:T(128)S(1)} %copy-done.2, bf16[64,4096]{1,0:T(8,128)(2,1)S(1)} %bitcast.6), custom_call_target="tpu_custom_call" | custom-call | tf_op jit(solution)/shard_map/pick/pallas_call | solution.py:222
  2.4 0.5 %collective-permute-start = (bf16[32,4096]{1,0:T(8,128)(2,1)S(1)}, bf16[32,4096]{1,0:T(8,128)(2,1)S(1)}, u32[]{:S(2)}, u32[]{:S(2)}) collective-permute-start(bf16[32,4096]{1,0:T(8,128)(2,1)S(1)} %get-tuple-element.28), channel_id=1, source_target_pairs={{0,1},{1,0},{2,3},{3,2},{6,7},{7,6},{4,5},{5,4},{8,9},{9,8},{10,11... | collective-permute-start | bytes 786440 | tf_op jit(solution)/shard_map/ppermute | solution.py:218
  2.9 2.6 %collective-permute-start.2 = (bf16[32,4096]{1,0:T(8,128)(2,1)S(1)}, bf16[32,4096]{1,0:T(8,128)(2,1)S(1)}, u32[]{:S(2)}, u32[]{:S(2)}) collective-permute-start(bf16[32,4096]{1,0:T(8,128)(2,1)S(1)} %get-tuple-element.33), channel_id=1, source_target_pairs={{0,4},{1,5},{2,0},{3,1},{6,2},{7,3},{4,6},{5,7},{8,12},{9,13},{10,... | collective-permute-start | bytes 786440 | tf_op jit(solution)/shard_map/ppermute | solution.py:218
  5.5 0.1 collective-permute-start.3
  5.5 0.8 %pad_maximum_fusion.factors_ref = f32[128,64]{1,0:T(8,128)S(1)} fusion(f32[64,64]{1,0:T(8,128)} %bitcast.7, f32[64,64]{1,0:T(8,128)} %bitcast.8), kind=kLoop, calls=%fused_computation | loop fusion | flops 8192 | bytes 65536 | tf_op jit(solution)/shard_map/concatenate | solution.py:249
  6.3 0.0 collective-permute-done.swap_ref
  6.3 3.3 %first.1 = (bf16[2048,1024]{1,0:T(8,128)(2,1)S(1)}, bf16[768,256]{1,0:T(8,128)(2,1)S(1)}, bf16[2,16,4096]{2,1,0:T(8,128)(2,1)S(1)}) custom-call(f32[128,64]{1,0:T(8,128)S(1)} %pad_maximum_fusion.factors_ref, bf16[16,4096]{1,0:T(8,128)(2,1)S(1)} %get-tuple-element.27.far_ref, bf16[32,4096]{1,0:T(8,128)(2,1)S(1)} %collective-permute-done.swap_ref), custom_call_target="tpu_custom_call" | custom-call | flops 1000 | bytes 1000 | tf_op jit(solution)/shard_map/first/pallas_call | solution.py:237
  9.7 3.0 %collective-permute-start.1 = (bf16[2,16,4096]{2,1,0:T(8,128)(2,1)S(1)}, bf16[2,16,4096]{2,1,0:T(8,128)(2,1)S(1)}, u32[]{:S(2)}, u32[]{:S(2)}) collective-permute-start(bf16[2,16,4096]{2,1,0:T(8,128)(2,1)S(1)} %get-tuple-element.29), channel_id=1, source_target_pairs={{0,6},{1,7},{2,4},{3,5},{6,0},{7,1},{4,2},{5,3},{8,14},{9,15},{10,... | collective-permute-start | bytes 786440 | tf_op jit(solution)/shard_map/ppermute | solution.py:218
  12.6 1.9 %self.1.done_ref = bf16[2,16,4096]{2,1,0:T(8,128)(2,1)S(1)} custom-call(bf16[2048,1024]{1,0:T(8,128)(2,1)S(1)} %get-tuple-element.30.left_ref, bf16[768,256]{1,0:T(8,128)(2,1)S(1)} %get-tuple-element.31.right_ref, bf16[16,4096]{1,0:T(8,128)(2,1)S(1)} %get-tuple-element.32.self_ref, bf16[32,4096]{1,0:T(8,128)(2,1)S(1)} %collective-permute-done.swap_ref), custom_call_target="tpu_custom_call" | custom-call | flops 1000 | bytes 1000 | tf_op jit(solution)/shard_map/self/pallas_call | solution.py:255
  14.5 0.0 collective-permute-done.2.refs_0_
  14.5 0.0 collective-permute-done.3.refs_1_
  14.5 0.1 collective-permute-start.4
  14.6 0.5 %collective-permute-start.5 = (bf16[16,4096]{1,0:T(8,128)(2,1)S(1)}, bf16[16,4096]{1,0:T(8,128)(2,1)S(1)}, u32[]{:S(2)}, u32[]{:S(2)}) collective-permute-start(bf16[16,4096]{1,0:T(8,128)(2,1)S(1)} %get-tuple-element.38), channel_id=1, source_target_pairs={{0,1},{1,0},{2,3},{3,2},{6,7},{7,6},{4,5},{5,4},{8,9},{9,8},{10,11... | collective-permute-start | bytes 393224 | tf_op jit(solution)/shard_map/ppermute | solution.py:218
  15.1 1.9 %near.1.done_ref = bf16[4,16,4096]{2,1,0:T(8,128)(2,1)S(1)} custom-call(bf16[2048,1024]{1,0:T(8,128)(2,1)S(1)} %get-tuple-element.30.left_ref, bf16[768,256]{1,0:T(8,128)(2,1)S(1)} %get-tuple-element.31.right_ref, bf16[2,16,4096]{2,1,0:T(8,128)(2,1)S(1)} %self.1.done_ref, bf16[32,4096]{1,0:T(8,128)(2,1)S(1)} %collective-permute-done.2.refs_0_, ...), custom_call_target="tpu_custom_call" | custom-call | flops 1000 | bytes 1000 | tf_op jit(solution)/shard_map/near/pallas_call | solution.py:275
  17.0 0.0 copy-start
  17.0 0.0 copy-start.3
  17.0 0.0 collective-permute-done.4.refs_0_
  17.0 0.0 collective-permute-done.5.refs_1_
  17.0 1.9 %crossed.1.early_ref = bf16[6,16,4096]{2,1,0:T(8,128)(2,1)S(1)} custom-call(bf16[2048,1024]{1,0:T(8,128)(2,1)S(1)} %get-tuple-element.30.left_ref, bf16[768,256]{1,0:T(8,128)(2,1)S(1)} %get-tuple-element.31.right_ref, bf16[4,16,4096]{2,1,0:T(8,128)(2,1)S(1)} %near.1.done_ref, bf16[16,4096]{1,0:T(8,128)(2,1)S(1)} %collective-permute-done.4.refs_0_, ...), custom_call_target="tpu_custom_call" | custom-call | flops 1000 | bytes 1000 | tf_op jit(solution)/shard_map/crossed/pallas_call | solution.py:275
  18.9 1.5 %collective-permute-done.1.late_ref = bf16[2,16,4096]{2,1,0:T(8,128)(2,1)S(1)} collective-permute-done((bf16[2,16,4096]{2,1,0:T(8,128)(2,1)S(1)}, bf16[2,16,4096]{2,1,0:T(8,128)(2,1)S(1)}, u32[]{:S(2)}, u32[]{:S(2)}) %collective-permute-start.1) | collective-permute-done | bytes 262176 | tf_op jit(solution)/shard_map/ppermute | solution.py:218
  20.4 0.0 copy-done
  20.4 0.0 copy-done.3
  20.4 2.0 %last.1 = (f32[24,512]{1,0:T(8,128)S(1)}, bf16[24,512]{1,0:T(8,128)(2,1)S(1)}, bf16[24,512]{1,0:T(8,128)(2,1)S(1)}, bf16[24,512]{1,0:T(8,128)(2,1)S(1)}) custom-call(s32[48]{0:T(128)S(1)} %copy-done.3, bf16[2,16,4096]{2,1,0:T(8,128)(2,1)S(1)} %collective-permute-done.1.late_ref, bf16[6,16,4096]{2,1,0:T(8,128)(2,1)S(1)} %crossed.1.early_ref, ...), custom_call_target="tpu_custom_call" | custom-call | tf_op jit(solution)/shard_map/last/pallas_call | solution.py:284
  22.4 1.6 %collective-permute-start.6 = (bf16[24,512]{1,0:T(8,128)(2,1)S(1)}, bf16[24,512]{1,0:T(8,128)(2,1)S(1)}, u32[]{:S(2)}, u32[]{:S(2)}) collective-permute-start(bf16[24,512]{1,0:T(8,128)(2,1)S(1)} %get-tuple-element.40), channel_id=1, source_target_pairs={{0,8},{8,16},{16,24},{24,0},{1,9},{9,17},{17,25},{25,1},{2,10},{10... | collective-permute-start | bytes 73736 | tf_op jit(solution)/shard_map/ppermute | solution.py:296
  24.1 2.6 %collective-permute-start.7 = (bf16[24,512]{1,0:T(8,128)(2,1)S(1)}, bf16[24,512]{1,0:T(8,128)(2,1)S(1)}, u32[]{:S(2)}, u32[]{:S(2)}) collective-permute-start(bf16[24,512]{1,0:T(8,128)(2,1)S(1)} %get-tuple-element.41), channel_id=1, source_target_pairs={{0,16},{8,24},{16,0},{24,8},{1,17},{9,25},{17,1},{25,9},{2,18},{10... | collective-permute-start | bytes 73736 | tf_op jit(solution)/shard_map/ppermute | solution.py:296
  26.7 1.3 %collective-permute-start.8 = (bf16[24,512]{1,0:T(8,128)(2,1)S(1)}, bf16[24,512]{1,0:T(8,128)(2,1)S(1)}, u32[]{:S(2)}, u32[]{:S(2)}) collective-permute-start(bf16[24,512]{1,0:T(8,128)(2,1)S(1)} %get-tuple-element.42), channel_id=1, source_target_pairs={{0,24},{8,0},{16,8},{24,16},{1,25},{9,1},{17,9},{25,17},{2,26},{10... | collective-permute-start | bytes 73736 | tf_op jit(solution)/shard_map/ppermute | solution.py:296
  28.0 0.4 %collective-permute-done.6.refs_1_ = bf16[24,512]{1,0:T(8,128)(2,1)S(1)} collective-permute-done((bf16[24,512]{1,0:T(8,128)(2,1)S(1)}, bf16[24,512]{1,0:T(8,128)(2,1)S(1)}, u32[]{:S(2)}, u32[]{:S(2)}) %collective-permute-start.6) | collective-permute-done | bytes 24608 | tf_op jit(solution)/shard_map/ppermute | solution.py:296
  28.4 0.4 %collective-permute-done.7.refs_2_ = bf16[24,512]{1,0:T(8,128)(2,1)S(1)} collective-permute-done((bf16[24,512]{1,0:T(8,128)(2,1)S(1)}, bf16[24,512]{1,0:T(8,128)(2,1)S(1)}, u32[]{:S(2)}, u32[]{:S(2)}) %collective-permute-start.7) | collective-permute-done | bytes 24608 | tf_op jit(solution)/shard_map/ppermute | solution.py:296
  28.8 1.7 %collective-permute-done.8.refs_3_ = bf16[24,512]{1,0:T(8,128)(2,1)S(1)} collective-permute-done((bf16[24,512]{1,0:T(8,128)(2,1)S(1)}, bf16[24,512]{1,0:T(8,128)(2,1)S(1)}, u32[]{:S(2)}, u32[]{:S(2)}) %collective-permute-start.8) | collective-permute-done | bytes 24608 | tf_op jit(solution)/shard_map/ppermute | solution.py:296
  30.5 0.6 %finish.1 = f32[6,4,512]{2,1,0:T(4,128)} custom-call(f32[24,512]{1,0:T(8,128)S(1)} %get-tuple-element.39.refs_0_, bf16[24,512]{1,0:T(8,128)(2,1)S(1)} %collective-permute-done.6.refs_1_, bf16[24,512]{1,0:T(8,128)(2,1)S(1)} %collective-permute-done.7.refs_2_, bf16[24,512]{1,0:T(8,128)(2,1)S(1)} %collective-permute-done.8.refs_3_), custom_call_target="tpu_custom_call" | custom-call | tf_op jit(solution)/shard_map/finish/pallas_call | solution.py:298
  (1 shorter events, 0.0 us)
Async XLA Ops:
  0.0 1.0 %copy-start.1 = (bf16[64,1,4096]{2,0,1:T(8,128)(2,1)S(1)}, bf16[64,1,4096]{2,0,1:T(8,128)(2,1)}, u32[]{:S(2)}) copy-start(bf16[64,1,4096]{2,0,1:T(8,128)(2,1)} %param.6) | copy-start | bytes 1572868
  1.0 0.7 %copy-start.2 = (s32[48]{0:T(128)S(1)}, s32[48]{0:T(128)}, u32[]{:S(2)}) copy-start(s32[48]{0:T(128)} %pairs_ref.3) | copy-start | bytes 580
  2.4 3.9 %collective-permute-start = (bf16[32,4096]{1,0:T(8,128)(2,1)S(1)}, bf16[32,4096]{1,0:T(8,128)(2,1)S(1)}, u32[]{:S(2)}, u32[]{:S(2)}) collective-permute-start(bf16[32,4096]{1,0:T(8,128)(2,1)S(1)} %get-tuple-element.28), channel_id=1, source_target_pairs={{0,1},{1,0},{2,3},{3,2},{6,7},{7,6},{4,5},{5,4},{8,9},{9,8},{10,11... | collective-permute-start | bytes 786440 | tf_op jit(solution)/shard_map/ppermute | solution.py:218
  2.9 11.6 %collective-permute-start.2 = (bf16[32,4096]{1,0:T(8,128)(2,1)S(1)}, bf16[32,4096]{1,0:T(8,128)(2,1)S(1)}, u32[]{:S(2)}, u32[]{:S(2)}) collective-permute-start(bf16[32,4096]{1,0:T(8,128)(2,1)S(1)} %get-tuple-element.33), channel_id=1, source_target_pairs={{0,4},{1,5},{2,0},{3,1},{6,2},{7,3},{4,6},{5,7},{8,12},{9,13},{10,... | collective-permute-start | bytes 786440 | tf_op jit(solution)/shard_map/ppermute | solution.py:218
  5.5 9.0 %collective-permute-start.3 = (bf16[32,4096]{1,0:T(8,128)(2,1)S(1)}, bf16[32,4096]{1,0:T(8,128)(2,1)S(1)}, u32[]{:S(2)}, u32[]{:S(2)}) collective-permute-start(bf16[32,4096]{1,0:T(8,128)(2,1)S(1)} %get-tuple-element.34), channel_id=1, source_target_pairs={{0,2},{1,3},{2,6},{3,7},{6,4},{7,5},{4,0},{5,1},{8,10},{9,11},{10,... | collective-permute-start | bytes 786440 | tf_op jit(solution)/shard_map/ppermute | solution.py:218
  9.7 10.7 %collective-permute-start.1 = (bf16[2,16,4096]{2,1,0:T(8,128)(2,1)S(1)}, bf16[2,16,4096]{2,1,0:T(8,128)(2,1)S(1)}, u32[]{:S(2)}, u32[]{:S(2)}) collective-permute-start(bf16[2,16,4096]{2,1,0:T(8,128)(2,1)S(1)} %get-tuple-element.29), channel_id=1, source_target_pairs={{0,6},{1,7},{2,4},{3,5},{6,0},{7,1},{4,2},{5,3},{8,14},{9,15},{10,... | collective-permute-start | bytes 786440 | tf_op jit(solution)/shard_map/ppermute | solution.py:218
  14.5 2.5 %collective-permute-start.4 = (bf16[16,4096]{1,0:T(8,128)(2,1)S(1)}, bf16[16,4096]{1,0:T(8,128)(2,1)S(1)}, u32[]{:S(2)}, u32[]{:S(2)}) collective-permute-start(bf16[16,4096]{1,0:T(8,128)(2,1)S(1)} %get-tuple-element.37), channel_id=1, source_target_pairs={{0,1},{1,0},{2,3},{3,2},{6,7},{7,6},{4,5},{5,4},{8,9},{9,8},{10,11... | collective-permute-start | bytes 393224 | tf_op jit(solution)/shard_map/ppermute | solution.py:218
  14.6 2.4 %collective-permute-start.5 = (bf16[16,4096]{1,0:T(8,128)(2,1)S(1)}, bf16[16,4096]{1,0:T(8,128)(2,1)S(1)}, u32[]{:S(2)}, u32[]{:S(2)}) collective-permute-start(bf16[16,4096]{1,0:T(8,128)(2,1)S(1)} %get-tuple-element.38), channel_id=1, source_target_pairs={{0,1},{1,0},{2,3},{3,2},{6,7},{7,6},{4,5},{5,4},{8,9},{9,8},{10,11... | collective-permute-start | bytes 393224 | tf_op jit(solution)/shard_map/ppermute | solution.py:218
  17.0 3.4 %copy-start = (bf16[512,1,4096]{2,0,1:T(8,128)(2,1)S(1)}, bf16[512,1,4096]{2,0,1:T(8,128)(2,1)}, u32[]{:S(2)}) copy-start(bf16[512,1,4096]{2,0,1:T(8,128)(2,1)} %param.5) | copy-start | bytes 12582916
  17.0 3.4 %copy-start.3 = (s32[48]{0:T(128)S(1)}, s32[48]{0:T(128)}, u32[]{:S(2)}) copy-start(s32[48]{0:T(128)} %pairs_ref.3) | copy-start | bytes 580
  22.4 5.9 %collective-permute-start.6 = (bf16[24,512]{1,0:T(8,128)(2,1)S(1)}, bf16[24,512]{1,0:T(8,128)(2,1)S(1)}, u32[]{:S(2)}, u32[]{:S(2)}) collective-permute-start(bf16[24,512]{1,0:T(8,128)(2,1)S(1)} %get-tuple-element.40), channel_id=1, source_target_pairs={{0,8},{8,16},{16,24},{24,0},{1,9},{9,17},{17,25},{25,1},{2,10},{10... | collective-permute-start | bytes 73736 | tf_op jit(solution)/shard_map/ppermute | solution.py:296
  24.1 4.7 %collective-permute-start.7 = (bf16[24,512]{1,0:T(8,128)(2,1)S(1)}, bf16[24,512]{1,0:T(8,128)(2,1)S(1)}, u32[]{:S(2)}, u32[]{:S(2)}) collective-permute-start(bf16[24,512]{1,0:T(8,128)(2,1)S(1)} %get-tuple-element.41), channel_id=1, source_target_pairs={{0,16},{8,24},{16,0},{24,8},{1,17},{9,25},{17,1},{25,9},{2,18},{10... | collective-permute-start | bytes 73736 | tf_op jit(solution)/shard_map/ppermute | solution.py:296
  26.7 3.8 %collective-permute-start.8 = (bf16[24,512]{1,0:T(8,128)(2,1)S(1)}, bf16[24,512]{1,0:T(8,128)(2,1)S(1)}, u32[]{:S(2)}, u32[]{:S(2)}) collective-permute-start(bf16[24,512]{1,0:T(8,128)(2,1)S(1)} %get-tuple-element.42), channel_id=1, source_target_pairs={{0,24},{8,0},{16,8},{24,16},{1,25},{9,1},{17,9},{25,17},{2,26},{10... | collective-permute-start | bytes 73736 | tf_op jit(solution)/shard_map/ppermute | solution.py:296
